TPU v7x, 32 devices: a whole 2x2x4 slice. The times are simulated.
32 devices in a mesh: dp: 4 (over y, x), seq: 8 (over z, core).
Axes of the slice: x: 2, y: 2, z: 4, core: 2. Of those that a mesh axis runs over, the one named last changes fastest.
Arguments:
- queries: bfloat16 [4, 8, 256, 40, 128], P('dp', 'seq'), may hold values from -6 to 6
- key_proj: bfloat16 [4, 8, 256, 40, 128], P('dp', 'seq'), may hold values from -6 to 6
- value_proj: bfloat16 [4, 8, 256, 40, 128], P('dp', 'seq'), may hold values from -6 to 6
- out_grad: bfloat16 [4, 8, 256, 40, 128], P('dp', 'seq'), may hold values from -6 to 6
- query_gain: float32 [40, 128], P('dp'), may hold values from 0.5 to 5
- key_gain: float32 [40, 128], P('dp'), may hold values from 0.5 to 5
Outputs:
- query_grad: bfloat16 [4, 8, 256, 40, 128], P('dp', 'seq')
- key_grad: bfloat16 [4, 8, 256, 40, 128], P('dp', 'seq')
- value_grad: bfloat16 [4, 8, 256, 40, 128], P('dp', 'seq')
- query_gain_grad: float32 [40, 128], P('dp')
- key_gain_grad: float32 [40, 128], P('dp')
All inputs are finite; a program needn't handle non-finite values.
Results may differ from a plain program's by a relative error of at most 0.0034.
The roundings to bfloat16 on the way count: a program that leaves them out, or rounds other values in their place, can miss the bound.
Values may be sent and summed in bfloat16 or wider, within the bound.
No kernel may reach another device: no remote copies, remote signals or barrier semaphores. Data moves between devices by JAX's collectives and lax.ppermute only.
A program may use at most 128 MiB of HBM per device.

v0:
```python
import math

import jax
import jax.numpy as jnp
from jax import lax
from jax.sharding import PartitionSpec as P

EPSILON = 1e-06


def normalize(values):
    wide = values.astype(jnp.float32)
    inverse = lax.rsqrt(jnp.mean(wide * wide, axis=-1, keepdims=True) + EPSILON)
    return (wide * inverse, inverse)


def norm_back(step, hat, inverse, gain):
    step_wide = step.astype(jnp.float32)
    gained = gain * step_wide
    result = (inverse * (gained - hat * jnp.mean(gained * hat, axis=-1, keepdims=True))).astype(
        jnp.bfloat16
    )
    gain_part = jnp.sum(step_wide * hat, axis=tuple(range(step.ndim - 2)))
    return (result, gain_part)


def attention_grads(query_norm, key_norm, value_in, grad_in):
    frames = query_norm.shape[1]
    scaling = 1.0 / math.sqrt(query_norm.shape[-1])
    scores = (
        jnp.einsum("efphd,egphd->ephfg", query_norm, key_norm, preferred_element_type=jnp.float32)
        * scaling
    )
    row_ids = lax.broadcasted_iota(jnp.int32, (frames, frames), 0)
    col_ids = lax.broadcasted_iota(jnp.int32, (frames, frames), 1)
    allowed = col_ids <= row_ids
    scores = jnp.where(allowed, scores, -jnp.inf)
    largest = jnp.max(scores, axis=-1, keepdims=True)
    expo = jnp.exp(scores - largest)
    probability = expo / jnp.sum(expo, axis=-1, keepdims=True)
    prob_low = probability.astype(jnp.bfloat16)
    attn_out = jnp.einsum(
        "ephfg,egphd->efphd", prob_low, value_in, preferred_element_type=jnp.float32
    )
    row_dots = jnp.transpose(jnp.sum(grad_in.astype(jnp.float32) * attn_out, axis=-1), (0, 2, 3, 1))
    prob_grad = jnp.einsum(
        "efphd,egphd->ephfg", grad_in, value_in, preferred_element_type=jnp.float32
    )
    score_low = (probability * (prob_grad - row_dots[..., None])).astype(jnp.bfloat16)
    query_step = (
        jnp.einsum("ephfg,egphd->efphd", score_low, key_norm, preferred_element_type=jnp.float32)
        * scaling
    ).astype(jnp.bfloat16)
    key_step = (
        jnp.einsum("ephfg,efphd->egphd", score_low, query_norm, preferred_element_type=jnp.float32)
        * scaling
    ).astype(jnp.bfloat16)
    value_step = jnp.einsum(
        "ephfg,efphd->egphd", prob_low, grad_in, preferred_element_type=jnp.float32
    ).astype(jnp.bfloat16)
    return (query_step, key_step, value_step)


def body(queries, key_proj, value_proj, out_grad, query_gain, key_gain):
    query_gains, key_gains = (
        lax.all_gather(query_gain, "dp", axis=0, tiled=True),
        lax.all_gather(key_gain, "dp", axis=0, tiled=True),
    )
    query_hat, query_inverse = normalize(queries)
    key_hat, key_inverse = normalize(key_proj)
    query_norm = (query_hat * query_gains).astype(jnp.bfloat16)
    key_norm = (key_hat * key_gains).astype(jnp.bfloat16)
    pieces = (
        lax.all_to_all(query_norm, "seq", split_axis=2, concat_axis=1, tiled=True),
        lax.all_to_all(key_norm, "seq", split_axis=2, concat_axis=1, tiled=True),
        lax.all_to_all(value_proj, "seq", split_axis=2, concat_axis=1, tiled=True),
        lax.all_to_all(out_grad, "seq", split_axis=2, concat_axis=1, tiled=True),
    )
    query_local, key_local, value_local = attention_grads(
        pieces[0], pieces[1], pieces[2], pieces[3]
    )
    query_step, key_step, value_step = (
        lax.all_to_all(query_local, "seq", split_axis=1, concat_axis=2, tiled=True),
        lax.all_to_all(key_local, "seq", split_axis=1, concat_axis=2, tiled=True),
        lax.all_to_all(value_local, "seq", split_axis=1, concat_axis=2, tiled=True),
    )
    query_grad, query_part = norm_back(query_step, query_hat, query_inverse, query_gains)
    key_grad, key_part = norm_back(key_step, key_hat, key_inverse, key_gains)
    totals = lax.psum((query_part, key_part), "seq")
    query_total, key_total = (
        lax.psum_scatter(totals[0], "dp", scatter_dimension=0, tiled=True),
        lax.psum_scatter(totals[1], "dp", scatter_dimension=0, tiled=True),
    )
    return (query_grad, key_grad, value_step, query_total, key_total)


def solution(mesh):
    in_specs = (
        P("dp", "seq", None, None, None),
        P("dp", "seq", None, None, None),
        P("dp", "seq", None, None, None),
        P("dp", "seq", None, None, None),
        P("dp", None),
        P("dp", None),
    )
    out_specs = (
        P("dp", "seq", None, None, None),
        P("dp", "seq", None, None, None),
        P("dp", "seq", None, None, None),
        P("dp", None),
        P("dp", None),
    )
    return jax.shard_map(body, mesh=mesh, in_specs=in_specs, out_specs=out_specs, check_vma=False)
```

profile of v0, /device:TPU:0, one launch (start us, length us, event | category | flops | bytes accessed | tf_op | source)
XLA Modules:
  0.0 538.4 jit_solution(5384754598689743485)
XLA Ops:
  0.6 3.2 fusion.18
  3.8 9.8 %all-gather.1 = f32[4,10,128]{2,1,0:T(8,128)S(1)} all-gather(f32[1,10,128]{2,1,0:T(8,128)} %bitcast.64), channel_id=1, replica_groups=mesh['dp'=4,'seq'=8] {'dp'}, dimensions={0}, use_global_device_ids=true | all-gather | bytes 25600 | tf_op jit(solution)/shard_map/all_gather | solution.py:67
  13.6 5.0 fusion.25
  18.7 4.9 all-to-all-start
  23.5 8.0 %all-gather = f32[4,10,128]{2,1,0:T(8,128)S(1)} all-gather(f32[1,10,128]{2,1,0:T(8,128)S(1)} %bitcast.65), channel_id=1, replica_groups=mesh['dp'=4,'seq'=8] {'dp'}, dimensions={0}, use_global_device_ids=true | all-gather | bytes 25600 | tf_op jit(solution)/shard_map/all_gather | solution.py:66
  33.0 3.1 fusion.26
  36.2 47.8 %all-to-all-done = bf16[1,1,256,40,128]{4,3,1,0,2:T(8,128)(2,1)} async-done(((bf16[1,1,256,40,128]{4,3,1,0,2:T(8,128)(2,1)}), bf16[1,1,256,40,128]{4,3,1,0,2:T(8,128)(2,1)}, u32[]{:S(2)}, u32[]{:S(2)}) %all-to-all-start) | async-done | bytes 2621472 | tf_op jit(solution)/shard_map/all_to_all | solution.py:75
  83.9 63.8 %all_to_all.31 = bf16[1,1,256,40,128]{4,3,1,0,2:T(8,128)(2,1)S(1)} all-to-all(bf16[1,1,256,40,128]{4,3,1,0,2:T(8,128)(2,1)} %fusion.26), channel_id=1, replica_groups=mesh['dp'=4,'seq'=8] {'seq'}, dimensions={2} | all-to-all | bytes 5242880 | tf_op jit(solution)/shard_map/all_to_all | solution.py:74
  147.8 64.7 %all_to_all.32 = bf16[1,1,256,40,128]{4,3,1,0,2:T(8,128)(2,1)} all-to-all(bf16[1,1,256,40,128]{4,3,1,0,2:T(8,128)(2,1)} %bitcast.62), channel_id=1, replica_groups=mesh['dp'=4,'seq'=8] {'seq'}, dimensions={2} | all-to-all | bytes 5242880 | tf_op jit(solution)/shard_map/all_to_all | solution.py:77
  212.5 4.6 all-to-all-start.3
  217.1 4.4 convert.5
  221.5 4.9 fusion.30
  226.4 5.4 %fusion.47 = (f32[32,40,8]{2,1,0:T(8,128)}, f32[32,40,8,8]{2,3,1,0:T(8,128)}) fusion(f32[32,40,8,8]{2,3,1,0:T(8,128)S(1)} %fusion.30, pred[8,8]{0,1:T(8,128)(4,1)S(1)} %iota_compare_fusion), kind=kOutput, calls=%fused_computation.66 | output fusion | flops 491527 | bytes 696384 | tf_op jit(solution)/shard_map/sub | solution.py:39
  231.8 45.4 %all-to-all-done.3 = bf16[1,1,256,40,128]{4,3,1,0,2:T(8,128)(2,1)} async-done(((bf16[1,1,256,40,128]{4,3,1,0,2:T(8,128)(2,1)}), bf16[1,1,256,40,128]{4,3,1,0,2:T(8,128)(2,1)}, u32[]{:S(2)}, u32[]{:S(2)}) %all-to-all-start.3) | async-done | bytes 2621472 | tf_op jit(solution)/shard_map/all_to_all | solution.py:76
  277.2 10.8 %fusion.21 = f32[8,32,40]{0,2,1:T(8,128)S(1)} fusion(f32[1,8,32,40,128]{4,3,2,1,0:T(8,128)} %convert.5, bf16[8,32,40,128]{3,2,1,0:T(8,128)(2,1)} %bitcast.9, f32[32,40,8,8]{2,3,1,0:T(8,128)} %get-tuple-element.14, f32[32,40,8]{2,1,0:T(8,128)} %get-tuple-element.13), kind=kOutput, calls=%fused_computation.30 | convolution fusion | flops 23746560 | bytes 8273920 | tf_op jit(solution)/shard_map/ephfg,egphd->efphd/dot_general | solution.py:42
  288.0 7.0 %multiply_convert_fusion.2 = bf16[32,40,8,8]{2,3,1,0:T(8,128)(2,1)S(1)} fusion(f32[32,40,8]{2,1,0:T(8,128)S(1)} %bitcast.66, bf16[8,32,40,128]{3,2,1,0:T(8,128)(2,1)} %bitcast.9, bf16[8,32,40,128]{3,2,1,0:T(8,128)(2,1)S(1)} %bitcast.61, f32[32,40,8,8]{2,3,1,0:T(8,128)} %get-tuple-element.14, f32[32,40,8]{2,1,0:T(8,128)S(1)} %copy-done.9), kind=kOutput, calls=%fused_computation.33 | convolution fusion | flops 21299200 | bytes 5816320 | tf_op jit(solution)/shard_map/efphd,egphd->ephfg/dot_general | solution.py:46
  295.1 2.2 fusion.24
  299.2 3.6 all-to-all-start.5
  302.8 4.3 fusion.23
  309.0 54.0 %all-to-all-done.5 = bf16[1,8,32,40,128]{4,3,2,0,1:T(8,128)(2,1)S(1)} async-done(((bf16[1,8,32,40,128]{4,3,2,0,1:T(8,128)(2,1)}), bf16[1,8,32,40,128]{4,3,2,0,1:T(8,128)(2,1)S(1)}, u32[]{:S(2)}, u32[]{:S(2)}) %all-to-all-start.5) | async-done | bytes 2621472 | tf_op jit(solution)/shard_map/all_to_all | solution.py:84
  363.0 4.4 all-to-all-start.4
  367.4 5.6 %convert_bitcast_fusion = bf16[1,8,32,40,128]{4,1,3,2,0:T(8,128)(2,1)S(1)} fusion(bf16[8,32,40,128]{3,2,1,0:T(8,128)(2,1)} %bitcast.60, f32[32,40,8,8]{2,3,1,0:T(8,128)} %get-tuple-element.14, f32[32,40,8]{2,1,0:T(8,128)} %get-tuple-element.13), kind=kOutput, calls=%fused_computation.41 | convolution fusion | flops 22446080 | bytes 5611520 | tf_op jit(solution)/shard_map/ephfg,efphd->egphd/dot_general | solution.py:58
  375.1 52.7 %all-to-all-done.4 = bf16[1,8,32,40,128]{4,3,2,0,1:T(8,128)(2,1)} async-done(((bf16[1,8,32,40,128]{4,3,2,0,1:T(8,128)(2,1)}), bf16[1,8,32,40,128]{4,3,2,0,1:T(8,128)(2,1)}, u32[]{:S(2)}, u32[]{:S(2)}) %all-to-all-start.4) | async-done | bytes 2621472 | tf_op jit(solution)/shard_map/all_to_all | solution.py:83
  427.7 4.6 all-to-all-start.6
  433.7 5.2 fusion.20
  438.9 5.1 fusion.19
  444.1 5.0 fusion.10
  449.1 6.2 %fusion.12 = bf16[1,1,256,40,128]{4,3,2,1,0:T(8,128)(2,1)} fusion(bf16[1,1,256,40,128]{4,3,2,1,0:T(8,128)(2,1)} %bitcast.30, bf16[1,1,256,40,128]{4,3,2,1,0:T(8,128)(2,1)S(1)} %copy-done.2, f32[256,40]{1,0:T(8,128)S(1)} %broadcast_multiply_fusion.1, f32[40,128]{1,0:T(8,128)S(1)} %reshape.217, f32[256,40]{1,0:T(8,128)S(1)} %add_rsqrt_fusion.1), kind=kLoop, calls=%fused_computation.20 | loop fusion | flops 10485760 | bytes 7966720 | tf_op jit(solution)/shard_map/convert_element_type | solution.py:20
  455.2 37.2 %all-to-all-done.6 = bf16[1,8,32,40,128]{4,3,2,0,1:T(8,128)(2,1)} async-done(((bf16[1,8,32,40,128]{4,3,2,0,1:T(8,128)(2,1)}), bf16[1,8,32,40,128]{4,3,2,0,1:T(8,128)(2,1)}, u32[]{:S(2)}, u32[]{:S(2)}) %all-to-all-start.6) | async-done | bytes 2621472 | tf_op jit(solution)/shard_map/all_to_all | solution.py:85
  492.4 15.8 %all-reduce.3 = (f32[40,128]{1,0:T(8,128)S(1)}, f32[40,128]{1,0:T(8,128)S(1)}) all-reduce(f32[40,128]{1,0:T(8,128)S(1)} %get-tuple-element.7, f32[40,128]{1,0:T(8,128)S(1)} %get-tuple-element.5), channel_id=2, replica_groups=mesh['dp'=4,'seq'=8] {'dp'}, use_global_device_ids=true, to_apply=%region_9.10.clone | all-reduce | flops 10240 | bytes 81920
  508.2 26.5 %all-reduce.2 = (f32[10,128]{1,0:T(8,128)}, f32[10,128]{1,0:T(8,128)}) all-reduce(f32[10,128]{1,0:T(8,128)S(1)} %get-tuple-element.16, f32[10,128]{1,0:T(8,128)S(1)} %get-tuple-element.15), channel_id=1, replica_groups=mesh['dp'=4,'seq'=8] {'seq'}, use_global_device_ids=true, to_apply=%region_8.9 | all-reduce | flops 2560 | bytes 20480 | tf_op jit(solution)/shard_map/psum | solution.py:89
  534.7 3.7 copy.74
  (33 shorter events, 7.9 us)
Async XLA Ops:
  13.6 9.9 %copy-start.7 = (f32[10,128]{1,0:T(8,128)S(1)}, f32[10,128]{1,0:T(8,128)}, u32[]{:S(2)}) copy-start(f32[10,128]{1,0:T(8,128)} %param.10) | copy-start | bytes 15364
  13.6 17.9 %copy-start.1 = (bf16[1,1,256,40,128]{4,3,2,1,0:T(8,128)(2,1)S(1)}, bf16[1,1,256,40,128]{4,3,2,1,0:T(8,128)(2,1)}, u32[]{:S(2)}) copy-start(bf16[1,1,256,40,128]{4,3,2,1,0:T(8,128)(2,1)} %param.6) | copy-start | bytes 7864324
  18.7 65.3 %all-to-all-start = ((bf16[1,1,256,40,128]{4,3,1,0,2:T(8,128)(2,1)}), bf16[1,1,256,40,128]{4,3,1,0,2:T(8,128)(2,1)}, u32[]{:S(2)}, u32[]{:S(2)}) async-start(bf16[1,1,256,40,128]{4,3,1,0,2:T(8,128)(2,1)} %fusion.25), calls=%async_computation | async-start | bytes 5242880 | tf_op jit(solution)/shard_map/all_to_all | solution.py:75
  212.5 64.7 %all-to-all-start.3 = ((bf16[1,1,256,40,128]{4,3,1,0,2:T(8,128)(2,1)}), bf16[1,1,256,40,128]{4,3,1,0,2:T(8,128)(2,1)}, u32[]{:S(2)}, u32[]{:S(2)}) async-start(bf16[1,1,256,40,128]{4,3,1,0,2:T(8,128)(2,1)} %bitcast.63), calls=%async_computation.3 | async-start | bytes 5242880 | tf_op jit(solution)/shard_map/all_to_all | solution.py:76
  277.2 10.8 %copy-start.5 = (bf16[1,1,256,40,128]{4,3,1,0,2:T(8,128)(2,1)S(1)}, bf16[1,1,256,40,128]{4,3,1,0,2:T(8,128)(2,1)}, u32[]{:S(2)}) copy-start(bf16[1,1,256,40,128]{4,3,1,0,2:T(8,128)(2,1)} %all_to_all.32) | copy-start | bytes 7864324
  277.2 10.8 %copy-start.9 = (f32[32,40,8]{2,1,0:T(8,128)S(1)}, f32[32,40,8]{2,1,0:T(8,128)}, u32[]{:S(2)}) copy-start(f32[32,40,8]{2,1,0:T(8,128)} %get-tuple-element.13) | copy-start | bytes 122884
  295.1 2.2 copy-start.6
  299.2 63.9 %all-to-all-start.5 = ((bf16[1,8,32,40,128]{4,3,2,0,1:T(8,128)(2,1)}), bf16[1,8,32,40,128]{4,3,2,0,1:T(8,128)(2,1)S(1)}, u32[]{:S(2)}, u32[]{:S(2)}) async-start(bf16[1,8,32,40,128]{4,3,2,0,1:T(8,128)(2,1)} %copy.47), calls=%async_computation.5 | async-start | bytes 5242880 | tf_op jit(solution)/shard_map/all_to_all | solution.py:84
  363.0 4.4 copy-start.3
  363.0 64.7 %all-to-all-start.4 = ((bf16[1,8,32,40,128]{4,3,2,0,1:T(8,128)(2,1)}), bf16[1,8,32,40,128]{4,3,2,0,1:T(8,128)(2,1)}, u32[]{:S(2)}, u32[]{:S(2)}) async-start(bf16[1,8,32,40,128]{4,3,2,0,1:T(8,128)(2,1)} %copy.44), calls=%async_computation.4 | async-start | bytes 5242880 | tf_op jit(solution)/shard_map/all_to_all | solution.py:83
  373.1 59.3 %copy-start.8 = (u32[32]{0:T(128)S(1)}, u32[32]{0:T(128)}, u32[]{:S(2)}) copy-start(u32[32]{0:T(128)} %constant.23) | copy-start | bytes 388
  373.1 60.5 %copy-start = (bf16[1,1,256,40,128]{4,3,2,1,0:T(8,128)(2,1)S(1)}, bf16[1,1,256,40,128]{4,3,2,1,0:T(8,128)(2,1)}, u32[]{:S(2)}) copy-start(bf16[1,1,256,40,128]{4,3,2,1,0:T(8,128)(2,1)} %param.7) | copy-start | bytes 7864324
  427.7 64.7 %all-to-all-start.6 = ((bf16[1,8,32,40,128]{4,3,2,0,1:T(8,128)(2,1)}), bf16[1,8,32,40,128]{4,3,2,0,1:T(8,128)(2,1)}, u32[]{:S(2)}, u32[]{:S(2)}) async-start(bf16[1,8,32,40,128]{4,3,2,0,1:T(8,128)(2,1)} %copy.50), calls=%async_computation.6 | async-start | bytes 5242880 | tf_op jit(solution)/shard_map/all_to_all | solution.py:85
  433.6 5.3 copy-start.2
  433.7 10.4 %copy-start.4 = (bf16[1,8,32,40,128]{4,3,2,0,1:T(8,128)(2,1)S(1)}, bf16[1,8,32,40,128]{4,3,2,0,1:T(8,128)(2,1)}, u32[]{:S(2)}) copy-start(bf16[1,8,32,40,128]{4,3,2,0,1:T(8,128)(2,1)} %copy-done.3) | copy-start | bytes 7864324
where the time goes:
time: 540 us; the launch traced here: 538 us
  waiting for transfers between devices  237 us (44%)
  blocking collectives  189 us (35%)
  other arithmetic  44.2 us (8%)
  matrix products  34.8 us (6%)
  starting transfers between devices  22.1 us (4%)
  local copies, waits for them, and re-layouts  10.1 us (2%)
    all_to_all x1, blocking collectives, body(): lax.all_to_all(out_grad, 'seq', split_axis=2, concat_axis=1, tiled=True)  64.7 us
    all_to_all x1, blocking collectives, body(): lax.all_to_all(query_norm, 'seq', split_axis=2, concat_axis=1, tiled=True)  63.8 us
    all_to_all x1, waiting for transfers between devices, body(): lax.all_to_all(key_local, 'seq', split_axis=1, concat_axis=2, tiled=True)  54 us
    all_to_all x1, waiting for transfers between devices, body(): lax.all_to_all(query_local, 'seq', split_axis=1, concat_axis=2, tiled=True)  52.7 us
    all_to_all x1, waiting for transfers between devices, body(): lax.all_to_all(key_norm, 'seq', split_axis=2, concat_axis=1, tiled=True)  47.8 us
    all_to_all x1, waiting for transfers between devices, body(): lax.all_to_all(value_proj, 'seq', split_axis=2, concat_axis=1, tiled=True)  45.4 us
    all_to_all x1, waiting for transfers between devices, body(): lax.all_to_all(value_local, 'seq', split_axis=1, concat_axis=2, tiled=True)  37.2 us
    psum x1, blocking collectives, body(): totals = lax.psum((query_part, key_part), 'seq')  26.5 us
  transfers between devices with their start and end apart: 5, of which 5 were waited for; matrix products, arithmetic and copies ran while one was open for 10% of the time, Pallas kernels for 0%

commit v1 on v0

v1 whole, which is shorter than its diff:
```python
import functools
import math

import jax
import jax.numpy as jnp
from jax import lax
from jax.experimental import pallas as pl
from jax.experimental.pallas import tpu as pltpu
from jax.sharding import PartitionSpec as P

EPSILON = 1e-06
BLOCK = 256
GROUP = 16
SLOTS = 4
WIDE = GROUP * SLOTS
CUTS = (5, 5, 5, 5)

EDGE_S = ((0, 2), (1, 3), (6, 4), (7, 5))
EDGE_X = ((0, 3), (1, 2), (6, 5), (7, 4))
INTRA = ((2, 3), (3, 2), (4, 5), (5, 4))
MID_S = ((2, 4), (3, 5), (4, 2), (5, 3))
MID_X = ((2, 5), (3, 4), (4, 3), (5, 2))
DOWN = ((4, 2), (5, 3))
BACK_S = tuple((b, a) for a, b in EDGE_S)
BACK_X = tuple((b, a) for a, b in EDGE_X)

F32 = jnp.float32
BF16 = jnp.bfloat16
ANY = pl.BlockSpec(memory_space=pl.ANY)
VMEM = pl.BlockSpec(memory_space=pltpu.VMEM)


def place():
    index = lax.axis_index("seq")
    chip, core = index // 2, index % 2
    return chip, core


def pack_kernel(start, rows, q, k, v, g, a_s, a_x, b_s, b_x, sems):
    chip, core = place()

    def move(first, second):
        for left, right in ((first, (a_s, a_x)), (second, (b_s, b_x))):
            for t in range(2):
                for x in range(2):
                    half = core if x == 0 else 1 - core
                    yield left[t].at[half, pl.ds(start, rows)], right[x].at[t]

    def run(first, second):
        copies = [
            pltpu.make_async_copy(src, dst, sems.at[i])
            for i, (src, dst) in enumerate(move(first, second))
        ]
        for copy in copies:
            copy.start()
        for copy in copies:
            copy.wait()

    @pl.when(chip < 2)
    def _():
        run((k, v), (q, g))

    @pl.when(chip >= 2)
    def _():
        run((q, g), (k, v))


def pack(start, rows, arrays):
    return pl.pallas_call(
        functools.partial(pack_kernel, start, rows),
        out_shape=[jax.ShapeDtypeStruct((2, rows, 128), BF16)] * 4,
        in_specs=[ANY] * 4,
        out_specs=[ANY] * 4,
        scratch_shapes=[pltpu.SemaphoreType.DMA((8,))],
        cost_estimate=pl.CostEstimate(flops=0, bytes_accessed=rows * 128 * 2 * 16, transcendentals=0),
        name="pack_rows",
    )(*arrays)


def place_kernel(start, rows, own, other, back_s, back_x, *refs):
    outs, sems = refs[-4:-1], refs[-1]
    chip, core = place()

    def run(near, far):
        copies = []
        for t in range(3):
            for x, src in enumerate((near, far)):
                half = core if x == 0 else 1 - core
                copies.append(
                    pltpu.make_async_copy(
                        src.at[t], outs[t].at[half, pl.ds(start, rows)], sems.at[t * 2 + x]
                    )
                )
        for copy in copies:
            copy.start()
        for copy in copies:
            copy.wait()

    hub = (chip == 1) | (chip == 2)

    @pl.when(hub)
    def _():
        run(own, other)

    @pl.when(jnp.logical_not(hub))
    def _():
        run(back_s, back_x)


def unpack(start, rows, half, pieces, outs):
    first = outs is None
    outs = () if first else outs
    return pl.pallas_call(
        functools.partial(place_kernel, start, rows),
        out_shape=[jax.ShapeDtypeStruct((2, half, 128), BF16)] * 3,
        in_specs=[ANY] * (4 + len(outs)),
        out_specs=[ANY] * 3,
        scratch_shapes=[pltpu.SemaphoreType.DMA((6,))],
        input_output_aliases={} if first else {4: 0, 5: 1, 6: 2},
        cost_estimate=pl.CostEstimate(flops=0, bytes_accessed=rows * 128 * 2 * 12, transcendentals=0),
        name="place_rows",
    )(*pieces, *outs)


def rms(values):
    wide = values.astype(F32)
    inverse = lax.rsqrt(jnp.mean(wide * wide, axis=-1, keepdims=True) + EPSILON)
    return wide * inverse, inverse


def norm_back(step, hat, inverse, gain):
    wide = step.astype(F32)
    gained = gain * wide
    result = inverse * (gained - hat * jnp.mean(gained * hat, axis=-1, keepdims=True))
    return result.astype(BF16), wide * hat


def mul_t(a, b):
    return lax.dot_general(a, b, (((1,), (1,)), ((), ())), preferred_element_type=F32)


def t_mul(a, b):
    return lax.dot_general(a, b, (((0,), (0,)), ((), ())), preferred_element_type=F32)


def mul(a, b):
    return jnp.dot(a, b, preferred_element_type=F32)


def iota(shape, axis):
    return lax.broadcasted_iota(jnp.int32, shape, axis)


def attend(qn, kn, grad, value, allowed):
    scaling = 1.0 / math.sqrt(qn.shape[-1])
    scores = jnp.where(allowed, mul_t(qn, kn) * scaling, -jnp.inf)
    expo = jnp.exp(scores - jnp.max(scores, axis=-1, keepdims=True))
    prob = expo / jnp.sum(expo, axis=-1, keepdims=True)
    prob_low = prob.astype(BF16)
    prob_grad = mul_t(grad, value)
    dots = jnp.sum(prob_low.astype(F32) * prob_grad, axis=-1, keepdims=True)
    score_low = (prob * (prob_grad - dots)).astype(BF16)
    return prob_low, score_low


def frame_of(slot, core, upper):
    cross = slot % 2
    side = slot // 2
    side = side if upper else 1 - side
    return 2 * side + cross + core - 2 * cross * core


def causal(core, upper):
    shape = (WIDE, 2 * WIDE if upper else WIDE)
    rows, cols = iota(shape, 0), iota(shape, 1)
    key = cols // GROUP
    frame = frame_of(key % SLOTS, core, upper)
    if upper:
        frame = jnp.where(key < SLOTS, -1, frame)
    late = frame <= frame_of(rows // GROUP, core, upper)
    return (rows % GROUP == cols % GROUP) & late


def cat(parts):
    return jnp.concatenate(parts, axis=0)


def gains_of(ref, base, j):
    gain = ref[pl.ds(pl.multiple_of(base + j * GROUP, GROUP), GROUP), :]
    return cat([gain] * SLOTS)


def fold(acc, base, j, part):
    rows = pl.ds(pl.multiple_of(base + j * GROUP, GROUP), GROUP)
    total = part[:GROUP]
    for t in range(1, SLOTS):
        total = total + part[t * GROUP : (t + 1) * GROUP]
    acc[rows, :] += total


def settle(outs, rows, parts):
    for t, part in enumerate(parts):
        for s, out in enumerate(outs):
            out[t, rows, :] = part[s * GROUP : (s + 1) * GROUP]


def sum_heads(acc, heads):
    total = acc[0:heads, :]
    for i in range(1, acc.shape[0] // heads):
        total = total + acc[i * heads : (i + 1) * heads, :]
    return total


def upper_kernel(first, steps, heads, *refs):
    data, (gain_q, gain_k), outs = refs[:12], refs[12:14], refs[14:18]
    packed, sum_q, sum_k, acc_q, acc_k = refs[18:]
    chip, core = place()
    acc_q[...] = jnp.zeros_like(acc_q)
    acc_k[...] = jnp.zeros_like(acc_k)
    cycle = acc_q.shape[0] // BLOCK

    def block(*blocks):
        a, b, m = blocks[0:4], blocks[4:8], blocks[8:12]
        out, pack_ref = blocks[12:16], blocks[16]
        base = ((first + pl.program_id(0)) % cycle) * BLOCK
        allowed = causal(core, True)
        scaling = 1.0 / math.sqrt(128)
        lanes = iota((WIDE, 128), 1) // 8
        spread_r, spread_c = iota((2 * WIDE, 128), 0), iota((2 * WIDE, 128), 1)
        spread = jnp.where(spread_r // GROUP == spread_c % 8, 1.0, 0.0).astype(BF16)

        def group(j, total):
            rows = pl.ds(pl.multiple_of(j * GROUP, GROUP), GROUP)
            gq, gk = gains_of(gain_q, base, j), gains_of(gain_k, base, j)
            q_hat, q_inv = rms(cat([r[0, rows, :] for r in a]))
            grad = cat([r[1, rows, :] for r in a])
            kl_hat, _ = rms(cat([r[0, rows, :] for r in m]))
            ku_hat, ku_inv = rms(cat([r[0, rows, :] for r in b]))
            value = cat([r[1, rows, :] for r in (*m, *b)])
            qn = (q_hat * gq).astype(BF16)
            kn = cat([(kl_hat * gk).astype(BF16), (ku_hat * gk).astype(BF16)])
            prob, score = attend(qn, kn, grad, value, allowed)
            q_step = (mul(score, kn) * scaling).astype(BF16)
            k_step = (t_mul(score[:, WIDE:], qn) * scaling).astype(BF16)
            v_step = t_mul(prob[:, WIDE:], grad).astype(BF16)
            dq, part_q = norm_back(q_step, q_hat, q_inv, gq)
            dk, part_k = norm_back(k_step, ku_hat, ku_inv, gk)
            settle(out, rows, (dq, dk, v_step))
            fold(acc_q, base, j, part_q)
            fold(acc_k, base, j, part_k)
            cross = jnp.concatenate([prob[:, :WIDE], score[:, :WIDE]], axis=1)
            return jnp.where(lanes == j, mul(cross, spread), total)

        total = lax.fori_loop(0, BLOCK // GROUP, group, jnp.zeros((WIDE, 128), F32))
        pack_ref[0] = total.astype(BF16)

    @pl.when(chip == 2)
    def _():
        pltpu.emit_pipeline(
            block,
            grid=(steps,),
            in_specs=[pl.BlockSpec((2, BLOCK, 128), lambda i: (0, i, 0))] * 12,
            out_specs=[pl.BlockSpec((3, BLOCK, 128), lambda i: (0, i, 0))] * 4
            + [pl.BlockSpec((1, WIDE, 128), lambda i: (i, 0, 0))],
        )(*data, *outs, packed)

    sum_q[...] = sum_heads(acc_q, heads)
    sum_k[...] = sum_heads(acc_k, heads)


def lower_kernel(first, steps, heads, *refs):
    data, packed, (gain_q, gain_k) = refs[:12], refs[12], refs[13:15]
    outs = refs[19:23]
    sum_q, sum_k, acc_q, acc_k = refs[23:]
    chip, core = place()
    acc_q[...] = jnp.zeros_like(acc_q)
    acc_k[...] = jnp.zeros_like(acc_k)
    cycle = acc_q.shape[0] // BLOCK

    def block(*blocks):
        a, b, m = blocks[0:4], blocks[4:8], blocks[8:12]
        pack_ref, out = blocks[12], blocks[13:17]
        base = ((first + pl.program_id(0)) % cycle) * BLOCK
        allowed = causal(core, False)
        both = iota((WIDE, 2 * WIDE), 0) % GROUP == iota((WIDE, 2 * WIDE), 1) % GROUP
        scaling = 1.0 / math.sqrt(128)
        lanes = iota((WIDE, 128), 1) // 8
        spread_r, spread_c = iota((128, 2 * WIDE), 0), iota((128, 2 * WIDE), 1)
        spread = jnp.where(spread_c // GROUP == spread_r % 8, 1.0, 0.0).astype(BF16)
        crossed = pack_ref[0].astype(F32)

        def group(j, carry):
            rows = pl.ds(pl.multiple_of(j * GROUP, GROUP), GROUP)
            gq, gk = gains_of(gain_q, base, j), gains_of(gain_k, base, j)
            k_hat, k_inv = rms(cat([r[0, rows, :] for r in a]))
            value = cat([r[1, rows, :] for r in a])
            q_hat, q_inv = rms(cat([r[0, rows, :] for r in b]))
            grad = cat([r[1, rows, :] for r in b])
            qu_hat, _ = rms(cat([r[0, rows, :] for r in m]))
            grad_u = cat([r[1, rows, :] for r in m])
            kn = (k_hat * gk).astype(BF16)
            qn = (q_hat * gq).astype(BF16)
            qn_u = (qu_hat * gq).astype(BF16)
            prob, score = attend(qn, kn, grad, value, allowed)
            mine = jnp.where(lanes == j, crossed, 0.0).astype(BF16)
            cross = jnp.where(both, mul(mine, spread), 0.0).astype(BF16)
            q_step = (mul(score, kn) * scaling).astype(BF16)
            k_step = t_mul(cat([score, cross[:, WIDE:]]), cat([qn, qn_u]))
            k_step = (k_step * scaling).astype(BF16)
            v_step = t_mul(cat([prob, cross[:, :WIDE]]), cat([grad, grad_u])).astype(BF16)
            dq, part_q = norm_back(q_step, q_hat, q_inv, gq)
            dk, part_k = norm_back(k_step, k_hat, k_inv, gk)
            settle(out, rows, (dq, dk, v_step))
            fold(acc_q, base, j, part_q)
            fold(acc_k, base, j, part_k)
            return carry

        lax.fori_loop(0, BLOCK // GROUP, group, 0)

    @pl.when(chip == 1)
    def _():
        pltpu.emit_pipeline(
            block,
            grid=(steps,),
            in_specs=[pl.BlockSpec((2, BLOCK, 128), lambda i: (0, i, 0))] * 12
            + [pl.BlockSpec((1, WIDE, 128), lambda i: (i, 0, 0))],
            out_specs=[pl.BlockSpec((3, BLOCK, 128), lambda i: (0, i, 0))] * 4,
        )(*data, packed, *outs)

    sum_q[...] = sum_heads(acc_q, heads)
    sum_k[...] = sum_heads(acc_k, heads)


def hub_cost(rows):
    return pl.CostEstimate(
        flops=rows * 60000, bytes_accessed=rows * 128 * 2 * 36, transcendentals=rows * 600
    )


def upper(first, steps, heads, data, gains):
    rows = steps * BLOCK
    cycle = gains[0].shape[0]
    return pl.pallas_call(
        functools.partial(upper_kernel, first, steps, heads),
        out_shape=[jax.ShapeDtypeStruct((3, rows, 128), BF16)] * 4
        + [jax.ShapeDtypeStruct((steps, WIDE, 128), BF16)]
        + [jax.ShapeDtypeStruct((heads, 128), F32)] * 2,
        in_specs=[ANY] * 12 + [VMEM] * 2,
        out_specs=[ANY] * 5 + [VMEM] * 2,
        scratch_shapes=[pltpu.VMEM((cycle, 128), F32)] * 2,
        compiler_params=pltpu.CompilerParams(vmem_limit_bytes=40 * 1024 * 1024),
        cost_estimate=hub_cost(rows),
        name="upper_frames",
    )(*data, *gains)


def lower(first, steps, heads, data, packed, gains, outs):
    rows = steps * BLOCK
    cycle = gains[0].shape[0]
    return pl.pallas_call(
        functools.partial(lower_kernel, first, steps, heads),
        out_shape=[jax.ShapeDtypeStruct((3, rows, 128), BF16)] * 4
        + [jax.ShapeDtypeStruct((heads, 128), F32)] * 2,
        in_specs=[ANY] * 13 + [VMEM] * 2 + [ANY] * 4,
        out_specs=[ANY] * 4 + [VMEM] * 2,
        scratch_shapes=[pltpu.VMEM((cycle, 128), F32)] * 2,
        input_output_aliases={15 + i: i for i in range(4)},
        compiler_params=pltpu.CompilerParams(vmem_limit_bytes=40 * 1024 * 1024),
        cost_estimate=hub_cost(rows),
        name="lower_frames",
    )(*data, packed, *gains, *outs)


def send(array, pairs):
    return lax.ppermute(array, "seq", pairs)


def hub_body(queries, key_proj, value_proj, out_grad, query_gain, key_gain):
    shape = queries.shape
    heads, width = shape[-2:]
    half = shape[2] // 2 * heads
    arrays = [x.reshape(2, half, width) for x in (queries, key_proj, value_proj, out_grad)]
    cycle = math.lcm(BLOCK, heads)
    both = lax.all_gather(jnp.stack([query_gain, key_gain]), "dp", axis=1, tiled=True)
    gains = [jnp.tile(both[t], (cycle // heads, 1)) for t in range(2)]

    outs = None
    sums = []
    starts = [sum(CUTS[:i]) for i in range(len(CUTS))]
    landed = []
    for first, steps in zip(starts, CUTS):
        rows = steps * BLOCK
        a_s, a_x, b_s, b_x = pack(first * BLOCK, rows, arrays)
        ea_s, ea_x = send(a_s, EDGE_S), send(a_x, EDGE_X)
        m_s, m_x = send(a_s, MID_S), send(a_x, MID_X)
        eb_s, eb_x = send(b_s, EDGE_S), send(b_x, EDGE_X)
        a_i, b_i = send(a_x, INTRA), send(b_x, INTRA)
        n_s, n_x = send(ea_s, MID_S), send(ea_x, MID_S)
        landed.append([a_s, a_i, ea_s, ea_x, b_s, b_i, eb_s, eb_x, m_s, m_x, n_s, n_x])
    for first, steps, data in zip(starts, CUTS, landed):
        rows = steps * BLOCK
        *grads, packed, sum_q, sum_k = upper(first, steps, heads, data, gains)
        sums.append((sum_q, sum_k))
        packed = send(packed, DOWN)
        *grads, sum_q, sum_k = lower(first, steps, heads, data, packed, gains, grads)
        sums.append((sum_q, sum_k))
        own, other, edge_s, edge_x = grads
        pieces = (own, send(other, INTRA), send(edge_s, BACK_S), send(edge_x, BACK_X))
        outs = unpack(first * BLOCK, rows, half, pieces, outs)

    totals = [functools.reduce(jnp.add, [s[t] for s in sums]) for t in range(2)]
    totals = lax.psum(jnp.stack(totals), ("dp", "seq"))
    mine = query_gain.shape[0]
    totals = lax.dynamic_slice_in_dim(totals, lax.axis_index("dp") * mine, mine, 1)
    return (*[x.reshape(shape) for x in outs], totals[0], totals[1])


def wide_attention(query_norm, key_norm, value_in, grad_in):
    frames = query_norm.shape[1]
    scaling = 1.0 / math.sqrt(query_norm.shape[-1])
    scores = (
        jnp.einsum("efphd,egphd->ephfg", query_norm, key_norm, preferred_element_type=F32) * scaling
    )
    allowed = iota((frames, frames), 1) <= iota((frames, frames), 0)
    scores = jnp.where(allowed, scores, -jnp.inf)
    expo = jnp.exp(scores - jnp.max(scores, axis=-1, keepdims=True))
    probability = expo / jnp.sum(expo, axis=-1, keepdims=True)
    prob_low = probability.astype(BF16)
    attn_out = jnp.einsum("ephfg,egphd->efphd", prob_low, value_in, preferred_element_type=F32)
    row_dots = jnp.transpose(jnp.sum(grad_in.astype(F32) * attn_out, axis=-1), (0, 2, 3, 1))
    prob_grad = jnp.einsum("efphd,egphd->ephfg", grad_in, value_in, preferred_element_type=F32)
    score_low = (probability * (prob_grad - row_dots[..., None])).astype(BF16)
    query_step = jnp.einsum("ephfg,egphd->efphd", score_low, key_norm, preferred_element_type=F32)
    key_step = jnp.einsum("ephfg,efphd->egphd", score_low, query_norm, preferred_element_type=F32)
    value_step = jnp.einsum("ephfg,efphd->egphd", prob_low, grad_in, preferred_element_type=F32)
    return (
        (query_step * scaling).astype(BF16),
        (key_step * scaling).astype(BF16),
        value_step.astype(BF16),
    )


def wide_body(queries, key_proj, value_proj, out_grad, query_gain, key_gain):
    gain_q = lax.all_gather(query_gain, "dp", axis=0, tiled=True)
    gain_k = lax.all_gather(key_gain, "dp", axis=0, tiled=True)
    q_hat, q_inv = rms(queries)
    k_hat, k_inv = rms(key_proj)
    pieces = [
        lax.all_to_all(x, "seq", split_axis=2, concat_axis=1, tiled=True)
        for x in ((q_hat * gain_q).astype(BF16), (k_hat * gain_k).astype(BF16), value_proj, out_grad)
    ]
    steps = [
        lax.all_to_all(x, "seq", split_axis=1, concat_axis=2, tiled=True)
        for x in wide_attention(*pieces)
    ]
    query_grad, part_q = norm_back(steps[0], q_hat, q_inv, gain_q)
    key_grad, part_k = norm_back(steps[1], k_hat, k_inv, gain_k)
    axes = tuple(range(part_q.ndim - 2))
    totals = lax.psum((jnp.sum(part_q, axis=axes), jnp.sum(part_k, axis=axes)), "seq")
    totals = [lax.psum_scatter(t, "dp", scatter_dimension=0, tiled=True) for t in totals]
    return (query_grad, key_grad, steps[2], *totals)


def body(*args):
    frames = lax.axis_size("seq")
    patches, heads, width = args[0].shape[2:]
    rows = patches // 2 * heads
    if frames == 8 and args[0].shape[:2] == (1, 1) and width == 128 and rows == sum(CUTS) * BLOCK:
        return hub_body(*args)
    return wide_body(*args)


def solution(mesh):
    whole = P("dp", "seq", None, None, None)
    gain = P("dp", None)
    return jax.shard_map(
        body,
        mesh=mesh,
        in_specs=(whole,) * 4 + (gain,) * 2,
        out_specs=(whole,) * 3 + (gain,) * 2,
        check_vma=False,
    )
```

time: 540 us -> 1340 us (2.48)
  Pallas kernels: 0 us -> 567 us
  waiting for transfers between devices: 237 us -> 480 us
  starting transfers between devices: 22.1 us -> 95.7 us
  other arithmetic: 44.2 us -> 0.05 us
  blocking collectives: 189 us -> 145 us
  matrix products: 34.8 us -> 0 us
  local copies, waits for them, and re-layouts: 10.1 us -> 43.2 us
    pallas_call x0 -> x16, Pallas kernels: none -> 567 us  [the longest x4 322 us: pack(): pl.pallas_call(functools.partial(pack_kernel, start, rows), out_shape=[ja...]
    ppermute x0 -> x56, waiting for transfers between devices: none -> 480 us  [send(): return lax.ppermute(array, 'seq', pairs)]
    all_to_all x5 -> x0, waiting for transfers between devices: 237 us -> none  [the longest x1 54 us: body(): lax.all_to_all(key_local, 'seq', split_axis=1, concat_axis=2, tiled=True)]
    all_to_all x2 -> x0, blocking collectives: 129 us -> none  [the longest x1 64.7 us: body(): lax.all_to_all(out_grad, 'seq', split_axis=2, concat_axis=1, tiled=True)]
    psum x1, blocking collectives: 26.5 us -> 137 us  [hub_body(): totals = lax.psum(jnp.stack(totals), ('dp', 'seq'))]
    ppermute x0 -> x56, starting transfers between devices: none -> 95.7 us  [send(): return lax.ppermute(array, 'seq', pairs)]
    unnamed x25 -> x172, local copies, waits for them, and re-layouts: 4.34 us -> 42.5 us
    dot_general x6 -> x0, matrix products: 34.8 us -> none  [the longest x1 10.8 us: attention_grads(): jnp.einsum('ephfg,egphd->efphd', prob_low, value_in, preferred_element_ty...]
  transfers between devices with their start and end apart: 5 -> 56, of which waited for: 5 -> 12; matrix products, arithmetic and copies ran while one was open for 10% -> 0% of each run, Pallas kernels for 0% -> 32%
where the time goes in v1:
time: 1340 us; the launch traced here: 1330 us
  Pallas kernels  567 us (42%)
  waiting for transfers between devices  480 us (36%)
  blocking collectives  145 us (11%)
  starting transfers between devices  95.7 us (7%)
  local copies, waits for them, and re-layouts  43.2 us (3%)
    ppermute x56, waiting for transfers between devices, send(): return lax.ppermute(array, 'seq', pairs)  480 us
    pallas_call x4, Pallas kernels, pack(): pl.pallas_call(functools.partial(pack_kernel, start, rows), out_shape=[ja...  322 us
    pallas_call x4, Pallas kernels, unpack(): pl.pallas_call(functools.partial(place_kernel, start, rows), out_shape=[j...  243 us
    psum x1, blocking collectives, hub_body(): totals = lax.psum(jnp.stack(totals), ('dp', 'seq'))  137 us
    ppermute x56, starting transfers between devices, send(): return lax.ppermute(array, 'seq', pairs)  95.7 us
    unnamed x172, local copies, waits for them, and re-layouts  42.5 us
  transfers between devices with their start and end apart: 56, of which 12 were waited for; matrix products, arithmetic and copies ran while one was open for 0% of the time, Pallas kernels for 32%

profile of v1, /device:TPU:0, one launch (start us, length us, event | category | flops | bytes accessed | tf_op | source)
XLA Modules:
  0.0 1332.9 jit_solution(1168337709423229516)
XLA Ops:
  0.6 80.6 %pack_rows.7 = (bf16[2,1280,128]{2,1,0:T(8,128)(2,1)}, bf16[2,1280,128]{2,1,0:T(8,128)(2,1)}, bf16[2,1280,128]{2,1,0:T(8,128)(2,1)}, bf16[2,1280,128]{2,1,0:T(8,128)(2,1)}) custom-call(bf16[2,5120,128]{2,1,0:T(8,128)(2,1)} %bitcast.35, bf16[2,5120,128]{2,1,0:T(8,128)(2,1)} %bitcast.39, bf16[2,5120,128]{2,1,0:T(8,128)(2,1)} %bitcast.43, ...), custom_call_target="tpu_custom_call" | custom-call | bytes 5242880 | tf_op jit(solution)/shard_map/pack_rows/pallas_call | solution.py:69
  81.2 5.8 collective-permute-start.43
  90.6 3.7 collective-permute-start.46
  94.2 7.4 collective-permute-done.43.refs_2_
  102.3 13.3 %collective-permute-done.44.refs_3_ = bf16[2,1280,128]{2,1,0:T(8,128)(2,1)} collective-permute-done((bf16[2,1280,128]{2,1,0:T(8,128)(2,1)}, bf16[2,1280,128]{2,1,0:T(8,128)(2,1)}, u32[]{:S(2)}, u32[]{:S(2)}) %collective-permute-start.44) | collective-permute-done | bytes 655392 | tf_op jit(solution)/shard_map/ppermute | solution.py:375
  117.2 5.2 collective-permute-start.47
  122.5 80.6 %pack_rows.6 = (bf16[2,1280,128]{2,1,0:T(8,128)(2,1)}, bf16[2,1280,128]{2,1,0:T(8,128)(2,1)}, bf16[2,1280,128]{2,1,0:T(8,128)(2,1)}, bf16[2,1280,128]{2,1,0:T(8,128)(2,1)}) custom-call(bf16[2,5120,128]{2,1,0:T(8,128)(2,1)} %bitcast.36, bf16[2,5120,128]{2,1,0:T(8,128)(2,1)} %bitcast.40, bf16[2,5120,128]{2,1,0:T(8,128)(2,1)} %bitcast.44, ...), custom_call_target="tpu_custom_call" | custom-call | bytes 5242880 | tf_op jit(solution)/shard_map/pack_rows/pallas_call | solution.py:69
  211.8 5.3 collective-permute-start.32
  217.1 3.8 collective-permute-done.29.refs_2_
  222.4 12.6 collective-permute-done.30.refs_3_
  236.5 5.4 collective-permute-start.33
  241.9 80.6 %pack_rows.5 = (bf16[2,1280,128]{2,1,0:T(8,128)(2,1)}, bf16[2,1280,128]{2,1,0:T(8,128)(2,1)}, bf16[2,1280,128]{2,1,0:T(8,128)(2,1)}, bf16[2,1280,128]{2,1,0:T(8,128)(2,1)}) custom-call(bf16[2,5120,128]{2,1,0:T(8,128)(2,1)} %bitcast.37, bf16[2,5120,128]{2,1,0:T(8,128)(2,1)} %bitcast.41, bf16[2,5120,128]{2,1,0:T(8,128)(2,1)} %bitcast.45, ...), custom_call_target="tpu_custom_call" | custom-call | bytes 5242880 | tf_op jit(solution)/shard_map/pack_rows/pallas_call | solution.py:69
  324.7 2.2 collective-permute-start.16
  329.1 3.2 collective-permute-start.18
  332.3 6.9 collective-permute-done.15.refs_2_
  340.7 12.5 collective-permute-done.16.refs_3_
  355.8 5.4 collective-permute-start.19
  361.2 80.6 %pack_rows.4 = (bf16[2,1280,128]{2,1,0:T(8,128)(2,1)}, bf16[2,1280,128]{2,1,0:T(8,128)(2,1)}, bf16[2,1280,128]{2,1,0:T(8,128)(2,1)}, bf16[2,1280,128]{2,1,0:T(8,128)(2,1)}) custom-call(bf16[2,5120,128]{2,1,0:T(8,128)(2,1)} %bitcast.38, bf16[2,5120,128]{2,1,0:T(8,128)(2,1)} %bitcast.42, bf16[2,5120,128]{2,1,0:T(8,128)(2,1)} %bitcast.46, ...), custom_call_target="tpu_custom_call" | custom-call | bytes 5242880 | tf_op jit(solution)/shard_map/pack_rows/pallas_call | solution.py:69
  446.6 11.9 collective-permute-done.1.refs_2_
  459.2 13.2 collective-permute-done.2.refs_3_
  472.3 4.1 collective-permute-start.4
  477.3 8.2 all_gather.3
  487.2 5.3 collective-permute-start.5
  545.1 141.5 %collective-permute-done.54.back_s = bf16[3,1280,128]{2,1,0:T(8,128)(2,1)} collective-permute-done((bf16[3,1280,128]{2,1,0:T(8,128)(2,1)}, bf16[3,1280,128]{2,1,0:T(8,128)(2,1)}, u32[]{:S(2)}, u32[]{:S(2)}) %collective-permute-start.54) | collective-permute-done | bytes 983072 | tf_op jit(solution)/shard_map/ppermute | solution.py:375
  688.4 89.5 %collective-permute-done.55.back_x = bf16[3,1280,128]{2,1,0:T(8,128)(2,1)} collective-permute-done((bf16[3,1280,128]{2,1,0:T(8,128)(2,1)}, bf16[3,1280,128]{2,1,0:T(8,128)(2,1)}, u32[]{:S(2)}, u32[]{:S(2)}) %collective-permute-start.55) | collective-permute-done | bytes 983072 | tf_op jit(solution)/shard_map/ppermute | solution.py:375
  780.6 151.3 %collective-permute-done.40.back_s = bf16[3,1280,128]{2,1,0:T(8,128)(2,1)} collective-permute-done((bf16[3,1280,128]{2,1,0:T(8,128)(2,1)}, bf16[3,1280,128]{2,1,0:T(8,128)(2,1)}, u32[]{:S(2)}, u32[]{:S(2)}) %collective-permute-start.40) | collective-permute-done | bytes 983072 | tf_op jit(solution)/shard_map/ppermute | solution.py:375
  932.6 16.4 %collective-permute-done.41.back_x = bf16[3,1280,128]{2,1,0:T(8,128)(2,1)} collective-permute-done((bf16[3,1280,128]{2,1,0:T(8,128)(2,1)}, bf16[3,1280,128]{2,1,0:T(8,128)(2,1)}, u32[]{:S(2)}, u32[]{:S(2)}) %collective-permute-start.41) | collective-permute-done | bytes 983072 | tf_op jit(solution)/shard_map/ppermute | solution.py:375
  951.7 136.7 %psum.7 = f32[2,40,128]{2,1,0:T(8,128)S(1)} all-reduce(f32[2,40,128]{2,1,0:T(8,128)S(1)} %pad_maximum_fusion), channel_id=1, replica_groups=mesh['dp'=4,'seq'=8] {'dp','seq'}, use_global_device_ids=true, to_apply=%region_0.0 | all-reduce | flops 10240 | bytes 81920 | tf_op jit(solution)/shard_map/psum | solution.py:412
  1089.0 60.7 %place_rows.4 = (bf16[2,5120,128]{2,1,0:T(8,128)(2,1)}, bf16[2,5120,128]{2,1,0:T(8,128)(2,1)}, bf16[2,5120,128]{2,1,0:T(8,128)(2,1)}) custom-call(bf16[3,1280,128]{2,1,0:T(8,128)(2,1)} %copy-done.3, bf16[3,1280,128]{2,1,0:T(8,128)(2,1)} %collective-permute-done.53.other, bf16[3,1280,128]{2,1,0:T(8,128)(2,1)} %collective-permute-done.54.back_s, ...), custom_call_target="tpu_custom_call" | custom-call | bytes 3932160 | tf_op jit(solution)/shard_map/place_rows/pallas_call | solution.py:113
  1149.7 60.7 %place_rows.5 = (bf16[2,5120,128]{2,1,0:T(8,128)(2,1)}, bf16[2,5120,128]{2,1,0:T(8,128)(2,1)}, bf16[2,5120,128]{2,1,0:T(8,128)(2,1)}) custom-call(bf16[3,1280,128]{2,1,0:T(8,128)(2,1)} %copy-done.2, bf16[3,1280,128]{2,1,0:T(8,128)(2,1)} %collective-permute-done.39.other, ...), custom_call_target="tpu_custom_call", output_to_operand_aliasing={{0}: (4, {}), {1}: (5, {}), {2}: (6, {})} | custom-call | bytes 3932160 | tf_op jit(solution)/shard_map/place_rows/pallas_call | solution.py:113
  1210.5 60.7 %place_rows.6 = (bf16[2,5120,128]{2,1,0:T(8,128)(2,1)}, bf16[2,5120,128]{2,1,0:T(8,128)(2,1)}, bf16[2,5120,128]{2,1,0:T(8,128)(2,1)}) custom-call(bf16[3,1280,128]{2,1,0:T(8,128)(2,1)} %copy-done.1, bf16[3,1280,128]{2,1,0:T(8,128)(2,1)} %collective-permute-done.25.other, ...), custom_call_target="tpu_custom_call", output_to_operand_aliasing={{0}: (4, {}), {1}: (5, {}), {2}: (6, {})} | custom-call | bytes 3932160 | tf_op jit(solution)/shard_map/place_rows/pallas_call | solution.py:113
  1272.2 60.7 %place_rows.7 = (bf16[2,5120,128]{2,1,0:T(8,128)(2,1)}, bf16[2,5120,128]{2,1,0:T(8,128)(2,1)}, bf16[2,5120,128]{2,1,0:T(8,128)(2,1)}) custom-call(bf16[3,1280,128]{2,1,0:T(8,128)(2,1)} %copy-done, bf16[3,1280,128]{2,1,0:T(8,128)(2,1)} %copy-done.83, ...), custom_call_target="tpu_custom_call", output_to_operand_aliasing={{0}: (4, {}), {1}: (5, {}), {2}: (6, {})} | custom-call | bytes 3932160 | tf_op jit(solution)/shard_map/place_rows/pallas_call | solution.py:113
  (279 shorter events, 94.8 us)
Async XLA Ops:
  89.9 113.2 %collective-permute-start.42 = (bf16[2,1280,128]{2,1,0:T(8,128)(2,1)}, bf16[2,1280,128]{2,1,0:T(8,128)(2,1)S(1)}, u32[]{:S(2)}, u32[]{:S(2)}) collective-permute-start(bf16[2,1280,128]{2,1,0:T(8,128)(2,1)} %get-tuple-element.125), channel_id=1, source_target_pairs={{2,3},{3,2},{4,5},{5,4},{10,11},{11,10},{12,13},{13,12},{18,19},{1... | collective-permute-start | bytes 1966088 | tf_op jit(solution)/shard_map/ppermute | solution.py:375
  90.6 115.1 %collective-permute-start.46 = (bf16[2,1280,128]{2,1,0:T(8,128)(2,1)}, bf16[2,1280,128]{2,1,0:T(8,128)(2,1)S(1)}, u32[]{:S(2)}, u32[]{:S(2)}) collective-permute-start(bf16[2,1280,128]{2,1,0:T(8,128)(2,1)} %get-tuple-element.126.refs_4_), channel_id=1, source_target_pairs={{0,2},{1,3},{6,4},{7,5},{8,10},{9,11},{14,12},{15,13},{16,18},{17,... | collective-permute-start | bytes 1966088 | tf_op jit(solution)/shard_map/ppermute | solution.py:375
  101.6 106.2 %collective-permute-start.49 = (bf16[2,1280,128]{2,1,0:T(8,128)(2,1)}, bf16[2,1280,128]{2,1,0:T(8,128)(2,1)S(1)}, u32[]{:S(2)}, u32[]{:S(2)}) collective-permute-start(bf16[2,1280,128]{2,1,0:T(8,128)(2,1)} %get-tuple-element.125), channel_id=1, source_target_pairs={{2,5},{3,4},{4,3},{5,2},{10,13},{11,12},{12,11},{13,10},{18,21},{1... | collective-permute-start | bytes 1966088 | tf_op jit(solution)/shard_map/ppermute | solution.py:375
  115.7 93.7 %collective-permute-start.45 = (bf16[2,1280,128]{2,1,0:T(8,128)(2,1)}, bf16[2,1280,128]{2,1,0:T(8,128)(2,1)S(1)}, u32[]{:S(2)}, u32[]{:S(2)}) collective-permute-start(bf16[2,1280,128]{2,1,0:T(8,128)(2,1)} %get-tuple-element.127), channel_id=1, source_target_pairs={{2,3},{3,2},{4,5},{5,4},{10,11},{11,10},{12,13},{13,12},{18,19},{1... | collective-permute-start | bytes 1966088 | tf_op jit(solution)/shard_map/ppermute | solution.py:375
  117.2 93.7 %collective-permute-start.47 = (bf16[2,1280,128]{2,1,0:T(8,128)(2,1)}, bf16[2,1280,128]{2,1,0:T(8,128)(2,1)S(1)}, u32[]{:S(2)}, u32[]{:S(2)}) collective-permute-start(bf16[2,1280,128]{2,1,0:T(8,128)(2,1)} %get-tuple-element.127), channel_id=1, source_target_pairs={{0,3},{1,2},{6,5},{7,4},{8,11},{9,10},{14,13},{15,12},{16,19},{17,... | collective-permute-start | bytes 1966088 | tf_op jit(solution)/shard_map/ppermute | solution.py:375
  210.2 112.3 %collective-permute-start.28 = (bf16[2,1280,128]{2,1,0:T(8,128)(2,1)}, bf16[2,1280,128]{2,1,0:T(8,128)(2,1)S(1)}, u32[]{:S(2)}, u32[]{:S(2)}) collective-permute-start(bf16[2,1280,128]{2,1,0:T(8,128)(2,1)} %get-tuple-element.112), channel_id=1, source_target_pairs={{2,3},{3,2},{4,5},{5,4},{10,11},{11,10},{12,13},{13,12},{18,19},{1... | collective-permute-start | bytes 1966088 | tf_op jit(solution)/shard_map/ppermute | solution.py:375
  211.8 112.9 %collective-permute-start.32 = (bf16[2,1280,128]{2,1,0:T(8,128)(2,1)}, bf16[2,1280,128]{2,1,0:T(8,128)(2,1)S(1)}, u32[]{:S(2)}, u32[]{:S(2)}) collective-permute-start(bf16[2,1280,128]{2,1,0:T(8,128)(2,1)} %get-tuple-element.113.refs_4_), channel_id=1, source_target_pairs={{0,2},{1,3},{6,4},{7,5},{8,10},{9,11},{14,12},{15,13},{16,18},{17,... | collective-permute-start | bytes 1966088 | tf_op jit(solution)/shard_map/ppermute | solution.py:375
  220.9 105.9 %collective-permute-start.35 = (bf16[2,1280,128]{2,1,0:T(8,128)(2,1)}, bf16[2,1280,128]{2,1,0:T(8,128)(2,1)}, u32[]{:S(2)}, u32[]{:S(2)}) collective-permute-start(bf16[2,1280,128]{2,1,0:T(8,128)(2,1)} %get-tuple-element.112), channel_id=1, source_target_pairs={{2,5},{3,4},{4,3},{5,2},{10,13},{11,12},{12,11},{13,10},{18,21},{1... | collective-permute-start | bytes 1966088 | tf_op jit(solution)/shard_map/ppermute | solution.py:375
  235.0 92.6 %collective-permute-start.31 = (bf16[2,1280,128]{2,1,0:T(8,128)(2,1)}, bf16[2,1280,128]{2,1,0:T(8,128)(2,1)}, u32[]{:S(2)}, u32[]{:S(2)}) collective-permute-start(bf16[2,1280,128]{2,1,0:T(8,128)(2,1)} %get-tuple-element.114), channel_id=1, source_target_pairs={{2,3},{3,2},{4,5},{5,4},{10,11},{11,10},{12,13},{13,12},{18,19},{1... | collective-permute-start | bytes 1966088 | tf_op jit(solution)/shard_map/ppermute | solution.py:375
  236.5 92.6 %collective-permute-start.33 = (bf16[2,1280,128]{2,1,0:T(8,128)(2,1)}, bf16[2,1280,128]{2,1,0:T(8,128)(2,1)}, u32[]{:S(2)}, u32[]{:S(2)}) collective-permute-start(bf16[2,1280,128]{2,1,0:T(8,128)(2,1)} %get-tuple-element.114), channel_id=1, source_target_pairs={{0,3},{1,2},{6,5},{7,4},{8,11},{9,10},{14,13},{15,12},{16,19},{17,... | collective-permute-start | bytes 1966088 | tf_op jit(solution)/shard_map/ppermute | solution.py:375
  327.6 114.2 %collective-permute-start.14 = (bf16[2,1280,128]{2,1,0:T(8,128)(2,1)}, bf16[2,1280,128]{2,1,0:T(8,128)(2,1)}, u32[]{:S(2)}, u32[]{:S(2)}) collective-permute-start(bf16[2,1280,128]{2,1,0:T(8,128)(2,1)} %get-tuple-element.99), channel_id=1, source_target_pairs={{2,3},{3,2},{4,5},{5,4},{10,11},{11,10},{12,13},{13,12},{18,19},{1... | collective-permute-start | bytes 1966088 | tf_op jit(solution)/shard_map/ppermute | solution.py:375
  329.1 114.0 %collective-permute-start.18 = (bf16[2,1280,128]{2,1,0:T(8,128)(2,1)}, bf16[2,1280,128]{2,1,0:T(8,128)(2,1)}, u32[]{:S(2)}, u32[]{:S(2)}) collective-permute-start(bf16[2,1280,128]{2,1,0:T(8,128)(2,1)} %get-tuple-element.100.refs_4_), channel_id=1, source_target_pairs={{0,2},{1,3},{6,4},{7,5},{8,10},{9,11},{14,12},{15,13},{16,18},{17,... | collective-permute-start | bytes 1966088 | tf_op jit(solution)/shard_map/ppermute | solution.py:375
  339.2 105.2 %collective-permute-start.21 = (bf16[2,1280,128]{2,1,0:T(8,128)(2,1)}, bf16[2,1280,128]{2,1,0:T(8,128)(2,1)}, u32[]{:S(2)}, u32[]{:S(2)}) collective-permute-start(bf16[2,1280,128]{2,1,0:T(8,128)(2,1)} %get-tuple-element.99), channel_id=1, source_target_pairs={{2,5},{3,4},{4,3},{5,2},{10,13},{11,12},{12,11},{13,10},{18,21},{1... | collective-permute-start | bytes 1966088 | tf_op jit(solution)/shard_map/ppermute | solution.py:375
  353.3 91.9 %collective-permute-start.17 = (bf16[2,1280,128]{2,1,0:T(8,128)(2,1)}, bf16[2,1280,128]{2,1,0:T(8,128)(2,1)}, u32[]{:S(2)}, u32[]{:S(2)}) collective-permute-start(bf16[2,1280,128]{2,1,0:T(8,128)(2,1)} %get-tuple-element.101), channel_id=1, source_target_pairs={{2,3},{3,2},{4,5},{5,4},{10,11},{11,10},{12,13},{13,12},{18,19},{1... | collective-permute-start | bytes 1966088 | tf_op jit(solution)/shard_map/ppermute | solution.py:375
  355.8 90.1 %collective-permute-start.19 = (bf16[2,1280,128]{2,1,0:T(8,128)(2,1)}, bf16[2,1280,128]{2,1,0:T(8,128)(2,1)}, u32[]{:S(2)}, u32[]{:S(2)}) collective-permute-start(bf16[2,1280,128]{2,1,0:T(8,128)(2,1)} %get-tuple-element.101), channel_id=1, source_target_pairs={{0,3},{1,2},{6,5},{7,4},{8,11},{9,10},{14,13},{15,12},{16,19},{17,... | collective-permute-start | bytes 1966088 | tf_op jit(solution)/shard_map/ppermute | solution.py:375
  444.5 32.0 %collective-permute-start.6 = (bf16[2,1280,128]{2,1,0:T(8,128)(2,1)}, bf16[2,1280,128]{2,1,0:T(8,128)(2,1)S(1)}, u32[]{:S(2)}, u32[]{:S(2)}) collective-permute-start(bf16[2,1280,128]{2,1,0:T(8,128)(2,1)} %get-tuple-element.85.refs_0_), channel_id=1, source_target_pairs={{2,4},{3,5},{4,2},{5,3},{10,12},{11,13},{12,10},{13,11},{18,20},{1... | collective-permute-start | bytes 1966088 | tf_op jit(solution)/shard_map/ppermute | solution.py:375
  445.2 40.3 %collective-permute-start.50 = (bf16[2,1280,128]{2,1,0:T(8,128)(2,1)}, bf16[2,1280,128]{2,1,0:T(8,128)(2,1)S(1)}, u32[]{:S(2)}, u32[]{:S(2)}) collective-permute-start(bf16[2,1280,128]{2,1,0:T(8,128)(2,1)} %collective-permute-done.43.refs_2_), channel_id=1, source_target_pairs={{2,4},{3,5},{4,2},{5,3},{10,12},{11,13},{12,10},{13,11},{18,20},{1... | collective-permute-start | bytes 1966088 | tf_op jit(solution)/shard_map/ppermute | solution.py:375
  445.9 40.3 %collective-permute-start.51 = (bf16[2,1280,128]{2,1,0:T(8,128)(2,1)}, bf16[2,1280,128]{2,1,0:T(8,128)(2,1)S(1)}, u32[]{:S(2)}, u32[]{:S(2)}) collective-permute-start(bf16[2,1280,128]{2,1,0:T(8,128)(2,1)} %collective-permute-done.44.refs_3_), channel_id=1, source_target_pairs={{2,4},{3,5},{4,2},{5,3},{10,12},{11,13},{12,10},{13,11},{18,20},{1... | collective-permute-start | bytes 1966088 | tf_op jit(solution)/shard_map/ppermute | solution.py:375
  458.5 45.2 %collective-permute-start = (bf16[2,1280,128]{2,1,0:T(8,128)(2,1)}, bf16[2,1280,128]{2,1,0:T(8,128)(2,1)S(1)}, u32[]{:S(2)}, u32[]{:S(2)}) collective-permute-start(bf16[2,1280,128]{2,1,0:T(8,128)(2,1)} %get-tuple-element.86), channel_id=1, source_target_pairs={{2,3},{3,2},{4,5},{5,4},{10,11},{11,10},{12,13},{13,12},{18,19},{1... | collective-permute-start | bytes 1966088 | tf_op jit(solution)/shard_map/ppermute | solution.py:375
  472.3 33.0 %collective-permute-start.4 = (bf16[2,1280,128]{2,1,0:T(8,128)(2,1)}, bf16[2,1280,128]{2,1,0:T(8,128)(2,1)S(1)}, u32[]{:S(2)}, u32[]{:S(2)}) collective-permute-start(bf16[2,1280,128]{2,1,0:T(8,128)(2,1)} %get-tuple-element.87.refs_4_), channel_id=1, source_target_pairs={{0,2},{1,3},{6,4},{7,5},{8,10},{9,11},{14,12},{15,13},{16,18},{17,... | collective-permute-start | bytes 1966088 | tf_op jit(solution)/shard_map/ppermute | solution.py:375
  512.6 31.2 %collective-permute-start.53 = (bf16[3,1280,128]{2,1,0:T(8,128)(2,1)}, bf16[3,1280,128]{2,1,0:T(8,128)(2,1)}, u32[]{:S(2)}, u32[]{:S(2)}) collective-permute-start(bf16[3,1280,128]{2,1,0:T(8,128)(2,1)} %get-tuple-element.134), channel_id=1, source_target_pairs={{2,3},{3,2},{4,5},{5,4},{10,11},{11,10},{12,13},{13,12},{18,19},{1... | collective-permute-start | bytes 2949128 | tf_op jit(solution)/shard_map/ppermute | solution.py:375
  515.2 171.4 %collective-permute-start.54 = (bf16[3,1280,128]{2,1,0:T(8,128)(2,1)}, bf16[3,1280,128]{2,1,0:T(8,128)(2,1)}, u32[]{:S(2)}, u32[]{:S(2)}) collective-permute-start(bf16[3,1280,128]{2,1,0:T(8,128)(2,1)} %copy-done.82), channel_id=1, source_target_pairs={{2,0},{3,1},{4,6},{5,7},{10,8},{11,9},{12,14},{13,15},{18,16},{19,... | collective-permute-start | bytes 2949128 | tf_op jit(solution)/shard_map/ppermute | solution.py:375
  532.3 245.6 %collective-permute-start.55 = (bf16[3,1280,128]{2,1,0:T(8,128)(2,1)}, bf16[3,1280,128]{2,1,0:T(8,128)(2,1)}, u32[]{:S(2)}, u32[]{:S(2)}) collective-permute-start(bf16[3,1280,128]{2,1,0:T(8,128)(2,1)} %get-tuple-element.136), channel_id=1, source_target_pairs={{3,0},{2,1},{5,6},{4,7},{11,8},{10,9},{13,14},{12,15},{19,16},{18,... | collective-permute-start | bytes 2949128 | tf_op jit(solution)/shard_map/ppermute | solution.py:375
  540.4 238.9 %collective-permute-start.39 = (bf16[3,1280,128]{2,1,0:T(8,128)(2,1)}, bf16[3,1280,128]{2,1,0:T(8,128)(2,1)}, u32[]{:S(2)}, u32[]{:S(2)}) collective-permute-start(bf16[3,1280,128]{2,1,0:T(8,128)(2,1)} %get-tuple-element.121), channel_id=1, source_target_pairs={{2,3},{3,2},{4,5},{5,4},{10,11},{11,10},{12,13},{13,12},{18,19},{1... | collective-permute-start | bytes 2949128 | tf_op jit(solution)/shard_map/ppermute | solution.py:375
  542.2 389.6 %collective-permute-start.40 = (bf16[3,1280,128]{2,1,0:T(8,128)(2,1)}, bf16[3,1280,128]{2,1,0:T(8,128)(2,1)}, u32[]{:S(2)}, u32[]{:S(2)}) collective-permute-start(bf16[3,1280,128]{2,1,0:T(8,128)(2,1)} %copy-done.78), channel_id=1, source_target_pairs={{2,0},{3,1},{4,6},{5,7},{10,8},{11,9},{12,14},{13,15},{18,16},{19,... | collective-permute-start | bytes 2949128 | tf_op jit(solution)/shard_map/ppermute | solution.py:375
  543.8 405.2 %collective-permute-start.41 = (bf16[3,1280,128]{2,1,0:T(8,128)(2,1)}, bf16[3,1280,128]{2,1,0:T(8,128)(2,1)}, u32[]{:S(2)}, u32[]{:S(2)}) collective-permute-start(bf16[3,1280,128]{2,1,0:T(8,128)(2,1)} %copy-done.81), channel_id=1, source_target_pairs={{3,0},{2,1},{5,6},{4,7},{11,8},{10,9},{13,14},{12,15},{19,16},{18,... | collective-permute-start | bytes 2949128 | tf_op jit(solution)/shard_map/ppermute | solution.py:375
  686.6 263.7 %collective-permute-start.25 = (bf16[3,1280,128]{2,1,0:T(8,128)(2,1)}, bf16[3,1280,128]{2,1,0:T(8,128)(2,1)}, u32[]{:S(2)}, u32[]{:S(2)}) collective-permute-start(bf16[3,1280,128]{2,1,0:T(8,128)(2,1)} %get-tuple-element.108), channel_id=1, source_target_pairs={{2,3},{3,2},{4,5},{5,4},{10,11},{11,10},{12,13},{13,12},{18,19},{1... | collective-permute-start | bytes 2949128 | tf_op jit(solution)/shard_map/ppermute | solution.py:375
  778.0 432.5 %collective-permute-start.26 = (bf16[3,1280,128]{2,1,0:T(8,128)(2,1)}, bf16[3,1280,128]{2,1,0:T(8,128)(2,1)}, u32[]{:S(2)}, u32[]{:S(2)}) collective-permute-start(bf16[3,1280,128]{2,1,0:T(8,128)(2,1)} %get-tuple-element.109), channel_id=1, source_target_pairs={{2,0},{3,1},{4,6},{5,7},{10,8},{11,9},{12,14},{13,15},{18,16},{19,... | collective-permute-start | bytes 2949128 | tf_op jit(solution)/shard_map/ppermute | solution.py:375
  779.3 431.2 %collective-permute-start.27 = (bf16[3,1280,128]{2,1,0:T(8,128)(2,1)}, bf16[3,1280,128]{2,1,0:T(8,128)(2,1)}, u32[]{:S(2)}, u32[]{:S(2)}) collective-permute-start(bf16[3,1280,128]{2,1,0:T(8,128)(2,1)} %get-tuple-element.110), channel_id=1, source_target_pairs={{3,0},{2,1},{5,6},{4,7},{11,8},{10,9},{13,14},{12,15},{19,16},{18,... | collective-permute-start | bytes 2949128 | tf_op jit(solution)/shard_map/ppermute | solution.py:375
  931.9 339.4 %collective-permute-start.11 = (bf16[3,1280,128]{2,1,0:T(8,128)(2,1)}, bf16[3,1280,128]{2,1,0:T(8,128)(2,1)S(1)}, u32[]{:S(2)}, u32[]{:S(2)}) collective-permute-start(bf16[3,1280,128]{2,1,0:T(8,128)(2,1)} %get-tuple-element.95), channel_id=1, source_target_pairs={{2,3},{3,2},{4,5},{5,4},{10,11},{11,10},{12,13},{13,12},{18,19},{1... | collective-permute-start | bytes 2949128 | tf_op jit(solution)/shard_map/ppermute | solution.py:375
  949.0 322.3 %collective-permute-start.12 = (bf16[3,1280,128]{2,1,0:T(8,128)(2,1)}, bf16[3,1280,128]{2,1,0:T(8,128)(2,1)}, u32[]{:S(2)}, u32[]{:S(2)}) collective-permute-start(bf16[3,1280,128]{2,1,0:T(8,128)(2,1)} %get-tuple-element.96), channel_id=1, source_target_pairs={{2,0},{3,1},{4,6},{5,7},{10,8},{11,9},{12,14},{13,15},{18,16},{19,... | collective-permute-start | bytes 2949128 | tf_op jit(solution)/shard_map/ppermute | solution.py:375
  950.3 321.0 %collective-permute-start.13 = (bf16[3,1280,128]{2,1,0:T(8,128)(2,1)}, bf16[3,1280,128]{2,1,0:T(8,128)(2,1)}, u32[]{:S(2)}, u32[]{:S(2)}) collective-permute-start(bf16[3,1280,128]{2,1,0:T(8,128)(2,1)} %get-tuple-element.97), channel_id=1, source_target_pairs={{3,0},{2,1},{5,6},{4,7},{11,8},{10,9},{13,14},{12,15},{19,16},{18,... | collective-permute-start | bytes 2949128 | tf_op jit(solution)/shard_map/ppermute | solution.py:375
  (110 other events, 3423.7 us)

commit v2 on v1

v2 whole, which is shorter than its diff:
```python
import functools
import math

import jax
import jax.numpy as jnp
from jax import lax
from jax.experimental import pallas as pl
from jax.experimental.pallas import tpu as pltpu
from jax.sharding import PartitionSpec as P

EPSILON = 1e-06
BLOCK = 256
GROUP = 16
SLOTS = 4
WIDE = GROUP * SLOTS
TOGETHER = 64
CUTS = (5, 5, 5, 5)

EDGE = ((0, 2), (1, 3), (6, 4), (7, 5))
MIDDLE = ((2, 4), (3, 5), (4, 2), (5, 3))
DOWN = ((4, 2), (5, 3))
BACK_S = ((2, 0), (3, 1), (4, 6), (5, 7))
BACK_X = ((2, 1), (3, 0), (4, 7), (5, 6))
SWAP = tuple((i, i ^ 1) for i in range(8))

F32 = jnp.float32
BF16 = jnp.bfloat16
ANY = pl.BlockSpec(memory_space=pltpu.HBM)
VMEM = pl.BlockSpec(memory_space=pltpu.VMEM)


def place():
    index = lax.axis_index("seq")
    chip, core = index // 2, index % 2
    return chip, core


def pack_kernel(first, steps, offset, q, k, v, g, x, a, b):
    chip, core = place()

    def run(pair_a, pair_b, index_a, index_b):
        def step(*refs):
            out_a, out_b = refs[-2:]
            for t in range(2):
                out_a[t] = refs[t][0]
                out_a[2 + t] = refs[4 + t][0]
                out_b[t] = refs[2 + t][0]
                out_b[2 + t] = refs[6 + t][0]

        def swapped(index):
            return pl.BlockSpec((1, BLOCK, 128), lambda i: (index, first - offset + i, 0))

        pltpu.emit_pipeline(
            step,
            grid=(steps,),
            in_specs=[pl.BlockSpec((1, BLOCK, 128), lambda i: (core, first + i, 0))] * 4
            + [swapped(index) for index in (*index_a, *index_b)],
            out_specs=[pl.BlockSpec((4, BLOCK, 128), lambda i: (0, i, 0))] * 2,
        )(*pair_a, *pair_b, *([x] * 4), a, b)

    @pl.when(chip < 2)
    def _():
        run((k, v), (q, g), (1, 2), (0, 3))

    @pl.when(chip >= 2)
    def _():
        run((q, g), (k, v), (0, 3), (1, 2))


def pack(first, steps, offset, arrays, swapped):
    rows = steps * BLOCK
    return pl.pallas_call(
        functools.partial(pack_kernel, first, steps, offset),
        out_shape=[jax.ShapeDtypeStruct((4, rows, 128), BF16)] * 2,
        in_specs=[ANY] * 5,
        out_specs=[ANY] * 2,
        compiler_params=pltpu.CompilerParams(vmem_limit_bytes=32 * 1024 * 1024),
        cost_estimate=pl.CostEstimate(flops=0, bytes_accessed=rows * 128 * 2 * 16, transcendentals=0),
        name="pack_rows",
    )(*arrays, swapped)


def place_kernel(slot, own, other, back_s, back_x, *refs):
    outs = refs[-3:]
    chip, core = place()
    hub = (chip == 1) | (chip == 2)

    def run(chunk, near, far):
        first, steps = sum(CUTS[:chunk]), CUTS[chunk]

        def step(half):
            def copy(src, *dsts):
                for t, dst in enumerate(dsts):
                    dst[0] = src[t]

            return copy

        for half, src in ((core, near), (1 - core, far)):
            pltpu.emit_pipeline(
                step(half),
                grid=(steps,),
                in_specs=[pl.BlockSpec((3, BLOCK, 128), lambda i: (0, i, 0))],
                out_specs=[pl.BlockSpec((1, BLOCK, 128), lambda i, half=half: (half, first + i, 0))] * 3,
            )(src, *outs)

    if slot < len(CUTS):

        @pl.when(chip == 2)
        def _():
            run(slot, own, other)

        @pl.when(chip == 3)
        def _():
            run(slot, back_s, back_x)

    if slot > 0:

        @pl.when(chip == 1)
        def _():
            run(slot - 1, own, other)

        @pl.when(chip == 0)
        def _():
            run(slot - 1, back_s, back_x)


def unpack(slot, half, pieces, outs):
    first = outs is None
    outs = () if first else outs
    return pl.pallas_call(
        functools.partial(place_kernel, slot),
        out_shape=[jax.ShapeDtypeStruct((2, half, 128), BF16)] * 3,
        in_specs=[ANY] * (4 + len(outs)),
        out_specs=[ANY] * 3,
        input_output_aliases={} if first else {4: 0, 5: 1, 6: 2},
        compiler_params=pltpu.CompilerParams(vmem_limit_bytes=32 * 1024 * 1024),
        cost_estimate=pl.CostEstimate(
            flops=0, bytes_accessed=max(CUTS) * BLOCK * 128 * 2 * 12, transcendentals=0
        ),
        name="place_rows",
    )(*pieces, *outs)


def rms(values):
    wide = values.astype(F32)
    inverse = lax.rsqrt(jnp.mean(wide * wide, axis=-1, keepdims=True) + EPSILON)
    return wide * inverse, inverse


def norm_back(step, hat, inverse, gain):
    wide = step.astype(F32)
    gained = gain * wide
    result = inverse * (gained - hat * jnp.mean(gained * hat, axis=-1, keepdims=True))
    return result.astype(BF16), wide * hat


def mul_t(a, b):
    return lax.dot_general(a, b, (((1,), (1,)), ((), ())), preferred_element_type=F32)


def t_mul(a, b):
    return lax.dot_general(a, b, (((0,), (0,)), ((), ())), preferred_element_type=F32)


def mul(a, b):
    return jnp.dot(a, b, preferred_element_type=F32)


def iota(shape, axis):
    return lax.broadcasted_iota(jnp.int32, shape, axis)


def frame_of(slot, core, upper):
    cross = slot % 2
    side = slot // 2
    side = side if upper else 1 - side
    return 2 * side + cross + core - 2 * cross * core


def causal(core, upper):
    shape = (WIDE, 2 * WIDE if upper else WIDE)
    rows, cols = iota(shape, 0), iota(shape, 1)
    key = cols // GROUP
    frame = frame_of(key % SLOTS, core, upper)
    if upper:
        frame = jnp.where(key < SLOTS, -1, frame)
    late = frame <= frame_of(rows // GROUP, core, upper)
    return (rows % GROUP == cols % GROUP) & late


def cat(parts):
    return jnp.concatenate(parts, axis=0)


def tiled(gain):
    return cat([gain] * SLOTS)


def group(wide, j):
    slots = wide.shape[0] // TOGETHER
    return cat([wide[s * TOGETHER + j * GROUP :][:GROUP] for s in range(slots)])


def ungroup(parts):
    return cat([part[s * GROUP :][:GROUP] for s in range(SLOTS) for part in parts])


def fold(acc, rows, part):
    total = part[:TOGETHER]
    for s in range(1, SLOTS):
        total = total + part[s * TOGETHER :][:TOGETHER]
    acc[rows, :] += total


def settle(outs, rows, parts):
    for t, part in enumerate(parts):
        for s, out in enumerate(outs):
            out[t, rows, :] = part[s * TOGETHER :][:TOGETHER]


def sum_heads(acc, heads):
    total = acc[0:heads, :]
    for i in range(1, acc.shape[0] // heads):
        total = total + acc[i * heads : (i + 1) * heads, :]
    return total


def read(refs, t, rows):
    return cat([ref[2 * x + t, rows, :] for ref in refs for x in range(2)])


def attend(qn, kn, grad, value, allowed):
    scaling = 1.0 / math.sqrt(qn.shape[-1])
    count = TOGETHER // GROUP
    scores = cat([mul_t(group(qn, j), group(kn, j)) for j in range(count)])
    prob_grad = cat([mul_t(group(grad, j), group(value, j)) for j in range(count)])
    mask = cat([allowed] * count)
    scores = jnp.where(mask > 0, scores * scaling, -jnp.inf)
    expo = jnp.exp(scores - jnp.max(scores, axis=-1, keepdims=True))
    prob = expo * (1.0 / jnp.sum(expo, axis=-1, keepdims=True))
    prob_low = prob.astype(BF16)
    dots = jnp.sum(prob_low.astype(F32) * prob_grad, axis=-1, keepdims=True)
    score_low = (prob * (prob_grad - dots)).astype(BF16)
    split = lambda x: [x[j * WIDE :][:WIDE] for j in range(count)]
    return split(prob_low), split(score_low)


def upper_kernel(first, steps, heads, own_a, edge_a, own_b, edge_b, other, far, gain_q, gain_k, *refs):
    outs, packed, (sum_q, sum_k, acc_q, acc_k, mask) = refs[:4], refs[4], refs[5:]
    chip, core = place()
    count = TOGETHER // GROUP
    acc_q[...] = jnp.zeros_like(acc_q)
    acc_k[...] = jnp.zeros_like(acc_k)
    cycle = acc_q.shape[0] // BLOCK

    def block(own_a, edge_a, own_b, edge_b, other, far, out_s, out_x, out_es, out_ex, pack_ref):
        base = ((first + pl.program_id(0)) % cycle) * BLOCK
        scaling = 1.0 / math.sqrt(128)
        lanes = iota((WIDE, 128), 1) // 8
        spread_r, spread_c = iota((2 * WIDE, 128), 0), iota((2 * WIDE, 128), 1)
        spread = jnp.where(spread_r // GROUP == spread_c % 8, 1.0, 0.0).astype(BF16)

        def some(i, total):
            rows = pl.ds(pl.multiple_of(i * TOGETHER, TOGETHER), TOGETHER)
            place = pl.ds(pl.multiple_of(base + i * TOGETHER, TOGETHER), TOGETHER)
            gq, gk = tiled(gain_q[place, :]), tiled(gain_k[place, :])
            q_hat, q_inv = rms(read((own_a, edge_a), 0, rows))
            grad = read((own_a, edge_a), 1, rows)
            kl_hat, _ = rms(read((other, far), 0, rows))
            ku_hat, ku_inv = rms(read((own_b, edge_b), 0, rows))
            value = cat([read((other, far), 1, rows), read((own_b, edge_b), 1, rows)])
            qn = (q_hat * gq).astype(BF16)
            kn = cat([(kl_hat * gk).astype(BF16), (ku_hat * gk).astype(BF16)])
            prob, score = attend(qn, kn, grad, value, mask[...])
            q_step = ungroup([mul(score[j], group(kn, j)) for j in range(count)])
            k_step = ungroup([t_mul(score[j][:, WIDE:], group(qn, j)) for j in range(count)])
            v_step = ungroup([t_mul(prob[j][:, WIDE:], group(grad, j)) for j in range(count)])
            q_step, k_step = (q_step * scaling).astype(BF16), (k_step * scaling).astype(BF16)
            dq, part_q = norm_back(q_step, q_hat, q_inv, gq)
            dk, part_k = norm_back(k_step, ku_hat, ku_inv, gk)
            settle((out_s, out_x, out_es, out_ex), rows, (dq, dk, v_step.astype(BF16)))
            fold(acc_q, place, part_q)
            fold(acc_k, place, part_k)
            for j in range(count):
                cross = jnp.concatenate([prob[j][:, :WIDE], score[j][:, :WIDE]], axis=1)
                total = jnp.where(lanes == i * count + j, mul(cross, spread), total)
            return total

        total = lax.fori_loop(0, BLOCK // TOGETHER, some, jnp.zeros((WIDE, 128), F32))
        pack_ref[0] = total.astype(BF16)

    @pl.when(chip == 2)
    def _():
        mask[...] = causal(core, True).astype(F32)
        pltpu.emit_pipeline(
            block,
            grid=(steps,),
            in_specs=[pl.BlockSpec((4, BLOCK, 128), lambda i: (0, i, 0))] * 6,
            out_specs=[pl.BlockSpec((3, BLOCK, 128), lambda i: (0, i, 0))] * 4
            + [pl.BlockSpec((1, WIDE, 128), lambda i: (i, 0, 0))],
        )(own_a, edge_a, own_b, edge_b, other, far, *outs, packed)

    sum_q[...] = sum_heads(acc_q, heads)
    sum_k[...] = sum_heads(acc_k, heads)


def lower_kernel(first, steps, heads, own_a, edge_a, own_b, edge_b, other, far, packed, gain_q, gain_k, *refs):
    outs, (sum_q, sum_k, acc_q, acc_k, mask) = refs[4:8], refs[8:]
    chip, core = place()
    count = TOGETHER // GROUP
    acc_q[...] = jnp.zeros_like(acc_q)
    acc_k[...] = jnp.zeros_like(acc_k)
    cycle = acc_q.shape[0] // BLOCK

    def block(own_a, edge_a, own_b, edge_b, other, far, pack_ref, out_s, out_x, out_es, out_ex):
        base = ((first + pl.program_id(0)) % cycle) * BLOCK
        both = iota((WIDE, 2 * WIDE), 0) % GROUP == iota((WIDE, 2 * WIDE), 1) % GROUP
        scaling = 1.0 / math.sqrt(128)
        lanes = iota((WIDE, 128), 1) // 8
        spread_r, spread_c = iota((128, 2 * WIDE), 0), iota((128, 2 * WIDE), 1)
        spread = jnp.where(spread_c // GROUP == spread_r % 8, 1.0, 0.0).astype(BF16)
        crossed = pack_ref[0].astype(F32)

        def some(i, carry):
            rows = pl.ds(pl.multiple_of(i * TOGETHER, TOGETHER), TOGETHER)
            place = pl.ds(pl.multiple_of(base + i * TOGETHER, TOGETHER), TOGETHER)
            gq, gk = tiled(gain_q[place, :]), tiled(gain_k[place, :])
            k_hat, k_inv = rms(read((own_a, edge_a), 0, rows))
            value = read((own_a, edge_a), 1, rows)
            q_hat, q_inv = rms(read((own_b, edge_b), 0, rows))
            grad = read((own_b, edge_b), 1, rows)
            qu_hat, _ = rms(read((other, far), 0, rows))
            grad_u = read((other, far), 1, rows)
            kn = (k_hat * gk).astype(BF16)
            qn = (q_hat * gq).astype(BF16)
            qn_u = (qu_hat * gq).astype(BF16)
            prob, score = attend(qn, kn, grad, value, mask[...])
            cross = []
            for j in range(count):
                mine = jnp.where(lanes == i * count + j, crossed, 0.0).astype(BF16)
                cross.append(jnp.where(both, mul(mine, spread), 0.0).astype(BF16))
            q_step = ungroup([mul(score[j], group(kn, j)) for j in range(count)])
            k_step = ungroup(
                [
                    t_mul(cat([score[j], cross[j][:, WIDE:]]), cat([group(qn, j), group(qn_u, j)]))
                    for j in range(count)
                ]
            )
            v_step = ungroup(
                [
                    t_mul(cat([prob[j], cross[j][:, :WIDE]]), cat([group(grad, j), group(grad_u, j)]))
                    for j in range(count)
                ]
            )
            q_step, k_step = (q_step * scaling).astype(BF16), (k_step * scaling).astype(BF16)
            dq, part_q = norm_back(q_step, q_hat, q_inv, gq)
            dk, part_k = norm_back(k_step, k_hat, k_inv, gk)
            settle((out_s, out_x, out_es, out_ex), rows, (dq, dk, v_step.astype(BF16)))
            fold(acc_q, place, part_q)
            fold(acc_k, place, part_k)
            return carry

        lax.fori_loop(0, BLOCK // TOGETHER, some, 0)

    @pl.when(chip == 1)
    def _():
        mask[...] = causal(core, False).astype(F32)
        pltpu.emit_pipeline(
            block,
            grid=(steps,),
            in_specs=[pl.BlockSpec((4, BLOCK, 128), lambda i: (0, i, 0))] * 6
            + [pl.BlockSpec((1, WIDE, 128), lambda i: (i, 0, 0))],
            out_specs=[pl.BlockSpec((3, BLOCK, 128), lambda i: (0, i, 0))] * 4,
        )(own_a, edge_a, own_b, edge_b, other, far, packed, *outs)

    sum_q[...] = sum_heads(acc_q, heads)
    sum_k[...] = sum_heads(acc_k, heads)


def hub_cost(rows):
    return pl.CostEstimate(
        flops=rows * 60000, bytes_accessed=rows * 128 * 2 * 36, transcendentals=rows * 600
    )


def out_rows(slot):
    return max(CUTS[max(slot - 1, 0) : slot + 1]) * BLOCK


def upper(slot, heads, data, gains):
    steps = CUTS[slot]
    cycle = gains[0].shape[0]
    return pl.pallas_call(
        functools.partial(upper_kernel, sum(CUTS[:slot]), steps, heads),
        out_shape=[jax.ShapeDtypeStruct((3, out_rows(slot), 128), BF16)] * 4
        + [jax.ShapeDtypeStruct((steps, WIDE, 128), BF16)]
        + [jax.ShapeDtypeStruct((heads, 128), F32)] * 2,
        in_specs=[ANY] * 6 + [VMEM] * 2,
        out_specs=[ANY] * 5 + [VMEM] * 2,
        scratch_shapes=[pltpu.VMEM((cycle, 128), F32)] * 2 + [pltpu.VMEM((WIDE, 2 * WIDE), F32)],
        compiler_params=pltpu.CompilerParams(vmem_limit_bytes=40 * 1024 * 1024),
        cost_estimate=hub_cost(steps * BLOCK),
        name="upper_frames",
    )(*data, *gains)


def lower(slot, heads, data, packed, gains, outs):
    chunk = slot - 1
    steps = CUTS[chunk]
    cycle = gains[0].shape[0]
    return pl.pallas_call(
        functools.partial(lower_kernel, sum(CUTS[:chunk]), steps, heads),
        out_shape=[jax.ShapeDtypeStruct((3, out_rows(slot), 128), BF16)] * 4
        + [jax.ShapeDtypeStruct((heads, 128), F32)] * 2,
        in_specs=[ANY] * 7 + [VMEM] * 2 + [ANY] * 4,
        out_specs=[ANY] * 4 + [VMEM] * 2,
        scratch_shapes=[pltpu.VMEM((cycle, 128), F32)] * 2 + [pltpu.VMEM((WIDE, WIDE), F32)],
        input_output_aliases={9 + i: i for i in range(4)},
        compiler_params=pltpu.CompilerParams(vmem_limit_bytes=40 * 1024 * 1024),
        cost_estimate=hub_cost(steps * BLOCK),
        name="lower_frames",
    )(*data, packed, *gains, *outs)


def blank(slot):
    def kernel(*refs):
        pass

    return pl.pallas_call(
        kernel,
        out_shape=[jax.ShapeDtypeStruct((3, out_rows(slot), 128), BF16)] * 4,
        out_specs=[ANY] * 4,
        name="blank_rows",
    )()


def send(array, pairs):
    return lax.ppermute(array, "seq", pairs)


def hub_body(queries, key_proj, value_proj, out_grad, query_gain, key_gain):
    shape = queries.shape
    heads, width = shape[-2:]
    half = shape[2] // 2 * heads
    arrays = [x.reshape(2, half, width) for x in (queries, key_proj, value_proj, out_grad)]
    cycle = math.lcm(BLOCK, heads)
    other = 1 - lax.axis_index("seq") % 2
    chunks = len(CUTS)

    swapped = []
    for low, high in ((0, CUTS[0]), (CUTS[0], sum(CUTS))):
        rows = [
            lax.dynamic_slice(x, (other, low * BLOCK, 0), (1, (high - low) * BLOCK, width))
            for x in arrays
        ]
        swapped.append((send(jnp.concatenate(rows, axis=0), SWAP), low))

    landed = []
    for chunk in range(chunks):
        own_a, own_b = pack(
            sum(CUTS[:chunk]), CUTS[chunk], swapped[min(chunk, 1)][1], arrays, swapped[min(chunk, 1)][0]
        )
        edge_a = send(own_a, EDGE)
        other_a = send(own_a, MIDDLE)
        edge_b = send(own_b, EDGE)
        far_a = send(edge_a, MIDDLE)
        landed.append((own_a, edge_a, own_b, edge_b, other_a, far_a))

    both = lax.all_gather(jnp.stack([query_gain, key_gain]), "dp", axis=1, tiled=True)
    gains = [jnp.tile(both[t], (cycle // heads, 1)) for t in range(2)]

    outs = None
    sums = []
    packed = None
    for slot in range(chunks + 1):
        last = packed
        if slot < chunks:
            *grads, packed, sum_q, sum_k = upper(slot, heads, landed[slot], gains)
            packed = send(packed, DOWN)
            sums.append((sum_q, sum_k))
        else:
            grads = blank(slot)
        if slot > 0:
            *grads, sum_q, sum_k = lower(slot, heads, landed[slot - 1], last, gains, grads)
            sums.append((sum_q, sum_k))
        own, cross, edge_s, edge_x = grads
        pieces = (own, send(cross, SWAP), send(edge_s, BACK_S), send(edge_x, BACK_X))
        outs = unpack(slot, half, pieces, outs)

    totals = [functools.reduce(jnp.add, [s[t] for s in sums]) for t in range(2)]
    totals = lax.psum(jnp.stack(totals), ("dp", "seq"))
    mine = query_gain.shape[0]
    totals = lax.dynamic_slice_in_dim(totals, lax.axis_index("dp") * mine, mine, 1)
    return (*[x.reshape(shape) for x in outs], totals[0], totals[1])


def wide_attention(query_norm, key_norm, value_in, grad_in):
    frames = query_norm.shape[1]
    scaling = 1.0 / math.sqrt(query_norm.shape[-1])
    scores = (
        jnp.einsum("efphd,egphd->ephfg", query_norm, key_norm, preferred_element_type=F32) * scaling
    )
    allowed = iota((frames, frames), 1) <= iota((frames, frames), 0)
    scores = jnp.where(allowed, scores, -jnp.inf)
    expo = jnp.exp(scores - jnp.max(scores, axis=-1, keepdims=True))
    probability = expo / jnp.sum(expo, axis=-1, keepdims=True)
    prob_low = probability.astype(BF16)
    attn_out = jnp.einsum("ephfg,egphd->efphd", prob_low, value_in, preferred_element_type=F32)
    row_dots = jnp.transpose(jnp.sum(grad_in.astype(F32) * attn_out, axis=-1), (0, 2, 3, 1))
    prob_grad = jnp.einsum("efphd,egphd->ephfg", grad_in, value_in, preferred_element_type=F32)
    score_low = (probability * (prob_grad - row_dots[..., None])).astype(BF16)
    query_step = jnp.einsum("ephfg,egphd->efphd", score_low, key_norm, preferred_element_type=F32)
    key_step = jnp.einsum("ephfg,efphd->egphd", score_low, query_norm, preferred_element_type=F32)
    value_step = jnp.einsum("ephfg,efphd->egphd", prob_low, grad_in, preferred_element_type=F32)
    return (
        (query_step * scaling).astype(BF16),
        (key_step * scaling).astype(BF16),
        value_step.astype(BF16),
    )


def wide_body(queries, key_proj, value_proj, out_grad, query_gain, key_gain):
    gain_q = lax.all_gather(query_gain, "dp", axis=0, tiled=True)
    gain_k = lax.all_gather(key_gain, "dp", axis=0, tiled=True)
    q_hat, q_inv = rms(queries)
    k_hat, k_inv = rms(key_proj)
    pieces = [
        lax.all_to_all(x, "seq", split_axis=2, concat_axis=1, tiled=True)
        for x in ((q_hat * gain_q).astype(BF16), (k_hat * gain_k).astype(BF16), value_proj, out_grad)
    ]
    steps = [
        lax.all_to_all(x, "seq", split_axis=1, concat_axis=2, tiled=True)
        for x in wide_attention(*pieces)
    ]
    query_grad, part_q = norm_back(steps[0], q_hat, q_inv, gain_q)
    key_grad, part_k = norm_back(steps[1], k_hat, k_inv, gain_k)
    axes = tuple(range(part_q.ndim - 2))
    totals = lax.psum((jnp.sum(part_q, axis=axes), jnp.sum(part_k, axis=axes)), "seq")
    totals = [lax.psum_scatter(t, "dp", scatter_dimension=0, tiled=True) for t in totals]
    return (query_grad, key_grad, steps[2], *totals)


def body(*args):
    frames = lax.axis_size("seq")
    patches, heads, width = args[0].shape[2:]
    rows = patches // 2 * heads
    if frames == 8 and args[0].shape[:2] == (1, 1) and width == 128 and rows == sum(CUTS) * BLOCK:
        return hub_body(*args)
    return wide_body(*args)


def solution(mesh):
    whole = P("dp", "seq", None, None, None)
    gain = P("dp", None)
    return jax.shard_map(
        body,
        mesh=mesh,
        in_specs=(whole,) * 4 + (gain,) * 2,
        out_specs=(whole,) * 3 + (gain,) * 2,
        check_vma=False,
    )
```

time: 1340 us -> 586 us (0.44)
  Pallas kernels: 567 us -> 47.1 us
  waiting for transfers between devices: 480 us -> 287 us
  blocking collectives: 145 us -> 114 us
    pallas_call x16 -> x18, Pallas kernels: 567 us -> 47.1 us  [the longest x5 28.9 us: unpack(): pl.pallas_call(functools.partial(place_kernel, slot), out_shape=[jax.Shap...]
    ppermute x56 -> x37, waiting for transfers between devices: 480 us -> 287 us  [send(): return lax.ppermute(array, 'seq', pairs)]
    psum x1, blocking collectives: 137 us -> 105 us  [hub_body(): totals = lax.psum(jnp.stack(totals), ('dp', 'seq'))]
    ppermute x56 -> x37, starting transfers between devices: 95.7 us -> 88.9 us  [send(): return lax.ppermute(array, 'seq', pairs)]
    unnamed x172 -> x124, local copies, waits for them, and re-layouts: 42.5 us -> 40.9 us
  transfers between devices with their start and end apart: 56 -> 37, of which waited for: 12 -> 13; matrix products, arithmetic and copies ran while one was open for 0% -> 0% of each run, Pallas kernels for 32% -> 7%
where the time goes in v2:
time: 586 us; the launch traced here: 584 us
  waiting for transfers between devices  287 us (49%)
  blocking collectives  114 us (19%)
  starting transfers between devices  88.9 us (15%)
  Pallas kernels  47.1 us (8%)
  local copies, waits for them, and re-layouts  44.9 us (8%)
    ppermute x37, waiting for transfers between devices, send(): return lax.ppermute(array, 'seq', pairs)  287 us
    psum x1, blocking collectives, hub_body(): totals = lax.psum(jnp.stack(totals), ('dp', 'seq'))  105 us
    ppermute x37, starting transfers between devices, send(): return lax.ppermute(array, 'seq', pairs)  88.9 us
    unnamed x124, local copies, waits for them, and re-layouts  40.9 us
    pallas_call x5, Pallas kernels, unpack(): pl.pallas_call(functools.partial(place_kernel, slot), out_shape=[jax.Shap...  28.9 us
    pallas_call x4, Pallas kernels, pack(): pl.pallas_call(functools.partial(pack_kernel, first, steps, offset), out_...  16.9 us
  transfers between devices with their start and end apart: 37, of which 13 were waited for; matrix products, arithmetic and copies ran while one was open for 0% of the time, Pallas kernels for 7%

profile of v2, /device:TPU:0, one launch (start us, length us, event | category | flops | bytes accessed | tf_op | source)
XLA Modules:
  0.0 584.0 jit_solution(13943023971876573391)
XLA Ops:
  8.4 5.3 collective-permute-done.25.x
  13.7 4.0 pack_rows.7
  17.7 4.9 collective-permute-start.26
  23.4 4.0 collective-permute-start.27
  27.4 24.2 %collective-permute-done.26.edge_a = bf16[4,1280,128]{2,1,0:T(8,128)(2,1)S(1)} collective-permute-done((bf16[4,1280,128]{2,1,0:T(8,128)(2,1)S(1)}, bf16[4,1280,128]{2,1,0:T(8,128)(2,1)S(1)}, u32[]{:S(2)}, u32[]{:S(2)}) %collective-permute-start.26) | collective-permute-done | bytes 1310752 | tf_op jit(solution)/shard_map/ppermute | solution.py:438
  52.5 4.1 pack_rows.4
  57.7 7.2 %collective-permute-start.1 = (bf16[4,1280,128]{2,1,0:T(8,128)(2,1)S(1)}, bf16[4,1280,128]{2,1,0:T(8,128)(2,1)S(1)}, u32[]{:S(2)}, u32[]{:S(2)}) collective-permute-start(bf16[4,1280,128]{2,1,0:T(8,128)(2,1)S(1)} %get-tuple-element.84.own_a), channel_id=1, source_target_pairs={{0,2},{1,3},{6,4},{7,5},{8,10},{9,11},{14,12},{15,13},{16,18},{17,... | collective-permute-start | bytes 3932168 | tf_op jit(solution)/shard_map/ppermute | solution.py:438
  64.9 8.2 %all_gather.3 = f32[2,40,128]{2,0,1:T(2,128)S(1)} all-gather(f32[2,10,128]{2,0,1:T(2,128)S(1)} %pad_maximum_fusion.3), channel_id=1, replica_groups=mesh['dp'=4,'seq'=8] {'dp'}, dimensions={1}, use_global_device_ids=true | all-gather | bytes 51200 | tf_op jit(solution)/shard_map/all_gather | solution.py:469
  73.2 6.5 %collective-permute-done.27.edge_b = bf16[4,1280,128]{2,1,0:T(8,128)(2,1)S(1)} collective-permute-done((bf16[4,1280,128]{2,1,0:T(8,128)(2,1)S(1)}, bf16[4,1280,128]{2,1,0:T(8,128)(2,1)S(1)}, u32[]{:S(2)}, u32[]{:S(2)}) %collective-permute-start.27) | collective-permute-done | bytes 1310752 | tf_op jit(solution)/shard_map/ppermute | solution.py:438
  94.9 2.1 copy-done.7
  97.0 4.0 pack_rows.6
  101.0 5.2 collective-permute-start.17
  108.9 4.8 pack_rows.5
  113.7 22.3 %collective-permute-start.9 = (bf16[4,1280,128]{2,1,0:T(8,128)(2,1)}, bf16[4,1280,128]{2,1,0:T(8,128)(2,1)}, u32[]{:S(2)}, u32[]{:S(2)}) collective-permute-start(bf16[4,1280,128]{2,1,0:T(8,128)(2,1)} %get-tuple-element.95.own_a), channel_id=1, source_target_pairs={{0,2},{1,3},{6,4},{7,5},{8,10},{9,11},{14,12},{15,13},{16,18},{17,... | collective-permute-start | bytes 3932168 | tf_op jit(solution)/shard_map/ppermute | solution.py:438
  139.9 23.5 %collective-permute-done.2.edge_b = bf16[4,1280,128]{2,1,0:T(8,128)(2,1)S(1)} collective-permute-done((bf16[4,1280,128]{2,1,0:T(8,128)(2,1)S(1)}, bf16[4,1280,128]{2,1,0:T(8,128)(2,1)S(1)}, u32[]{:S(2)}, u32[]{:S(2)}) %collective-permute-start.2) | collective-permute-done | bytes 1310752 | tf_op jit(solution)/shard_map/ppermute | solution.py:438
  164.2 27.5 %collective-permute-done.9.edge_a = bf16[4,1280,128]{2,1,0:T(8,128)(2,1)} collective-permute-done((bf16[4,1280,128]{2,1,0:T(8,128)(2,1)}, bf16[4,1280,128]{2,1,0:T(8,128)(2,1)}, u32[]{:S(2)}, u32[]{:S(2)}) %collective-permute-start.9) | collective-permute-done | bytes 1310752 | tf_op jit(solution)/shard_map/ppermute | solution.py:438
  191.6 5.7 collective-permute-start.10
  197.3 22.3 %collective-permute-done.18.edge_b = bf16[4,1280,128]{2,1,0:T(8,128)(2,1)S(1)} collective-permute-done((bf16[4,1280,128]{2,1,0:T(8,128)(2,1)S(1)}, bf16[4,1280,128]{2,1,0:T(8,128)(2,1)S(1)}, u32[]{:S(2)}, u32[]{:S(2)}) %collective-permute-start.18) | collective-permute-done | bytes 1310752 | tf_op jit(solution)/shard_map/ppermute | solution.py:438
  226.4 21.2 %collective-permute-done.10.edge_b = bf16[4,1280,128]{2,1,0:T(8,128)(2,1)} collective-permute-done((bf16[4,1280,128]{2,1,0:T(8,128)(2,1)}, bf16[4,1280,128]{2,1,0:T(8,128)(2,1)}, u32[]{:S(2)}, u32[]{:S(2)}) %collective-permute-start.10) | collective-permute-done | bytes 1310752 | tf_op jit(solution)/shard_map/ppermute | solution.py:438
  262.6 14.8 %collective-permute-done.35.back_s = bf16[3,1280,128]{2,1,0:T(8,128)(2,1)} collective-permute-done((bf16[3,1280,128]{2,1,0:T(8,128)(2,1)}, bf16[3,1280,128]{2,1,0:T(8,128)(2,1)}, u32[]{:S(2)}, u32[]{:S(2)}) %collective-permute-start.35) | collective-permute-done | bytes 983072 | tf_op jit(solution)/shard_map/ppermute | solution.py:438
  278.7 15.3 %collective-permute-done.36.back_x = bf16[3,1280,128]{2,1,0:T(8,128)(2,1)} collective-permute-done((bf16[3,1280,128]{2,1,0:T(8,128)(2,1)}, bf16[3,1280,128]{2,1,0:T(8,128)(2,1)}, u32[]{:S(2)}, u32[]{:S(2)}) %collective-permute-start.36) | collective-permute-done | bytes 983072 | tf_op jit(solution)/shard_map/ppermute | solution.py:438
  294.0 2.1 collective-permute-start.14
  297.4 28.6 %collective-permute-done.32.back_s = bf16[3,1280,128]{2,1,0:T(8,128)(2,1)} collective-permute-done((bf16[3,1280,128]{2,1,0:T(8,128)(2,1)}, bf16[3,1280,128]{2,1,0:T(8,128)(2,1)}, u32[]{:S(2)}, u32[]{:S(2)}) %collective-permute-start.32) | collective-permute-done | bytes 983072 | tf_op jit(solution)/shard_map/ppermute | solution.py:438
  334.8 68.4 %collective-permute-done.33.back_x = bf16[3,1280,128]{2,1,0:T(8,128)(2,1)} collective-permute-done((bf16[3,1280,128]{2,1,0:T(8,128)(2,1)}, bf16[3,1280,128]{2,1,0:T(8,128)(2,1)}, u32[]{:S(2)}, u32[]{:S(2)}) %collective-permute-start.33) | collective-permute-done | bytes 983072 | tf_op jit(solution)/shard_map/ppermute | solution.py:438
  405.9 8.5 %collective-permute-start.6 = (bf16[3,1280,128]{2,1,0:T(8,128)(2,1)}, bf16[3,1280,128]{2,1,0:T(8,128)(2,1)S(1)}, u32[]{:S(2)}, u32[]{:S(2)}) collective-permute-start(bf16[3,1280,128]{2,1,0:T(8,128)(2,1)} %get-tuple-element.92), channel_id=1, source_target_pairs={{0,1},{1,0},{2,3},{3,2},{4,5},{5,4},{6,7},{7,6},{8,9},{9,8},{10,11... | collective-permute-start | bytes 2949128 | tf_op jit(solution)/shard_map/ppermute | solution.py:438
  414.4 18.6 %collective-permute-done.23.back_s = bf16[3,1280,128]{2,1,0:T(8,128)(2,1)} collective-permute-done((bf16[3,1280,128]{2,1,0:T(8,128)(2,1)}, bf16[3,1280,128]{2,1,0:T(8,128)(2,1)}, u32[]{:S(2)}, u32[]{:S(2)}) %collective-permute-start.23) | collective-permute-done | bytes 983072 | tf_op jit(solution)/shard_map/ppermute | solution.py:438
  434.3 11.1 %collective-permute-done.24.back_x = bf16[3,1280,128]{2,1,0:T(8,128)(2,1)} collective-permute-done((bf16[3,1280,128]{2,1,0:T(8,128)(2,1)}, bf16[3,1280,128]{2,1,0:T(8,128)(2,1)}, u32[]{:S(2)}, u32[]{:S(2)}) %collective-permute-start.24) | collective-permute-done | bytes 983072 | tf_op jit(solution)/shard_map/ppermute | solution.py:438
  449.1 105.3 %psum.7 = f32[2,40,128]{2,1,0:T(8,128)S(1)} all-reduce(f32[2,40,128]{2,1,0:T(8,128)S(1)} %pad_maximum_fusion.2), channel_id=1, replica_groups=mesh['dp'=4,'seq'=8] {'dp','seq'}, use_global_device_ids=true, to_apply=%region_0.1 | all-reduce | flops 10240 | bytes 81920 | tf_op jit(solution)/shard_map/psum | solution.py:491
  555.1 7.6 %place_rows.6 = (bf16[2,5120,128]{2,1,0:T(8,128)(2,1)}, bf16[2,5120,128]{2,1,0:T(8,128)(2,1)}, bf16[2,5120,128]{2,1,0:T(8,128)(2,1)}) custom-call(bf16[3,1280,128]{2,1,0:T(8,128)(2,1)S(1)} %copy-done.48, bf16[3,1280,128]{2,1,0:T(8,128)(2,1)} %collective-permute-done.31.other, ...), custom_call_target="tpu_custom_call", output_to_operand_aliasing={{0}: (4, {}), {1}: (5, {}), {2}: (6, {})} | custom-call | bytes 3932160 | tf_op jit(solution)/shard_map/place_rows/pallas_call | solution.py:130
  562.6 7.6 %place_rows.7 = (bf16[2,5120,128]{2,1,0:T(8,128)(2,1)}, bf16[2,5120,128]{2,1,0:T(8,128)(2,1)}, bf16[2,5120,128]{2,1,0:T(8,128)(2,1)}) custom-call(bf16[3,1280,128]{2,1,0:T(8,128)(2,1)S(1)} %copy-done.46, bf16[3,1280,128]{2,1,0:T(8,128)(2,1)} %collective-permute-done.22.other, ...), custom_call_target="tpu_custom_call", output_to_operand_aliasing={{0}: (4, {}), {1}: (5, {}), {2}: (6, {})} | custom-call | bytes 3932160 | tf_op jit(solution)/shard_map/place_rows/pallas_call | solution.py:130
  570.3 7.6 %place_rows.8 = (bf16[2,5120,128]{2,1,0:T(8,128)(2,1)}, bf16[2,5120,128]{2,1,0:T(8,128)(2,1)}, bf16[2,5120,128]{2,1,0:T(8,128)(2,1)}) custom-call(bf16[3,1280,128]{2,1,0:T(8,128)(2,1)S(1)} %copy-done.50, bf16[3,1280,128]{2,1,0:T(8,128)(2,1)} %collective-permute-done.14.other, ...), custom_call_target="tpu_custom_call", output_to_operand_aliasing={{0}: (4, {}), {1}: (5, {}), {2}: (6, {})} | custom-call | bytes 3932160 | tf_op jit(solution)/shard_map/place_rows/pallas_call | solution.py:130
  577.9 6.1 %place_rows.9 = (bf16[2,5120,128]{2,1,0:T(8,128)(2,1)}, bf16[2,5120,128]{2,1,0:T(8,128)(2,1)}, bf16[2,5120,128]{2,1,0:T(8,128)(2,1)}) custom-call(bf16[3,1280,128]{2,1,0:T(8,128)(2,1)S(1)} %copy-done.53, bf16[3,1280,128]{2,1,0:T(8,128)(2,1)S(1)} %collective-permute-done.6.other, ...), custom_call_target="tpu_custom_call", output_to_operand_aliasing={{0}: (4, {}), {1}: (5, {}), {2}: (6, {})} | custom-call | bytes 3932160 | tf_op jit(solution)/shard_map/place_rows/pallas_call | solution.py:130
  (202 shorter events, 73.7 us)
Async XLA Ops:
  4.9 47.6 %collective-permute-start = (bf16[4,3840,128]{2,1,0:T(8,128)(2,1)S(1)}, bf16[4,3840,128]{2,1,0:T(8,128)(2,1)S(1)}, u32[]{:S(2)}, u32[]{:S(2)}) collective-permute-start(bf16[4,3840,128]{2,1,0:T(8,128)(2,1)S(1)} %pad_maximum_fusion), channel_id=1, source_target_pairs={{0,1},{1,0},{2,3},{3,2},{4,5},{5,4},{6,7},{7,6},{8,9},{9,8},{10,11... | collective-permute-start | bytes 11796488 | tf_op jit(solution)/shard_map/ppermute | solution.py:438
  17.7 34.0 %collective-permute-start.26 = (bf16[4,1280,128]{2,1,0:T(8,128)(2,1)S(1)}, bf16[4,1280,128]{2,1,0:T(8,128)(2,1)S(1)}, u32[]{:S(2)}, u32[]{:S(2)}) collective-permute-start(bf16[4,1280,128]{2,1,0:T(8,128)(2,1)S(1)} %get-tuple-element.117.own_a), channel_id=1, source_target_pairs={{0,2},{1,3},{6,4},{7,5},{8,10},{9,11},{14,12},{15,13},{16,18},{17,... | collective-permute-start | bytes 3932168 | tf_op jit(solution)/shard_map/ppermute | solution.py:438
  22.6 58.2 %collective-permute-start.28 = (bf16[4,1280,128]{2,1,0:T(8,128)(2,1)S(1)}, bf16[4,1280,128]{2,1,0:T(8,128)(2,1)S(1)}, u32[]{:S(2)}, u32[]{:S(2)}) collective-permute-start(bf16[4,1280,128]{2,1,0:T(8,128)(2,1)S(1)} %get-tuple-element.117.own_a), channel_id=1, source_target_pairs={{2,4},{3,5},{4,2},{5,3},{10,12},{11,13},{12,10},{13,11},{18,20},{1... | collective-permute-start | bytes 3932168 | tf_op jit(solution)/shard_map/ppermute | solution.py:438
  23.4 56.4 %collective-permute-start.27 = (bf16[4,1280,128]{2,1,0:T(8,128)(2,1)S(1)}, bf16[4,1280,128]{2,1,0:T(8,128)(2,1)S(1)}, u32[]{:S(2)}, u32[]{:S(2)}) collective-permute-start(bf16[4,1280,128]{2,1,0:T(8,128)(2,1)S(1)} %get-tuple-element.118.own_b), channel_id=1, source_target_pairs={{0,2},{1,3},{6,4},{7,5},{8,10},{9,11},{14,12},{15,13},{16,18},{17,... | collective-permute-start | bytes 3932168 | tf_op jit(solution)/shard_map/ppermute | solution.py:438
  57.7 80.7 %collective-permute-start.1 = (bf16[4,1280,128]{2,1,0:T(8,128)(2,1)S(1)}, bf16[4,1280,128]{2,1,0:T(8,128)(2,1)S(1)}, u32[]{:S(2)}, u32[]{:S(2)}) collective-permute-start(bf16[4,1280,128]{2,1,0:T(8,128)(2,1)S(1)} %get-tuple-element.84.own_a), channel_id=1, source_target_pairs={{0,2},{1,3},{6,4},{7,5},{8,10},{9,11},{14,12},{15,13},{16,18},{17,... | collective-permute-start | bytes 3932168 | tf_op jit(solution)/shard_map/ppermute | solution.py:438
  93.1 42.9 %collective-permute-start.34 = (bf16[3,1280,128]{2,1,0:T(8,128)(2,1)}, bf16[3,1280,128]{2,1,0:T(8,128)(2,1)S(1)}, u32[]{:S(2)}, u32[]{:S(2)}) collective-permute-start(bf16[3,1280,128]{2,1,0:T(8,128)(2,1)} %get-tuple-element.129), channel_id=1, source_target_pairs={{0,1},{1,0},{2,3},{3,2},{4,5},{5,4},{6,7},{7,6},{8,9},{9,8},{10,11... | collective-permute-start | bytes 2949128 | tf_op jit(solution)/shard_map/ppermute | solution.py:438
  101.0 38.1 %collective-permute-start.17 = (bf16[4,1280,128]{2,1,0:T(8,128)(2,1)S(1)}, bf16[4,1280,128]{2,1,0:T(8,128)(2,1)S(1)}, u32[]{:S(2)}, u32[]{:S(2)}) collective-permute-start(bf16[4,1280,128]{2,1,0:T(8,128)(2,1)S(1)} %get-tuple-element.106.own_a), channel_id=1, source_target_pairs={{0,2},{1,3},{6,4},{7,5},{8,10},{9,11},{14,12},{15,13},{16,18},{17,... | collective-permute-start | bytes 3932168 | tf_op jit(solution)/shard_map/ppermute | solution.py:438
  107.0 56.5 %collective-permute-start.2 = (bf16[4,1280,128]{2,1,0:T(8,128)(2,1)S(1)}, bf16[4,1280,128]{2,1,0:T(8,128)(2,1)S(1)}, u32[]{:S(2)}, u32[]{:S(2)}) collective-permute-start(bf16[4,1280,128]{2,1,0:T(8,128)(2,1)S(1)} %copy-done.11), channel_id=1, source_target_pairs={{0,2},{1,3},{6,4},{7,5},{8,10},{9,11},{14,12},{15,13},{16,18},{17,... | collective-permute-start | bytes 3932168 | tf_op jit(solution)/shard_map/ppermute | solution.py:438
  113.7 77.9 %collective-permute-start.9 = (bf16[4,1280,128]{2,1,0:T(8,128)(2,1)}, bf16[4,1280,128]{2,1,0:T(8,128)(2,1)}, u32[]{:S(2)}, u32[]{:S(2)}) collective-permute-start(bf16[4,1280,128]{2,1,0:T(8,128)(2,1)} %get-tuple-element.95.own_a), channel_id=1, source_target_pairs={{0,2},{1,3},{6,4},{7,5},{8,10},{9,11},{14,12},{15,13},{16,18},{17,... | collective-permute-start | bytes 3932168 | tf_op jit(solution)/shard_map/ppermute | solution.py:438
  137.0 82.6 %collective-permute-start.18 = (bf16[4,1280,128]{2,1,0:T(8,128)(2,1)S(1)}, bf16[4,1280,128]{2,1,0:T(8,128)(2,1)S(1)}, u32[]{:S(2)}, u32[]{:S(2)}) collective-permute-start(bf16[4,1280,128]{2,1,0:T(8,128)(2,1)S(1)} %get-tuple-element.107.own_b), channel_id=1, source_target_pairs={{0,2},{1,3},{6,4},{7,5},{8,10},{9,11},{14,12},{15,13},{16,18},{17,... | collective-permute-start | bytes 3932168 | tf_op jit(solution)/shard_map/ppermute | solution.py:438
  138.4 83.0 %collective-permute-start.19 = (bf16[4,1280,128]{2,1,0:T(8,128)(2,1)S(1)}, bf16[4,1280,128]{2,1,0:T(8,128)(2,1)S(1)}, u32[]{:S(2)}, u32[]{:S(2)}) collective-permute-start(bf16[4,1280,128]{2,1,0:T(8,128)(2,1)S(1)} %get-tuple-element.106.own_a), channel_id=1, source_target_pairs={{2,4},{3,5},{4,2},{5,3},{10,12},{11,13},{12,10},{13,11},{18,20},{1... | collective-permute-start | bytes 3932168 | tf_op jit(solution)/shard_map/ppermute | solution.py:438
  139.1 83.9 %collective-permute-start.20 = (bf16[4,1280,128]{2,1,0:T(8,128)(2,1)S(1)}, bf16[4,1280,128]{2,1,0:T(8,128)(2,1)S(1)}, u32[]{:S(2)}, u32[]{:S(2)}) collective-permute-start(bf16[4,1280,128]{2,1,0:T(8,128)(2,1)S(1)} %collective-permute-done.17.edge_a), channel_id=1, source_target_pairs={{2,4},{3,5},{4,2},{5,3},{10,12},{11,13},{12,10},{13,11},{18,20},{1... | collective-permute-start | bytes 3932168 | tf_op jit(solution)/shard_map/ppermute | solution.py:438
  163.4 61.6 %collective-permute-start.3 = (bf16[4,1280,128]{2,1,0:T(8,128)(2,1)S(1)}, bf16[4,1280,128]{2,1,0:T(8,128)(2,1)S(1)}, u32[]{:S(2)}, u32[]{:S(2)}) collective-permute-start(bf16[4,1280,128]{2,1,0:T(8,128)(2,1)S(1)} %get-tuple-element.84.own_a), channel_id=1, source_target_pairs={{2,4},{3,5},{4,2},{5,3},{10,12},{11,13},{12,10},{13,11},{18,20},{1... | collective-permute-start | bytes 3932168 | tf_op jit(solution)/shard_map/ppermute | solution.py:438
  191.6 55.9 %collective-permute-start.10 = (bf16[4,1280,128]{2,1,0:T(8,128)(2,1)}, bf16[4,1280,128]{2,1,0:T(8,128)(2,1)}, u32[]{:S(2)}, u32[]{:S(2)}) collective-permute-start(bf16[4,1280,128]{2,1,0:T(8,128)(2,1)} %get-tuple-element.96.own_b), channel_id=1, source_target_pairs={{0,2},{1,3},{6,4},{7,5},{8,10},{9,11},{14,12},{15,13},{16,18},{17,... | collective-permute-start | bytes 3932168 | tf_op jit(solution)/shard_map/ppermute | solution.py:438
  219.6 34.4 %collective-permute-start.11 = (bf16[4,1280,128]{2,1,0:T(8,128)(2,1)}, bf16[4,1280,128]{2,1,0:T(8,128)(2,1)}, u32[]{:S(2)}, u32[]{:S(2)}) collective-permute-start(bf16[4,1280,128]{2,1,0:T(8,128)(2,1)} %get-tuple-element.95.own_a), channel_id=1, source_target_pairs={{2,4},{3,5},{4,2},{5,3},{10,12},{11,13},{12,10},{13,11},{18,20},{1... | collective-permute-start | bytes 3932168 | tf_op jit(solution)/shard_map/ppermute | solution.py:438
  221.3 32.6 %collective-permute-start.12 = (bf16[4,1280,128]{2,1,0:T(8,128)(2,1)}, bf16[4,1280,128]{2,1,0:T(8,128)(2,1)}, u32[]{:S(2)}, u32[]{:S(2)}) collective-permute-start(bf16[4,1280,128]{2,1,0:T(8,128)(2,1)} %collective-permute-done.9.edge_a), channel_id=1, source_target_pairs={{2,4},{3,5},{4,2},{5,3},{10,12},{11,13},{12,10},{13,11},{18,20},{1... | collective-permute-start | bytes 3932168 | tf_op jit(solution)/shard_map/ppermute | solution.py:438
  223.1 33.3 %collective-permute-start.4 = (bf16[4,1280,128]{2,1,0:T(8,128)(2,1)S(1)}, bf16[4,1280,128]{2,1,0:T(8,128)(2,1)}, u32[]{:S(2)}, u32[]{:S(2)}) collective-permute-start(bf16[4,1280,128]{2,1,0:T(8,128)(2,1)S(1)} %collective-permute-done.1.edge_a), channel_id=1, source_target_pairs={{2,4},{3,5},{4,2},{5,3},{10,12},{11,13},{12,10},{13,11},{18,20},{1... | collective-permute-start | bytes 3932168 | tf_op jit(solution)/shard_map/ppermute | solution.py:438
  225.1 52.3 %collective-permute-start.35 = (bf16[3,1280,128]{2,1,0:T(8,128)(2,1)}, bf16[3,1280,128]{2,1,0:T(8,128)(2,1)}, u32[]{:S(2)}, u32[]{:S(2)}) collective-permute-start(bf16[3,1280,128]{2,1,0:T(8,128)(2,1)} %copy-done.59), channel_id=1, source_target_pairs={{2,0},{3,1},{4,6},{5,7},{10,8},{11,9},{12,14},{13,15},{18,16},{19,... | collective-permute-start | bytes 2949128 | tf_op jit(solution)/shard_map/ppermute | solution.py:438
  247.6 46.4 %collective-permute-start.36 = (bf16[3,1280,128]{2,1,0:T(8,128)(2,1)}, bf16[3,1280,128]{2,1,0:T(8,128)(2,1)}, u32[]{:S(2)}, u32[]{:S(2)}) collective-permute-start(bf16[3,1280,128]{2,1,0:T(8,128)(2,1)} %copy-done.58), channel_id=1, source_target_pairs={{2,1},{3,0},{4,7},{5,6},{10,9},{11,8},{12,15},{13,14},{18,17},{19,... | collective-permute-start | bytes 2949128 | tf_op jit(solution)/shard_map/ppermute | solution.py:438
  254.0 42.1 %collective-permute-start.31 = (bf16[3,1280,128]{2,1,0:T(8,128)(2,1)}, bf16[3,1280,128]{2,1,0:T(8,128)(2,1)}, u32[]{:S(2)}, u32[]{:S(2)}) collective-permute-start(bf16[3,1280,128]{2,1,0:T(8,128)(2,1)} %get-tuple-element.125), channel_id=1, source_target_pairs={{0,1},{1,0},{2,3},{3,2},{4,5},{5,4},{6,7},{7,6},{8,9},{9,8},{10,11... | collective-permute-start | bytes 2949128 | tf_op jit(solution)/shard_map/ppermute | solution.py:438
  254.0 71.9 %collective-permute-start.32 = (bf16[3,1280,128]{2,1,0:T(8,128)(2,1)}, bf16[3,1280,128]{2,1,0:T(8,128)(2,1)}, u32[]{:S(2)}, u32[]{:S(2)}) collective-permute-start(bf16[3,1280,128]{2,1,0:T(8,128)(2,1)} %get-tuple-element.126), channel_id=1, source_target_pairs={{2,0},{3,1},{4,6},{5,7},{10,8},{11,9},{12,14},{13,15},{18,16},{19,... | collective-permute-start | bytes 2949128 | tf_op jit(solution)/shard_map/ppermute | solution.py:438
  257.9 38.1 %collective-permute-start.5 = (bf16[5,64,128]{2,1,0:T(8,128)(2,1)S(1)}, bf16[5,64,128]{2,1,0:T(8,128)(2,1)S(1)}, u32[]{:S(2)}, u32[]{:S(2)}) collective-permute-start(bf16[5,64,128]{2,1,0:T(8,128)(2,1)S(1)} %get-tuple-element.86), channel_id=1, source_target_pairs={{4,2},{5,3},{12,10},{13,11},{20,18},{21,19},{28,26},{29,27}} | collective-permute-start | bytes 245768 | tf_op jit(solution)/shard_map/ppermute | solution.py:438
  277.4 125.8 %collective-permute-start.33 = (bf16[3,1280,128]{2,1,0:T(8,128)(2,1)}, bf16[3,1280,128]{2,1,0:T(8,128)(2,1)}, u32[]{:S(2)}, u32[]{:S(2)}) collective-permute-start(bf16[3,1280,128]{2,1,0:T(8,128)(2,1)} %get-tuple-element.127), channel_id=1, source_target_pairs={{2,1},{3,0},{4,7},{5,6},{10,9},{11,8},{12,15},{13,14},{18,17},{19,... | collective-permute-start | bytes 2949128 | tf_op jit(solution)/shard_map/ppermute | solution.py:438
  294.0 110.6 %collective-permute-start.14 = (bf16[3,1280,128]{2,1,0:T(8,128)(2,1)}, bf16[3,1280,128]{2,1,0:T(8,128)(2,1)}, u32[]{:S(2)}, u32[]{:S(2)}) collective-permute-start(bf16[3,1280,128]{2,1,0:T(8,128)(2,1)} %get-tuple-element.103), channel_id=1, source_target_pairs={{0,1},{1,0},{2,3},{3,2},{4,5},{5,4},{6,7},{7,6},{8,9},{9,8},{10,11... | collective-permute-start | bytes 2949128 | tf_op jit(solution)/shard_map/ppermute | solution.py:438
  296.1 109.8 %collective-permute-start.22 = (bf16[3,1280,128]{2,1,0:T(8,128)(2,1)}, bf16[3,1280,128]{2,1,0:T(8,128)(2,1)}, u32[]{:S(2)}, u32[]{:S(2)}) collective-permute-start(bf16[3,1280,128]{2,1,0:T(8,128)(2,1)} %get-tuple-element.114), channel_id=1, source_target_pairs={{0,1},{1,0},{2,3},{3,2},{4,5},{5,4},{6,7},{7,6},{8,9},{9,8},{10,11... | collective-permute-start | bytes 2949128 | tf_op jit(solution)/shard_map/ppermute | solution.py:438
  296.1 136.9 %collective-permute-start.23 = (bf16[3,1280,128]{2,1,0:T(8,128)(2,1)}, bf16[3,1280,128]{2,1,0:T(8,128)(2,1)}, u32[]{:S(2)}, u32[]{:S(2)}) collective-permute-start(bf16[3,1280,128]{2,1,0:T(8,128)(2,1)} %get-tuple-element.115), channel_id=1, source_target_pairs={{2,0},{3,1},{4,6},{5,7},{10,8},{11,9},{12,14},{13,15},{18,16},{19,... | collective-permute-start | bytes 2949128 | tf_op jit(solution)/shard_map/ppermute | solution.py:438
  325.9 119.5 %collective-permute-start.24 = (bf16[3,1280,128]{2,1,0:T(8,128)(2,1)}, bf16[3,1280,128]{2,1,0:T(8,128)(2,1)}, u32[]{:S(2)}, u32[]{:S(2)}) collective-permute-start(bf16[3,1280,128]{2,1,0:T(8,128)(2,1)} %get-tuple-element.116), channel_id=1, source_target_pairs={{2,1},{3,0},{4,7},{5,6},{10,9},{11,8},{12,15},{13,14},{18,17},{19,... | collective-permute-start | bytes 2949128 | tf_op jit(solution)/shard_map/ppermute | solution.py:438
  403.2 167.0 %collective-permute-start.15 = (bf16[3,1280,128]{2,1,0:T(8,128)(2,1)}, bf16[3,1280,128]{2,1,0:T(8,128)(2,1)}, u32[]{:S(2)}, u32[]{:S(2)}) collective-permute-start(bf16[3,1280,128]{2,1,0:T(8,128)(2,1)} %get-tuple-element.104), channel_id=1, source_target_pairs={{2,0},{3,1},{4,6},{5,7},{10,8},{11,9},{12,14},{13,15},{18,16},{19,... | collective-permute-start | bytes 2949128 | tf_op jit(solution)/shard_map/ppermute | solution.py:438
  404.5 165.7 %collective-permute-start.16 = (bf16[3,1280,128]{2,1,0:T(8,128)(2,1)}, bf16[3,1280,128]{2,1,0:T(8,128)(2,1)}, u32[]{:S(2)}, u32[]{:S(2)}) collective-permute-start(bf16[3,1280,128]{2,1,0:T(8,128)(2,1)} %get-tuple-element.105), channel_id=1, source_target_pairs={{2,1},{3,0},{4,7},{5,6},{10,9},{11,8},{12,15},{13,14},{18,17},{19,... | collective-permute-start | bytes 2949128 | tf_op jit(solution)/shard_map/ppermute | solution.py:438
  405.9 172.0 %collective-permute-start.6 = (bf16[3,1280,128]{2,1,0:T(8,128)(2,1)}, bf16[3,1280,128]{2,1,0:T(8,128)(2,1)S(1)}, u32[]{:S(2)}, u32[]{:S(2)}) collective-permute-start(bf16[3,1280,128]{2,1,0:T(8,128)(2,1)} %get-tuple-element.92), channel_id=1, source_target_pairs={{0,1},{1,0},{2,3},{3,2},{4,5},{5,4},{6,7},{7,6},{8,9},{9,8},{10,11... | collective-permute-start | bytes 2949128 | tf_op jit(solution)/shard_map/ppermute | solution.py:438
  433.0 144.9 %collective-permute-start.7 = (bf16[3,1280,128]{2,1,0:T(8,128)(2,1)}, bf16[3,1280,128]{2,1,0:T(8,128)(2,1)S(1)}, u32[]{:S(2)}, u32[]{:S(2)}) collective-permute-start(bf16[3,1280,128]{2,1,0:T(8,128)(2,1)} %get-tuple-element.93), channel_id=1, source_target_pairs={{2,0},{3,1},{4,6},{5,7},{10,8},{11,9},{12,14},{13,15},{18,16},{19,... | collective-permute-start | bytes 2949128 | tf_op jit(solution)/shard_map/ppermute | solution.py:438
  445.4 132.5 %collective-permute-start.8 = (bf16[3,1280,128]{2,1,0:T(8,128)(2,1)}, bf16[3,1280,128]{2,1,0:T(8,128)(2,1)}, u32[]{:S(2)}, u32[]{:S(2)}) collective-permute-start(bf16[3,1280,128]{2,1,0:T(8,128)(2,1)} %get-tuple-element.94), channel_id=1, source_target_pairs={{2,1},{3,0},{4,7},{5,6},{10,9},{11,8},{12,15},{13,14},{18,17},{19,... | collective-permute-start | bytes 2949128 | tf_op jit(solution)/shard_map/ppermute | solution.py:438
  (67 other events, 1237.5 us)

commit v3 on v2

--- a/solution.py
+++ b/solution.py
@@ -14,7 +14,7 @@
 SLOTS = 4
 WIDE = GROUP * SLOTS
 TOGETHER = 64
-CUTS = (5, 5, 5, 5)
+CUTS = (3, 5, 6, 4, 2)
 
 EDGE = ((0, 2), (1, 3), (6, 4), (7, 5))
 MIDDLE = ((2, 4), (3, 5), (4, 2), (5, 3))
@@ -25,7 +25,7 @@
 
 F32 = jnp.float32
 BF16 = jnp.bfloat16
-ANY = pl.BlockSpec(memory_space=pltpu.HBM)
+ANY = pl.BlockSpec(memory_space=pl.ANY)
 VMEM = pl.BlockSpec(memory_space=pltpu.VMEM)
 
 
@@ -33,6 +33,50 @@
     index = lax.axis_index("seq")
     chip, core = index // 2, index % 2
     return chip, core
+
+
+def call(kernel, inputs, in_specs, after=(), **kwargs):
+    count, extra = len(inputs), len(after)
+
+    def trimmed(*refs):
+        kernel(*refs[:count], *refs[count + extra :])
+
+    return pl.pallas_call(
+        trimmed,
+        in_specs=list(in_specs) + [ANY] * extra,
+        compiler_params=pltpu.CompilerParams(vmem_limit_bytes=56 * 1024 * 1024),
+        **kwargs,
+    )(*inputs, *after)
+
+
+def halves_kernel(first, steps, *refs):
+    ins, out = refs[:4], refs[4]
+    _, core = place()
+
+    def step(*blocks):
+        for t in range(4):
+            blocks[4][t] = blocks[t][0]
+
+    pltpu.emit_pipeline(
+        step,
+        grid=(steps,),
+        in_specs=[pl.BlockSpec((1, BLOCK, 128), lambda i: (1 - core, first + i, 0))] * 4,
+        out_specs=[pl.BlockSpec((4, BLOCK, 128), lambda i: (0, i, 0))],
+    )(*ins, out)
+
+
+def halves(first, steps, arrays, after):
+    rows = steps * BLOCK
+    return call(
+        functools.partial(halves_kernel, first, steps),
+        arrays,
+        [ANY] * 4,
+        after,
+        out_shape=jax.ShapeDtypeStruct((4, rows, 128), BF16),
+        out_specs=ANY,
+        cost_estimate=pl.CostEstimate(flops=0, bytes_accessed=rows * 128 * 2 * 8, transcendentals=0),
+        name="other_half",
+    )
 
 
 def pack_kernel(first, steps, offset, q, k, v, g, x, a, b):
@@ -67,17 +111,18 @@
         run((q, g), (k, v), (0, 3), (1, 2))
 
 
-def pack(first, steps, offset, arrays, swapped):
+def pack(first, steps, offset, arrays, swapped, after):
     rows = steps * BLOCK
-    return pl.pallas_call(
+    return call(
         functools.partial(pack_kernel, first, steps, offset),
+        (*arrays, swapped),
+        [ANY] * 5,
+        after,
         out_shape=[jax.ShapeDtypeStruct((4, rows, 128), BF16)] * 2,
-        in_specs=[ANY] * 5,
         out_specs=[ANY] * 2,
-        compiler_params=pltpu.CompilerParams(vmem_limit_bytes=32 * 1024 * 1024),
         cost_estimate=pl.CostEstimate(flops=0, bytes_accessed=rows * 128 * 2 * 16, transcendentals=0),
         name="pack_rows",
-    )(*arrays, swapped)
+    )
 
 
 def place_kernel(slot, own, other, back_s, back_x, *refs):
@@ -127,18 +172,18 @@
 def unpack(slot, half, pieces, outs):
     first = outs is None
     outs = () if first else outs
-    return pl.pallas_call(
+    return call(
         functools.partial(place_kernel, slot),
+        (*pieces, *outs),
+        [ANY] * (4 + len(outs)),
         out_shape=[jax.ShapeDtypeStruct((2, half, 128), BF16)] * 3,
-        in_specs=[ANY] * (4 + len(outs)),
         out_specs=[ANY] * 3,
         input_output_aliases={} if first else {4: 0, 5: 1, 6: 2},
-        compiler_params=pltpu.CompilerParams(vmem_limit_bytes=32 * 1024 * 1024),
         cost_estimate=pl.CostEstimate(
-            flops=0, bytes_accessed=max(CUTS) * BLOCK * 128 * 2 * 12, transcendentals=0
+            flops=0, bytes_accessed=out_rows(slot) * 128 * 2 * 12, transcendentals=0
         ),
         name="place_rows",
-    )(*pieces, *outs)
+    )
 
 
 def rms(values):
@@ -387,55 +432,79 @@
     return max(CUTS[max(slot - 1, 0) : slot + 1]) * BLOCK
 
 
-def upper(slot, heads, data, gains):
+def upper(slot, heads, data, gains, after):
     steps = CUTS[slot]
     cycle = gains[0].shape[0]
-    return pl.pallas_call(
+    return call(
         functools.partial(upper_kernel, sum(CUTS[:slot]), steps, heads),
+        (*data, *gains),
+        [ANY] * 6 + [VMEM] * 2,
+        after,
         out_shape=[jax.ShapeDtypeStruct((3, out_rows(slot), 128), BF16)] * 4
         + [jax.ShapeDtypeStruct((steps, WIDE, 128), BF16)]
         + [jax.ShapeDtypeStruct((heads, 128), F32)] * 2,
-        in_specs=[ANY] * 6 + [VMEM] * 2,
         out_specs=[ANY] * 5 + [VMEM] * 2,
         scratch_shapes=[pltpu.VMEM((cycle, 128), F32)] * 2 + [pltpu.VMEM((WIDE, 2 * WIDE), F32)],
-        compiler_params=pltpu.CompilerParams(vmem_limit_bytes=40 * 1024 * 1024),
         cost_estimate=hub_cost(steps * BLOCK),
         name="upper_frames",
-    )(*data, *gains)
-
-
-def lower(slot, heads, data, packed, gains, outs):
+    )
+
+
+def lower(slot, heads, data, packed, gains, outs, after):
     chunk = slot - 1
     steps = CUTS[chunk]
     cycle = gains[0].shape[0]
-    return pl.pallas_call(
+    return call(
         functools.partial(lower_kernel, sum(CUTS[:chunk]), steps, heads),
+        (*data, packed, *gains, *outs),
+        [ANY] * 7 + [VMEM] * 2 + [ANY] * 4,
+        after,
         out_shape=[jax.ShapeDtypeStruct((3, out_rows(slot), 128), BF16)] * 4
         + [jax.ShapeDtypeStruct((heads, 128), F32)] * 2,
-        in_specs=[ANY] * 7 + [VMEM] * 2 + [ANY] * 4,
         out_specs=[ANY] * 4 + [VMEM] * 2,
         scratch_shapes=[pltpu.VMEM((cycle, 128), F32)] * 2 + [pltpu.VMEM((WIDE, WIDE), F32)],
         input_output_aliases={9 + i: i for i in range(4)},
-        compiler_params=pltpu.CompilerParams(vmem_limit_bytes=40 * 1024 * 1024),
         cost_estimate=hub_cost(steps * BLOCK),
         name="lower_frames",
-    )(*data, packed, *gains, *outs)
-
-
-def blank(slot):
+    )
+
+
+def blank(slot, after):
     def kernel(*refs):
         pass
 
-    return pl.pallas_call(
+    return call(
         kernel,
+        (),
+        [],
+        after,
         out_shape=[jax.ShapeDtypeStruct((3, out_rows(slot), 128), BF16)] * 4,
         out_specs=[ANY] * 4,
         name="blank_rows",
-    )()
+    )
 
 
 def send(array, pairs):
     return lax.ppermute(array, "seq", pairs)
+
+
+def sum_gains(part):
+    count = lax.axis_size("dp")
+    mine = part.shape[1] // count
+    index = lax.axis_index("dp")
+
+    def heads_of(who):
+        return lax.dynamic_slice_in_dim(part, who % count * mine, mine, 1)
+
+    total = heads_of(index)
+    for shift in range(1, count):
+        pairs = [(i, (i + shift) % count) for i in range(count)]
+        total = total + lax.ppermute(heads_of(index + shift), "dp", pairs)
+    total = total + send(total, SWAP)
+    total = total + send(total, MIDDLE)
+    edge = send(total, BACK_S)
+    chip, _ = place()
+    return jnp.where((chip == 1) | (chip == 2), total, edge)
 
 
 def hub_body(queries, key_proj, value_proj, out_grad, query_gain, key_gain):
@@ -444,54 +513,60 @@
     half = shape[2] // 2 * heads
     arrays = [x.reshape(2, half, width) for x in (queries, key_proj, value_proj, out_grad)]
     cycle = math.lcm(BLOCK, heads)
-    other = 1 - lax.axis_index("seq") % 2
     chunks = len(CUTS)
 
-    swapped = []
-    for low, high in ((0, CUTS[0]), (CUTS[0], sum(CUTS))):
-        rows = [
-            lax.dynamic_slice(x, (other, low * BLOCK, 0), (1, (high - low) * BLOCK, width))
-            for x in arrays
-        ]
-        swapped.append((send(jnp.concatenate(rows, axis=0), SWAP), low))
-
-    landed = []
-    for chunk in range(chunks):
-        own_a, own_b = pack(
-            sum(CUTS[:chunk]), CUTS[chunk], swapped[min(chunk, 1)][1], arrays, swapped[min(chunk, 1)][0]
-        )
+    near = halves(0, CUTS[0], arrays, ())
+    rest = halves(CUTS[0], sum(CUTS[1:]), arrays, (near,))
+    near, rest = send(near, SWAP), send(rest, SWAP)
+
+    both = lax.all_gather(jnp.stack([query_gain, key_gain]), "dp", axis=1, tiled=True)
+    gains = [jnp.tile(both[t], (cycle // heads, 1)) for t in range(2)]
+
+    landed, grads, packed, outs = {}, {}, {}, {-1: None}
+    sums = []
+
+    def bring(chunk):
+        after = []
+        if chunk >= 2:
+            after.append(landed[chunk - 2][1])
+        if chunk >= 3:
+            after.append(grads[chunk - 3][0])
+        swapped, offset = (near, 0) if chunk == 0 else (rest, CUTS[0])
+        own_a, own_b = pack(sum(CUTS[:chunk]), CUTS[chunk], offset, arrays, swapped, after)
         edge_a = send(own_a, EDGE)
         other_a = send(own_a, MIDDLE)
         edge_b = send(own_b, EDGE)
         far_a = send(edge_a, MIDDLE)
-        landed.append((own_a, edge_a, own_b, edge_b, other_a, far_a))
-
-    both = lax.all_gather(jnp.stack([query_gain, key_gain]), "dp", axis=1, tiled=True)
-    gains = [jnp.tile(both[t], (cycle // heads, 1)) for t in range(2)]
-
-    outs = None
-    sums = []
-    packed = None
-    for slot in range(chunks + 1):
-        last = packed
+        landed[chunk] = (own_a, edge_a, own_b, edge_b, other_a, far_a)
+
+    def work(slot):
+        after = list(outs[slot - 2][:1]) if slot >= 2 else []
         if slot < chunks:
-            *grads, packed, sum_q, sum_k = upper(slot, heads, landed[slot], gains)
-            packed = send(packed, DOWN)
+            *parts, cross, sum_q, sum_k = upper(slot, heads, landed[slot], gains, after)
+            packed[slot] = send(cross, DOWN)
             sums.append((sum_q, sum_k))
         else:
-            grads = blank(slot)
+            parts = blank(slot, after)
         if slot > 0:
-            *grads, sum_q, sum_k = lower(slot, heads, landed[slot - 1], last, gains, grads)
+            *parts, sum_q, sum_k = lower(
+                slot, heads, landed[slot - 1], packed[slot - 1], gains, parts, after
+            )
             sums.append((sum_q, sum_k))
-        own, cross, edge_s, edge_x = grads
+        grads[slot] = parts
+        own, cross, edge_s, edge_x = parts
         pieces = (own, send(cross, SWAP), send(edge_s, BACK_S), send(edge_x, BACK_X))
-        outs = unpack(slot, half, pieces, outs)
-
-    totals = [functools.reduce(jnp.add, [s[t] for s in sums]) for t in range(2)]
-    totals = lax.psum(jnp.stack(totals), ("dp", "seq"))
-    mine = query_gain.shape[0]
-    totals = lax.dynamic_slice_in_dim(totals, lax.axis_index("dp") * mine, mine, 1)
-    return (*[x.reshape(shape) for x in outs], totals[0], totals[1])
+        outs[slot] = unpack(slot, half, pieces, outs[slot - 1])
+
+    for chunk in range(min(3, chunks)):
+        bring(chunk)
+    for slot in range(chunks + 1):
+        work(slot)
+        if slot + 3 < chunks:
+            bring(slot + 3)
+
+    totals = jnp.stack([functools.reduce(jnp.add, [s[t] for s in sums]) for t in range(2)])
+    totals = sum_gains(totals)
+    return (*[x.reshape(shape) for x in outs[chunks]], totals[0], totals[1])
 
 
 def wide_attention(query_norm, key_norm, value_in, grad_in):

time: 586 us -> 523 us (0.89)
  blocking collectives: 114 us -> 8.24 us
  starting transfers between devices: 88.9 us -> 182 us
  waiting for transfers between devices: 287 us -> 229 us
  Pallas kernels: 47.1 us -> 85.2 us
  local copies, waits for them, and re-layouts: 44.9 us -> 9.79 us
    psum x1 -> x0, blocking collectives: 105 us -> none  [hub_body(): totals = lax.psum(jnp.stack(totals), ('dp', 'seq'))]
    ppermute x37 -> x48, starting transfers between devices: 88.9 us -> 178 us  [send(): return lax.ppermute(array, 'seq', pairs)]
    ppermute x37 -> x48, waiting for transfers between devices: 287 us -> 225 us  [send(): return lax.ppermute(array, 'seq', pairs)]
    pallas_call x18 -> x24, Pallas kernels: 47.1 us -> 85.2 us  [call(): pl.pallas_call(trimmed, in_specs=list(in_specs) + [ANY] * extra, compiler...]
    unnamed x124 -> x126, local copies, waits for them, and re-layouts: 40.9 us -> 7.32 us
  transfers between devices with their start and end apart: 37 -> 51, of which waited for: 13 -> 20; matrix products, arithmetic and copies ran while one was open for 0% -> 1% of each run, Pallas kernels for 7% -> 13%
where the time goes in v3:
time: 523 us; the launch traced here: 517 us
  waiting for transfers between devices  229 us (44%)
  starting transfers between devices  182 us (35%)
  Pallas kernels  85.2 us (16%)
  local copies, waits for them, and re-layouts  9.79 us (2%)
  blocking collectives  8.24 us (2%)
    ppermute x48, waiting for transfers between devices, send(): return lax.ppermute(array, 'seq', pairs)  225 us
    ppermute x48, starting transfers between devices, send(): return lax.ppermute(array, 'seq', pairs)  178 us
    pallas_call x24, Pallas kernels, call(): pl.pallas_call(trimmed, in_specs=list(in_specs) + [ANY] * extra, compiler...  85.2 us
  transfers between devices with their start and end apart: 51, of which 20 were waited for; matrix products, arithmetic and copies ran while one was open for 1% of the time, Pallas kernels for 13%

profile of v3, /device:TPU:0, one launch (start us, length us, event | category | flops | bytes accessed | tf_op | source)
XLA Modules:
  0.0 517.2 jit_solution(5291208298746944761)
XLA Ops:
  3.5 10.8 %other_half.3 = bf16[4,4352,128]{2,1,0:T(8,128)(2,1)} custom-call(bf16[2,5120,128]{2,1,0:T(8,128)(2,1)} %bitcast.21, bf16[2,5120,128]{2,1,0:T(8,128)(2,1)} %bitcast.28, bf16[2,5120,128]{2,1,0:T(8,128)(2,1)} %bitcast.35, bf16[2,5120,128]{2,1,0:T(8,128)(2,1)} %bitcast.42, bf16[4,768,128]{2,1,0:T(8,128)(2,1)} %other_half.2.refs_4_), custom_call_target="tpu_custom_call" | custom-call | bytes 8912896 | tf_op jit(solution)/shard_map/other_half/pallas_call | solution.py:44
  14.8 7.4 %collective-permute-done.1.refs_4_ = bf16[4,768,128]{2,1,0:T(8,128)(2,1)S(1)} collective-permute-done((bf16[4,768,128]{2,1,0:T(8,128)(2,1)S(1)}, bf16[4,768,128]{2,1,0:T(8,128)(2,1)S(1)}, u32[]{:S(2)}, u32[]{:S(2)}) %collective-permute-start.1) | collective-permute-done | bytes 786464 | tf_op jit(solution)/shard_map/ppermute | solution.py:488
  26.4 5.2 collective-permute-start.2
  32.3 4.1 collective-permute-start.4
  36.4 13.3 %collective-permute-done.2.refs_5_.refs_1_ = bf16[4,768,128]{2,1,0:T(8,128)(2,1)S(1)} collective-permute-done((bf16[4,768,128]{2,1,0:T(8,128)(2,1)}, bf16[4,768,128]{2,1,0:T(8,128)(2,1)S(1)}, u32[]{:S(2)}, u32[]{:S(2)}) %collective-permute-start.2) | collective-permute-done | bytes 786464 | tf_op jit(solution)/shard_map/ppermute | solution.py:488
  50.5 8.2 %all_gather.3 = f32[2,40,128]{2,0,1:T(2,128)S(1)} all-gather(f32[2,10,128]{2,0,1:T(2,128)S(1)} %pad_maximum_fusion), channel_id=1, replica_groups=mesh['dp'=4,'seq'=8] {'dp'}, dimensions={1}, use_global_device_ids=true | all-gather | bytes 51200 | tf_op jit(solution)/shard_map/all_gather | solution.py:522
  58.8 7.2 %collective-permute-done.4.refs_3_ = bf16[4,768,128]{2,1,0:T(8,128)(2,1)S(1)} collective-permute-done((bf16[4,768,128]{2,1,0:T(8,128)(2,1)}, bf16[4,768,128]{2,1,0:T(8,128)(2,1)S(1)}, u32[]{:S(2)}, u32[]{:S(2)}) %collective-permute-start.4) | collective-permute-done | bytes 786464 | tf_op jit(solution)/shard_map/ppermute | solution.py:488
  72.0 4.6 pack_rows.7
  76.6 8.4 %collective-permute-start.8 = (bf16[4,1280,128]{2,1,0:T(8,128)(2,1)}, bf16[4,1280,128]{2,1,0:T(8,128)(2,1)S(1)}, u32[]{:S(2)}, u32[]{:S(2)}) collective-permute-start(bf16[4,1280,128]{2,1,0:T(8,128)(2,1)} %get-tuple-element.106.refs_0_), channel_id=1, source_target_pairs={{0,2},{1,3},{6,4},{7,5},{8,10},{9,11},{14,12},{15,13},{16,18},{17,... | collective-permute-start | bytes 3932168 | tf_op jit(solution)/shard_map/ppermute | solution.py:488
  86.5 5.3 %pack_rows.6 = (bf16[4,1536,128]{2,1,0:T(8,128)(2,1)}, bf16[4,1536,128]{2,1,0:T(8,128)(2,1)}) custom-call(bf16[2,5120,128]{2,1,0:T(8,128)(2,1)} %bitcast.24, bf16[2,5120,128]{2,1,0:T(8,128)(2,1)} %bitcast.31, bf16[2,5120,128]{2,1,0:T(8,128)(2,1)} %bitcast.38, bf16[2,5120,128]{2,1,0:T(8,128)(2,1)} %bitcast.45, bf16[4,4352,128]{2,1,0:T(8,128)(2,1)} %copy-done, ...), custom_call_target="tpu_custom_call" | custom-call | bytes 6291456 | tf_op jit(solution)/shard_map/pack_rows/pallas_call | solution.py:44
  91.8 5.5 %collective-permute-start.3 = (bf16[4,1536,128]{2,1,0:T(8,128)(2,1)}, bf16[4,1536,128]{2,1,0:T(8,128)(2,1)S(1)}, u32[]{:S(2)}, u32[]{:S(2)}) collective-permute-start(bf16[4,1536,128]{2,1,0:T(8,128)(2,1)} %get-tuple-element.103.refs_0_), channel_id=1, source_target_pairs={{0,2},{1,3},{6,4},{7,5},{8,10},{9,11},{14,12},{15,13},{16,18},{17,... | collective-permute-start | bytes 4718600 | tf_op jit(solution)/shard_map/ppermute | solution.py:488
  103.4 26.4 %collective-permute-done.22.refs_3_ = bf16[3,768,128]{2,1,0:T(8,128)(2,1)S(1)} collective-permute-done((bf16[3,768,128]{2,1,0:T(8,128)(2,1)S(1)}, bf16[3,768,128]{2,1,0:T(8,128)(2,1)S(1)}, u32[]{:S(2)}, u32[]{:S(2)}) %collective-permute-start.22) | collective-permute-done | bytes 589856 | tf_op jit(solution)/shard_map/ppermute | solution.py:488
  129.8 3.9 collective-permute-start.9
  135.5 15.2 %collective-permute-start.17 = (bf16[4,1536,128]{2,1,0:T(8,128)(2,1)}, bf16[4,1536,128]{2,1,0:T(8,128)(2,1)S(1)}, u32[]{:S(2)}, u32[]{:S(2)}) collective-permute-start(bf16[4,1536,128]{2,1,0:T(8,128)(2,1)} %get-tuple-element.116.refs_2_), channel_id=1, source_target_pairs={{0,2},{1,3},{6,4},{7,5},{8,10},{9,11},{14,12},{15,13},{16,18},{17,... | collective-permute-start | bytes 4718600 | tf_op jit(solution)/shard_map/ppermute | solution.py:488
  155.3 20.8 %collective-permute-done.9.refs_3_ = bf16[4,1280,128]{2,1,0:T(8,128)(2,1)} collective-permute-done((bf16[4,1280,128]{2,1,0:T(8,128)(2,1)}, bf16[4,1280,128]{2,1,0:T(8,128)(2,1)}, u32[]{:S(2)}, u32[]{:S(2)}) %collective-permute-start.9) | collective-permute-done | bytes 1310752 | tf_op jit(solution)/shard_map/ppermute | solution.py:488
  176.1 5.4 %collective-permute-start.31 = (bf16[4,1024,128]{2,1,0:T(8,128)(2,1)}, bf16[4,1024,128]{2,1,0:T(8,128)(2,1)}, u32[]{:S(2)}, u32[]{:S(2)}) collective-permute-start(bf16[4,1024,128]{2,1,0:T(8,128)(2,1)} %get-tuple-element.141.refs_0_), channel_id=1, source_target_pairs={{0,2},{1,3},{6,4},{7,5},{8,10},{9,11},{14,12},{15,13},{16,18},{17,... | collective-permute-start | bytes 3145736 | tf_op jit(solution)/shard_map/ppermute | solution.py:488
  192.3 17.5 %collective-permute-done.17.refs_3_ = bf16[4,1536,128]{2,1,0:T(8,128)(2,1)S(1)} collective-permute-done((bf16[4,1536,128]{2,1,0:T(8,128)(2,1)}, bf16[4,1536,128]{2,1,0:T(8,128)(2,1)S(1)}, u32[]{:S(2)}, u32[]{:S(2)}) %collective-permute-start.17) | collective-permute-done | bytes 1572896 | tf_op jit(solution)/shard_map/ppermute | solution.py:488
  209.8 24.6 %collective-permute-start.12 = (bf16[4,512,128]{2,1,0:T(8,128)(2,1)}, bf16[4,512,128]{2,1,0:T(8,128)(2,1)}, u32[]{:S(2)}, u32[]{:S(2)}) collective-permute-start(bf16[4,512,128]{2,1,0:T(8,128)(2,1)} %get-tuple-element.113.refs_0_), channel_id=1, source_target_pairs={{0,2},{1,3},{6,4},{7,5},{8,10},{9,11},{14,12},{15,13},{16,18},{17,... | collective-permute-start | bytes 1572872 | tf_op jit(solution)/shard_map/ppermute | solution.py:488
  235.1 19.6 %collective-permute-done.32.refs_3_ = bf16[4,1024,128]{2,1,0:T(8,128)(2,1)} collective-permute-done((bf16[4,1024,128]{2,1,0:T(8,128)(2,1)}, bf16[4,1024,128]{2,1,0:T(8,128)(2,1)}, u32[]{:S(2)}, u32[]{:S(2)}) %collective-permute-start.32) | collective-permute-done | bytes 1048608 | tf_op jit(solution)/shard_map/ppermute | solution.py:488
  261.7 4.0 collective-permute-done.12.refs_1_
  268.9 66.2 %collective-permute-start.13 = (bf16[4,512,128]{2,1,0:T(8,128)(2,1)S(1)}, bf16[4,512,128]{2,1,0:T(8,128)(2,1)S(1)}, u32[]{:S(2)}, u32[]{:S(2)}) collective-permute-start(bf16[4,512,128]{2,1,0:T(8,128)(2,1)S(1)} %copy-done.16), channel_id=1, source_target_pairs={{0,2},{1,3},{6,4},{7,5},{8,10},{9,11},{14,12},{15,13},{16,18},{17,... | collective-permute-start | bytes 1572872 | tf_op jit(solution)/shard_map/ppermute | solution.py:488
  335.9 16.3 %collective-permute-done.28.refs_3_ = bf16[3,1280,128]{2,1,0:T(8,128)(2,1)S(1)} collective-permute-done((bf16[3,1280,128]{2,1,0:T(8,128)(2,1)}, bf16[3,1280,128]{2,1,0:T(8,128)(2,1)S(1)}, u32[]{:S(2)}, u32[]{:S(2)}) %collective-permute-start.28) | collective-permute-done | bytes 983072 | tf_op jit(solution)/shard_map/ppermute | solution.py:488
  354.5 5.5 %place_rows.7 = (bf16[2,5120,128]{2,1,0:T(8,128)(2,1)}, bf16[2,5120,128]{2,1,0:T(8,128)(2,1)}, bf16[2,5120,128]{2,1,0:T(8,128)(2,1)}) custom-call(bf16[3,1280,128]{2,1,0:T(8,128)(2,1)} %get-tuple-element.112.refs_6_.refs_0_, bf16[3,1280,128]{2,1,0:T(8,128)(2,1)} %collective-permute-done.26.refs_1_, ...), custom_call_target="tpu_custom_call", output_to_operand_aliasing={{0}: (4, {}), {1}: (5, {}), {2}: (6, {})} | custom-call | bytes 3932160 | tf_op jit(solution)/shard_map/place_rows/pallas_call | solution.py:44
  369.2 10.7 %collective-permute-done.24.refs_2_ = bf16[3,1536,128]{2,1,0:T(8,128)(2,1)S(1)} collective-permute-done((bf16[3,1536,128]{2,1,0:T(8,128)(2,1)}, bf16[3,1536,128]{2,1,0:T(8,128)(2,1)S(1)}, u32[]{:S(2)}, u32[]{:S(2)}) %collective-permute-start.24) | collective-permute-done | bytes 1179680 | tf_op jit(solution)/shard_map/ppermute | solution.py:488
  380.6 22.2 %collective-permute-done.25.refs_3_ = bf16[3,1536,128]{2,1,0:T(8,128)(2,1)S(1)} collective-permute-done((bf16[3,1536,128]{2,1,0:T(8,128)(2,1)}, bf16[3,1536,128]{2,1,0:T(8,128)(2,1)S(1)}, u32[]{:S(2)}, u32[]{:S(2)}) %collective-permute-start.25) | collective-permute-done | bytes 1179680 | tf_op jit(solution)/shard_map/ppermute | solution.py:488
  403.8 7.5 %place_rows.8 = (bf16[2,5120,128]{2,1,0:T(8,128)(2,1)}, bf16[2,5120,128]{2,1,0:T(8,128)(2,1)}, bf16[2,5120,128]{2,1,0:T(8,128)(2,1)}) custom-call(bf16[3,1536,128]{2,1,0:T(8,128)(2,1)} %get-tuple-element.126.refs_0_, bf16[3,1536,128]{2,1,0:T(8,128)(2,1)} %copy-done.22, ...), custom_call_target="tpu_custom_call", output_to_operand_aliasing={{0}: (4, {}), {1}: (5, {}), {2}: (6, {})} | custom-call | bytes 4718592 | tf_op jit(solution)/shard_map/place_rows/pallas_call | solution.py:44
  421.0 9.4 %collective-permute-done.36.refs_2_ = bf16[3,1536,128]{2,1,0:T(8,128)(2,1)S(1)} collective-permute-done((bf16[3,1536,128]{2,1,0:T(8,128)(2,1)}, bf16[3,1536,128]{2,1,0:T(8,128)(2,1)S(1)}, u32[]{:S(2)}, u32[]{:S(2)}) %collective-permute-start.36) | collective-permute-done | bytes 1179680 | tf_op jit(solution)/shard_map/ppermute | solution.py:488
  431.7 21.7 %collective-permute-done.37.refs_3_ = bf16[3,1536,128]{2,1,0:T(8,128)(2,1)} collective-permute-done((bf16[3,1536,128]{2,1,0:T(8,128)(2,1)}, bf16[3,1536,128]{2,1,0:T(8,128)(2,1)}, u32[]{:S(2)}, u32[]{:S(2)}) %collective-permute-start.37) | collective-permute-done | bytes 1179680 | tf_op jit(solution)/shard_map/ppermute | solution.py:488
  453.4 8.7 %place_rows.9 = (bf16[2,5120,128]{2,1,0:T(8,128)(2,1)}, bf16[2,5120,128]{2,1,0:T(8,128)(2,1)}, bf16[2,5120,128]{2,1,0:T(8,128)(2,1)}) custom-call(bf16[3,1536,128]{2,1,0:T(8,128)(2,1)} %get-tuple-element.147.refs_0_, bf16[3,1536,128]{2,1,0:T(8,128)(2,1)} %copy-done.20, ...), custom_call_target="tpu_custom_call", output_to_operand_aliasing={{0}: (4, {}), {1}: (5, {}), {2}: (6, {})} | custom-call | bytes 4718592 | tf_op jit(solution)/shard_map/place_rows/pallas_call | solution.py:44
  478.9 17.4 %collective-permute-done.50 = f32[2,10,128]{2,1,0:T(8,128)S(1)} collective-permute-done((f32[2,10,128]{2,1,0:T(8,128)S(1)}, f32[2,10,128]{2,1,0:T(8,128)S(1)}, u32[]{:S(2)}, u32[]{:S(2)}) %collective-permute-start.50) | collective-permute-done | bytes 10272 | tf_op jit(solution)/shard_map/ppermute | solution.py:488
  499.5 6.5 %place_rows.10 = (bf16[2,5120,128]{2,1,0:T(8,128)(2,1)}, bf16[2,5120,128]{2,1,0:T(8,128)(2,1)}, bf16[2,5120,128]{2,1,0:T(8,128)(2,1)}) custom-call(bf16[3,1024,128]{2,1,0:T(8,128)(2,1)} %get-tuple-element.167.refs_0_, bf16[3,1024,128]{2,1,0:T(8,128)(2,1)} %collective-permute-done.42.refs_1_, ...), custom_call_target="tpu_custom_call", output_to_operand_aliasing={{0}: (4, {}), {1}: (5, {}), {2}: (6, {})} | custom-call | bytes 3145728 | tf_op jit(solution)/shard_map/place_rows/pallas_call | solution.py:44
  506.0 4.4 collective-permute-done.39.refs_2_
  (235 shorter events, 101.7 us)
Async XLA Ops:
  14.3 55.7 %collective-permute-start = (bf16[4,4352,128]{2,1,0:T(8,128)(2,1)}, bf16[4,4352,128]{2,1,0:T(8,128)(2,1)S(1)}, u32[]{:S(2)}, u32[]{:S(2)}) collective-permute-start(bf16[4,4352,128]{2,1,0:T(8,128)(2,1)} %other_half.3), channel_id=1, source_target_pairs={{0,1},{1,0},{2,3},{3,2},{4,5},{5,4},{6,7},{7,6},{8,9},{9,8},{10,11... | collective-permute-start | bytes 13369352 | tf_op jit(solution)/shard_map/ppermute | solution.py:488
  32.3 33.7 %collective-permute-start.4 = (bf16[4,768,128]{2,1,0:T(8,128)(2,1)}, bf16[4,768,128]{2,1,0:T(8,128)(2,1)S(1)}, u32[]{:S(2)}, u32[]{:S(2)}) collective-permute-start(bf16[4,768,128]{2,1,0:T(8,128)(2,1)} %get-tuple-element.104.refs_2_), channel_id=1, source_target_pairs={{0,2},{1,3},{6,4},{7,5},{8,10},{9,11},{14,12},{15,13},{16,18},{17,... | collective-permute-start | bytes 2359304 | tf_op jit(solution)/shard_map/ppermute | solution.py:488
  69.9 28.8 %collective-permute-start.20 = (bf16[3,768,128]{2,1,0:T(8,128)(2,1)}, bf16[3,768,128]{2,1,0:T(8,128)(2,1)S(1)}, u32[]{:S(2)}, u32[]{:S(2)}) collective-permute-start(bf16[3,768,128]{2,1,0:T(8,128)(2,1)} %get-tuple-element.118), channel_id=1, source_target_pairs={{0,1},{1,0},{2,3},{3,2},{4,5},{5,4},{6,7},{7,6},{8,9},{9,8},{10,11... | collective-permute-start | bytes 1769480 | tf_op jit(solution)/shard_map/ppermute | solution.py:488
  76.6 57.1 %collective-permute-start.8 = (bf16[4,1280,128]{2,1,0:T(8,128)(2,1)}, bf16[4,1280,128]{2,1,0:T(8,128)(2,1)S(1)}, u32[]{:S(2)}, u32[]{:S(2)}) collective-permute-start(bf16[4,1280,128]{2,1,0:T(8,128)(2,1)} %get-tuple-element.106.refs_0_), channel_id=1, source_target_pairs={{0,2},{1,3},{6,4},{7,5},{8,10},{9,11},{14,12},{15,13},{16,18},{17,... | collective-permute-start | bytes 3932168 | tf_op jit(solution)/shard_map/ppermute | solution.py:488
  91.8 58.9 %collective-permute-start.3 = (bf16[4,1536,128]{2,1,0:T(8,128)(2,1)}, bf16[4,1536,128]{2,1,0:T(8,128)(2,1)S(1)}, u32[]{:S(2)}, u32[]{:S(2)}) collective-permute-start(bf16[4,1536,128]{2,1,0:T(8,128)(2,1)} %get-tuple-element.103.refs_0_), channel_id=1, source_target_pairs={{0,2},{1,3},{6,4},{7,5},{8,10},{9,11},{14,12},{15,13},{16,18},{17,... | collective-permute-start | bytes 4718600 | tf_op jit(solution)/shard_map/ppermute | solution.py:488
  97.9 37.5 %collective-permute-start.10 = (bf16[4,1280,128]{2,1,0:T(8,128)(2,1)S(1)}, bf16[4,1280,128]{2,1,0:T(8,128)(2,1)S(1)}, u32[]{:S(2)}, u32[]{:S(2)}) collective-permute-start(bf16[4,1280,128]{2,1,0:T(8,128)(2,1)S(1)} %copy-done.7), channel_id=1, source_target_pairs={{2,4},{3,5},{4,2},{5,3},{10,12},{11,13},{12,10},{13,11},{18,20},{1... | collective-permute-start | bytes 3932168 | tf_op jit(solution)/shard_map/ppermute | solution.py:488
  98.7 31.1 %collective-permute-start.22 = (bf16[3,768,128]{2,1,0:T(8,128)(2,1)S(1)}, bf16[3,768,128]{2,1,0:T(8,128)(2,1)S(1)}, u32[]{:S(2)}, u32[]{:S(2)}) collective-permute-start(bf16[3,768,128]{2,1,0:T(8,128)(2,1)S(1)} %copy-done.57), channel_id=1, source_target_pairs={{2,1},{3,0},{4,7},{5,6},{10,9},{11,8},{12,15},{13,14},{18,17},{19,... | collective-permute-start | bytes 1769480 | tf_op jit(solution)/shard_map/ppermute | solution.py:488
  102.6 78.8 %collective-permute-start.18 = (bf16[4,1536,128]{2,1,0:T(8,128)(2,1)}, bf16[4,1536,128]{2,1,0:T(8,128)(2,1)S(1)}, u32[]{:S(2)}, u32[]{:S(2)}) collective-permute-start(bf16[4,1536,128]{2,1,0:T(8,128)(2,1)} %get-tuple-element.103.refs_0_), channel_id=1, source_target_pairs={{2,4},{3,5},{4,2},{5,3},{10,12},{11,13},{12,10},{13,11},{18,20},{1... | collective-permute-start | bytes 4718600 | tf_op jit(solution)/shard_map/ppermute | solution.py:488
  129.8 46.3 %collective-permute-start.9 = (bf16[4,1280,128]{2,1,0:T(8,128)(2,1)}, bf16[4,1280,128]{2,1,0:T(8,128)(2,1)}, u32[]{:S(2)}, u32[]{:S(2)}) collective-permute-start(bf16[4,1280,128]{2,1,0:T(8,128)(2,1)} %get-tuple-element.107.refs_2_), channel_id=1, source_target_pairs={{0,2},{1,3},{6,4},{7,5},{8,10},{9,11},{14,12},{15,13},{16,18},{17,... | collective-permute-start | bytes 3932168 | tf_op jit(solution)/shard_map/ppermute | solution.py:488
  133.7 51.6 %collective-permute-start.11 = (bf16[4,1280,128]{2,1,0:T(8,128)(2,1)S(1)}, bf16[4,1280,128]{2,1,0:T(8,128)(2,1)}, u32[]{:S(2)}, u32[]{:S(2)}) collective-permute-start(bf16[4,1280,128]{2,1,0:T(8,128)(2,1)S(1)} %collective-permute-done.8.refs_1_.refs_5_), channel_id=1, source_target_pairs={{2,4},{3,5},{4,2},{5,3},{10,12},{11,13},{12,10},{13,11},{18,20},{1... | collective-permute-start | bytes 3932168 | tf_op jit(solution)/shard_map/ppermute | solution.py:488
  135.5 74.4 %collective-permute-start.17 = (bf16[4,1536,128]{2,1,0:T(8,128)(2,1)}, bf16[4,1536,128]{2,1,0:T(8,128)(2,1)S(1)}, u32[]{:S(2)}, u32[]{:S(2)}) collective-permute-start(bf16[4,1536,128]{2,1,0:T(8,128)(2,1)} %get-tuple-element.116.refs_2_), channel_id=1, source_target_pairs={{0,2},{1,3},{6,4},{7,5},{8,10},{9,11},{14,12},{15,13},{16,18},{17,... | collective-permute-start | bytes 4718600 | tf_op jit(solution)/shard_map/ppermute | solution.py:488
  150.7 104.8 %collective-permute-start.19 = (bf16[4,1536,128]{2,1,0:T(8,128)(2,1)S(1)}, bf16[4,1536,128]{2,1,0:T(8,128)(2,1)S(1)}, u32[]{:S(2)}, u32[]{:S(2)}) collective-permute-start(bf16[4,1536,128]{2,1,0:T(8,128)(2,1)S(1)} %collective-permute-done.3.refs_5_.refs_1_), channel_id=1, source_target_pairs={{2,4},{3,5},{4,2},{5,3},{10,12},{11,13},{12,10},{13,11},{18,20},{1... | collective-permute-start | bytes 4718600 | tf_op jit(solution)/shard_map/ppermute | solution.py:488
  176.1 58.3 %collective-permute-start.31 = (bf16[4,1024,128]{2,1,0:T(8,128)(2,1)}, bf16[4,1024,128]{2,1,0:T(8,128)(2,1)}, u32[]{:S(2)}, u32[]{:S(2)}) collective-permute-start(bf16[4,1024,128]{2,1,0:T(8,128)(2,1)} %get-tuple-element.141.refs_0_), channel_id=1, source_target_pairs={{0,2},{1,3},{6,4},{7,5},{8,10},{9,11},{14,12},{15,13},{16,18},{17,... | collective-permute-start | bytes 3145736 | tf_op jit(solution)/shard_map/ppermute | solution.py:488
  181.5 73.3 %collective-permute-start.32 = (bf16[4,1024,128]{2,1,0:T(8,128)(2,1)}, bf16[4,1024,128]{2,1,0:T(8,128)(2,1)}, u32[]{:S(2)}, u32[]{:S(2)}) collective-permute-start(bf16[4,1024,128]{2,1,0:T(8,128)(2,1)} %get-tuple-element.142.refs_2_), channel_id=1, source_target_pairs={{0,2},{1,3},{6,4},{7,5},{8,10},{9,11},{14,12},{15,13},{16,18},{17,... | collective-permute-start | bytes 3145736 | tf_op jit(solution)/shard_map/ppermute | solution.py:488
  185.3 75.8 %collective-permute-start.33 = (bf16[4,1024,128]{2,1,0:T(8,128)(2,1)}, bf16[4,1024,128]{2,1,0:T(8,128)(2,1)S(1)}, u32[]{:S(2)}, u32[]{:S(2)}) collective-permute-start(bf16[4,1024,128]{2,1,0:T(8,128)(2,1)} %get-tuple-element.141.refs_0_), channel_id=1, source_target_pairs={{2,4},{3,5},{4,2},{5,3},{10,12},{11,13},{12,10},{13,11},{18,20},{1... | collective-permute-start | bytes 3145736 | tf_op jit(solution)/shard_map/ppermute | solution.py:488
  209.8 55.8 %collective-permute-start.12 = (bf16[4,512,128]{2,1,0:T(8,128)(2,1)}, bf16[4,512,128]{2,1,0:T(8,128)(2,1)}, u32[]{:S(2)}, u32[]{:S(2)}) collective-permute-start(bf16[4,512,128]{2,1,0:T(8,128)(2,1)} %get-tuple-element.113.refs_0_), channel_id=1, source_target_pairs={{0,2},{1,3},{6,4},{7,5},{8,10},{9,11},{14,12},{15,13},{16,18},{17,... | collective-permute-start | bytes 1572872 | tf_op jit(solution)/shard_map/ppermute | solution.py:488
  234.4 33.2 %collective-permute-start.34 = (bf16[4,1024,128]{2,1,0:T(8,128)(2,1)}, bf16[4,1024,128]{2,1,0:T(8,128)(2,1)S(1)}, u32[]{:S(2)}, u32[]{:S(2)}) collective-permute-start(bf16[4,1024,128]{2,1,0:T(8,128)(2,1)} %collective-permute-done.31.refs_1_), channel_id=1, source_target_pairs={{2,4},{3,5},{4,2},{5,3},{10,12},{11,13},{12,10},{13,11},{18,20},{1... | collective-permute-start | bytes 3145736 | tf_op jit(solution)/shard_map/ppermute | solution.py:488
  255.6 79.6 %collective-permute-start.27 = (bf16[3,1280,128]{2,1,0:T(8,128)(2,1)}, bf16[3,1280,128]{2,1,0:T(8,128)(2,1)}, u32[]{:S(2)}, u32[]{:S(2)}) collective-permute-start(bf16[3,1280,128]{2,1,0:T(8,128)(2,1)} %get-tuple-element.131), channel_id=1, source_target_pairs={{2,0},{3,1},{4,6},{5,7},{10,8},{11,9},{12,14},{13,15},{18,16},{19,... | collective-permute-start | bytes 2949128 | tf_op jit(solution)/shard_map/ppermute | solution.py:488
  261.1 106.7 %collective-permute-start.23 = (bf16[3,1536,128]{2,1,0:T(8,128)(2,1)}, bf16[3,1536,128]{2,1,0:T(8,128)(2,1)S(1)}, u32[]{:S(2)}, u32[]{:S(2)}) collective-permute-start(bf16[3,1536,128]{2,1,0:T(8,128)(2,1)} %get-tuple-element.127), channel_id=1, source_target_pairs={{0,1},{1,0},{2,3},{3,2},{4,5},{5,4},{6,7},{7,6},{8,9},{9,8},{10,11... | collective-permute-start | bytes 3538952 | tf_op jit(solution)/shard_map/ppermute | solution.py:488
  266.3 85.9 %collective-permute-start.28 = (bf16[3,1280,128]{2,1,0:T(8,128)(2,1)}, bf16[3,1280,128]{2,1,0:T(8,128)(2,1)S(1)}, u32[]{:S(2)}, u32[]{:S(2)}) collective-permute-start(bf16[3,1280,128]{2,1,0:T(8,128)(2,1)} %get-tuple-element.132), channel_id=1, source_target_pairs={{2,1},{3,0},{4,7},{5,6},{10,9},{11,8},{12,15},{13,14},{18,17},{19,... | collective-permute-start | bytes 2949128 | tf_op jit(solution)/shard_map/ppermute | solution.py:488
  267.6 112.2 %collective-permute-start.24 = (bf16[3,1536,128]{2,1,0:T(8,128)(2,1)}, bf16[3,1536,128]{2,1,0:T(8,128)(2,1)S(1)}, u32[]{:S(2)}, u32[]{:S(2)}) collective-permute-start(bf16[3,1536,128]{2,1,0:T(8,128)(2,1)} %get-tuple-element.128), channel_id=1, source_target_pairs={{2,0},{3,1},{4,6},{5,7},{10,8},{11,9},{12,14},{13,15},{18,16},{19,... | collective-permute-start | bytes 3538952 | tf_op jit(solution)/shard_map/ppermute | solution.py:488
  268.9 95.3 %collective-permute-start.13 = (bf16[4,512,128]{2,1,0:T(8,128)(2,1)S(1)}, bf16[4,512,128]{2,1,0:T(8,128)(2,1)S(1)}, u32[]{:S(2)}, u32[]{:S(2)}) collective-permute-start(bf16[4,512,128]{2,1,0:T(8,128)(2,1)S(1)} %copy-done.16), channel_id=1, source_target_pairs={{0,2},{1,3},{6,4},{7,5},{8,10},{9,11},{14,12},{15,13},{16,18},{17,... | collective-permute-start | bytes 1572872 | tf_op jit(solution)/shard_map/ppermute | solution.py:488
  335.2 31.3 %collective-permute-start.14 = (bf16[4,512,128]{2,1,0:T(8,128)(2,1)S(1)}, bf16[4,512,128]{2,1,0:T(8,128)(2,1)S(1)}, u32[]{:S(2)}, u32[]{:S(2)}) collective-permute-start(bf16[4,512,128]{2,1,0:T(8,128)(2,1)S(1)} %copy-done.15), channel_id=1, source_target_pairs={{2,4},{3,5},{4,2},{5,3},{10,12},{11,13},{12,10},{13,11},{18,20},{1... | collective-permute-start | bytes 1572872 | tf_op jit(solution)/shard_map/ppermute | solution.py:488
  353.2 49.5 %collective-permute-start.25 = (bf16[3,1536,128]{2,1,0:T(8,128)(2,1)}, bf16[3,1536,128]{2,1,0:T(8,128)(2,1)S(1)}, u32[]{:S(2)}, u32[]{:S(2)}) collective-permute-start(bf16[3,1536,128]{2,1,0:T(8,128)(2,1)} %get-tuple-element.129), channel_id=1, source_target_pairs={{2,1},{3,0},{4,7},{5,6},{10,9},{11,8},{12,15},{13,14},{18,17},{19,... | collective-permute-start | bytes 3538952 | tf_op jit(solution)/shard_map/ppermute | solution.py:488
  364.3 55.5 %collective-permute-start.35 = (bf16[3,1536,128]{2,1,0:T(8,128)(2,1)}, bf16[3,1536,128]{2,1,0:T(8,128)(2,1)S(1)}, u32[]{:S(2)}, u32[]{:S(2)}) collective-permute-start(bf16[3,1536,128]{2,1,0:T(8,128)(2,1)} %get-tuple-element.148), channel_id=1, source_target_pairs={{0,1},{1,0},{2,3},{3,2},{4,5},{5,4},{6,7},{7,6},{8,9},{9,8},{10,11... | collective-permute-start | bytes 3538952 | tf_op jit(solution)/shard_map/ppermute | solution.py:488
  366.6 63.9 %collective-permute-start.36 = (bf16[3,1536,128]{2,1,0:T(8,128)(2,1)}, bf16[3,1536,128]{2,1,0:T(8,128)(2,1)S(1)}, u32[]{:S(2)}, u32[]{:S(2)}) collective-permute-start(bf16[3,1536,128]{2,1,0:T(8,128)(2,1)} %get-tuple-element.149), channel_id=1, source_target_pairs={{2,0},{3,1},{4,6},{5,7},{10,8},{11,9},{12,14},{13,15},{18,16},{19,... | collective-permute-start | bytes 3538952 | tf_op jit(solution)/shard_map/ppermute | solution.py:488
  367.9 85.6 %collective-permute-start.37 = (bf16[3,1536,128]{2,1,0:T(8,128)(2,1)}, bf16[3,1536,128]{2,1,0:T(8,128)(2,1)}, u32[]{:S(2)}, u32[]{:S(2)}) collective-permute-start(bf16[3,1536,128]{2,1,0:T(8,128)(2,1)} %get-tuple-element.150), channel_id=1, source_target_pairs={{2,1},{3,0},{4,7},{5,6},{10,9},{11,8},{12,15},{13,14},{18,17},{19,... | collective-permute-start | bytes 3538952 | tf_op jit(solution)/shard_map/ppermute | solution.py:488
  379.9 31.4 %collective-permute-start.15 = (bf16[4,512,128]{2,1,0:T(8,128)(2,1)}, bf16[4,512,128]{2,1,0:T(8,128)(2,1)S(1)}, u32[]{:S(2)}, u32[]{:S(2)}) collective-permute-start(bf16[4,512,128]{2,1,0:T(8,128)(2,1)} %collective-permute-done.12.refs_1_), channel_id=1, source_target_pairs={{2,4},{3,5},{4,2},{5,3},{10,12},{11,13},{12,10},{13,11},{18,20},{1... | collective-permute-start | bytes 1572872 | tf_op jit(solution)/shard_map/ppermute | solution.py:488
  414.1 47.9 %collective-permute-start.29 = (bf16[2,64,128]{2,1,0:T(8,128)(2,1)}, bf16[2,64,128]{2,1,0:T(8,128)(2,1)S(1)}, u32[]{:S(2)}, u32[]{:S(2)}) collective-permute-start(bf16[2,64,128]{2,1,0:T(8,128)(2,1)} %get-tuple-element.139), channel_id=1, source_target_pairs={{4,2},{5,3},{12,10},{13,11},{20,18},{21,19},{28,26},{29,27}} | collective-permute-start | bytes 98312 | tf_op jit(solution)/shard_map/ppermute | solution.py:488
  417.5 80.0 %collective-permute-start.42 = (bf16[3,1024,128]{2,1,0:T(8,128)(2,1)}, bf16[3,1024,128]{2,1,0:T(8,128)(2,1)}, u32[]{:S(2)}, u32[]{:S(2)}) collective-permute-start(bf16[3,1024,128]{2,1,0:T(8,128)(2,1)} %get-tuple-element.168), channel_id=1, source_target_pairs={{0,1},{1,0},{2,3},{3,2},{4,5},{5,4},{6,7},{7,6},{8,9},{9,8},{10,11... | collective-permute-start | bytes 2359304 | tf_op jit(solution)/shard_map/ppermute | solution.py:488
  419.8 79.8 %collective-permute-start.43 = (bf16[3,1024,128]{2,1,0:T(8,128)(2,1)}, bf16[3,1024,128]{2,1,0:T(8,128)(2,1)}, u32[]{:S(2)}, u32[]{:S(2)}) collective-permute-start(bf16[3,1024,128]{2,1,0:T(8,128)(2,1)} %get-tuple-element.169), channel_id=1, source_target_pairs={{2,0},{3,1},{4,6},{5,7},{10,8},{11,9},{12,14},{13,15},{18,16},{19,... | collective-permute-start | bytes 2359304 | tf_op jit(solution)/shard_map/ppermute | solution.py:488
  430.4 69.1 %collective-permute-start.44 = (bf16[3,1024,128]{2,1,0:T(8,128)(2,1)}, bf16[3,1024,128]{2,1,0:T(8,128)(2,1)}, u32[]{:S(2)}, u32[]{:S(2)}) collective-permute-start(bf16[3,1024,128]{2,1,0:T(8,128)(2,1)} %get-tuple-element.170), channel_id=1, source_target_pairs={{2,1},{3,0},{4,7},{5,6},{10,9},{11,8},{12,15},{13,14},{18,17},{19,... | collective-permute-start | bytes 2359304 | tf_op jit(solution)/shard_map/ppermute | solution.py:488
  (82 other events, 1351.5 us)

commit v4 on v3

v4 whole, which is shorter than its diff:
```python
import functools
import math

import jax
import jax.numpy as jnp
from jax import lax
from jax.experimental import pallas as pl
from jax.experimental.pallas import tpu as pltpu
from jax.sharding import PartitionSpec as P

EPSILON = 1e-06
BLOCK = 256
GROUP = 16
SLOTS = 4
WIDE = GROUP * SLOTS
TOGETHER = 64
CUTS = (2, 4, 5, 5, 3, 1)

EDGE = ((0, 2), (1, 3), (6, 4), (7, 5))
MIDDLE = ((2, 4), (3, 5), (4, 2), (5, 3))
DOWN = ((4, 2), (5, 3))
BACK_S = ((2, 0), (3, 1), (4, 6), (5, 7))
BACK_X = ((2, 1), (3, 0), (4, 7), (5, 6))
SWAP = tuple((i, i ^ 1) for i in range(8))

F32 = jnp.float32
BF16 = jnp.bfloat16
ANY = pl.BlockSpec(memory_space=pl.ANY)
VMEM = pl.BlockSpec(memory_space=pltpu.VMEM)


def place():
    index = lax.axis_index("seq")
    chip, core = index // 2, index % 2
    return chip, core


def call(kernel, inputs, in_specs, after=(), **kwargs):
    count, extra = len(inputs), len(after)

    def trimmed(*refs):
        kernel(*refs[:count], *refs[count + extra :])

    return pl.pallas_call(
        trimmed,
        in_specs=list(in_specs) + [ANY] * extra,
        compiler_params=pltpu.CompilerParams(vmem_limit_bytes=56 * 1024 * 1024),
        **kwargs,
    )(*inputs, *after)


def first_of(chunk):
    return sum(CUTS[:chunk]) * BLOCK


def rows_of(chunk):
    return CUTS[chunk] * BLOCK


def out_rows(slot):
    return max(CUTS[max(slot - 1, 0) : slot + 1]) * BLOCK


def copy_cost(rows, tensors):
    return pl.CostEstimate(flops=0, bytes_accessed=rows * 128 * 2 * 2 * tensors, transcendentals=0)


def tile_of(rows):
    return next(rows // k for k in range(2, rows) if rows % (16 * k) == 0 and rows // k <= 1024)


def stream(rows, sources, sinks, move):
    tile = tile_of(rows)

    def spec(ref):
        return pl.BlockSpec((ref.shape[0], tile, 128), lambda i: (0, i, 0))

    pltpu.emit_pipeline(
        move,
        grid=(rows // tile,),
        in_specs=[spec(ref) for ref in sources],
        out_specs=[spec(ref) for ref in sinks],
    )(*sources, *sinks)


def window(ref, index, start, rows, count=1):
    return ref.at[pl.ds(index, count), pl.ds(start, rows)]


def halves_kernel(start, rows, q, k, v, g, out):
    _, core = place()

    def move(*blocks):
        for t in range(4):
            blocks[4][t] = blocks[t][0]

    stream(rows, [window(ref, 1 - core, start, rows) for ref in (q, k, v, g)], [out], move)


def halves(start, rows, arrays, after):
    return call(
        functools.partial(halves_kernel, start, rows),
        arrays,
        [ANY] * 4,
        after,
        out_shape=jax.ShapeDtypeStruct((4, rows, 128), BF16),
        out_specs=ANY,
        cost_estimate=copy_cost(rows, 4),
        name="other_half",
    )


def pack_kernel(start, rows, offset, q, k, v, g, x, edge, middle):
    chip, core = place()

    def run(order):
        def move(*blocks):
            sent, crossing = blocks[8:]
            for pair in range(2):
                for t in range(2):
                    for frame in range(2):
                        value = blocks[4 * frame + 2 * pair + t][0]
                        sent[4 * pair + 2 * frame + t] = value
                        if pair == 0:
                            crossing[2 * frame + t] = value

        own = [window((q, k, v, g)[t], core, start, rows) for t in order]
        other = [window(x, t, start - offset, rows) for t in order]
        stream(rows, own + other, [edge, middle], move)

    @pl.when(chip < 2)
    def _():
        run((1, 2, 0, 3))

    @pl.when(chip >= 2)
    def _():
        run((0, 3, 1, 2))


def pack(chunk, offset, arrays, swapped, after):
    rows = rows_of(chunk)
    return call(
        functools.partial(pack_kernel, first_of(chunk), rows, offset),
        (*arrays, swapped),
        [ANY] * 5,
        after,
        out_shape=[jax.ShapeDtypeStruct((n, rows, 128), BF16) for n in (8, 4)],
        out_specs=[ANY] * 2,
        cost_estimate=copy_cost(rows, 10),
        name="pack_rows",
    )


def forward_kernel(rows, extra, edge, *refs):
    packed, out = refs[:-1], refs[-1]
    chip, _ = place()

    def move(src, dst):
        dst[...] = src[...]

    def move_packed(src, dst):
        dst[...] = src[...]

    @pl.when((chip == 1) | (chip == 2))
    def _():
        tile = tile_of(rows)
        pltpu.emit_pipeline(
            lambda src, dst: move(src.at[0], dst),
            grid=(4, rows // tile),
            in_specs=[pl.BlockSpec((1, tile, 128), lambda q, i: (q, i, 0))],
            out_specs=[pl.BlockSpec((tile, 128), lambda q, i: (q * (rows // tile) + i, 0))],
        )(edge, out.at[pl.ds(0, 4 * rows)])
        for ref in packed:
            pltpu.emit_pipeline(
                move_packed,
                grid=(1,),
                in_specs=[pl.BlockSpec((extra, 128), lambda i: (0, 0))],
                out_specs=[pl.BlockSpec((extra, 128), lambda i: (0, 0))],
            )(ref, out.at[pl.ds(4 * rows, extra)])


def forward(chunk, edge, packed, after):
    rows = rows_of(chunk)
    extra = 0 if packed is None else packed.shape[0]
    inputs = (edge,) if packed is None else (edge, packed)
    return call(
        functools.partial(forward_kernel, rows, extra),
        inputs,
        [ANY] * len(inputs),
        after,
        out_shape=jax.ShapeDtypeStruct((4 * rows + extra, 128), BF16),
        out_specs=ANY,
        cost_estimate=copy_cost(rows, 4),
        name="forward_rows",
    )


def copy_three(src, *dsts):
    for t, dst in enumerate(dsts):
        dst[0] = src[t]


def copy_all(src, dst):
    dst[...] = src[...]


def by_chip(slot, run):
    chip, _ = place()
    for which in range(4):
        chunk = slot if which >= 2 else slot - 1
        if 0 <= chunk < len(CUTS):
            pl.when(chip == which)(functools.partial(run, chunk, which in (1, 2)))


def place_kernel(slot, own, other, back, *refs):
    outs, late = refs[-4:-1], refs[-1]
    _, core = place()

    def run(chunk, hub):
        start, rows = first_of(chunk), rows_of(chunk)
        near = own.at[:, pl.ds(0, rows)] if hub else window(back, 0, 0, rows, 3)
        far = other.at[:, pl.ds(0, rows)] if hub else window(back, 3, 0, rows, 3)
        stream(rows, [near], [window(out, core, start, rows) for out in outs], copy_three)
        stream(rows, [far], [window(late, 0, start, rows, 3)], copy_all)

    by_chip(slot, run)


def place_last_kernel(slot, own, other, back_s, back_x, *refs):
    outs = refs[-3:]
    _, core = place()

    def run(chunk, hub):
        start, rows = first_of(chunk), rows_of(chunk)
        for half, src in ((core, own if hub else back_s), (1 - core, other if hub else back_x)):
            sinks = [window(out, half, start, rows) for out in outs]
            stream(rows, [src.at[:, pl.ds(0, rows)]], sinks, copy_three)

    by_chip(slot, run)


def place_late_kernel(slot, late, *refs):
    outs = refs[-3:]
    chip, core = place()

    def run(rows):
        sinks = [window(out, 1 - core, 0, rows) for out in outs]
        stream(rows, [window(late, 0, 0, rows, 3)], sinks, copy_three)

    @pl.when(chip < 2)
    def _():
        run(first_of(slot))

    @pl.when(chip >= 2)
    def _():
        run(first_of(slot + 1))


def settle_rows(kernel, half, pieces, kept, count, rows, after=()):
    kept = kept or ()
    return call(
        kernel,
        (*pieces, *kept),
        [ANY] * (len(pieces) + len(kept)),
        after,
        out_shape=[jax.ShapeDtypeStruct((n, half, 128), BF16) for n in (2, 2, 2, 3)[:count]],
        out_specs=[ANY] * count,
        input_output_aliases={len(pieces) + i: i for i in range(len(kept))},
        cost_estimate=copy_cost(rows, 6),
        name="place_rows",
    )


def rms(values):
    wide = values.astype(F32)
    inverse = lax.rsqrt(jnp.mean(wide * wide, axis=-1, keepdims=True) + EPSILON)
    return wide * inverse, inverse


def norm_back(step, hat, inverse, gain):
    wide = step.astype(F32)
    gained = gain * wide
    result = inverse * (gained - hat * jnp.mean(gained * hat, axis=-1, keepdims=True))
    return result.astype(BF16), wide * hat


def mul_t(a, b):
    return lax.dot_general(a, b, (((1,), (1,)), ((), ())), preferred_element_type=F32)


def t_mul(a, b):
    return lax.dot_general(a, b, (((0,), (0,)), ((), ())), preferred_element_type=F32)


def mul(a, b):
    return jnp.dot(a, b, preferred_element_type=F32)


def iota(shape, axis):
    return lax.broadcasted_iota(jnp.int32, shape, axis)


def frame_of(slot, core, upper):
    cross = slot % 2
    side = slot // 2
    side = side if upper else 1 - side
    return 2 * side + cross + core - 2 * cross * core


def causal(core, upper):
    shape = (WIDE, 2 * WIDE if upper else WIDE)
    rows, cols = iota(shape, 0), iota(shape, 1)
    key = cols // GROUP
    frame = frame_of(key % SLOTS, core, upper)
    if upper:
        frame = jnp.where(key < SLOTS, -1, frame)
    late = frame <= frame_of(rows // GROUP, core, upper)
    return (rows % GROUP == cols % GROUP) & late


def cat(parts):
    return jnp.concatenate(parts, axis=0)


def tiled(gain):
    return cat([gain] * SLOTS)


def group(wide, j):
    slots = wide.shape[0] // TOGETHER
    return cat([wide[s * TOGETHER + j * GROUP :][:GROUP] for s in range(slots)])


def ungroup(parts):
    return cat([part[s * GROUP :][:GROUP] for s in range(SLOTS) for part in parts])


def fold(acc, rows, part):
    total = part[:TOGETHER]
    for s in range(1, SLOTS):
        total = total + part[s * TOGETHER :][:TOGETHER]
    acc[rows, :] += total


def settle(outs, rows, parts):
    for t, part in enumerate(parts):
        for s, out in enumerate(outs):
            out[t, rows, :] = part[s * TOGETHER :][:TOGETHER]


def sum_heads(acc, heads):
    total = acc[0:heads, :]
    for i in range(1, acc.shape[0] // heads):
        total = total + acc[i * heads : (i + 1) * heads, :]
    return total


def read(refs, t, rows):
    return cat([ref[2 * x + t, rows, :] for ref in refs for x in range(2)])


def read_met(near, far, t, rows):
    return cat([near[2 * x + t, rows, :] for x in range(2)] + [far[2 * x + t][rows, :] for x in range(2)])


def hub_specs(steps):
    four = lambda n: pl.BlockSpec((4, BLOCK, 128), lambda i: (n, i, 0))
    flat = lambda q: pl.BlockSpec((BLOCK, 128), lambda i: (q * steps + i, 0))
    return [four(0), four(1), four(0), four(1), four(0)] + [flat(q) for q in range(4)]


def hub_refs(steps, own, edge, other, far):
    return [own, own, edge, edge, other] + [far.at[pl.ds(0, 4 * steps * BLOCK)]] * 4


def grad_specs():
    return [pl.BlockSpec((3, BLOCK, 128), lambda i: (0, i, 0))] * 4


def grad_refs(outs):
    if len(outs) == 4:
        return list(outs)
    return [outs[0], outs[1], outs[2].at[pl.ds(0, 3)], outs[2].at[pl.ds(3, 3)]]


def gain_spec(first, cycle):
    return pl.BlockSpec((BLOCK, 128), lambda i: ((first + i) % cycle, 0))


def attend(qn, kn, grad, value, allowed):
    scaling = 1.0 / math.sqrt(qn.shape[-1])
    count = TOGETHER // GROUP
    scores = cat([mul_t(group(qn, j), group(kn, j)) for j in range(count)])
    prob_grad = cat([mul_t(group(grad, j), group(value, j)) for j in range(count)])
    mask = cat([allowed] * count)
    scores = jnp.where(mask > 0, scores * scaling, -jnp.inf)
    expo = jnp.exp(scores - jnp.max(scores, axis=-1, keepdims=True))
    prob = expo * (1.0 / jnp.sum(expo, axis=-1, keepdims=True))
    prob_low = prob.astype(BF16)
    dots = jnp.sum(prob_low.astype(F32) * prob_grad, axis=-1, keepdims=True)
    score_low = (prob * (prob_grad - dots)).astype(BF16)
    split = lambda x: [x[j * WIDE :][:WIDE] for j in range(count)]
    return split(prob_low), split(score_low)


def upper_kernel(chunk, heads, own, edge, other, far, gain_q, gain_k, *refs):
    outs, (packed, sum_q, sum_k, acc_q, acc_k, mask) = refs[:-6], refs[-6:]
    chip, core = place()
    first, steps = sum(CUTS[:chunk]), CUTS[chunk]
    count = TOGETHER // GROUP
    cycle = acc_q.shape[0] // BLOCK

    def block(own_a, own_b, edge_a, edge_b, other, f0, f1, f2, f3, gain_q, gain_k, *results):
        out, pack_ref = results[:4], results[4]
        far = (f0, f1, f2, f3)
        base = ((first + pl.program_id(0)) % cycle) * BLOCK
        scaling = 1.0 / math.sqrt(128)
        lanes = iota((WIDE, 128), 1) // 8
        spread_r, spread_c = iota((2 * WIDE, 128), 0), iota((2 * WIDE, 128), 1)
        spread = jnp.where(spread_r // GROUP == spread_c % 8, 1.0, 0.0).astype(BF16)

        def some(i, total):
            rows = pl.ds(pl.multiple_of(i * TOGETHER, TOGETHER), TOGETHER)
            place = pl.ds(pl.multiple_of(base + i * TOGETHER, TOGETHER), TOGETHER)
            gq, gk = tiled(gain_q[rows, :]), tiled(gain_k[rows, :])
            q_hat, q_inv = rms(read((own_a, edge_a), 0, rows))
            grad = read((own_a, edge_a), 1, rows)
            kl_hat, _ = rms(read_met(other, far, 0, rows))
            ku_hat, ku_inv = rms(read((own_b, edge_b), 0, rows))
            value = cat([read_met(other, far, 1, rows), read((own_b, edge_b), 1, rows)])
            qn = (q_hat * gq).astype(BF16)
            kn = cat([(kl_hat * gk).astype(BF16), (ku_hat * gk).astype(BF16)])
            prob, score = attend(qn, kn, grad, value, mask[...])
            q_step = ungroup([mul(score[j], group(kn, j)) for j in range(count)])
            k_step = ungroup([t_mul(score[j][:, WIDE:], group(qn, j)) for j in range(count)])
            v_step = ungroup([t_mul(prob[j][:, WIDE:], group(grad, j)) for j in range(count)])
            q_step, k_step = (q_step * scaling).astype(BF16), (k_step * scaling).astype(BF16)
            dq, part_q = norm_back(q_step, q_hat, q_inv, gq)
            dk, part_k = norm_back(k_step, ku_hat, ku_inv, gk)
            settle(out, rows, (dq, dk, v_step.astype(BF16)))
            fold(acc_q, place, part_q)
            fold(acc_k, place, part_k)
            for j in range(count):
                cross = jnp.concatenate([prob[j][:, :WIDE], score[j][:, :WIDE]], axis=1)
                total = jnp.where(lanes == i * count + j, mul(cross, spread), total)
            return total

        total = lax.fori_loop(0, BLOCK // TOGETHER, some, jnp.zeros((WIDE, 128), F32))
        pack_ref[...] = total.astype(BF16)

    @pl.when(chip == 2)
    def _():
        acc_q[...] = jnp.zeros_like(acc_q)
        acc_k[...] = jnp.zeros_like(acc_k)
        mask[...] = causal(core, True).astype(F32)
        pltpu.emit_pipeline(
            block,
            grid=(steps,),
            in_specs=hub_specs(steps) + [gain_spec(first, cycle)] * 2,
            out_specs=grad_specs() + [pl.BlockSpec((WIDE, 128), lambda i: (i, 0))],
        )(*hub_refs(steps, own, edge, other, far), gain_q, gain_k, *grad_refs(outs), packed)
        sum_q[...] = sum_heads(acc_q, heads)
        sum_k[...] = sum_heads(acc_k, heads)

    @pl.when(chip != 2)
    def _():
        sum_q[...] = jnp.zeros_like(sum_q)
        sum_k[...] = jnp.zeros_like(sum_k)


def lower_kernel(chunk, skip, heads, own, edge, other, far, packed, gain_q, gain_k, *refs):
    outs, (sum_q, sum_k, acc_q, acc_k, mask) = refs[:-5], refs[-5:]
    outs = outs[len(outs) // 2 :]
    chip, core = place()
    first, steps = sum(CUTS[:chunk]), CUTS[chunk]
    count = TOGETHER // GROUP
    cycle = acc_q.shape[0] // BLOCK

    def block(own_a, own_b, edge_a, edge_b, other, f0, f1, f2, f3, gain_q, gain_k, pack_ref, *out):
        far = (f0, f1, f2, f3)
        base = ((first + pl.program_id(0)) % cycle) * BLOCK
        both = iota((WIDE, 2 * WIDE), 0) % GROUP == iota((WIDE, 2 * WIDE), 1) % GROUP
        scaling = 1.0 / math.sqrt(128)
        lanes = iota((WIDE, 128), 1) // 8
        spread_r, spread_c = iota((128, 2 * WIDE), 0), iota((128, 2 * WIDE), 1)
        spread = jnp.where(spread_c // GROUP == spread_r % 8, 1.0, 0.0).astype(BF16)
        crossed = pack_ref[...].astype(F32)

        def some(i, carry):
            rows = pl.ds(pl.multiple_of(i * TOGETHER, TOGETHER), TOGETHER)
            place = pl.ds(pl.multiple_of(base + i * TOGETHER, TOGETHER), TOGETHER)
            gq, gk = tiled(gain_q[rows, :]), tiled(gain_k[rows, :])
            k_hat, k_inv = rms(read((own_a, edge_a), 0, rows))
            value = read((own_a, edge_a), 1, rows)
            q_hat, q_inv = rms(read((own_b, edge_b), 0, rows))
            grad = read((own_b, edge_b), 1, rows)
            qu_hat, _ = rms(read_met(other, far, 0, rows))
            grad_u = read_met(other, far, 1, rows)
            kn = (k_hat * gk).astype(BF16)
            qn = (q_hat * gq).astype(BF16)
            qn_u = (qu_hat * gq).astype(BF16)
            prob, score = attend(qn, kn, grad, value, mask[...])
            cross = []
            for j in range(count):
                mine = jnp.where(lanes == i * count + j, crossed, 0.0).astype(BF16)
                cross.append(jnp.where(both, mul(mine, spread), 0.0).astype(BF16))
            q_step = ungroup([mul(score[j], group(kn, j)) for j in range(count)])
            k_step = ungroup(
                [
                    t_mul(cat([score[j], cross[j][:, WIDE:]]), cat([group(qn, j), group(qn_u, j)]))
                    for j in range(count)
                ]
            )
            v_step = ungroup(
                [
                    t_mul(cat([prob[j], cross[j][:, :WIDE]]), cat([group(grad, j), group(grad_u, j)]))
                    for j in range(count)
                ]
            )
            q_step, k_step = (q_step * scaling).astype(BF16), (k_step * scaling).astype(BF16)
            dq, part_q = norm_back(q_step, q_hat, q_inv, gq)
            dk, part_k = norm_back(k_step, k_hat, k_inv, gk)
            settle(out, rows, (dq, dk, v_step.astype(BF16)))
            fold(acc_q, place, part_q)
            fold(acc_k, place, part_k)
            return carry

        lax.fori_loop(0, BLOCK // TOGETHER, some, 0)

    @pl.when(chip == 1)
    def _():
        acc_q[...] = jnp.zeros_like(acc_q)
        acc_k[...] = jnp.zeros_like(acc_k)
        mask[...] = causal(core, False).astype(F32)
        pltpu.emit_pipeline(
            block,
            grid=(steps,),
            in_specs=hub_specs(steps)
            + [gain_spec(first, cycle)] * 2
            + [pl.BlockSpec((WIDE, 128), lambda i: (i, 0))],
            out_specs=grad_specs(),
        )(
            *hub_refs(steps, own, edge, other, far),
            gain_q,
            gain_k,
            packed.at[pl.ds(skip, steps * WIDE)],
            *grad_refs(outs),
        )
        sum_q[...] = sum_heads(acc_q, heads)
        sum_k[...] = sum_heads(acc_k, heads)

    @pl.when(chip != 1)
    def _():
        sum_q[...] = jnp.zeros_like(sum_q)
        sum_k[...] = jnp.zeros_like(sum_k)


def hub_cost(rows):
    return pl.CostEstimate(
        flops=rows * 60000, bytes_accessed=rows * 128 * 2 * 36, transcendentals=rows * 600
    )


def grad_shapes(slot):
    sizes = (3, 3, 6) if slot < len(CUTS) - 1 else (3, 3, 3, 3)
    return [jax.ShapeDtypeStruct((n, out_rows(slot), 128), BF16) for n in sizes]


def upper(slot, heads, data, gains, after):
    steps = CUTS[slot]
    cycle = gains[0].shape[0]
    shapes = grad_shapes(slot)
    return call(
        functools.partial(upper_kernel, slot, heads),
        (*data, *gains),
        [ANY] * 6,
        after,
        out_shape=shapes
        + [jax.ShapeDtypeStruct((steps * WIDE, 128), BF16)]
        + [jax.ShapeDtypeStruct((heads, 128), F32)] * 2,
        out_specs=[ANY] * (len(shapes) + 1) + [VMEM] * 2,
        scratch_shapes=[pltpu.VMEM((cycle, 128), F32)] * 2 + [pltpu.VMEM((WIDE, 2 * WIDE), F32)],
        cost_estimate=hub_cost(steps * BLOCK),
        name="upper_frames",
    )


def lower(slot, heads, data, packed, skip, gains, outs, after):
    chunk = slot - 1
    cycle = gains[0].shape[0]
    shapes = grad_shapes(slot)
    return call(
        functools.partial(lower_kernel, chunk, skip, heads),
        (*data, packed, *gains, *outs),
        [ANY] * (7 + len(outs)),
        after,
        out_shape=shapes + [jax.ShapeDtypeStruct((heads, 128), F32)] * 2,
        out_specs=[ANY] * len(shapes) + [VMEM] * 2,
        scratch_shapes=[pltpu.VMEM((cycle, 128), F32)] * 2 + [pltpu.VMEM((WIDE, WIDE), F32)],
        input_output_aliases={7 + i: i for i in range(len(outs))},
        cost_estimate=hub_cost(rows_of(chunk)),
        name="lower_frames",
    )


def blank(slot, after):
    def kernel(*refs):
        pass

    shapes = grad_shapes(slot)
    return call(
        kernel, (), [], after, out_shape=shapes, out_specs=[ANY] * len(shapes), name="blank_rows"
    )


def send(array, pairs):
    return lax.ppermute(array, "seq", pairs)


def sum_gains(part):
    count = lax.axis_size("dp")
    mine = part.shape[1] // count
    pieces = part.reshape(2, count, mine, part.shape[2])
    total = jnp.sum(lax.all_to_all(pieces, "dp", split_axis=1, concat_axis=1, tiled=True), axis=1)
    total = total + send(total, SWAP)
    total = total + send(total, MIDDLE)
    edge = send(total, BACK_S)
    chip, _ = place()
    return jnp.where((chip == 1) | (chip == 2), total, edge)


def hub_body(queries, key_proj, value_proj, out_grad, query_gain, key_gain):
    shape = queries.shape
    heads, width = shape[-2:]
    half = shape[2] // 2 * heads
    arrays = [x.reshape(2, half, width) for x in (queries, key_proj, value_proj, out_grad)]
    cycle = math.lcm(BLOCK, heads)
    chunks = len(CUTS)

    near = send(halves(0, rows_of(0), arrays, ()), SWAP)
    traded = [(near, 0)]

    edges, others, fars, grads, packed = {}, {}, {}, {}, {}
    passed, sums, kept = {}, [], {-1: None}

    def bring(chunk):
        after = []
        if chunk >= 2:
            after += [passed[chunk - 2], edges[chunk - 2][1]]
        if chunk >= 3:
            after.append(grads[chunk - 3][0])
        swapped, offset = traded[min(chunk, 1)]
        to_hub, to_middle = pack(chunk, offset, arrays, swapped, after)
        edges[chunk] = (to_hub, send(to_hub, EDGE))
        others[chunk] = send(to_middle, MIDDLE)
        return to_hub

    def pass_on(chunk):
        after = [grads[chunk - 1][0]] if chunk else []
        passed[chunk] = forward(chunk, edges[chunk][1], packed.get(chunk - 1), after)
        fars[chunk] = send(passed[chunk], MIDDLE)

    def work(slot):
        after = list(kept[slot - 2][:1]) if slot >= 2 else []
        if slot < chunks:
            data = (*edges[slot], others[slot], fars[slot])
            *parts, packed[slot], sum_q, sum_k = upper(slot, heads, data, gains, after)
            sums.append((sum_q, sum_k))
        else:
            parts = blank(slot, after)
        if slot > 0:
            chunk = slot - 1
            data = (*edges[chunk], others[chunk], fars[chunk])
            if slot < chunks:
                cross, skip = fars[slot], 4 * rows_of(slot)
            else:
                cross, skip = send(packed[chunk], DOWN), 0
            *parts, sum_q, sum_k = lower(slot, heads, data, cross, skip, gains, parts, after)
            sums.append((sum_q, sum_k))
        grads[slot] = parts

    def give(slot):
        own, other, *edge = grads[slot]
        rows = out_rows(slot)
        if slot < chunks - 1:
            pieces = (own, other, send(edge[0], BACK_S))
            kernel = functools.partial(place_kernel, slot)
            kept[slot] = settle_rows(kernel, half, pieces, kept[slot - 1], 4, rows)
            return
        if slot == chunks - 1:
            *outs, late = kept[slot - 1]
            kernel = functools.partial(place_late_kernel, slot - 1)
            kept[slot - 1] = settle_rows(kernel, half, (send(late, SWAP),), outs, 3, half // 2)
        pieces = (own, send(other, SWAP), send(edge[0], BACK_S), send(edge[1], BACK_X))
        kernel = functools.partial(place_last_kernel, slot)
        kept[slot] = settle_rows(kernel, half, pieces, kept[slot - 1], 3, rows)

    first = bring(0)
    rest = halves(rows_of(0), half - rows_of(0), arrays, (first,))
    traded.append((send(rest, SWAP), rows_of(0)))
    bring(1)
    both = lax.all_gather(jnp.stack([query_gain, key_gain]), "dp", axis=1, tiled=True)
    gains = [jnp.tile(both[t], (cycle // heads, 1)) for t in range(2)]
    for slot in range(chunks + 1):
        if slot < chunks:
            pass_on(slot)
        if slot + 2 < chunks:
            bring(slot + 2)
        work(slot)
        give(slot)

    totals = jnp.stack([functools.reduce(jnp.add, [s[t] for s in sums]) for t in range(2)])
    totals = sum_gains(totals)
    return (*[x.reshape(shape) for x in kept[chunks]], totals[0], totals[1])


def wide_attention(query_norm, key_norm, value_in, grad_in):
    frames = query_norm.shape[1]
    scaling = 1.0 / math.sqrt(query_norm.shape[-1])
    scores = (
        jnp.einsum("efphd,egphd->ephfg", query_norm, key_norm, preferred_element_type=F32) * scaling
    )
    allowed = iota((frames, frames), 1) <= iota((frames, frames), 0)
    scores = jnp.where(allowed, scores, -jnp.inf)
    expo = jnp.exp(scores - jnp.max(scores, axis=-1, keepdims=True))
    probability = expo / jnp.sum(expo, axis=-1, keepdims=True)
    prob_low = probability.astype(BF16)
    attn_out = jnp.einsum("ephfg,egphd->efphd", prob_low, value_in, preferred_element_type=F32)
    row_dots = jnp.transpose(jnp.sum(grad_in.astype(F32) * attn_out, axis=-1), (0, 2, 3, 1))
    prob_grad = jnp.einsum("efphd,egphd->ephfg", grad_in, value_in, preferred_element_type=F32)
    score_low = (probability * (prob_grad - row_dots[..., None])).astype(BF16)
    query_step = jnp.einsum("ephfg,egphd->efphd", score_low, key_norm, preferred_element_type=F32)
    key_step = jnp.einsum("ephfg,efphd->egphd", score_low, query_norm, preferred_element_type=F32)
    value_step = jnp.einsum("ephfg,efphd->egphd", prob_low, grad_in, preferred_element_type=F32)
    return (
        (query_step * scaling).astype(BF16),
        (key_step * scaling).astype(BF16),
        value_step.astype(BF16),
    )


def wide_body(queries, key_proj, value_proj, out_grad, query_gain, key_gain):
    gain_q = lax.all_gather(query_gain, "dp", axis=0, tiled=True)
    gain_k = lax.all_gather(key_gain, "dp", axis=0, tiled=True)
    q_hat, q_inv = rms(queries)
    k_hat, k_inv = rms(key_proj)
    pieces = [
        lax.all_to_all(x, "seq", split_axis=2, concat_axis=1, tiled=True)
        for x in ((q_hat * gain_q).astype(BF16), (k_hat * gain_k).astype(BF16), value_proj, out_grad)
    ]
    steps = [
        lax.all_to_all(x, "seq", split_axis=1, concat_axis=2, tiled=True)
        for x in wide_attention(*pieces)
    ]
    query_grad, part_q = norm_back(steps[0], q_hat, q_inv, gain_q)
    key_grad, part_k = norm_back(steps[1], k_hat, k_inv, gain_k)
    axes = tuple(range(part_q.ndim - 2))
    totals = lax.psum((jnp.sum(part_q, axis=axes), jnp.sum(part_k, axis=axes)), "seq")
    totals = [lax.psum_scatter(t, "dp", scatter_dimension=0, tiled=True) for t in totals]
    return (query_grad, key_grad, steps[2], *totals)


def body(*args):
    frames = lax.axis_size("seq")
    patches, heads, width = args[0].shape[2:]
    rows = patches // 2 * heads
    if frames == 8 and args[0].shape[:2] == (1, 1) and width == 128 and rows == sum(CUTS) * BLOCK:
        return hub_body(*args)
    return wide_body(*args)


def solution(mesh):
    whole = P("dp", "seq", None, None, None)
    gain = P("dp", None)
    return jax.shard_map(
        body,
        mesh=mesh,
        in_specs=(whole,) * 4 + (gain,) * 2,
        out_specs=(whole,) * 3 + (gain,) * 2,
        check_vma=False,
    )
```

time: 523 us -> 544 us (1.040)
  waiting for transfers between devices: 229 us -> 274 us
  Pallas kernels: 85.2 us -> 58.5 us
  starting transfers between devices: 182 us -> 156 us
  local copies, waits for them, and re-layouts: 9.79 us -> 28.5 us
  blocking collectives: 8.24 us -> 16.7 us
    ppermute x48 -> x36, waiting for transfers between devices: 225 us -> 274 us  [send(): return lax.ppermute(array, 'seq', pairs)]
    pallas_call x24 -> x35, Pallas kernels: 85.2 us -> 58.5 us  [call(): pl.pallas_call(trimmed, in_specs=list(in_specs) + [ANY] * extra, compiler...]
    ppermute x48 -> x36, starting transfers between devices: 178 us -> 156 us  [send(): return lax.ppermute(array, 'seq', pairs)]
    unnamed x126 -> x103, local copies, waits for them, and re-layouts: 7.32 us -> 23.8 us
    all_to_all x0 -> x1, blocking collectives: none -> 8.42 us  [sum_gains(): lax.all_to_all(pieces, 'dp', split_axis=1, concat_axis=1, tiled=True)]
  transfers between devices with their start and end apart: 51 -> 36, of which waited for: 20 -> 16; matrix products, arithmetic and copies ran while one was open for 1% -> 2% of each run, Pallas kernels for 13% -> 8%
where the time goes in v4:
time: 544 us; the launch traced here: 540 us
  waiting for transfers between devices  274 us (50%)
  starting transfers between devices  156 us (29%)
  Pallas kernels  58.5 us (11%)
  local copies, waits for them, and re-layouts  28.5 us (5%)
  blocking collectives  16.7 us (3%)
    ppermute x36, waiting for transfers between devices, send(): return lax.ppermute(array, 'seq', pairs)  274 us
    ppermute x36, starting transfers between devices, send(): return lax.ppermute(array, 'seq', pairs)  156 us
    pallas_call x35, Pallas kernels, call(): pl.pallas_call(trimmed, in_specs=list(in_specs) + [ANY] * extra, compiler...  58.5 us
    unnamed x103, local copies, waits for them, and re-layouts  23.8 us
  transfers between devices with their start and end apart: 36, of which 16 were waited for; matrix products, arithmetic and copies ran while one was open for 2% of the time, Pallas kernels for 8%

profile of v4, /device:TPU:0, one launch (start us, length us, event | category | flops | bytes accessed | tf_op | source)
XLA Modules:
  0.0 540.2 jit_solution(10398500558856924986)
XLA Ops:
  5.4 2.2 pack_rows.6
  7.7 6.0 %other_half.3 = bf16[4,4608,128]{2,1,0:T(8,128)(2,1)} custom-call(bf16[2,5120,128]{2,1,0:T(8,128)(2,1)} %bitcast.18, bf16[2,5120,128]{2,1,0:T(8,128)(2,1)} %bitcast.26, bf16[2,5120,128]{2,1,0:T(8,128)(2,1)} %bitcast.34, bf16[2,5120,128]{2,1,0:T(8,128)(2,1)} %bitcast.42, bf16[8,512,128]{2,1,0:T(8,128)(2,1)} %get-tuple-element.119.refs_4_.refs_0_), custom_call_target="tpu_custom_call" | custom-call | bytes 9437184 | tf_op jit(solution)/shard_map/other_half/pallas_call | solution.py:44
  14.1 5.6 %collective-permute-start.3 = (bf16[8,512,128]{2,1,0:T(8,128)(2,1)}, bf16[8,512,128]{2,1,0:T(8,128)(2,1)}, u32[]{:S(2)}, u32[]{:S(2)}) collective-permute-start(bf16[8,512,128]{2,1,0:T(8,128)(2,1)} %get-tuple-element.119.refs_4_.refs_0_), channel_id=1, source_target_pairs={{0,2},{1,3},{6,4},{7,5},{8,10},{9,11},{14,12},{15,13},{16,18},{17,... | collective-permute-start | bytes 3145736 | tf_op jit(solution)/shard_map/ppermute | solution.py:617
  24.0 3.1 pack_rows.7
  27.1 5.0 collective-permute-start.2
  32.1 10.4 %collective-permute-done.3.refs_0_.refs_1_.refs_6_ = bf16[8,512,128]{2,1,0:T(8,128)(2,1)} collective-permute-done((bf16[8,512,128]{2,1,0:T(8,128)(2,1)}, bf16[8,512,128]{2,1,0:T(8,128)(2,1)}, u32[]{:S(2)}, u32[]{:S(2)}) %collective-permute-start.3) | collective-permute-done | bytes 1048608 | tf_op jit(solution)/shard_map/ppermute | solution.py:617
  42.5 3.6 pack_rows.9
  46.1 9.3 %collective-permute-start.7 = (bf16[8,1280,128]{2,1,0:T(8,128)(2,1)}, bf16[8,1280,128]{2,1,0:T(8,128)(2,1)S(1)}, u32[]{:S(2)}, u32[]{:S(2)}) collective-permute-start(bf16[8,1280,128]{2,1,0:T(8,128)(2,1)} %get-tuple-element.125.refs_0_), channel_id=1, source_target_pairs={{0,2},{1,3},{6,4},{7,5},{8,10},{9,11},{14,12},{15,13},{16,18},{17,... | collective-permute-start | bytes 7864328 | tf_op jit(solution)/shard_map/ppermute | solution.py:617
  56.9 8.3 %all_gather.3 = f32[2,40,128]{2,0,1:T(2,128)S(1)} all-gather(f32[2,10,128]{2,0,1:T(2,128)S(1)} %pad_maximum_fusion.1), channel_id=1, replica_groups=mesh['dp'=4,'seq'=8] {'dp'}, dimensions={1}, use_global_device_ids=true | all-gather | bytes 51200 | tf_op jit(solution)/shard_map/all_gather | solution.py:702
  67.7 19.7 %collective-permute-done.2.refs_0_.refs_6_.refs_1_ = bf16[8,1024,128]{2,1,0:T(8,128)(2,1)S(1)} collective-permute-done((bf16[8,1024,128]{2,1,0:T(8,128)(2,1)}, bf16[8,1024,128]{2,1,0:T(8,128)(2,1)S(1)}, u32[]{:S(2)}, u32[]{:S(2)}) %collective-permute-start.2) | collective-permute-done | bytes 2097184 | tf_op jit(solution)/shard_map/ppermute | solution.py:617
  88.8 3.5 pack_rows.8
  92.3 11.0 %collective-permute-start.6 = (bf16[8,1280,128]{2,1,0:T(8,128)(2,1)}, bf16[8,1280,128]{2,1,0:T(8,128)(2,1)S(1)}, u32[]{:S(2)}, u32[]{:S(2)}) collective-permute-start(bf16[8,1280,128]{2,1,0:T(8,128)(2,1)} %get-tuple-element.124.refs_0_), channel_id=1, source_target_pairs={{0,2},{1,3},{6,4},{7,5},{8,10},{9,11},{14,12},{15,13},{16,18},{17,... | collective-permute-start | bytes 7864328 | tf_op jit(solution)/shard_map/ppermute | solution.py:617
  107.8 35.8 %collective-permute-done.7.refs_0_.refs_1_.refs_6_ = bf16[8,1280,128]{2,1,0:T(8,128)(2,1)S(1)} collective-permute-done((bf16[8,1280,128]{2,1,0:T(8,128)(2,1)}, bf16[8,1280,128]{2,1,0:T(8,128)(2,1)S(1)}, u32[]{:S(2)}, u32[]{:S(2)}) %collective-permute-start.7) | collective-permute-done | bytes 2621472 | tf_op jit(solution)/shard_map/ppermute | solution.py:617
  149.2 2.8 pack_rows.11
  152.0 55.7 %collective-permute-done.12.refs_2_ = bf16[6,512,128]{2,1,0:T(8,128)(2,1)S(1)} collective-permute-done((bf16[6,512,128]{2,1,0:T(8,128)(2,1)}, bf16[6,512,128]{2,1,0:T(8,128)(2,1)S(1)}, u32[]{:S(2)}, u32[]{:S(2)}) %collective-permute-start.12) | collective-permute-done | bytes 786464 | tf_op jit(solution)/shard_map/ppermute | solution.py:617
  216.5 21.2 %collective-permute-done.19.refs_2_ = bf16[6,1024,128]{2,1,0:T(8,128)(2,1)} collective-permute-done((bf16[6,1024,128]{2,1,0:T(8,128)(2,1)}, bf16[6,1024,128]{2,1,0:T(8,128)(2,1)}, u32[]{:S(2)}, u32[]{:S(2)}) %collective-permute-start.19) | collective-permute-done | bytes 1572896 | tf_op jit(solution)/shard_map/ppermute | solution.py:617
  237.7 3.4 place_rows.9
  247.7 72.6 %collective-permute-done.21.refs_2_ = bf16[6,1280,128]{2,1,0:T(8,128)(2,1)S(1)} collective-permute-done((bf16[6,1280,128]{2,1,0:T(8,128)(2,1)}, bf16[6,1280,128]{2,1,0:T(8,128)(2,1)S(1)}, u32[]{:S(2)}, u32[]{:S(2)}) %collective-permute-start.21) | collective-permute-done | bytes 1966112 | tf_op jit(solution)/shard_map/ppermute | solution.py:617
  321.6 3.8 place_rows.10
  331.0 97.9 %collective-permute-start.13 = (bf16[8,256,128]{2,1,0:T(8,128)(2,1)}, bf16[8,256,128]{2,1,0:T(8,128)(2,1)S(1)}, u32[]{:S(2)}, u32[]{:S(2)}) collective-permute-start(bf16[8,256,128]{2,1,0:T(8,128)(2,1)} %get-tuple-element.141.refs_0_), channel_id=1, source_target_pairs={{0,2},{1,3},{6,4},{7,5},{8,10},{9,11},{14,12},{15,13},{16,18},{17,... | collective-permute-start | bytes 1572872 | tf_op jit(solution)/shard_map/ppermute | solution.py:617
  428.9 7.0 %collective-permute-done.13.refs_0_.refs_1_ = bf16[8,256,128]{2,1,0:T(8,128)(2,1)S(1)} collective-permute-done((bf16[8,256,128]{2,1,0:T(8,128)(2,1)}, bf16[8,256,128]{2,1,0:T(8,128)(2,1)S(1)}, u32[]{:S(2)}, u32[]{:S(2)}) %collective-permute-start.13) | collective-permute-done | bytes 524320 | tf_op jit(solution)/shard_map/ppermute | solution.py:617
  439.2 4.0 place_rows.11
  445.3 17.6 %collective-permute-done.25.refs_2_ = bf16[6,1280,128]{2,1,0:T(8,128)(2,1)S(1)} collective-permute-done((bf16[6,1280,128]{2,1,0:T(8,128)(2,1)}, bf16[6,1280,128]{2,1,0:T(8,128)(2,1)S(1)}, u32[]{:S(2)}, u32[]{:S(2)}) %collective-permute-start.25) | collective-permute-done | bytes 1966112 | tf_op jit(solution)/shard_map/ppermute | solution.py:617
  464.1 4.2 place_rows.12
  472.1 3.1 collective-permute-done.26.refs_0_
  477.2 4.1 place_rows.13
  489.2 8.4 %all_to_all.5 = f32[2,4,10,128]{3,0,2,1:T(2,128)} all-to-all(f32[2,4,10,128]{3,0,2,1:T(2,128)S(1)} %copy.57), channel_id=1, replica_groups=mesh['dp'=4,'seq'=8] {'dp'}, dimensions={1} | all-to-all | bytes 81920 | tf_op jit(solution)/shard_map/all_to_all | solution.py:624
  506.8 3.5 place_rows.14
  510.3 16.2 %collective-permute-done.35 = f32[2,10,128]{2,0,1:T(2,128)} collective-permute-done((f32[2,10,128]{2,0,1:T(2,128)S(1)}, f32[2,10,128]{2,0,1:T(2,128)}, u32[]{:S(2)}, u32[]{:S(2)}) %collective-permute-start.35) | collective-permute-done | bytes 10272 | tf_op jit(solution)/shard_map/ppermute | solution.py:617
  527.8 4.8 collective-permute-done.28.refs_2_
  532.6 3.8 collective-permute-done.29.refs_3_
  537.1 3.1 place_rows.15
  (197 shorter events, 78.3 us)
Async XLA Ops:
  13.7 8.1 %collective-permute-start.1 = (bf16[4,4608,128]{2,1,0:T(8,128)(2,1)}, bf16[4,4608,128]{2,1,0:T(8,128)(2,1)S(1)}, u32[]{:S(2)}, u32[]{:S(2)}) collective-permute-start(bf16[4,4608,128]{2,1,0:T(8,128)(2,1)} %other_half.3), channel_id=1, source_target_pairs={{0,1},{1,0},{2,3},{3,2},{4,5},{5,4},{6,7},{7,6},{8,9},{9,8},{10,11... | collective-permute-start | bytes 14155784 | tf_op jit(solution)/shard_map/ppermute | solution.py:617
  14.1 28.4 %collective-permute-start.3 = (bf16[8,512,128]{2,1,0:T(8,128)(2,1)}, bf16[8,512,128]{2,1,0:T(8,128)(2,1)}, u32[]{:S(2)}, u32[]{:S(2)}) collective-permute-start(bf16[8,512,128]{2,1,0:T(8,128)(2,1)} %get-tuple-element.119.refs_4_.refs_0_), channel_id=1, source_target_pairs={{0,2},{1,3},{6,4},{7,5},{8,10},{9,11},{14,12},{15,13},{16,18},{17,... | collective-permute-start | bytes 3145736 | tf_op jit(solution)/shard_map/ppermute | solution.py:617
  27.1 60.3 %collective-permute-start.2 = (bf16[8,1024,128]{2,1,0:T(8,128)(2,1)}, bf16[8,1024,128]{2,1,0:T(8,128)(2,1)S(1)}, u32[]{:S(2)}, u32[]{:S(2)}) collective-permute-start(bf16[8,1024,128]{2,1,0:T(8,128)(2,1)} %get-tuple-element.120.refs_0_), channel_id=1, source_target_pairs={{0,2},{1,3},{6,4},{7,5},{8,10},{9,11},{14,12},{15,13},{16,18},{17,... | collective-permute-start | bytes 6291464 | tf_op jit(solution)/shard_map/ppermute | solution.py:617
  46.1 97.5 %collective-permute-start.7 = (bf16[8,1280,128]{2,1,0:T(8,128)(2,1)}, bf16[8,1280,128]{2,1,0:T(8,128)(2,1)S(1)}, u32[]{:S(2)}, u32[]{:S(2)}) collective-permute-start(bf16[8,1280,128]{2,1,0:T(8,128)(2,1)} %get-tuple-element.125.refs_0_), channel_id=1, source_target_pairs={{0,2},{1,3},{6,4},{7,5},{8,10},{9,11},{14,12},{15,13},{16,18},{17,... | collective-permute-start | bytes 7864328 | tf_op jit(solution)/shard_map/ppermute | solution.py:617
  55.4 9.8 %collective-permute-start.4 = (bf16[4,512,128]{2,1,0:T(8,128)(2,1)S(1)}, bf16[4,512,128]{2,1,0:T(8,128)(2,1)S(1)}, u32[]{:S(2)}, u32[]{:S(2)}) collective-permute-start(bf16[4,512,128]{2,1,0:T(8,128)(2,1)S(1)} %copy-done.49), channel_id=1, source_target_pairs={{2,4},{3,5},{4,2},{5,3},{10,12},{11,13},{12,10},{13,11},{18,20},{1... | collective-permute-start | bytes 1572872 | tf_op jit(solution)/shard_map/ppermute | solution.py:617
  56.1 9.1 %collective-permute-start.5 = (bf16[2048,128]{1,0:T(8,128)(2,1)S(1)}, bf16[2048,128]{1,0:T(8,128)(2,1)S(1)}, u32[]{:S(2)}, u32[]{:S(2)}) collective-permute-start(bf16[2048,128]{1,0:T(8,128)(2,1)S(1)} %copy-done.18), channel_id=1, source_target_pairs={{2,4},{3,5},{4,2},{5,3},{10,12},{11,13},{12,10},{13,11},{18,20},{1... | collective-permute-start | bytes 1572872 | tf_op jit(solution)/shard_map/ppermute | solution.py:617
  92.3 119.9 %collective-permute-start.6 = (bf16[8,1280,128]{2,1,0:T(8,128)(2,1)}, bf16[8,1280,128]{2,1,0:T(8,128)(2,1)S(1)}, u32[]{:S(2)}, u32[]{:S(2)}) collective-permute-start(bf16[8,1280,128]{2,1,0:T(8,128)(2,1)} %get-tuple-element.124.refs_0_), channel_id=1, source_target_pairs={{0,2},{1,3},{6,4},{7,5},{8,10},{9,11},{14,12},{15,13},{16,18},{17,... | collective-permute-start | bytes 7864328 | tf_op jit(solution)/shard_map/ppermute | solution.py:617
  103.2 2.4 collective-permute-start.10
  145.1 64.4 %collective-permute-start.11 = (bf16[5376,128]{1,0:T(8,128)(2,1)}, bf16[5376,128]{1,0:T(8,128)(2,1)S(1)}, u32[]{:S(2)}, u32[]{:S(2)}) collective-permute-start(bf16[5376,128]{1,0:T(8,128)(2,1)} %forward_rows.8.refs_5_), channel_id=1, source_target_pairs={{2,4},{3,5},{4,2},{5,3},{10,12},{11,13},{12,10},{13,11},{18,20},{1... | collective-permute-start | bytes 4128776 | tf_op jit(solution)/shard_map/ppermute | solution.py:617
  145.8 63.6 %collective-permute-start.8 = (bf16[4,1280,128]{2,1,0:T(8,128)(2,1)}, bf16[4,1280,128]{2,1,0:T(8,128)(2,1)S(1)}, u32[]{:S(2)}, u32[]{:S(2)}) collective-permute-start(bf16[4,1280,128]{2,1,0:T(8,128)(2,1)} %get-tuple-element.126), channel_id=1, source_target_pairs={{2,4},{3,5},{4,2},{5,3},{10,12},{11,13},{12,10},{13,11},{18,20},{1... | collective-permute-start | bytes 3932168 | tf_op jit(solution)/shard_map/ppermute | solution.py:617
  146.6 61.1 %collective-permute-start.12 = (bf16[6,512,128]{2,1,0:T(8,128)(2,1)}, bf16[6,512,128]{2,1,0:T(8,128)(2,1)S(1)}, u32[]{:S(2)}, u32[]{:S(2)}) collective-permute-start(bf16[6,512,128]{2,1,0:T(8,128)(2,1)} %get-tuple-element.134), channel_id=1, source_target_pairs={{2,0},{3,1},{4,6},{5,7},{10,8},{11,9},{12,14},{13,15},{18,16},{19,... | collective-permute-start | bytes 2359304 | tf_op jit(solution)/shard_map/ppermute | solution.py:617
  147.9 89.8 %collective-permute-start.19 = (bf16[6,1024,128]{2,1,0:T(8,128)(2,1)}, bf16[6,1024,128]{2,1,0:T(8,128)(2,1)}, u32[]{:S(2)}, u32[]{:S(2)}) collective-permute-start(bf16[6,1024,128]{2,1,0:T(8,128)(2,1)} %get-tuple-element.147), channel_id=1, source_target_pairs={{2,0},{3,1},{4,6},{5,7},{10,8},{11,9},{12,14},{13,15},{18,16},{19,... | collective-permute-start | bytes 4718600 | tf_op jit(solution)/shard_map/ppermute | solution.py:617
  207.7 36.1 %collective-permute-start.15 = (bf16[8,768,128]{2,1,0:T(8,128)(2,1)}, bf16[8,768,128]{2,1,0:T(8,128)(2,1)S(1)}, u32[]{:S(2)}, u32[]{:S(2)}) collective-permute-start(bf16[8,768,128]{2,1,0:T(8,128)(2,1)} %get-tuple-element.143.refs_0_), channel_id=1, source_target_pairs={{0,2},{1,3},{6,4},{7,5},{8,10},{9,11},{14,12},{15,13},{16,18},{17,... | collective-permute-start | bytes 4718600 | tf_op jit(solution)/shard_map/ppermute | solution.py:617
  213.7 27.4 %collective-permute-start.18 = (bf16[5440,128]{1,0:T(8,128)(2,1)}, bf16[5440,128]{1,0:T(8,128)(2,1)S(1)}, u32[]{:S(2)}, u32[]{:S(2)}) collective-permute-start(bf16[5440,128]{1,0:T(8,128)(2,1)} %forward_rows.9.refs_5_), channel_id=1, source_target_pairs={{2,4},{3,5},{4,2},{5,3},{10,12},{11,13},{12,10},{13,11},{18,20},{1... | collective-permute-start | bytes 4177928 | tf_op jit(solution)/shard_map/ppermute | solution.py:617
  214.4 26.6 %collective-permute-start.17 = (bf16[4,1280,128]{2,1,0:T(8,128)(2,1)}, bf16[4,1280,128]{2,1,0:T(8,128)(2,1)S(1)}, u32[]{:S(2)}, u32[]{:S(2)}) collective-permute-start(bf16[4,1280,128]{2,1,0:T(8,128)(2,1)} %get-tuple-element.145), channel_id=1, source_target_pairs={{2,4},{3,5},{4,2},{5,3},{10,12},{11,13},{12,10},{13,11},{18,20},{1... | collective-permute-start | bytes 3932168 | tf_op jit(solution)/shard_map/ppermute | solution.py:617
  215.2 105.2 %collective-permute-start.21 = (bf16[6,1280,128]{2,1,0:T(8,128)(2,1)}, bf16[6,1280,128]{2,1,0:T(8,128)(2,1)S(1)}, u32[]{:S(2)}, u32[]{:S(2)}) collective-permute-start(bf16[6,1280,128]{2,1,0:T(8,128)(2,1)} %get-tuple-element.158), channel_id=1, source_target_pairs={{2,0},{3,1},{4,6},{5,7},{10,8},{11,9},{12,14},{13,15},{18,16},{19,... | collective-permute-start | bytes 5898248 | tf_op jit(solution)/shard_map/ppermute | solution.py:617
  245.0 80.5 %collective-permute-start.20 = (bf16[3392,128]{1,0:T(8,128)(2,1)}, bf16[3392,128]{1,0:T(8,128)(2,1)S(1)}, u32[]{:S(2)}, u32[]{:S(2)}) collective-permute-start(bf16[3392,128]{1,0:T(8,128)(2,1)} %forward_rows.10), channel_id=1, source_target_pairs={{2,4},{3,5},{4,2},{5,3},{10,12},{11,13},{12,10},{13,11},{18,20},{1... | collective-permute-start | bytes 2605064 | tf_op jit(solution)/shard_map/ppermute | solution.py:617
  245.7 79.7 %collective-permute-start.16 = (bf16[4,768,128]{2,1,0:T(8,128)(2,1)S(1)}, bf16[4,768,128]{2,1,0:T(8,128)(2,1)S(1)}, u32[]{:S(2)}, u32[]{:S(2)}) collective-permute-start(bf16[4,768,128]{2,1,0:T(8,128)(2,1)S(1)} %copy-done.48), channel_id=1, source_target_pairs={{2,4},{3,5},{4,2},{5,3},{10,12},{11,13},{12,10},{13,11},{18,20},{1... | collective-permute-start | bytes 2359304 | tf_op jit(solution)/shard_map/ppermute | solution.py:617
  246.4 191.6 %collective-permute-start.23 = (bf16[6,1280,128]{2,1,0:T(8,128)(2,1)}, bf16[6,1280,128]{2,1,0:T(8,128)(2,1)S(1)}, u32[]{:S(2)}, u32[]{:S(2)}) collective-permute-start(bf16[6,1280,128]{2,1,0:T(8,128)(2,1)} %get-tuple-element.169), channel_id=1, source_target_pairs={{2,0},{3,1},{4,6},{5,7},{10,8},{11,9},{12,14},{13,15},{18,16},{19,... | collective-permute-start | bytes 5898248 | tf_op jit(solution)/shard_map/ppermute | solution.py:617
  327.9 135.0 %collective-permute-start.25 = (bf16[6,1280,128]{2,1,0:T(8,128)(2,1)}, bf16[6,1280,128]{2,1,0:T(8,128)(2,1)S(1)}, u32[]{:S(2)}, u32[]{:S(2)}) collective-permute-start(bf16[6,1280,128]{2,1,0:T(8,128)(2,1)} %get-tuple-element.176), channel_id=1, source_target_pairs={{2,0},{3,1},{4,6},{5,7},{10,8},{11,9},{12,14},{13,15},{18,16},{19,... | collective-permute-start | bytes 5898248 | tf_op jit(solution)/shard_map/ppermute | solution.py:617
  331.0 104.9 %collective-permute-start.13 = (bf16[8,256,128]{2,1,0:T(8,128)(2,1)}, bf16[8,256,128]{2,1,0:T(8,128)(2,1)S(1)}, u32[]{:S(2)}, u32[]{:S(2)}) collective-permute-start(bf16[8,256,128]{2,1,0:T(8,128)(2,1)} %get-tuple-element.141.refs_0_), channel_id=1, source_target_pairs={{0,2},{1,3},{6,4},{7,5},{8,10},{9,11},{14,12},{15,13},{16,18},{17,... | collective-permute-start | bytes 1572872 | tf_op jit(solution)/shard_map/ppermute | solution.py:617
  436.6 6.6 %collective-permute-start.22 = (bf16[1216,128]{1,0:T(8,128)(2,1)}, bf16[1216,128]{1,0:T(8,128)(2,1)S(1)}, u32[]{:S(2)}, u32[]{:S(2)}) collective-permute-start(bf16[1216,128]{1,0:T(8,128)(2,1)} %forward_rows.11), channel_id=1, source_target_pairs={{2,4},{3,5},{4,2},{5,3},{10,12},{11,13},{12,10},{13,11},{18,20},{1... | collective-permute-start | bytes 933896 | tf_op jit(solution)/shard_map/ppermute | solution.py:617
  437.3 5.9 %collective-permute-start.14 = (bf16[4,256,128]{2,1,0:T(8,128)(2,1)}, bf16[4,256,128]{2,1,0:T(8,128)(2,1)S(1)}, u32[]{:S(2)}, u32[]{:S(2)}) collective-permute-start(bf16[4,256,128]{2,1,0:T(8,128)(2,1)} %get-tuple-element.142), channel_id=1, source_target_pairs={{2,4},{3,5},{4,2},{5,3},{10,12},{11,13},{12,10},{13,11},{18,20},{1... | collective-permute-start | bytes 786440 | tf_op jit(solution)/shard_map/ppermute | solution.py:617
  468.3 7.0 %collective-permute-start.26 = (bf16[3,5120,128]{2,1,0:T(8,128)(2,1)}, bf16[3,5120,128]{2,1,0:T(8,128)(2,1)S(1)}, u32[]{:S(2)}, u32[]{:S(2)}) collective-permute-start(bf16[3,5120,128]{2,1,0:T(8,128)(2,1)} %get-tuple-element.180), channel_id=1, source_target_pairs={{0,1},{1,0},{2,3},{3,2},{4,5},{5,4},{6,7},{7,6},{8,9},{9,8},{10,11... | collective-permute-start | bytes 11796488 | tf_op jit(solution)/shard_map/ppermute | solution.py:617
  468.3 13.0 %collective-permute-start.24 = (bf16[64,128]{1,0:T(8,128)(2,1)S(1)}, bf16[64,128]{1,0:T(8,128)(2,1)S(1)}, u32[]{:S(2)}, u32[]{:S(2)}) collective-permute-start(bf16[64,128]{1,0:T(8,128)(2,1)S(1)} %copy-done.50), channel_id=1, source_target_pairs={{4,2},{5,3},{12,10},{13,11},{20,18},{21,19},{28,26},{29,27}} | collective-permute-start | bytes 49160 | tf_op jit(solution)/shard_map/ppermute | solution.py:617
  469.0 32.9 %collective-permute-start.30 = (bf16[3,768,128]{2,1,0:T(8,128)(2,1)S(1)}, bf16[3,768,128]{2,1,0:T(8,128)(2,1)S(1)}, u32[]{:S(2)}, u32[]{:S(2)}) collective-permute-start(bf16[3,768,128]{2,1,0:T(8,128)(2,1)S(1)} %copy-done.27), channel_id=1, source_target_pairs={{0,1},{1,0},{2,3},{3,2},{4,5},{5,4},{6,7},{7,6},{8,9},{9,8},{10,11... | collective-permute-start | bytes 1769480 | tf_op jit(solution)/shard_map/ppermute | solution.py:617
  469.5 33.7 %collective-permute-start.31 = (bf16[3,768,128]{2,1,0:T(8,128)(2,1)S(1)}, bf16[3,768,128]{2,1,0:T(8,128)(2,1)S(1)}, u32[]{:S(2)}, u32[]{:S(2)}) collective-permute-start(bf16[3,768,128]{2,1,0:T(8,128)(2,1)S(1)} %copy-done.28), channel_id=1, source_target_pairs={{2,0},{3,1},{4,6},{5,7},{10,8},{11,9},{12,14},{13,15},{18,16},{19,... | collective-permute-start | bytes 1769480 | tf_op jit(solution)/shard_map/ppermute | solution.py:617
  470.8 35.1 %collective-permute-start.32 = (bf16[3,768,128]{2,1,0:T(8,128)(2,1)S(1)}, bf16[3,768,128]{2,1,0:T(8,128)(2,1)S(1)}, u32[]{:S(2)}, u32[]{:S(2)}) collective-permute-start(bf16[3,768,128]{2,1,0:T(8,128)(2,1)S(1)} %copy-done.29), channel_id=1, source_target_pairs={{2,1},{3,0},{4,7},{5,6},{10,9},{11,8},{12,15},{13,14},{18,17},{19,... | collective-permute-start | bytes 1769480 | tf_op jit(solution)/shard_map/ppermute | solution.py:617
  500.4 26.1 %collective-permute-start.35 = (f32[2,10,128]{2,0,1:T(2,128)S(1)}, f32[2,10,128]{2,0,1:T(2,128)}, u32[]{:S(2)}, u32[]{:S(2)}) collective-permute-start(f32[2,10,128]{2,0,1:T(2,128)S(1)} %add.96), channel_id=1, source_target_pairs={{2,0},{3,1},{4,6},{5,7},{10,8},{11,9},{12,14},{13,15},{18,16},{19,... | collective-permute-start | bytes 30728 | tf_op jit(solution)/shard_map/ppermute | solution.py:617
  501.7 26.1 %collective-permute-start.27 = (bf16[3,256,128]{2,1,0:T(8,128)(2,1)}, bf16[3,256,128]{2,1,0:T(8,128)(2,1)S(1)}, u32[]{:S(2)}, u32[]{:S(2)}) collective-permute-start(bf16[3,256,128]{2,1,0:T(8,128)(2,1)} %get-tuple-element.190), channel_id=1, source_target_pairs={{0,1},{1,0},{2,3},{3,2},{4,5},{5,4},{6,7},{7,6},{8,9},{9,8},{10,11... | collective-permute-start | bytes 589832 | tf_op jit(solution)/shard_map/ppermute | solution.py:617
  501.9 30.6 %collective-permute-start.28 = (bf16[3,256,128]{2,1,0:T(8,128)(2,1)}, bf16[3,256,128]{2,1,0:T(8,128)(2,1)S(1)}, u32[]{:S(2)}, u32[]{:S(2)}) collective-permute-start(bf16[3,256,128]{2,1,0:T(8,128)(2,1)} %get-tuple-element.191), channel_id=1, source_target_pairs={{2,0},{3,1},{4,6},{5,7},{10,8},{11,9},{12,14},{13,15},{18,16},{19,... | collective-permute-start | bytes 589832 | tf_op jit(solution)/shard_map/ppermute | solution.py:617
  503.2 33.2 %collective-permute-start.29 = (bf16[3,256,128]{2,1,0:T(8,128)(2,1)}, bf16[3,256,128]{2,1,0:T(8,128)(2,1)S(1)}, u32[]{:S(2)}, u32[]{:S(2)}) collective-permute-start(bf16[3,256,128]{2,1,0:T(8,128)(2,1)} %get-tuple-element.192), channel_id=1, source_target_pairs={{2,1},{3,0},{4,7},{5,6},{10,9},{11,8},{12,15},{13,14},{18,17},{19,... | collective-permute-start | bytes 589832 | tf_op jit(solution)/shard_map/ppermute | solution.py:617
  (55 other events, 158.5 us)

commit v5 on v0

v5 whole, which is shorter than its diff:
```python
import functools
import math

import jax
import jax.numpy as jnp
from jax import lax
from jax.experimental import pallas as pl
from jax.experimental.pallas import tpu as pltpu
from jax.sharding import PartitionSpec as P

EPSILON = 1e-06
BLOCK = 512
GROUP = 16
PAIR = 2 * GROUP
HOPS = 4
TOGETHER = 64
CUTS = (2, 3, 3, 1, 1)

UP = tuple((i, i + 2) for i in range(6))
DOWN = tuple((i + 2, i) for i in range(6))
SWAP = tuple((i, i ^ 1) for i in range(8))
NEAR = tuple((i, i ^ 2) for i in range(8))
FAR = tuple((i, i ^ 4) for i in range(8))

F32 = jnp.float32
BF16 = jnp.bfloat16
ANY = pl.BlockSpec(memory_space=pl.ANY)
VMEM = pl.BlockSpec(memory_space=pltpu.VMEM)


def place():
    index = lax.axis_index("seq")
    chip, core = index // 2, index % 2
    return chip, core


def call(kernel, inputs, in_specs, after=(), **kwargs):
    count, extra = len(inputs), len(after)

    def trimmed(*refs):
        kernel(*refs[:count], *refs[count + extra :])

    return pl.pallas_call(
        trimmed,
        in_specs=list(in_specs) + [ANY] * extra,
        compiler_params=pltpu.CompilerParams(vmem_limit_bytes=56 * 1024 * 1024),
        **kwargs,
    )(*inputs, *after)


def first_of(chunk):
    return sum(CUTS[:chunk]) * BLOCK


def rows_of(chunk):
    return CUTS[chunk] * BLOCK


def copy_cost(rows, tensors):
    return pl.CostEstimate(flops=0, bytes_accessed=rows * 128 * 2 * 2 * tensors, transcendentals=0)


def tile_of(rows):
    return next(rows // k for k in range(2, rows) if rows % (16 * k) == 0 and rows // k <= 1024)


def stream(rows, sources, sinks, move):
    tile = tile_of(rows)

    def spec(ref):
        return pl.BlockSpec((ref.shape[0], tile, 128), lambda i: (0, i, 0))

    pltpu.emit_pipeline(
        move,
        grid=(rows // tile,),
        in_specs=[spec(ref) for ref in sources],
        out_specs=[spec(ref) for ref in sinks],
    )(*sources, *sinks)


def window(ref, index, start, rows, count=1):
    return ref.at[pl.ds(index, count), pl.ds(start, rows)]


def halves_kernel(start, rows, q, k, v, g, out):
    _, core = place()

    def move(*blocks):
        for t in range(4):
            blocks[4][t] = blocks[t][0]

    stream(rows, [window(ref, 1 - core, start, rows) for ref in (q, k, v, g)], [out], move)


def halves(start, rows, arrays, after):
    return call(
        functools.partial(halves_kernel, start, rows),
        arrays,
        [ANY] * 4,
        after,
        out_shape=jax.ShapeDtypeStruct((4, rows, 128), BF16),
        out_specs=ANY,
        cost_estimate=copy_cost(rows, 4),
        name="other_half",
    )


def pack_kernel(start, rows, offset, q, k, v, g, x, up, down):
    _, core = place()

    def move(*blocks):
        for t in range(2):
            for frame in range(2):
                blocks[8][2 * frame + t] = blocks[4 * frame + 1 + t][0]
                blocks[9][2 * frame + t] = blocks[4 * frame + 3 * t][0]

    own = [window(ref, core, start, rows) for ref in (q, k, v, g)]
    other = [window(x, t, start - offset, rows) for t in range(4)]
    stream(rows, own + other, [up, down], move)


def pack(chunk, offset, arrays, swapped, after):
    rows = rows_of(chunk)
    return call(
        functools.partial(pack_kernel, first_of(chunk), rows, offset),
        (*arrays, swapped),
        [ANY] * 5,
        after,
        out_shape=[jax.ShapeDtypeStruct((4, rows, 128), BF16)] * 2,
        out_specs=[ANY] * 2,
        cost_estimate=copy_cost(rows, 8),
        name="pack_rows",
    )


def place_kernel(start, rows, swapped, *refs):
    outs = refs[3:]
    _, core = place()

    def move(src, *dsts):
        for t, dst in enumerate(dsts):
            dst[0] = src[t]

    stream(rows, [swapped], [window(out, 1 - core, start, rows) for out in outs], move)


def settle_rows(chunk, swapped, outs):
    rows = rows_of(chunk)
    return call(
        functools.partial(place_kernel, first_of(chunk), rows),
        (swapped, *outs),
        [ANY] * 4,
        out_shape=[jax.ShapeDtypeStruct(out.shape, BF16) for out in outs],
        out_specs=[ANY] * 3,
        input_output_aliases={1 + i: i for i in range(3)},
        cost_estimate=copy_cost(rows, 3),
        name="place_rows",
    )


def rms(values):
    wide = values.astype(F32)
    inverse = lax.rsqrt(jnp.mean(wide * wide, axis=-1, keepdims=True) + EPSILON)
    return wide * inverse, inverse


def norm_back(step, hat, inverse, gain):
    wide = step.astype(F32)
    gained = gain * wide
    result = inverse * (gained - hat * jnp.mean(gained * hat, axis=-1, keepdims=True))
    return result.astype(BF16), wide * hat


def mul_t(a, b):
    return lax.dot_general(a, b, (((1,), (1,)), ((), ())), preferred_element_type=F32)


def t_mul(a, b):
    return lax.dot_general(a, b, (((0,), (0,)), ((), ())), preferred_element_type=F32)


def mul(a, b):
    return jnp.dot(a, b, preferred_element_type=F32)


def iota(shape, axis):
    return lax.broadcasted_iota(jnp.int32, shape, axis)


def allowed_pairs(chip, core):
    shape = (PAIR, HOPS * PAIR)
    rows, cols = iota(shape, 0), iota(shape, 1)
    hop = cols // PAIR

    def parity(index):
        cross = index // GROUP % 2
        return cross + core - 2 * cross * core

    late = ((hop == 0) & (parity(cols) <= parity(rows))) | ((hop > 0) & (hop <= chip))
    return (rows % GROUP == cols % GROUP) & late


def cat(parts):
    return jnp.concatenate(parts, axis=0)


def group(wide, j):
    frames = wide.shape[0] // TOGETHER
    return cat([wide[s * TOGETHER + j * GROUP :][:GROUP] for s in range(frames)])


def ungroup(parts):
    return cat([part[s * GROUP :][:GROUP] for s in range(2) for part in parts])


def read(refs, t, rows):
    return cat([ref[2 * x + t, rows, :] for ref in refs for x in range(2)])


def split_rows(x, size):
    return [x[j * size :][:size] for j in range(x.shape[0] // size)]


def attend(qn, kn, grad, value, mask):
    scaling = 1.0 / math.sqrt(qn.shape[-1])
    count = TOGETHER // GROUP
    scores = cat([mul_t(group(qn, j), group(kn, j)) for j in range(count)])
    prob_grad = cat([mul_t(group(grad, j), group(value, j)) for j in range(count)])
    scores = jnp.where(cat([mask] * count) > 0, scores * scaling, -jnp.inf)
    expo = jnp.exp(scores - jnp.max(scores, axis=-1, keepdims=True))
    prob = expo * (1.0 / jnp.sum(expo, axis=-1, keepdims=True))
    prob_low = prob.astype(BF16)
    dots = jnp.sum(prob_low.astype(F32) * prob_grad, axis=-1, keepdims=True)
    score_low = (prob * (prob_grad - dots)).astype(BF16)
    return prob_low, score_low


def fold(acc, rows, part):
    acc[rows, :] += part[:TOGETHER] + part[TOGETHER:]


def settle(own, other, rows, part):
    own[0, rows, :] = part[:TOGETHER]
    other[0, rows, :] = part[TOGETHER:]


def sum_heads(acc, heads):
    total = acc[0:heads, :]
    for i in range(1, acc.shape[0] // heads):
        total = total + acc[i * heads : (i + 1) * heads, :]
    return total


def row_spec(count):
    return pl.BlockSpec((count, BLOCK, 128), lambda i: (0, i, 0))


def gain_spec(first, cycle):
    return pl.BlockSpec((BLOCK, 128), lambda i: ((first + i) % cycle, 0))


PACKED = pl.BlockSpec((PAIR, 128), lambda i: (i, 0))


def query_kernel(chunk, heads, down, up, u1, u2, u3, gain_q, gain_k, _, out, swap, t0, t1, t2, t3, total, acc, mask):
    chip, core = place()
    first, steps = sum(CUTS[:chunk]), CUTS[chunk]
    count = TOGETHER // GROUP
    cycle = acc.shape[0] // BLOCK
    acc[...] = jnp.zeros_like(acc)
    mask[...] = allowed_pairs(chip, core).astype(F32)

    def block(down, up, u1, u2, u3, gain_q, gain_k, out, swap, *packs):
        base = ((first + pl.program_id(0)) % cycle) * BLOCK
        scaling = 1.0 / math.sqrt(128)
        lanes = iota((PAIR, HOPS * 128), 1) % 128 // 4
        source, sink = iota((2 * HOPS * PAIR, HOPS * 128), 0), iota((2 * HOPS * PAIR, HOPS * 128), 1)
        same = source % (HOPS * PAIR) // PAIR == sink // 128
        value = source // (HOPS * PAIR) * 2 + source // GROUP % 2
        spread = jnp.where(same & (value == sink % 4), 1.0, 0.0).astype(BF16)

        def some(i, total):
            rows = pl.ds(pl.multiple_of(i * TOGETHER, TOGETHER), TOGETHER)
            where = pl.ds(pl.multiple_of(base + i * TOGETHER, TOGETHER), TOGETHER)
            gq, gk = cat([gain_q[rows, :]] * 2), cat([gain_k[rows, :]] * 2 * HOPS)
            q_hat, q_inv = rms(read((down,), 0, rows))
            grad = read((down,), 1, rows)
            k_hat, _ = rms(read((up, u1, u2, u3), 0, rows))
            value = read((up, u1, u2, u3), 1, rows)
            qn, kn = (q_hat * gq).astype(BF16), (k_hat * gk).astype(BF16)
            prob, score = attend(qn, kn, grad, value, mask[...])
            steps = [mul(part, group(kn, j)) for j, part in enumerate(split_rows(score, PAIR))]
            step = (ungroup(steps) * scaling).astype(BF16)
            result, part = norm_back(step, q_hat, q_inv, gq)
            settle(out, swap, rows, result)
            fold(acc, where, part)
            wide = mul(jnp.concatenate([prob, score], axis=1), spread)
            for j, part in enumerate(split_rows(wide, PAIR)):
                total = jnp.where(lanes == i * count + j, part, total)
            return total

        total = lax.fori_loop(0, BLOCK // TOGETHER, some, jnp.zeros((PAIR, HOPS * 128), F32))
        for h, pack in enumerate(packs):
            pack[...] = total[:, h * 128 : (h + 1) * 128].astype(BF16)

    start, rows = first_of(chunk), rows_of(chunk)
    pltpu.emit_pipeline(
        block,
        grid=(steps,),
        in_specs=[row_spec(4)] * 5 + [gain_spec(first, cycle)] * 2,
        out_specs=[row_spec(1)] * 2 + [PACKED] * 4,
    )(down, up, u1, u2, u3, gain_q, gain_k, window(out, core, start, rows), swap.at[pl.ds(0, 1)], t0, t1, t2, t3)
    total[...] = sum_heads(acc, heads)


def key_kernel(
    chunk, heads, up, down, d1, d2, d3, t0, t1, t2, t3, gain_q, gain_k, *refs
):
    out_k, out_v, swap, total, acc = refs[3:]
    _, core = place()
    first, steps = sum(CUTS[:chunk]), CUTS[chunk]
    count = TOGETHER // GROUP
    cycle = acc.shape[0] // BLOCK
    acc[...] = jnp.zeros_like(acc)

    def block(up, down, d1, d2, d3, t0, t1, t2, t3, gain_q, gain_k, out_k, out_v, swap_k, swap_v):
        base = ((first + pl.program_id(0)) % cycle) * BLOCK
        scaling = 1.0 / math.sqrt(128)
        same = iota((HOPS * PAIR, PAIR), 0) % GROUP == iota((HOPS * PAIR, PAIR), 1) % GROUP
        lanes = iota((HOPS * PAIR, 128), 1) // 4
        value, sink = iota((128, PAIR), 0) % 4, iota((128, PAIR), 1) // GROUP
        take_p = jnp.where(value == sink, 1.0, 0.0).astype(BF16)
        take_s = jnp.where(value == sink + 2, 1.0, 0.0).astype(BF16)
        packed = cat([t[...] for t in (t0, t1, t2, t3)]).astype(F32)

        def some(i, carry):
            rows = pl.ds(pl.multiple_of(i * TOGETHER, TOGETHER), TOGETHER)
            where = pl.ds(pl.multiple_of(base + i * TOGETHER, TOGETHER), TOGETHER)
            gq, gk = cat([gain_q[rows, :]] * 2 * HOPS), cat([gain_k[rows, :]] * 2)
            k_hat, k_inv = rms(read((up,), 0, rows))
            q_hat, _ = rms(read((down, d1, d2, d3), 0, rows))
            grad = read((down, d1, d2, d3), 1, rows)
            qn = (q_hat * gq).astype(BF16)
            k_steps, v_steps = [], []
            for j in range(count):
                mine = jnp.where(lanes == i * count + j, packed, 0.0).astype(BF16)
                prob = jnp.where(same, mul(mine, take_p), 0.0).astype(BF16)
                score = jnp.where(same, mul(mine, take_s), 0.0).astype(BF16)
                k_steps.append(t_mul(score, group(qn, j)))
                v_steps.append(t_mul(prob, group(grad, j)))
            step = (ungroup(k_steps) * scaling).astype(BF16)
            result, part = norm_back(step, k_hat, k_inv, gk)
            settle(out_k, swap_k, rows, result)
            settle(out_v, swap_v, rows, ungroup(v_steps).astype(BF16))
            fold(acc, where, part)
            return carry

        lax.fori_loop(0, BLOCK // TOGETHER, some, 0)

    start, rows = first_of(chunk), rows_of(chunk)
    pltpu.emit_pipeline(
        block,
        grid=(steps,),
        in_specs=[row_spec(4)] * 5 + [PACKED] * 4 + [gain_spec(first, cycle)] * 2,
        out_specs=[row_spec(1)] * 4,
    )(
        up, down, d1, d2, d3, t0, t1, t2, t3, gain_q, gain_k,
        window(out_k, core, start, rows), window(out_v, core, start, rows),
        swap.at[pl.ds(1, 1)], swap.at[pl.ds(2, 1)],
    )
    total[...] = sum_heads(acc, heads)


def side_cost(rows):
    return pl.CostEstimate(
        flops=rows * 40000, bytes_accessed=rows * 128 * 2 * 24, transcendentals=rows * 300
    )


def query_side(chunk, heads, data, gains, out, after):
    rows, cycle = rows_of(chunk), gains[0].shape[0]
    return call(
        functools.partial(query_kernel, chunk, heads),
        (*data, *gains, out),
        [ANY] * 8,
        after,
        out_shape=[jax.ShapeDtypeStruct(out.shape, BF16), jax.ShapeDtypeStruct((3, rows, 128), BF16)]
        + [jax.ShapeDtypeStruct((CUTS[chunk] * PAIR, 128), BF16)] * 4
        + [jax.ShapeDtypeStruct((heads, 128), F32)],
        out_specs=[ANY] * 6 + [VMEM],
        scratch_shapes=[pltpu.VMEM((cycle, 128), F32), pltpu.VMEM((PAIR, HOPS * PAIR), F32)],
        input_output_aliases={7: 0},
        cost_estimate=side_cost(rows),
        name="query_side",
    )


def key_side(chunk, heads, data, packed, gains, outs, swap, after):
    rows, cycle = rows_of(chunk), gains[0].shape[0]
    return call(
        functools.partial(key_kernel, chunk, heads),
        (*data, *packed, *gains, *outs, swap),
        [ANY] * 14,
        after,
        out_shape=[jax.ShapeDtypeStruct(x.shape, BF16) for x in (*outs, swap)]
        + [jax.ShapeDtypeStruct((heads, 128), F32)],
        out_specs=[ANY] * 3 + [VMEM],
        scratch_shapes=[pltpu.VMEM((cycle, 128), F32)],
        input_output_aliases={11: 0, 12: 1, 13: 2},
        cost_estimate=side_cost(rows),
        name="key_side",
    )


def blank(half):
    def kernel(*refs):
        pass

    return call(
        kernel,
        (),
        [],
        out_shape=[jax.ShapeDtypeStruct((2, half, 128), BF16)] * 3,
        out_specs=[ANY] * 3,
        name="blank_rows",
    )


def send(array, pairs):
    return lax.ppermute(array, "seq", pairs)


def sum_gains(part):
    count = lax.axis_size("dp")
    mine = part.shape[1] // count
    pieces = part.reshape(2, count, mine, part.shape[2])
    total = jnp.sum(lax.all_to_all(pieces, "dp", split_axis=1, concat_axis=1, tiled=True), axis=1)
    for pairs in (SWAP, NEAR, FAR):
        total = total + send(total, pairs)
    return total


def line_body(queries, key_proj, value_proj, out_grad, query_gain, key_gain):
    shape = queries.shape
    heads, width = shape[-2:]
    half = shape[2] // 2 * heads
    arrays = [x.reshape(2, half, width) for x in (queries, key_proj, value_proj, out_grad)]
    cycle = math.lcm(BLOCK, heads)
    chunks = len(CUTS)

    near = send(halves(0, rows_of(0), arrays, ()), SWAP)
    traded = [(near, 0)]
    ups, downs, packs, swaps, sums = {}, {}, {}, {}, []

    def bring(chunk):
        after = []
        if chunk >= 1:
            after += [ups[chunk - 1][2], downs[chunk - 1][2]]
        if chunk >= 2:
            after.append(packs[chunk - 2][0])
        swapped, offset = traded[min(chunk, 1)]
        up, down = pack(chunk, offset, arrays, swapped, after)
        ups[chunk], downs[chunk] = [up], [down]
        for _ in range(HOPS - 1):
            ups[chunk].append(send(ups[chunk][-1], UP))
            downs[chunk].append(send(downs[chunk][-1], DOWN))
        return up

    first = bring(0)
    rest = halves(rows_of(0), half - rows_of(0), arrays, (first,))
    traded.append((send(rest, SWAP), rows_of(0)))
    both = lax.all_gather(jnp.stack([query_gain, key_gain]), "dp", axis=1, tiled=True)
    gains = [jnp.tile(both[t], (cycle // heads, 1)) for t in range(2)]

    outs = list(blank(half))
    bring(1)
    for chunk in range(chunks):
        own_up, own_down = ups[chunk][0], downs[chunk][0]
        data = (own_down, *ups[chunk])
        outs[0], swap, *packed, sum_q = query_side(chunk, heads, data, gains, outs[0], ())
        packs[chunk] = packed
        if chunk + 2 < chunks:
            bring(chunk + 2)
        met = [packed[0]] + [
            send(packed[h], [(i, i - 2 * h) for i in range(2 * h, 2 * HOPS)]) for h in range(1, HOPS)
        ]
        data = (own_up, *downs[chunk])
        outs[1], outs[2], swap, sum_k = key_side(chunk, heads, data, met, gains, outs[1:], swap, ())
        outs = list(settle_rows(chunk, send(swap, SWAP), outs))
        sums.append((sum_q, sum_k))

    totals = jnp.stack([functools.reduce(jnp.add, [s[t] for s in sums]) for t in range(2)])
    totals = sum_gains(totals)
    return (*[x.reshape(shape) for x in outs], totals[0], totals[1])


def wide_attention(query_norm, key_norm, value_in, grad_in):
    frames = query_norm.shape[1]
    scaling = 1.0 / math.sqrt(query_norm.shape[-1])
    scores = (
        jnp.einsum("efphd,egphd->ephfg", query_norm, key_norm, preferred_element_type=F32) * scaling
    )
    allowed = iota((frames, frames), 1) <= iota((frames, frames), 0)
    scores = jnp.where(allowed, scores, -jnp.inf)
    expo = jnp.exp(scores - jnp.max(scores, axis=-1, keepdims=True))
    probability = expo / jnp.sum(expo, axis=-1, keepdims=True)
    prob_low = probability.astype(BF16)
    attn_out = jnp.einsum("ephfg,egphd->efphd", prob_low, value_in, preferred_element_type=F32)
    row_dots = jnp.transpose(jnp.sum(grad_in.astype(F32) * attn_out, axis=-1), (0, 2, 3, 1))
    prob_grad = jnp.einsum("efphd,egphd->ephfg", grad_in, value_in, preferred_element_type=F32)
    score_low = (probability * (prob_grad - row_dots[..., None])).astype(BF16)
    query_step = jnp.einsum("ephfg,egphd->efphd", score_low, key_norm, preferred_element_type=F32)
    key_step = jnp.einsum("ephfg,efphd->egphd", score_low, query_norm, preferred_element_type=F32)
    value_step = jnp.einsum("ephfg,efphd->egphd", prob_low, grad_in, preferred_element_type=F32)
    return (
        (query_step * scaling).astype(BF16),
        (key_step * scaling).astype(BF16),
        value_step.astype(BF16),
    )


def wide_body(queries, key_proj, value_proj, out_grad, query_gain, key_gain):
    gain_q = lax.all_gather(query_gain, "dp", axis=0, tiled=True)
    gain_k = lax.all_gather(key_gain, "dp", axis=0, tiled=True)
    q_hat, q_inv = rms(queries)
    k_hat, k_inv = rms(key_proj)
    pieces = [
        lax.all_to_all(x, "seq", split_axis=2, concat_axis=1, tiled=True)
        for x in ((q_hat * gain_q).astype(BF16), (k_hat * gain_k).astype(BF16), value_proj, out_grad)
    ]
    steps = [
        lax.all_to_all(x, "seq", split_axis=1, concat_axis=2, tiled=True)
        for x in wide_attention(*pieces)
    ]
    query_grad, part_q = norm_back(steps[0], q_hat, q_inv, gain_q)
    key_grad, part_k = norm_back(steps[1], k_hat, k_inv, gain_k)
    axes = tuple(range(part_q.ndim - 2))
    totals = lax.psum((jnp.sum(part_q, axis=axes), jnp.sum(part_k, axis=axes)), "seq")
    totals = [lax.psum_scatter(t, "dp", scatter_dimension=0, tiled=True) for t in totals]
    return (query_grad, key_grad, steps[2], *totals)


def body(*args):
    frames = lax.axis_size("seq")
    patches, heads, width = args[0].shape[2:]
    rows = patches // 2 * heads
    if frames == 8 and args[0].shape[:2] == (1, 1) and width == 128 and rows == sum(CUTS) * BLOCK:
        return line_body(*args)
    return wide_body(*args)


def solution(mesh):
    whole = P("dp", "seq", None, None, None)
    gain = P("dp", None)
    return jax.shard_map(
        body,
        mesh=mesh,
        in_specs=(whole,) * 4 + (gain,) * 2,
        out_specs=(whole,) * 3 + (gain,) * 2,
        check_vma=False,
    )
```

time: 540 us -> 692 us (1.28)
  Pallas kernels: 0 us -> 237 us
  blocking collectives: 189 us -> 16.5 us
  waiting for transfers between devices: 237 us -> 314 us
  starting transfers between devices: 22.1 us -> 97.3 us
  other arithmetic: 44.2 us -> 1.55 us
  matrix products: 34.8 us -> 0 us
  local copies, waits for them, and re-layouts: 10.1 us -> 20.8 us
    ppermute x0 -> x55, waiting for transfers between devices: none -> 314 us  [send(): return lax.ppermute(array, 'seq', pairs)]
    all_to_all x5 -> x0, waiting for transfers between devices: 237 us -> none  [the longest x1 54 us: body(): lax.all_to_all(key_local, 'seq', split_axis=1, concat_axis=2, tiled=True)]
    pallas_call x0 -> x23, Pallas kernels: none -> 237 us  [call(): pl.pallas_call(trimmed, in_specs=list(in_specs) + [ANY] * extra, compiler...]
    all_to_all x2 -> x1, blocking collectives: 129 us -> 8.3 us  [sum_gains(): lax.all_to_all(pieces, 'dp', split_axis=1, concat_axis=1, tiled=True)]
    ppermute x0 -> x55, starting transfers between devices: none -> 97.3 us  [send(): return lax.ppermute(array, 'seq', pairs)]
    dot_general x6 -> x0, matrix products: 34.8 us -> none  [the longest x1 10.8 us: attention_grads(): jnp.einsum('ephfg,egphd->efphd', prob_low, value_in, preferred_element_ty...]
    psum x1 -> x0, blocking collectives: 26.5 us -> none  [body(): totals = lax.psum((query_part, key_part), 'seq')]
    convert_element_type x5 -> x0, other arithmetic: 23.7 us -> none  [the longest x2 11.1 us: norm_back(): (inverse * (gained - hat * jnp.mean(gained * hat, axis=-1, keepdims=True)...]
  transfers between devices with their start and end apart: 5 -> 55, of which waited for: 5 -> 31; matrix products, arithmetic and copies ran while one was open for 10% -> 1% of each run, Pallas kernels for 0% -> 29%
where the time goes in v5:
time: 692 us; the launch traced here: 689 us
  waiting for transfers between devices  314 us (45%)
  Pallas kernels  237 us (34%)
  starting transfers between devices  97.3 us (14%)
  local copies, waits for them, and re-layouts  20.8 us (3%)
  blocking collectives  16.5 us (2%)
    ppermute x55, waiting for transfers between devices, send(): return lax.ppermute(array, 'seq', pairs)  314 us
    pallas_call x23, Pallas kernels, call(): pl.pallas_call(trimmed, in_specs=list(in_specs) + [ANY] * extra, compiler...  237 us
    ppermute x55, starting transfers between devices, send(): return lax.ppermute(array, 'seq', pairs)  97.3 us
    unnamed x129, local copies, waits for them, and re-layouts  18.2 us
  transfers between devices with their start and end apart: 55, of which 31 were waited for; matrix products, arithmetic and copies ran while one was open for 1% of the time, Pallas kernels for 29%

profile of v5, /device:TPU:0, one launch (start us, length us, event | category | flops | bytes accessed | tf_op | source)
XLA Modules:
  0.0 688.5 jit_solution(13804550784583433392)
XLA Ops:
  9.3 4.9 other_half.3
  14.6 4.7 collective-permute-start.2
  20.6 21.5 %collective-permute-done.2.refs_2_ = bf16[4,1024,128]{2,1,0:T(8,128)(2,1)S(1)} collective-permute-done((bf16[4,1024,128]{2,1,0:T(8,128)(2,1)S(1)}, bf16[4,1024,128]{2,1,0:T(8,128)(2,1)S(1)}, u32[]{:S(2)}, u32[]{:S(2)}) %collective-permute-start.2) | collective-permute-done | bytes 1048608 | tf_op jit(solution)/shard_map/ppermute | solution.py:430
  42.1 4.4 collective-permute-start.3
  47.9 20.7 %collective-permute-done.3.refs_5_.refs_3_ = bf16[4,1024,128]{2,1,0:T(8,128)(2,1)S(1)} collective-permute-done((bf16[4,1024,128]{2,1,0:T(8,128)(2,1)S(1)}, bf16[4,1024,128]{2,1,0:T(8,128)(2,1)S(1)}, u32[]{:S(2)}, u32[]{:S(2)}) %collective-permute-start.3) | collective-permute-done | bytes 1048608 | tf_op jit(solution)/shard_map/ppermute | solution.py:430
  83.9 31.1 %collective-permute-done.6.refs_2_ = bf16[4,1536,128]{2,1,0:T(8,128)(2,1)S(1)} collective-permute-done((bf16[4,1536,128]{2,1,0:T(8,128)(2,1)}, bf16[4,1536,128]{2,1,0:T(8,128)(2,1)S(1)}, u32[]{:S(2)}, u32[]{:S(2)}) %collective-permute-start.6) | collective-permute-done | bytes 1572896 | tf_op jit(solution)/shard_map/ppermute | solution.py:430
  120.7 4.6 collective-permute-start.10
  125.4 8.2 %all_gather.3 = f32[2,40,128]{2,0,1:T(2,128)S(1)} all-gather(f32[2,10,128]{2,0,1:T(2,128)S(1)} %pad_maximum_fusion.1), channel_id=1, replica_groups=mesh['dp'=4,'seq'=8] {'dp'}, dimensions={1}, use_global_device_ids=true | all-gather | bytes 51200 | tf_op jit(solution)/shard_map/all_gather | solution.py:472
  133.6 39.4 %collective-permute-done.10.refs_4_ = bf16[4,1024,128]{2,1,0:T(8,128)(2,1)S(1)} collective-permute-done((bf16[4,1024,128]{2,1,0:T(8,128)(2,1)}, bf16[4,1024,128]{2,1,0:T(8,128)(2,1)S(1)}, u32[]{:S(2)}, u32[]{:S(2)}) %collective-permute-start.10) | collective-permute-done | bytes 1048608 | tf_op jit(solution)/shard_map/ppermute | solution.py:430
  175.5 15.4 %query_side.5 = (bf16[2,5120,128]{2,1,0:T(8,128)(2,1)}, bf16[3,1024,128]{2,1,0:T(8,128)(2,1)}, bf16[64,128]{1,0:T(8,128)(2,1)}, bf16[64,128]{1,0:T(8,128)(2,1)},...) custom-call(bf16[4,1024,128]{2,1,0:T(8,128)(2,1)} %get-tuple-element., ...), custom_call_target="tpu_custom_call", output_to_operand_aliasing={{0}: (7, {})} | custom-call | flops 40960000 | bytes 6291456 | tf_op jit(solution)/shard_map/query_side/pallas_call | solution.py:43
  201.6 29.2 %collective-permute-done.11.refs_2_ = bf16[4,1536,128]{2,1,0:T(8,128)(2,1)S(1)} collective-permute-done((bf16[4,1536,128]{2,1,0:T(8,128)(2,1)}, bf16[4,1536,128]{2,1,0:T(8,128)(2,1)S(1)}, u32[]{:S(2)}, u32[]{:S(2)}) %collective-permute-start.11) | collective-permute-done | bytes 1572896 | tf_op jit(solution)/shard_map/ppermute | solution.py:430
  237.9 6.3 collective-permute-start.15
  245.5 51.5 %collective-permute-done.16.refs_4_ = bf16[4,1024,128]{2,1,0:T(8,128)(2,1)S(1)} collective-permute-done((bf16[4,1024,128]{2,1,0:T(8,128)(2,1)S(1)}, bf16[4,1024,128]{2,1,0:T(8,128)(2,1)S(1)}, u32[]{:S(2)}, u32[]{:S(2)}) %collective-permute-start.16) | collective-permute-done | bytes 1048608 | tf_op jit(solution)/shard_map/ppermute | solution.py:430
  299.3 26.1 %collective-permute-done.17.refs_6_ = bf16[64,128]{1,0:T(8,128)(2,1)S(1)} collective-permute-done((bf16[64,128]{1,0:T(8,128)(2,1)S(1)}, bf16[64,128]{1,0:T(8,128)(2,1)S(1)}, u32[]{:S(2)}, u32[]{:S(2)}) %collective-permute-start.17) | collective-permute-done | bytes 16416 | tf_op jit(solution)/shard_map/ppermute | solution.py:430
  326.7 5.4 collective-permute-done.18.refs_7_
  333.3 6.1 collective-permute-done.19.refs_8_
  340.1 19.4 %key_side.5 = (bf16[2,5120,128]{2,1,0:T(8,128)(2,1)}, bf16[2,5120,128]{2,1,0:T(8,128)(2,1)}, bf16[3,1024,128]{2,1,0:T(8,128)(2,1)}, f32[40,128]{1,0:T(8,128)}) custom-call(bf16[4,1024,128]{2,1,0:T(8,128)(2,1)} %get-tuple-element.88.refs_4_.refs_1_.refs_0_, ...), custom_call_target="tpu_custom_call", output_to_operand_aliasing={{0}: (11, {}), {1}: (12, {}), {2}: (13, {})} | custom-call | flops 40960000 | bytes 6291456 | tf_op jit(solution)/shard_map/key_side/pallas_call | solution.py:43
  365.0 21.5 %query_side.6 = (bf16[2,5120,128]{2,1,0:T(8,128)(2,1)}, bf16[3,1536,128]{2,1,0:T(8,128)(2,1)}, bf16[96,128]{1,0:T(8,128)(2,1)}, bf16[96,128]{1,0:T(8,128)(2,1)},...) custom-call(bf16[4,1536,128]{2,1,0:T(8,128)(2,1)} %get-tuple-element., ...), custom_call_target="tpu_custom_call", output_to_operand_aliasing={{0}: (7, {})} | custom-call | flops 61440000 | bytes 9437184 | tf_op jit(solution)/shard_map/query_side/pallas_call | solution.py:43
  390.4 10.5 %collective-permute-done.27.refs_6_ = bf16[96,128]{1,0:T(8,128)(2,1)S(1)} collective-permute-done((bf16[96,128]{1,0:T(8,128)(2,1)}, bf16[96,128]{1,0:T(8,128)(2,1)S(1)}, u32[]{:S(2)}, u32[]{:S(2)}) %collective-permute-start.27) | collective-permute-done | bytes 24608 | tf_op jit(solution)/shard_map/ppermute | solution.py:430
  401.8 27.5 %key_side.6 = (bf16[2,5120,128]{2,1,0:T(8,128)(2,1)}, bf16[2,5120,128]{2,1,0:T(8,128)(2,1)}, bf16[3,1536,128]{2,1,0:T(8,128)(2,1)}, f32[40,128]{1,0:T(8,128)}) custom-call(bf16[4,1536,128]{2,1,0:T(8,128)(2,1)} %get-tuple-element.90.refs_1_.refs_0_, ...), custom_call_target="tpu_custom_call", output_to_operand_aliasing={{0}: (11, {}), {1}: (12, {}), {2}: (13, {})} | custom-call | flops 61440000 | bytes 9437184 | tf_op jit(solution)/shard_map/key_side/pallas_call | solution.py:43
  435.7 10.1 %collective-permute-done.21.refs_2_ = bf16[4,512,128]{2,1,0:T(8,128)(2,1)} collective-permute-done((bf16[4,512,128]{2,1,0:T(8,128)(2,1)}, bf16[4,512,128]{2,1,0:T(8,128)(2,1)}, u32[]{:S(2)}, u32[]{:S(2)}) %collective-permute-start.21) | collective-permute-done | bytes 524320 | tf_op jit(solution)/shard_map/ppermute | solution.py:430
  455.1 21.5 %query_side.7 = (bf16[2,5120,128]{2,1,0:T(8,128)(2,1)}, bf16[3,1536,128]{2,1,0:T(8,128)(2,1)}, bf16[96,128]{1,0:T(8,128)(2,1)}, bf16[96,128]{1,0:T(8,128)(2,1)},...) custom-call(bf16[4,1536,128]{2,1,0:T(8,128)(2,1)} %get-tuple-element., ...), custom_call_target="tpu_custom_call", output_to_operand_aliasing={{0}: (7, {})} | custom-call | flops 61440000 | bytes 9437184 | tf_op jit(solution)/shard_map/query_side/pallas_call | solution.py:43
  489.3 27.5 %key_side.7 = (bf16[2,5120,128]{2,1,0:T(8,128)(2,1)}, bf16[2,5120,128]{2,1,0:T(8,128)(2,1)}, bf16[3,1536,128]{2,1,0:T(8,128)(2,1)}, f32[40,128]{1,0:T(8,128)}) custom-call(bf16[4,1536,128]{2,1,0:T(8,128)(2,1)} %get-tuple-element.94.refs_1_.refs_0_, ...), custom_call_target="tpu_custom_call", output_to_operand_aliasing={{0}: (11, {}), {1}: (12, {}), {2}: (13, {})} | custom-call | flops 61440000 | bytes 9437184 | tf_op jit(solution)/shard_map/key_side/pallas_call | solution.py:43
  523.2 11.1 %collective-permute-done.34.refs_2_ = bf16[4,512,128]{2,1,0:T(8,128)(2,1)S(1)} collective-permute-done((bf16[4,512,128]{2,1,0:T(8,128)(2,1)}, bf16[4,512,128]{2,1,0:T(8,128)(2,1)S(1)}, u32[]{:S(2)}, u32[]{:S(2)}) %collective-permute-start.34) | collective-permute-done | bytes 524320 | tf_op jit(solution)/shard_map/ppermute | solution.py:430
  543.1 7.7 %collective-permute-done.35.refs_3_ = bf16[4,512,128]{2,1,0:T(8,128)(2,1)S(1)} collective-permute-done((bf16[4,512,128]{2,1,0:T(8,128)(2,1)S(1)}, bf16[4,512,128]{2,1,0:T(8,128)(2,1)S(1)}, u32[]{:S(2)}, u32[]{:S(2)}) %collective-permute-start.35) | collective-permute-done | bytes 524320 | tf_op jit(solution)/shard_map/ppermute | solution.py:430
  550.9 4.4 collective-permute-start.36
  563.0 16.7 %query_side.8 = (bf16[2,5120,128]{2,1,0:T(8,128)(2,1)}, bf16[3,512,128]{2,1,0:T(8,128)(2,1)}, bf16[32,128]{1,0:T(8,128)(2,1)}, bf16[32,128]{1,0:T(8,128)(2,1)}, ...) custom-call(bf16[4,512,128]{2,1,0:T(8,128)(2,1)} %get-tuple-element.10, ...), custom_call_target="tpu_custom_call", output_to_operand_aliasing={{0}: (7, {})} | custom-call | flops 20480000 | bytes 3145728 | tf_op jit(solution)/shard_map/query_side/pallas_call | solution.py:43
  592.0 20.4 %key_side.8 = (bf16[2,5120,128]{2,1,0:T(8,128)(2,1)}, bf16[2,5120,128]{2,1,0:T(8,128)(2,1)}, bf16[3,512,128]{2,1,0:T(8,128)(2,1)}, f32[40,128]{1,0:T(8,128)}) custom-call(bf16[4,512,128]{2,1,0:T(8,128)(2,1)} %get-tuple-element.108.refs_1_.refs_0_, ...), custom_call_target="tpu_custom_call", output_to_operand_aliasing={{0}: (11, {}), {1}: (12, {}), {2}: (13, {})} | custom-call | flops 20480000 | bytes 3145728 | tf_op jit(solution)/shard_map/key_side/pallas_call | solution.py:43
  617.6 16.7 %query_side.9 = (bf16[2,5120,128]{2,1,0:T(8,128)(2,1)}, bf16[3,512,128]{2,1,0:T(8,128)(2,1)}, bf16[32,128]{1,0:T(8,128)(2,1)}, bf16[32,128]{1,0:T(8,128)(2,1)}, ...) custom-call(bf16[4,512,128]{2,1,0:T(8,128)(2,1)} %get-tuple-element.12, ...), custom_call_target="tpu_custom_call", output_to_operand_aliasing={{0}: (7, {})} | custom-call | flops 20480000 | bytes 3145728 | tf_op jit(solution)/shard_map/query_side/pallas_call | solution.py:43
  646.3 20.4 %key_side.9 = (bf16[2,5120,128]{2,1,0:T(8,128)(2,1)}, bf16[2,5120,128]{2,1,0:T(8,128)(2,1)}, bf16[3,512,128]{2,1,0:T(8,128)(2,1)}, f32[40,128]{1,0:T(8,128)}) custom-call(bf16[4,512,128]{2,1,0:T(8,128)(2,1)} %get-tuple-element.122.refs_1_.refs_0_, ...), custom_call_target="tpu_custom_call", output_to_operand_aliasing={{0}: (11, {}), {1}: (12, {}), {2}: (13, {})} | custom-call | flops 20480000 | bytes 3145728 | tf_op jit(solution)/shard_map/key_side/pallas_call | solution.py:43
  667.5 8.3 %all_to_all.5 = f32[2,4,10,128]{3,0,2,1:T(2,128)S(1)} all-to-all(f32[2,4,10,128]{3,0,2,1:T(2,128)S(1)} %copy.47), channel_id=1, replica_groups=mesh['dp'=4,'seq'=8] {'dp'}, dimensions={1} | all-to-all | bytes 81920 | tf_op jit(solution)/shard_map/all_to_all | solution.py:437
  681.0 4.5 collective-permute-done.54
  (249 shorter events, 159.2 us)
Async XLA Ops:
  14.2 58.6 %collective-permute-start.1 = (bf16[4,4096,128]{2,1,0:T(8,128)(2,1)}, bf16[4,4096,128]{2,1,0:T(8,128)(2,1)S(1)}, u32[]{:S(2)}, u32[]{:S(2)}) collective-permute-start(bf16[4,4096,128]{2,1,0:T(8,128)(2,1)} %other_half.3), channel_id=1, source_target_pairs={{0,1},{1,0},{2,3},{3,2},{4,5},{5,4},{6,7},{7,6},{8,9},{9,8},{10,11... | collective-permute-start | bytes 12582920 | tf_op jit(solution)/shard_map/ppermute | solution.py:430
  14.6 27.5 %collective-permute-start.2 = (bf16[4,1024,128]{2,1,0:T(8,128)(2,1)S(1)}, bf16[4,1024,128]{2,1,0:T(8,128)(2,1)S(1)}, u32[]{:S(2)}, u32[]{:S(2)}) collective-permute-start(bf16[4,1024,128]{2,1,0:T(8,128)(2,1)S(1)} %copy-done.1), channel_id=1, source_target_pairs={{0,2},{1,3},{2,4},{3,5},{4,6},{5,7},{8,10},{9,11},{10,12},{11,13},... | collective-permute-start | bytes 3145736 | tf_op jit(solution)/shard_map/ppermute | solution.py:430
  19.3 27.3 %collective-permute-start.4 = (bf16[4,1024,128]{2,1,0:T(8,128)(2,1)S(1)}, bf16[4,1024,128]{2,1,0:T(8,128)(2,1)S(1)}, u32[]{:S(2)}, u32[]{:S(2)}) collective-permute-start(bf16[4,1024,128]{2,1,0:T(8,128)(2,1)S(1)} %copy-done.7), channel_id=1, source_target_pairs={{2,0},{3,1},{4,2},{5,3},{6,4},{7,5},{10,8},{11,9},{12,10},{13,11},... | collective-permute-start | bytes 3145736 | tf_op jit(solution)/shard_map/ppermute | solution.py:430
  42.1 26.5 %collective-permute-start.3 = (bf16[4,1024,128]{2,1,0:T(8,128)(2,1)S(1)}, bf16[4,1024,128]{2,1,0:T(8,128)(2,1)S(1)}, u32[]{:S(2)}, u32[]{:S(2)}) collective-permute-start(bf16[4,1024,128]{2,1,0:T(8,128)(2,1)S(1)} %collective-permute-done.2.refs_2_), channel_id=1, source_target_pairs={{0,2},{1,3},{2,4},{3,5},{4,6},{5,7},{8,10},{9,11},{10,12},{11,13},... | collective-permute-start | bytes 3145736 | tf_op jit(solution)/shard_map/ppermute | solution.py:430
  46.6 26.2 %collective-permute-start.5 = (bf16[4,1024,128]{2,1,0:T(8,128)(2,1)S(1)}, bf16[4,1024,128]{2,1,0:T(8,128)(2,1)S(1)}, u32[]{:S(2)}, u32[]{:S(2)}) collective-permute-start(bf16[4,1024,128]{2,1,0:T(8,128)(2,1)S(1)} %collective-permute-done.4.refs_2_), channel_id=1, source_target_pairs={{2,0},{3,1},{4,2},{5,3},{6,4},{7,5},{10,8},{11,9},{12,10},{13,11},... | collective-permute-start | bytes 3145736 | tf_op jit(solution)/shard_map/ppermute | solution.py:430
  79.1 35.9 %collective-permute-start.6 = (bf16[4,1536,128]{2,1,0:T(8,128)(2,1)}, bf16[4,1536,128]{2,1,0:T(8,128)(2,1)S(1)}, u32[]{:S(2)}, u32[]{:S(2)}) collective-permute-start(bf16[4,1536,128]{2,1,0:T(8,128)(2,1)} %get-tuple-element.90.refs_1_.refs_0_), channel_id=1, source_target_pairs={{0,2},{1,3},{2,4},{3,5},{4,6},{5,7},{8,10},{9,11},{10,12},{11,13},... | collective-permute-start | bytes 4718600 | tf_op jit(solution)/shard_map/ppermute | solution.py:430
  82.6 36.8 %collective-permute-start.8 = (bf16[4,1536,128]{2,1,0:T(8,128)(2,1)}, bf16[4,1536,128]{2,1,0:T(8,128)(2,1)S(1)}, u32[]{:S(2)}, u32[]{:S(2)}) collective-permute-start(bf16[4,1536,128]{2,1,0:T(8,128)(2,1)} %get-tuple-element.91.refs_0_.refs_1_), channel_id=1, source_target_pairs={{2,0},{3,1},{4,2},{5,3},{6,4},{7,5},{10,8},{11,9},{12,10},{13,11},... | collective-permute-start | bytes 4718600 | tf_op jit(solution)/shard_map/ppermute | solution.py:430
  115.0 76.0 %collective-permute-start.7 = (bf16[4,1536,128]{2,1,0:T(8,128)(2,1)S(1)}, bf16[4,1536,128]{2,1,0:T(8,128)(2,1)S(1)}, u32[]{:S(2)}, u32[]{:S(2)}) collective-permute-start(bf16[4,1536,128]{2,1,0:T(8,128)(2,1)S(1)} %collective-permute-done.6.refs_2_), channel_id=1, source_target_pairs={{0,2},{1,3},{2,4},{3,5},{4,6},{5,7},{8,10},{9,11},{10,12},{11,13},... | collective-permute-start | bytes 4718600 | tf_op jit(solution)/shard_map/ppermute | solution.py:430
  119.4 71.6 %collective-permute-start.9 = (bf16[4,1536,128]{2,1,0:T(8,128)(2,1)S(1)}, bf16[4,1536,128]{2,1,0:T(8,128)(2,1)S(1)}, u32[]{:S(2)}, u32[]{:S(2)}) collective-permute-start(bf16[4,1536,128]{2,1,0:T(8,128)(2,1)S(1)} %collective-permute-done.8.refs_2_), channel_id=1, source_target_pairs={{2,0},{3,1},{4,2},{5,3},{6,4},{7,5},{10,8},{11,9},{12,10},{13,11},... | collective-permute-start | bytes 4718600 | tf_op jit(solution)/shard_map/ppermute | solution.py:430
  120.7 52.4 %collective-permute-start.10 = (bf16[4,1024,128]{2,1,0:T(8,128)(2,1)}, bf16[4,1024,128]{2,1,0:T(8,128)(2,1)S(1)}, u32[]{:S(2)}, u32[]{:S(2)}) collective-permute-start(bf16[4,1024,128]{2,1,0:T(8,128)(2,1)} %copy-done.6), channel_id=1, source_target_pairs={{0,2},{1,3},{2,4},{3,5},{4,6},{5,7},{8,10},{9,11},{10,12},{11,13},... | collective-permute-start | bytes 3145736 | tf_op jit(solution)/shard_map/ppermute | solution.py:430
  196.0 34.9 %collective-permute-start.11 = (bf16[4,1536,128]{2,1,0:T(8,128)(2,1)}, bf16[4,1536,128]{2,1,0:T(8,128)(2,1)S(1)}, u32[]{:S(2)}, u32[]{:S(2)}) collective-permute-start(bf16[4,1536,128]{2,1,0:T(8,128)(2,1)} %get-tuple-element.94.refs_1_.refs_0_), channel_id=1, source_target_pairs={{0,2},{1,3},{2,4},{3,5},{4,6},{5,7},{8,10},{9,11},{10,12},{11,13},... | collective-permute-start | bytes 4718600 | tf_op jit(solution)/shard_map/ppermute | solution.py:430
  200.3 34.9 %collective-permute-start.13 = (bf16[4,1536,128]{2,1,0:T(8,128)(2,1)}, bf16[4,1536,128]{2,1,0:T(8,128)(2,1)S(1)}, u32[]{:S(2)}, u32[]{:S(2)}) collective-permute-start(bf16[4,1536,128]{2,1,0:T(8,128)(2,1)} %get-tuple-element.95.refs_0_.refs_1_), channel_id=1, source_target_pairs={{2,0},{3,1},{4,2},{5,3},{6,4},{7,5},{10,8},{11,9},{12,10},{13,11},... | collective-permute-start | bytes 4718600 | tf_op jit(solution)/shard_map/ppermute | solution.py:430
  230.9 128.6 %collective-permute-start.12 = (bf16[4,1536,128]{2,1,0:T(8,128)(2,1)S(1)}, bf16[4,1536,128]{2,1,0:T(8,128)(2,1)S(1)}, u32[]{:S(2)}, u32[]{:S(2)}) collective-permute-start(bf16[4,1536,128]{2,1,0:T(8,128)(2,1)S(1)} %collective-permute-done.11.refs_2_), channel_id=1, source_target_pairs={{0,2},{1,3},{2,4},{3,5},{4,6},{5,7},{8,10},{9,11},{10,12},{11,13},... | collective-permute-start | bytes 4718600 | tf_op jit(solution)/shard_map/ppermute | solution.py:430
  235.3 125.7 %collective-permute-start.14 = (bf16[4,1536,128]{2,1,0:T(8,128)(2,1)S(1)}, bf16[4,1536,128]{2,1,0:T(8,128)(2,1)S(1)}, u32[]{:S(2)}, u32[]{:S(2)}) collective-permute-start(bf16[4,1536,128]{2,1,0:T(8,128)(2,1)S(1)} %collective-permute-done.13.refs_2_), channel_id=1, source_target_pairs={{2,0},{3,1},{4,2},{5,3},{6,4},{7,5},{10,8},{11,9},{12,10},{13,11},... | collective-permute-start | bytes 4718600 | tf_op jit(solution)/shard_map/ppermute | solution.py:430
  236.6 60.4 %collective-permute-start.16 = (bf16[4,1024,128]{2,1,0:T(8,128)(2,1)S(1)}, bf16[4,1024,128]{2,1,0:T(8,128)(2,1)S(1)}, u32[]{:S(2)}, u32[]{:S(2)}) collective-permute-start(bf16[4,1024,128]{2,1,0:T(8,128)(2,1)S(1)} %copy-done.9), channel_id=1, source_target_pairs={{2,0},{3,1},{4,2},{5,3},{6,4},{7,5},{10,8},{11,9},{12,10},{13,11},... | collective-permute-start | bytes 3145736 | tf_op jit(solution)/shard_map/ppermute | solution.py:430
  237.9 127.1 %collective-permute-start.15 = (bf16[4,1536,128]{2,1,0:T(8,128)(2,1)}, bf16[4,1536,128]{2,1,0:T(8,128)(2,1)}, u32[]{:S(2)}, u32[]{:S(2)}) collective-permute-start(bf16[4,1536,128]{2,1,0:T(8,128)(2,1)} %copy-done.5), channel_id=1, source_target_pairs={{0,2},{1,3},{2,4},{3,5},{4,6},{5,7},{8,10},{9,11},{10,12},{11,13},... | collective-permute-start | bytes 4718600 | tf_op jit(solution)/shard_map/ppermute | solution.py:430
  244.2 144.9 %collective-permute-start.26 = (bf16[4,1536,128]{2,1,0:T(8,128)(2,1)}, bf16[4,1536,128]{2,1,0:T(8,128)(2,1)}, u32[]{:S(2)}, u32[]{:S(2)}) collective-permute-start(bf16[4,1536,128]{2,1,0:T(8,128)(2,1)} %copy-done.3), channel_id=1, source_target_pairs={{2,0},{3,1},{4,2},{5,3},{6,4},{7,5},{10,8},{11,9},{12,10},{13,11},... | collective-permute-start | bytes 4718600 | tf_op jit(solution)/shard_map/ppermute | solution.py:430
  298.0 27.4 %collective-permute-start.17 = (bf16[64,128]{1,0:T(8,128)(2,1)S(1)}, bf16[64,128]{1,0:T(8,128)(2,1)S(1)}, u32[]{:S(2)}, u32[]{:S(2)}) collective-permute-start(bf16[64,128]{1,0:T(8,128)(2,1)S(1)} %copy-done.63), channel_id=1, source_target_pairs={{2,0},{3,1},{4,2},{5,3},{6,4},{7,5},{10,8},{11,9},{12,10},{13,11},... | collective-permute-start | bytes 49160 | tf_op jit(solution)/shard_map/ppermute | solution.py:430
  359.5 94.4 %collective-permute-start.25 = (bf16[4,1536,128]{2,1,0:T(8,128)(2,1)S(1)}, bf16[4,1536,128]{2,1,0:T(8,128)(2,1)S(1)}, u32[]{:S(2)}, u32[]{:S(2)}) collective-permute-start(bf16[4,1536,128]{2,1,0:T(8,128)(2,1)S(1)} %collective-permute-done.12.refs_5_.refs_3_), channel_id=1, source_target_pairs={{0,2},{1,3},{2,4},{3,5},{4,6},{5,7},{8,10},{9,11},{10,12},{11,13},... | collective-permute-start | bytes 4718600 | tf_op jit(solution)/shard_map/ppermute | solution.py:430
  360.9 118.2 %collective-permute-start.39 = (bf16[4,1536,128]{2,1,0:T(8,128)(2,1)S(1)}, bf16[4,1536,128]{2,1,0:T(8,128)(2,1)S(1)}, u32[]{:S(2)}, u32[]{:S(2)}) collective-permute-start(bf16[4,1536,128]{2,1,0:T(8,128)(2,1)S(1)} %collective-permute-done.14.refs_6_.refs_3_), channel_id=1, source_target_pairs={{2,0},{3,1},{4,2},{5,3},{6,4},{7,5},{10,8},{11,9},{12,10},{13,11},... | collective-permute-start | bytes 4718600 | tf_op jit(solution)/shard_map/ppermute | solution.py:430
  429.3 22.6 %collective-permute-start.30 = (bf16[3,1536,128]{2,1,0:T(8,128)(2,1)}, bf16[3,1536,128]{2,1,0:T(8,128)(2,1)}, u32[]{:S(2)}, u32[]{:S(2)}) collective-permute-start(bf16[3,1536,128]{2,1,0:T(8,128)(2,1)} %get-tuple-element.116), channel_id=1, source_target_pairs={{0,1},{1,0},{2,3},{3,2},{4,5},{5,4},{6,7},{7,6},{8,9},{9,8},{10,11... | collective-permute-start | bytes 3538952 | tf_op jit(solution)/shard_map/ppermute | solution.py:430
  434.4 16.1 %collective-permute-start.23 = (bf16[4,512,128]{2,1,0:T(8,128)(2,1)}, bf16[4,512,128]{2,1,0:T(8,128)(2,1)S(1)}, u32[]{:S(2)}, u32[]{:S(2)}) collective-permute-start(bf16[4,512,128]{2,1,0:T(8,128)(2,1)} %get-tuple-element.109.refs_0_.refs_1_), channel_id=1, source_target_pairs={{2,0},{3,1},{4,2},{5,3},{6,4},{7,5},{10,8},{11,9},{12,10},{13,11},... | collective-permute-start | bytes 1572872 | tf_op jit(solution)/shard_map/ppermute | solution.py:430
  445.7 71.1 %collective-permute-start.22 = (bf16[4,512,128]{2,1,0:T(8,128)(2,1)}, bf16[4,512,128]{2,1,0:T(8,128)(2,1)S(1)}, u32[]{:S(2)}, u32[]{:S(2)}) collective-permute-start(bf16[4,512,128]{2,1,0:T(8,128)(2,1)} %collective-permute-done.21.refs_2_), channel_id=1, source_target_pairs={{0,2},{1,3},{2,4},{3,5},{4,6},{5,7},{8,10},{9,11},{10,12},{11,13},... | collective-permute-start | bytes 1572872 | tf_op jit(solution)/shard_map/ppermute | solution.py:430
  450.5 66.3 %collective-permute-start.24 = (bf16[4,512,128]{2,1,0:T(8,128)(2,1)S(1)}, bf16[4,512,128]{2,1,0:T(8,128)(2,1)S(1)}, u32[]{:S(2)}, u32[]{:S(2)}) collective-permute-start(bf16[4,512,128]{2,1,0:T(8,128)(2,1)S(1)} %collective-permute-done.23.refs_2_), channel_id=1, source_target_pairs={{2,0},{3,1},{4,2},{5,3},{6,4},{7,5},{10,8},{11,9},{12,10},{13,11},... | collective-permute-start | bytes 1572872 | tf_op jit(solution)/shard_map/ppermute | solution.py:430
  516.8 38.4 %collective-permute-start.43 = (bf16[3,1536,128]{2,1,0:T(8,128)(2,1)}, bf16[3,1536,128]{2,1,0:T(8,128)(2,1)S(1)}, u32[]{:S(2)}, u32[]{:S(2)}) collective-permute-start(bf16[3,1536,128]{2,1,0:T(8,128)(2,1)} %get-tuple-element.130), channel_id=1, source_target_pairs={{0,1},{1,0},{2,3},{3,2},{4,5},{5,4},{6,7},{7,6},{8,9},{9,8},{10,11... | collective-permute-start | bytes 3538952 | tf_op jit(solution)/shard_map/ppermute | solution.py:430
  521.9 19.9 %collective-permute-start.31 = (bf16[4,512,128]{2,1,0:T(8,128)(2,1)}, bf16[4,512,128]{2,1,0:T(8,128)(2,1)S(1)}, u32[]{:S(2)}, u32[]{:S(2)}) collective-permute-start(bf16[4,512,128]{2,1,0:T(8,128)(2,1)} %get-tuple-element.123.refs_0_.refs_1_), channel_id=1, source_target_pairs={{2,0},{3,1},{4,2},{5,3},{6,4},{7,5},{10,8},{11,9},{12,10},{13,11},... | collective-permute-start | bytes 1572872 | tf_op jit(solution)/shard_map/ppermute | solution.py:430
  534.3 16.6 %collective-permute-start.35 = (bf16[4,512,128]{2,1,0:T(8,128)(2,1)S(1)}, bf16[4,512,128]{2,1,0:T(8,128)(2,1)S(1)}, u32[]{:S(2)}, u32[]{:S(2)}) collective-permute-start(bf16[4,512,128]{2,1,0:T(8,128)(2,1)S(1)} %collective-permute-done.34.refs_2_), channel_id=1, source_target_pairs={{0,2},{1,3},{2,4},{3,5},{4,6},{5,7},{8,10},{9,11},{10,12},{11,13},... | collective-permute-start | bytes 1572872 | tf_op jit(solution)/shard_map/ppermute | solution.py:430
  538.6 23.6 %collective-permute-start.38 = (bf16[4,512,128]{2,1,0:T(8,128)(2,1)}, bf16[4,512,128]{2,1,0:T(8,128)(2,1)S(1)}, u32[]{:S(2)}, u32[]{:S(2)}) collective-permute-start(bf16[4,512,128]{2,1,0:T(8,128)(2,1)} %copy-done.11), channel_id=1, source_target_pairs={{0,2},{1,3},{2,4},{3,5},{4,6},{5,7},{8,10},{9,11},{10,12},{11,13},... | collective-permute-start | bytes 1572872 | tf_op jit(solution)/shard_map/ppermute | solution.py:430
  540.5 41.8 %collective-permute-start.37 = (bf16[4,512,128]{2,1,0:T(8,128)(2,1)}, bf16[4,512,128]{2,1,0:T(8,128)(2,1)S(1)}, u32[]{:S(2)}, u32[]{:S(2)}) collective-permute-start(bf16[4,512,128]{2,1,0:T(8,128)(2,1)} %copy-done.10), channel_id=1, source_target_pairs={{2,0},{3,1},{4,2},{5,3},{6,4},{7,5},{10,8},{11,9},{12,10},{13,11},... | collective-permute-start | bytes 1572872 | tf_op jit(solution)/shard_map/ppermute | solution.py:430
  541.8 70.6 %collective-permute-start.32 = (bf16[4,512,128]{2,1,0:T(8,128)(2,1)S(1)}, bf16[4,512,128]{2,1,0:T(8,128)(2,1)S(1)}, u32[]{:S(2)}, u32[]{:S(2)}) collective-permute-start(bf16[4,512,128]{2,1,0:T(8,128)(2,1)S(1)} %collective-permute-done.31.refs_2_), channel_id=1, source_target_pairs={{2,0},{3,1},{4,2},{5,3},{6,4},{7,5},{10,8},{11,9},{12,10},{13,11},... | collective-permute-start | bytes 1572872 | tf_op jit(solution)/shard_map/ppermute | solution.py:430
  550.9 66.0 %collective-permute-start.36 = (bf16[4,512,128]{2,1,0:T(8,128)(2,1)S(1)}, bf16[4,512,128]{2,1,0:T(8,128)(2,1)S(1)}, u32[]{:S(2)}, u32[]{:S(2)}) collective-permute-start(bf16[4,512,128]{2,1,0:T(8,128)(2,1)S(1)} %collective-permute-done.35.refs_3_), channel_id=1, source_target_pairs={{0,2},{1,3},{2,4},{3,5},{4,6},{5,7},{8,10},{9,11},{10,12},{11,13},... | collective-permute-start | bytes 1572872 | tf_op jit(solution)/shard_map/ppermute | solution.py:430
  612.4 26.6 %collective-permute-start.33 = (bf16[4,512,128]{2,1,0:T(8,128)(2,1)S(1)}, bf16[4,512,128]{2,1,0:T(8,128)(2,1)S(1)}, u32[]{:S(2)}, u32[]{:S(2)}) collective-permute-start(bf16[4,512,128]{2,1,0:T(8,128)(2,1)S(1)} %collective-permute-done.32.refs_3_), channel_id=1, source_target_pairs={{2,0},{3,1},{4,2},{5,3},{6,4},{7,5},{10,8},{11,9},{12,10},{13,11},... | collective-permute-start | bytes 1572872 | tf_op jit(solution)/shard_map/ppermute | solution.py:430
  (87 other events, 1677.5 us)

commit v6 on v4

--- a/solution.py
+++ b/solution.py
@@ -14,7 +14,7 @@
 SLOTS = 4
 WIDE = GROUP * SLOTS
 TOGETHER = 64
-CUTS = (2, 4, 5, 5, 3, 1)
+CUTS = (3, 3, 3, 3, 3, 2, 2, 1)
 
 EDGE = ((0, 2), (1, 3), (6, 4), (7, 5))
 MIDDLE = ((2, 4), (3, 5), (4, 2), (5, 3))
@@ -110,23 +110,20 @@
     )
 
 
-def pack_kernel(start, rows, offset, q, k, v, g, x, edge, middle):
+def pack_kernel(start, rows, offset, q, k, v, g, x, edge):
     chip, core = place()
 
     def run(order):
         def move(*blocks):
-            sent, crossing = blocks[8:]
+            sent = blocks[8]
             for pair in range(2):
                 for t in range(2):
                     for frame in range(2):
-                        value = blocks[4 * frame + 2 * pair + t][0]
-                        sent[4 * pair + 2 * frame + t] = value
-                        if pair == 0:
-                            crossing[2 * frame + t] = value
+                        sent[4 * pair + 2 * frame + t] = blocks[4 * frame + 2 * pair + t][0]
 
         own = [window((q, k, v, g)[t], core, start, rows) for t in order]
         other = [window(x, t, start - offset, rows) for t in order]
-        stream(rows, own + other, [edge, middle], move)
+        stream(rows, own + other, [edge], move)
 
     @pl.when(chip < 2)
     def _():
@@ -144,53 +141,45 @@
         (*arrays, swapped),
         [ANY] * 5,
         after,
-        out_shape=[jax.ShapeDtypeStruct((n, rows, 128), BF16) for n in (8, 4)],
-        out_specs=[ANY] * 2,
-        cost_estimate=copy_cost(rows, 10),
+        out_shape=jax.ShapeDtypeStruct((8, rows, 128), BF16),
+        out_specs=ANY,
+        cost_estimate=copy_cost(rows, 8),
         name="pack_rows",
     )
 
 
-def forward_kernel(rows, extra, edge, *refs):
-    packed, out = refs[:-1], refs[-1]
+def forward_kernel(sizes, *refs):
+    sources, out = refs[:-1], refs[-1]
     chip, _ = place()
 
-    def move(src, dst):
-        dst[...] = src[...]
-
-    def move_packed(src, dst):
-        dst[...] = src[...]
+    def move(src, *dsts):
+        for q, dst in enumerate(dsts):
+            dst[...] = src[q]
 
     @pl.when((chip == 1) | (chip == 2))
     def _():
-        tile = tile_of(rows)
-        pltpu.emit_pipeline(
-            lambda src, dst: move(src.at[0], dst),
-            grid=(4, rows // tile),
-            in_specs=[pl.BlockSpec((1, tile, 128), lambda q, i: (q, i, 0))],
-            out_specs=[pl.BlockSpec((tile, 128), lambda q, i: (q * (rows // tile) + i, 0))],
-        )(edge, out.at[pl.ds(0, 4 * rows)])
-        for ref in packed:
+        start = 0
+        for rows, src in zip(sizes, sources):
+            tile = tile_of(rows)
             pltpu.emit_pipeline(
-                move_packed,
-                grid=(1,),
-                in_specs=[pl.BlockSpec((extra, 128), lambda i: (0, 0))],
-                out_specs=[pl.BlockSpec((extra, 128), lambda i: (0, 0))],
-            )(ref, out.at[pl.ds(4 * rows, extra)])
-
-
-def forward(chunk, edge, packed, after):
-    rows = rows_of(chunk)
-    extra = 0 if packed is None else packed.shape[0]
-    inputs = (edge,) if packed is None else (edge, packed)
+                move,
+                grid=(rows // tile,),
+                in_specs=[pl.BlockSpec((4, tile, 128), lambda i: (0, i, 0))],
+                out_specs=[pl.BlockSpec((tile, 128), lambda i: (i, 0))] * 4,
+            )(src, *[out.at[pl.ds(start + q * rows, rows)] for q in range(4)])
+            start += 4 * rows
+
+
+def forward(sources, after):
+    sizes = [x.shape[1] for x in sources]
     return call(
-        functools.partial(forward_kernel, rows, extra),
-        inputs,
-        [ANY] * len(inputs),
+        functools.partial(forward_kernel, sizes),
+        sources,
+        [ANY] * len(sources),
         after,
-        out_shape=jax.ShapeDtypeStruct((4 * rows + extra, 128), BF16),
+        out_shape=jax.ShapeDtypeStruct((4 * sum(sizes), 128), BF16),
         out_specs=ANY,
-        cost_estimate=copy_cost(rows, 4),
+        cost_estimate=copy_cost(sum(sizes), 4),
         name="forward_rows",
     )
 
@@ -213,7 +202,8 @@
 
 
 def place_kernel(slot, own, other, back, *refs):
-    outs, late = refs[-4:-1], refs[-1]
+    outs, late, token = refs[-5:-2], refs[-2], refs[-1]
+    token[...] = jnp.zeros_like(token)
     _, core = place()
 
     def run(chunk, hub):
@@ -227,7 +217,8 @@
 
 
 def place_last_kernel(slot, own, other, back_s, back_x, *refs):
-    outs = refs[-3:]
+    outs, token = refs[-4:-1], refs[-1]
+    token[...] = jnp.zeros_like(token)
     _, core = place()
 
     def run(chunk, hub):
@@ -240,7 +231,8 @@
 
 
 def place_late_kernel(slot, late, *refs):
-    outs = refs[-3:]
+    outs, token = refs[-4:-1], refs[-1]
+    token[...] = jnp.zeros_like(token)
     chip, core = place()
 
     def run(rows):
@@ -263,8 +255,9 @@
         (*pieces, *kept),
         [ANY] * (len(pieces) + len(kept)),
         after,
-        out_shape=[jax.ShapeDtypeStruct((n, half, 128), BF16) for n in (2, 2, 2, 3)[:count]],
-        out_specs=[ANY] * count,
+        out_shape=[jax.ShapeDtypeStruct((n, half, 128), BF16) for n in (2, 2, 2, 3)[:count]]
+        + [jax.ShapeDtypeStruct((8, 128), F32)],
+        out_specs=[ANY] * count + [VMEM],
         input_output_aliases={len(pieces) + i: i for i in range(len(kept))},
         cost_estimate=copy_cost(rows, 6),
         name="place_rows",
@@ -360,17 +353,18 @@
 
 
 def read_met(near, far, t, rows):
-    return cat([near[2 * x + t, rows, :] for x in range(2)] + [far[2 * x + t][rows, :] for x in range(2)])
+    return cat([side[2 * x + t][rows, :] for side in (near, far) for x in range(2)])
 
 
 def hub_specs(steps):
     four = lambda n: pl.BlockSpec((4, BLOCK, 128), lambda i: (n, i, 0))
     flat = lambda q: pl.BlockSpec((BLOCK, 128), lambda i: (q * steps + i, 0))
-    return [four(0), four(1), four(0), four(1), four(0)] + [flat(q) for q in range(4)]
-
-
-def hub_refs(steps, own, edge, other, far):
-    return [own, own, edge, edge, other] + [far.at[pl.ds(0, 4 * steps * BLOCK)]] * 4
+    return [four(0), four(1), four(0), four(1)] + [flat(q) for q in range(4)] * 2
+
+
+def hub_refs(steps, skip, own, edge, other, far):
+    rows = 4 * steps * BLOCK
+    return [own, own, edge, edge] + [other.at[pl.ds(skip, rows)]] * 4 + [far.at[pl.ds(0, rows)]] * 4
 
 
 def grad_specs():
@@ -403,16 +397,15 @@
     return split(prob_low), split(score_low)
 
 
-def upper_kernel(chunk, heads, own, edge, other, far, gain_q, gain_k, *refs):
+def upper_kernel(chunk, skip, heads, own, edge, other, far, gain_q, gain_k, *refs):
     outs, (packed, sum_q, sum_k, acc_q, acc_k, mask) = refs[:-6], refs[-6:]
     chip, core = place()
     first, steps = sum(CUTS[:chunk]), CUTS[chunk]
     count = TOGETHER // GROUP
     cycle = acc_q.shape[0] // BLOCK
 
-    def block(own_a, own_b, edge_a, edge_b, other, f0, f1, f2, f3, gain_q, gain_k, *results):
-        out, pack_ref = results[:4], results[4]
-        far = (f0, f1, f2, f3)
+    def block(own_a, own_b, edge_a, edge_b, *refs):
+        other, far, (gain_q, gain_k), out, pack_ref = refs[:4], refs[4:8], refs[8:10], refs[10:14], refs[14]
         base = ((first + pl.program_id(0)) % cycle) * BLOCK
         scaling = 1.0 / math.sqrt(128)
         lanes = iota((WIDE, 128), 1) // 8
@@ -458,7 +451,7 @@
             grid=(steps,),
             in_specs=hub_specs(steps) + [gain_spec(first, cycle)] * 2,
             out_specs=grad_specs() + [pl.BlockSpec((WIDE, 128), lambda i: (i, 0))],
-        )(*hub_refs(steps, own, edge, other, far), gain_q, gain_k, *grad_refs(outs), packed)
+        )(*hub_refs(steps, skip, own, edge, other, far), gain_q, gain_k, *grad_refs(outs), packed)
         sum_q[...] = sum_heads(acc_q, heads)
         sum_k[...] = sum_heads(acc_k, heads)
 
@@ -476,8 +469,8 @@
     count = TOGETHER // GROUP
     cycle = acc_q.shape[0] // BLOCK
 
-    def block(own_a, own_b, edge_a, edge_b, other, f0, f1, f2, f3, gain_q, gain_k, pack_ref, *out):
-        far = (f0, f1, f2, f3)
+    def block(own_a, own_b, edge_a, edge_b, *refs):
+        other, far, (gain_q, gain_k, pack_ref), out = refs[:4], refs[4:8], refs[8:11], refs[11:]
         base = ((first + pl.program_id(0)) % cycle) * BLOCK
         both = iota((WIDE, 2 * WIDE), 0) % GROUP == iota((WIDE, 2 * WIDE), 1) % GROUP
         scaling = 1.0 / math.sqrt(128)
@@ -540,10 +533,10 @@
             + [pl.BlockSpec((WIDE, 128), lambda i: (i, 0))],
             out_specs=grad_specs(),
         )(
-            *hub_refs(steps, own, edge, other, far),
+            *hub_refs(steps, skip, own, edge, other, far),
             gain_q,
             gain_k,
-            packed.at[pl.ds(skip, steps * WIDE)],
+            packed,
             *grad_refs(outs),
         )
         sum_q[...] = sum_heads(acc_q, heads)
@@ -566,12 +559,12 @@
     return [jax.ShapeDtypeStruct((n, out_rows(slot), 128), BF16) for n in sizes]
 
 
-def upper(slot, heads, data, gains, after):
+def upper(slot, skip, heads, data, gains, after):
     steps = CUTS[slot]
     cycle = gains[0].shape[0]
     shapes = grad_shapes(slot)
     return call(
-        functools.partial(upper_kernel, slot, heads),
+        functools.partial(upper_kernel, slot, skip, heads),
         (*data, *gains),
         [ANY] * 6,
         after,
@@ -637,77 +630,97 @@
     cycle = math.lcm(BLOCK, heads)
     chunks = len(CUTS)
 
-    near = send(halves(0, rows_of(0), arrays, ()), SWAP)
-    traded = [(near, 0)]
-
-    edges, others, fars, grads, packed = {}, {}, {}, {}, {}
-    passed, sums, kept = {}, [], {-1: None}
+    edges, grads, crossed, middle, traded = {}, {}, {}, {}, []
+    sums, kept, chain = [], {-1: None}, []
+
+    def then(token):
+        chain[:] = [token]
+
+    def trade(low, high):
+        rows = halves(low, high - low, arrays, chain)
+        then(rows)
+        traded.append((send(rows, SWAP), low))
 
     def bring(chunk):
-        after = []
+        swapped, offset = traded[min(chunk, 1)]
+        rows = pack(chunk, offset, arrays, swapped, chain)
+        then(rows)
+        edges[chunk] = (rows, send(rows, EDGE))
+
+    def cross(chunk):
+        sources = [edges[chunk][1]] if chunk >= 0 else []
+        if chunk + 1 < chunks:
+            sources.append(edges[chunk + 1][0])
+        if chunk == 0:
+            chain.append(middle[-1])
         if chunk >= 2:
-            after += [passed[chunk - 2], edges[chunk - 2][1]]
-        if chunk >= 3:
-            after.append(grads[chunk - 3][0])
-        swapped, offset = traded[min(chunk, 1)]
-        to_hub, to_middle = pack(chunk, offset, arrays, swapped, after)
-        edges[chunk] = (to_hub, send(to_hub, EDGE))
-        others[chunk] = send(to_middle, MIDDLE)
-        return to_hub
-
-    def pass_on(chunk):
-        after = [grads[chunk - 1][0]] if chunk else []
-        passed[chunk] = forward(chunk, edges[chunk][1], packed.get(chunk - 1), after)
-        fars[chunk] = send(passed[chunk], MIDDLE)
+            chain.append(crossed[chunk - 2])
+        rows = forward(sources, chain)
+        then(rows)
+        middle[chunk] = send(rows, MIDDLE)
+
+    def data_of(chunk):
+        return (*edges[chunk], middle[chunk - 1], middle[chunk])
+
+    def skip_of(chunk):
+        return 4 * rows_of(chunk - 1) if chunk else 0
 
     def work(slot):
-        after = list(kept[slot - 2][:1]) if slot >= 2 else []
         if slot < chunks:
-            data = (*edges[slot], others[slot], fars[slot])
-            *parts, packed[slot], sum_q, sum_k = upper(slot, heads, data, gains, after)
+            *parts, packed, sum_q, sum_k = upper(slot, skip_of(slot), heads, data_of(slot), gains, chain)
+            crossed[slot] = send(packed, DOWN)
             sums.append((sum_q, sum_k))
         else:
-            parts = blank(slot, after)
+            parts = blank(slot, chain)
         if slot > 0:
             chunk = slot - 1
-            data = (*edges[chunk], others[chunk], fars[chunk])
-            if slot < chunks:
-                cross, skip = fars[slot], 4 * rows_of(slot)
-            else:
-                cross, skip = send(packed[chunk], DOWN), 0
-            *parts, sum_q, sum_k = lower(slot, heads, data, cross, skip, gains, parts, after)
+            *parts, sum_q, sum_k = lower(
+                slot, heads, data_of(chunk), crossed[chunk], skip_of(chunk), gains, parts, [sum_q] if slot < chunks else ()
+            )
             sums.append((sum_q, sum_k))
-        grads[slot] = parts
-
-    def give(slot):
-        own, other, *edge = grads[slot]
+        then(sum_q)
+        own, other, *edge = parts
+        if slot < chunks - 1:
+            grads[slot] = (own, other, send(edge[0], BACK_S))
+        else:
+            grads[slot] = (own, send(other, SWAP), send(edge[0], BACK_S), send(edge[1], BACK_X))
+
+    def settle_slot(slot):
         rows = out_rows(slot)
         if slot < chunks - 1:
-            pieces = (own, other, send(edge[0], BACK_S))
             kernel = functools.partial(place_kernel, slot)
-            kept[slot] = settle_rows(kernel, half, pieces, kept[slot - 1], 4, rows)
-            return
-        if slot == chunks - 1:
-            *outs, late = kept[slot - 1]
-            kernel = functools.partial(place_late_kernel, slot - 1)
-            kept[slot - 1] = settle_rows(kernel, half, (send(late, SWAP),), outs, 3, half // 2)
-        pieces = (own, send(other, SWAP), send(edge[0], BACK_S), send(edge[1], BACK_X))
-        kernel = functools.partial(place_last_kernel, slot)
-        kept[slot] = settle_rows(kernel, half, pieces, kept[slot - 1], 3, rows)
-
-    first = bring(0)
-    rest = halves(rows_of(0), half - rows_of(0), arrays, (first,))
-    traded.append((send(rest, SWAP), rows_of(0)))
+            *kept[slot], token = settle_rows(kernel, half, grads[slot], kept[slot - 1], 4, rows, chain)
+            if slot == chunks - 2:
+                grads["late"] = send(kept[slot][3], SWAP)
+        else:
+            outs = kept[slot - 1]
+            if slot == chunks - 1:
+                kernel = functools.partial(place_late_kernel, slot - 1)
+                *outs, token = settle_rows(kernel, half, (grads["late"],), outs[:3], 3, half // 2, chain)
+                then(token)
+            kernel = functools.partial(place_last_kernel, slot)
+            *kept[slot], token = settle_rows(kernel, half, grads[slot], outs, 3, rows, chain)
+        then(token)
+
+    trade(0, rows_of(0))
+    bring(0)
+    cross(-1)
+    trade(rows_of(0), half)
     bring(1)
     both = lax.all_gather(jnp.stack([query_gain, key_gain]), "dp", axis=1, tiled=True)
     gains = [jnp.tile(both[t], (cycle // heads, 1)) for t in range(2)]
+    cross(0)
+    bring(2)
     for slot in range(chunks + 1):
-        if slot < chunks:
-            pass_on(slot)
-        if slot + 2 < chunks:
-            bring(slot + 2)
+        if slot + 1 < chunks:
+            cross(slot + 1)
+        if slot + 3 < chunks:
+            bring(slot + 3)
         work(slot)
-        give(slot)
+        if slot >= 1:
+            settle_slot(slot - 1)
+    for slot in range(chunks + 1 - 1, chunks + 1):
+        settle_slot(slot)
 
     totals = jnp.stack([functools.reduce(jnp.add, [s[t] for s in sums]) for t in range(2)])
     totals = sum_gains(totals)

time: 544 us -> 435 us (0.80)
  waiting for transfers between devices: 274 us -> 151 us
  Pallas kernels: 58.5 us -> 76.9 us
    ppermute x36 -> x44, waiting for transfers between devices: 274 us -> 151 us  [send(): return lax.ppermute(array, 'seq', pairs)]
    pallas_call x35 -> x46, Pallas kernels: 58.5 us -> 76.9 us  [call(): pl.pallas_call(trimmed, in_specs=list(in_specs) + [ANY] * extra, compiler...]
    unnamed x103 -> x167, local copies, waits for them, and re-layouts: 23.8 us -> 25.4 us
    ppermute x36 -> x44, starting transfers between devices: 156 us -> 157 us  [send(): return lax.ppermute(array, 'seq', pairs)]
  transfers between devices with their start and end apart: 36 -> 44, of which waited for: 16 -> 14; matrix products, arithmetic and copies ran while one was open for 2% -> 1% of each run, Pallas kernels for 8% -> 13%
where the time goes in v6:
time: 435 us; the launch traced here: 432 us
  starting transfers between devices  157 us (36%)
  waiting for transfers between devices  151 us (35%)
  Pallas kernels  76.9 us (18%)
  local copies, waits for them, and re-layouts  27.3 us (6%)
  blocking collectives  16.5 us (4%)
    ppermute x44, starting transfers between devices, send(): return lax.ppermute(array, 'seq', pairs)  157 us
    ppermute x44, waiting for transfers between devices, send(): return lax.ppermute(array, 'seq', pairs)  151 us
    pallas_call x46, Pallas kernels, call(): pl.pallas_call(trimmed, in_specs=list(in_specs) + [ANY] * extra, compiler...  76.9 us
    unnamed x167, local copies, waits for them, and re-layouts  25.4 us
  transfers between devices with their start and end apart: 44, of which 14 were waited for; matrix products, arithmetic and copies ran while one was open for 1% of the time, Pallas kernels for 13%

profile of v6, /device:TPU:0, one launch (start us, length us, event | category | flops | bytes accessed | tf_op | source)
XLA Modules:
  0.0 432.0 jit_solution(12761122240897623034)
XLA Ops:
  8.5 6.9 %other_half.3.refs_5_ = bf16[4,4352,128]{2,1,0:T(8,128)(2,1)} custom-call(bf16[2,5120,128]{2,1,0:T(8,128)(2,1)} %bitcast.17, bf16[2,5120,128]{2,1,0:T(8,128)(2,1)} %bitcast.27, bf16[2,5120,128]{2,1,0:T(8,128)(2,1)} %bitcast.37, bf16[2,5120,128]{2,1,0:T(8,128)(2,1)} %bitcast.47, bf16[3072,128]{1,0:T(8,128)(2,1)} %forward_rows.9.refs_4_), custom_call_target="tpu_custom_call" | custom-call | bytes 8912896 | tf_op jit(solution)/shard_map/other_half/pallas_call | solution.py:44
  15.7 7.7 %collective-permute-start.3 = (bf16[8,768,128]{2,1,0:T(8,128)(2,1)S(1)}, bf16[8,768,128]{2,1,0:T(8,128)(2,1)}, u32[]{:S(2)}, u32[]{:S(2)}) collective-permute-start(bf16[8,768,128]{2,1,0:T(8,128)(2,1)S(1)} %copy-done.1), channel_id=1, source_target_pairs={{0,2},{1,3},{6,4},{7,5},{8,10},{9,11},{14,12},{15,13},{16,18},{17,... | collective-permute-start | bytes 4718600 | tf_op jit(solution)/shard_map/ppermute | solution.py:610
  29.5 5.0 %collective-permute-start.2 = (bf16[8,768,128]{2,1,0:T(8,128)(2,1)}, bf16[8,768,128]{2,1,0:T(8,128)(2,1)S(1)}, u32[]{:S(2)}, u32[]{:S(2)}) collective-permute-start(bf16[8,768,128]{2,1,0:T(8,128)(2,1)} %pack_rows.9.refs_1_.refs_2_.refs_0_), channel_id=1, source_target_pairs={{0,2},{1,3},{6,4},{7,5},{8,10},{9,11},{14,12},{15,13},{16,18},{17,... | collective-permute-start | bytes 4718600 | tf_op jit(solution)/shard_map/ppermute | solution.py:610
  34.5 22.5 %collective-permute-done.3.refs_0_.refs_1_ = bf16[8,768,128]{2,1,0:T(8,128)(2,1)} collective-permute-done((bf16[8,768,128]{2,1,0:T(8,128)(2,1)S(1)}, bf16[8,768,128]{2,1,0:T(8,128)(2,1)}, u32[]{:S(2)}, u32[]{:S(2)}) %collective-permute-start.3) | collective-permute-done | bytes 1572896 | tf_op jit(solution)/shard_map/ppermute | solution.py:610
  60.1 11.2 %collective-permute-start.6 = (bf16[8,768,128]{2,1,0:T(8,128)(2,1)}, bf16[8,768,128]{2,1,0:T(8,128)(2,1)S(1)}, u32[]{:S(2)}, u32[]{:S(2)}) collective-permute-start(bf16[8,768,128]{2,1,0:T(8,128)(2,1)} %pack_rows.10.refs_1_.refs_2_.refs_0_), channel_id=1, source_target_pairs={{0,2},{1,3},{6,4},{7,5},{8,10},{9,11},{14,12},{15,13},{16,18},{17,... | collective-permute-start | bytes 4718600 | tf_op jit(solution)/shard_map/ppermute | solution.py:610
  71.3 19.4 %collective-permute-done.2.refs_0_.refs_1_ = bf16[8,768,128]{2,1,0:T(8,128)(2,1)S(1)} collective-permute-done((bf16[8,768,128]{2,1,0:T(8,128)(2,1)}, bf16[8,768,128]{2,1,0:T(8,128)(2,1)S(1)}, u32[]{:S(2)}, u32[]{:S(2)}) %collective-permute-start.2) | collective-permute-done | bytes 1572896 | tf_op jit(solution)/shard_map/ppermute | solution.py:610
  92.8 2.4 pack_rows.11.refs_6_.refs_1_.refs_0_
  95.3 10.8 %collective-permute-start.5 = (bf16[8,768,128]{2,1,0:T(8,128)(2,1)}, bf16[8,768,128]{2,1,0:T(8,128)(2,1)S(1)}, u32[]{:S(2)}, u32[]{:S(2)}) collective-permute-start(bf16[8,768,128]{2,1,0:T(8,128)(2,1)} %pack_rows.11.refs_6_.refs_1_.refs_0_), channel_id=1, source_target_pairs={{0,2},{1,3},{6,4},{7,5},{8,10},{9,11},{14,12},{15,13},{16,18},{17,... | collective-permute-start | bytes 4718600 | tf_op jit(solution)/shard_map/ppermute | solution.py:610
  106.1 8.2 %all_gather.3 = f32[2,40,128]{2,0,1:T(2,128)S(1)} all-gather(f32[2,10,128]{2,0,1:T(2,128)S(1)} %pad_maximum_fusion.1), channel_id=1, replica_groups=mesh['dp'=4,'seq'=8] {'dp'}, dimensions={1}, use_global_device_ids=true | all-gather | bytes 51200 | tf_op jit(solution)/shard_map/all_gather | solution.py:710
  118.8 5.6 %collective-permute-done.6.refs_0_.refs_1_ = bf16[8,768,128]{2,1,0:T(8,128)(2,1)S(1)} collective-permute-done((bf16[8,768,128]{2,1,0:T(8,128)(2,1)}, bf16[8,768,128]{2,1,0:T(8,128)(2,1)S(1)}, u32[]{:S(2)}, u32[]{:S(2)}) %collective-permute-start.6) | collective-permute-done | bytes 1572896 | tf_op jit(solution)/shard_map/ppermute | solution.py:610
  128.8 19.6 %collective-permute-start.13 = (bf16[8,768,128]{2,1,0:T(8,128)(2,1)}, bf16[8,768,128]{2,1,0:T(8,128)(2,1)}, u32[]{:S(2)}, u32[]{:S(2)}) collective-permute-start(bf16[8,768,128]{2,1,0:T(8,128)(2,1)} %pack_rows.12.refs_6_.refs_1_.refs_0_), channel_id=1, source_target_pairs={{0,2},{1,3},{6,4},{7,5},{8,10},{9,11},{14,12},{15,13},{16,18},{17,... | collective-permute-start | bytes 4718600 | tf_op jit(solution)/shard_map/ppermute | solution.py:610
  153.8 4.4 %collective-permute-done.5.refs_0_.refs_1_ = bf16[8,768,128]{2,1,0:T(8,128)(2,1)S(1)} collective-permute-done((bf16[8,768,128]{2,1,0:T(8,128)(2,1)}, bf16[8,768,128]{2,1,0:T(8,128)(2,1)S(1)}, u32[]{:S(2)}, u32[]{:S(2)}) %collective-permute-start.5) | collective-permute-done | bytes 1572896 | tf_op jit(solution)/shard_map/ppermute | solution.py:610
  166.6 21.4 %collective-permute-done.14.refs_2_ = bf16[6,768,128]{2,1,0:T(8,128)(2,1)S(1)} collective-permute-done((bf16[6,768,128]{2,1,0:T(8,128)(2,1)}, bf16[6,768,128]{2,1,0:T(8,128)(2,1)S(1)}, u32[]{:S(2)}, u32[]{:S(2)}) %collective-permute-start.14) | collective-permute-done | bytes 1179680 | tf_op jit(solution)/shard_map/ppermute | solution.py:610
  189.0 4.2 place_rows.11
  194.5 33.3 %collective-permute-start.12 = (bf16[8,512,128]{2,1,0:T(8,128)(2,1)S(1)}, bf16[8,512,128]{2,1,0:T(8,128)(2,1)S(1)}, u32[]{:S(2)}, u32[]{:S(2)}) collective-permute-start(bf16[8,512,128]{2,1,0:T(8,128)(2,1)S(1)} %copy-done.2), channel_id=1, source_target_pairs={{0,2},{1,3},{6,4},{7,5},{8,10},{9,11},{14,12},{15,13},{16,18},{17,... | collective-permute-start | bytes 3145736 | tf_op jit(solution)/shard_map/ppermute | solution.py:610
  233.7 15.6 %collective-permute-start.21 = (bf16[8,512,128]{2,1,0:T(8,128)(2,1)S(1)}, bf16[8,512,128]{2,1,0:T(8,128)(2,1)S(1)}, u32[]{:S(2)}, u32[]{:S(2)}) collective-permute-start(bf16[8,512,128]{2,1,0:T(8,128)(2,1)S(1)} %copy-done.3), channel_id=1, source_target_pairs={{0,2},{1,3},{6,4},{7,5},{8,10},{9,11},{14,12},{15,13},{16,18},{17,... | collective-permute-start | bytes 3145736 | tf_op jit(solution)/shard_map/ppermute | solution.py:610
  250.4 4.2 place_rows.12
  262.3 6.8 %collective-permute-done.22.refs_2_ = bf16[6,768,128]{2,1,0:T(8,128)(2,1)} collective-permute-done((bf16[6,768,128]{2,1,0:T(8,128)(2,1)}, bf16[6,768,128]{2,1,0:T(8,128)(2,1)}, u32[]{:S(2)}, u32[]{:S(2)}) %collective-permute-start.22) | collective-permute-done | bytes 1179680 | tf_op jit(solution)/shard_map/ppermute | solution.py:610
  269.1 4.2 place_rows.13
  275.0 23.5 %collective-permute-start.20 = (bf16[8,256,128]{2,1,0:T(8,128)(2,1)S(1)}, bf16[8,256,128]{2,1,0:T(8,128)(2,1)S(1)}, u32[]{:S(2)}, u32[]{:S(2)}) collective-permute-start(bf16[8,256,128]{2,1,0:T(8,128)(2,1)S(1)} %copy-done.13), channel_id=1, source_target_pairs={{0,2},{1,3},{6,4},{7,5},{8,10},{9,11},{14,12},{15,13},{16,18},{17,... | collective-permute-start | bytes 1572872 | tf_op jit(solution)/shard_map/ppermute | solution.py:610
  305.1 4.2 place_rows.14
  314.9 24.3 %collective-permute-done.30.refs_2_ = bf16[6,768,128]{2,1,0:T(8,128)(2,1)S(1)} collective-permute-done((bf16[6,768,128]{2,1,0:T(8,128)(2,1)}, bf16[6,768,128]{2,1,0:T(8,128)(2,1)S(1)}, u32[]{:S(2)}, u32[]{:S(2)}) %collective-permute-start.30) | collective-permute-done | bytes 1179680 | tf_op jit(solution)/shard_map/ppermute | solution.py:610
  340.3 4.2 place_rows.15
  347.1 6.0 %collective-permute-done.32.refs_2_ = bf16[6,512,128]{2,1,0:T(8,128)(2,1)S(1)} collective-permute-done((bf16[6,512,128]{2,1,0:T(8,128)(2,1)}, bf16[6,512,128]{2,1,0:T(8,128)(2,1)S(1)}, u32[]{:S(2)}, u32[]{:S(2)}) %collective-permute-start.32) | collective-permute-done | bytes 786464 | tf_op jit(solution)/shard_map/ppermute | solution.py:610
  353.9 4.0 place_rows.16
  362.2 8.3 %all_to_all.5 = f32[2,4,10,128]{3,0,2,1:T(2,128)S(1)} all-to-all(f32[2,4,10,128]{3,0,2,1:T(2,128)S(1)} %copy.71), channel_id=1, replica_groups=mesh['dp'=4,'seq'=8] {'dp'}, dimensions={1} | all-to-all | bytes 81920 | tf_op jit(solution)/shard_map/all_to_all | solution.py:617
  376.6 24.8 %collective-permute-done.43 = f32[2,10,128]{2,0,1:T(2,128)S(1)} collective-permute-done((f32[2,10,128]{2,0,1:T(2,128)S(1)}, f32[2,10,128]{2,0,1:T(2,128)S(1)}, u32[]{:S(2)}, u32[]{:S(2)}) %collective-permute-start.43) | collective-permute-done | bytes 10272 | tf_op jit(solution)/shard_map/ppermute | solution.py:610
  404.7 6.7 %place_rows.17 = (bf16[2,5120,128]{2,1,0:T(8,128)(2,1)}, bf16[2,5120,128]{2,1,0:T(8,128)(2,1)}, bf16[2,5120,128]{2,1,0:T(8,128)(2,1)}, f32[8,128]{1,0:T(8,128)}) custom-call(bf16[3,5120,128]{2,1,0:T(8,128)(2,1)} %collective-permute-done.40.refs_0_, ...), custom_call_target="tpu_custom_call", output_to_operand_aliasing={{0}: (1, {}), {1}: (2, {}), {2}: (3, {})} | custom-call | bytes 7864320 | tf_op jit(solution)/shard_map/place_rows/pallas_call | solution.py:44
  411.4 7.7 %collective-permute-done.39.refs_3_ = bf16[3,512,128]{2,1,0:T(8,128)(2,1)S(1)} collective-permute-done((bf16[3,512,128]{2,1,0:T(8,128)(2,1)S(1)}, bf16[3,512,128]{2,1,0:T(8,128)(2,1)S(1)}, u32[]{:S(2)}, u32[]{:S(2)}) %collective-permute-start.39) | collective-permute-done | bytes 393248 | tf_op jit(solution)/shard_map/ppermute | solution.py:610
  419.9 4.0 place_rows.18
  423.9 3.7 collective-permute-done.36.refs_3_
  428.2 3.7 place_rows.19
  (288 shorter events, 91.7 us)
Async XLA Ops:
  15.7 41.2 %collective-permute-start.3 = (bf16[8,768,128]{2,1,0:T(8,128)(2,1)S(1)}, bf16[8,768,128]{2,1,0:T(8,128)(2,1)}, u32[]{:S(2)}, u32[]{:S(2)}) collective-permute-start(bf16[8,768,128]{2,1,0:T(8,128)(2,1)S(1)} %copy-done.1), channel_id=1, source_target_pairs={{0,2},{1,3},{6,4},{7,5},{8,10},{9,11},{14,12},{15,13},{16,18},{17,... | collective-permute-start | bytes 4718600 | tf_op jit(solution)/shard_map/ppermute | solution.py:610
  29.5 61.3 %collective-permute-start.2 = (bf16[8,768,128]{2,1,0:T(8,128)(2,1)}, bf16[8,768,128]{2,1,0:T(8,128)(2,1)S(1)}, u32[]{:S(2)}, u32[]{:S(2)}) collective-permute-start(bf16[8,768,128]{2,1,0:T(8,128)(2,1)} %pack_rows.9.refs_1_.refs_2_.refs_0_), channel_id=1, source_target_pairs={{0,2},{1,3},{6,4},{7,5},{8,10},{9,11},{14,12},{15,13},{16,18},{17,... | collective-permute-start | bytes 4718600 | tf_op jit(solution)/shard_map/ppermute | solution.py:610
  56.9 57.4 %collective-permute-start.7 = (bf16[6144,128]{1,0:T(8,128)(2,1)}, bf16[6144,128]{1,0:T(8,128)(2,1)S(1)}, u32[]{:S(2)}, u32[]{:S(2)}) collective-permute-start(bf16[6144,128]{1,0:T(8,128)(2,1)} %forward_rows.10.refs_5_), channel_id=1, source_target_pairs={{2,4},{3,5},{4,2},{5,3},{10,12},{11,13},{12,10},{13,11},{18,20},{1... | collective-permute-start | bytes 4718600 | tf_op jit(solution)/shard_map/ppermute | solution.py:610
  60.1 64.3 %collective-permute-start.6 = (bf16[8,768,128]{2,1,0:T(8,128)(2,1)}, bf16[8,768,128]{2,1,0:T(8,128)(2,1)S(1)}, u32[]{:S(2)}, u32[]{:S(2)}) collective-permute-start(bf16[8,768,128]{2,1,0:T(8,128)(2,1)} %pack_rows.10.refs_1_.refs_2_.refs_0_), channel_id=1, source_target_pairs={{0,2},{1,3},{6,4},{7,5},{8,10},{9,11},{14,12},{15,13},{16,18},{17,... | collective-permute-start | bytes 4718600 | tf_op jit(solution)/shard_map/ppermute | solution.py:610
  92.0 56.4 %collective-permute-start.10 = (bf16[6144,128]{1,0:T(8,128)(2,1)}, bf16[6144,128]{1,0:T(8,128)(2,1)S(1)}, u32[]{:S(2)}, u32[]{:S(2)}) collective-permute-start(bf16[6144,128]{1,0:T(8,128)(2,1)} %forward_rows.11.refs_5_), channel_id=1, source_target_pairs={{2,4},{3,5},{4,2},{5,3},{10,12},{11,13},{12,10},{13,11},{18,20},{1... | collective-permute-start | bytes 4718600 | tf_op jit(solution)/shard_map/ppermute | solution.py:610
  95.3 62.9 %collective-permute-start.5 = (bf16[8,768,128]{2,1,0:T(8,128)(2,1)}, bf16[8,768,128]{2,1,0:T(8,128)(2,1)S(1)}, u32[]{:S(2)}, u32[]{:S(2)}) collective-permute-start(bf16[8,768,128]{2,1,0:T(8,128)(2,1)} %pack_rows.11.refs_6_.refs_1_.refs_0_), channel_id=1, source_target_pairs={{0,2},{1,3},{6,4},{7,5},{8,10},{9,11},{14,12},{15,13},{16,18},{17,... | collective-permute-start | bytes 4718600 | tf_op jit(solution)/shard_map/ppermute | solution.py:610
  116.9 35.2 %collective-permute-start.9 = (bf16[6,768,128]{2,1,0:T(8,128)(2,1)}, bf16[6,768,128]{2,1,0:T(8,128)(2,1)S(1)}, u32[]{:S(2)}, u32[]{:S(2)}) collective-permute-start(bf16[6,768,128]{2,1,0:T(8,128)(2,1)} %get-tuple-element.150), channel_id=1, source_target_pairs={{2,0},{3,1},{4,6},{5,7},{10,8},{11,9},{12,14},{13,15},{18,16},{19,... | collective-permute-start | bytes 3538952 | tf_op jit(solution)/shard_map/ppermute | solution.py:610
  125.7 36.5 %collective-permute-start.15 = (bf16[6144,128]{1,0:T(8,128)(2,1)}, bf16[6144,128]{1,0:T(8,128)(2,1)S(1)}, u32[]{:S(2)}, u32[]{:S(2)}) collective-permute-start(bf16[6144,128]{1,0:T(8,128)(2,1)} %forward_rows.12.refs_5_), channel_id=1, source_target_pairs={{2,4},{3,5},{4,2},{5,3},{10,12},{11,13},{12,10},{13,11},{18,20},{1... | collective-permute-start | bytes 4718600 | tf_op jit(solution)/shard_map/ppermute | solution.py:610
  128.8 64.3 %collective-permute-start.13 = (bf16[8,768,128]{2,1,0:T(8,128)(2,1)}, bf16[8,768,128]{2,1,0:T(8,128)(2,1)}, u32[]{:S(2)}, u32[]{:S(2)}) collective-permute-start(bf16[8,768,128]{2,1,0:T(8,128)(2,1)} %pack_rows.12.refs_6_.refs_1_.refs_0_), channel_id=1, source_target_pairs={{0,2},{1,3},{6,4},{7,5},{8,10},{9,11},{14,12},{15,13},{16,18},{17,... | collective-permute-start | bytes 4718600 | tf_op jit(solution)/shard_map/ppermute | solution.py:610
  150.8 37.1 %collective-permute-start.14 = (bf16[6,768,128]{2,1,0:T(8,128)(2,1)}, bf16[6,768,128]{2,1,0:T(8,128)(2,1)S(1)}, u32[]{:S(2)}, u32[]{:S(2)}) collective-permute-start(bf16[6,768,128]{2,1,0:T(8,128)(2,1)} %get-tuple-element.160), channel_id=1, source_target_pairs={{2,0},{3,1},{4,6},{5,7},{10,8},{11,9},{12,14},{13,15},{18,16},{19,... | collective-permute-start | bytes 3538952 | tf_op jit(solution)/shard_map/ppermute | solution.py:610
  159.4 70.6 %collective-permute-start.18 = (bf16[6144,128]{1,0:T(8,128)(2,1)}, bf16[6144,128]{1,0:T(8,128)(2,1)S(1)}, u32[]{:S(2)}, u32[]{:S(2)}) collective-permute-start(bf16[6144,128]{1,0:T(8,128)(2,1)} %forward_rows.13.refs_5_), channel_id=1, source_target_pairs={{2,4},{3,5},{4,2},{5,3},{10,12},{11,13},{12,10},{13,11},{18,20},{1... | collective-permute-start | bytes 4718600 | tf_op jit(solution)/shard_map/ppermute | solution.py:610
  164.6 84.7 %collective-permute-start.17 = (bf16[6,768,128]{2,1,0:T(8,128)(2,1)}, bf16[6,768,128]{2,1,0:T(8,128)(2,1)S(1)}, u32[]{:S(2)}, u32[]{:S(2)}) collective-permute-start(bf16[6,768,128]{2,1,0:T(8,128)(2,1)} %get-tuple-element.174), channel_id=1, source_target_pairs={{2,0},{3,1},{4,6},{5,7},{10,8},{11,9},{12,14},{13,15},{18,16},{19,... | collective-permute-start | bytes 3538952 | tf_op jit(solution)/shard_map/ppermute | solution.py:610
  165.9 27.2 %collective-permute-start.16 = (bf16[192,128]{1,0:T(8,128)(2,1)S(1)}, bf16[192,128]{1,0:T(8,128)(2,1)S(1)}, u32[]{:S(2)}, u32[]{:S(2)}) collective-permute-start(bf16[192,128]{1,0:T(8,128)(2,1)S(1)} %copy-done.77), channel_id=1, source_target_pairs={{4,2},{5,3},{12,10},{13,11},{20,18},{21,19},{28,26},{29,27}} | collective-permute-start | bytes 147464 | tf_op jit(solution)/shard_map/ppermute | solution.py:610
  193.8 64.3 %collective-permute-start.23 = (bf16[5120,128]{1,0:T(8,128)(2,1)}, bf16[5120,128]{1,0:T(8,128)(2,1)S(1)}, u32[]{:S(2)}, u32[]{:S(2)}) collective-permute-start(bf16[5120,128]{1,0:T(8,128)(2,1)} %forward_rows.14.refs_5_), channel_id=1, source_target_pairs={{2,4},{3,5},{4,2},{5,3},{10,12},{11,13},{12,10},{13,11},{18,20},{1... | collective-permute-start | bytes 3932168 | tf_op jit(solution)/shard_map/ppermute | solution.py:610
  194.5 60.0 %collective-permute-start.12 = (bf16[8,512,128]{2,1,0:T(8,128)(2,1)S(1)}, bf16[8,512,128]{2,1,0:T(8,128)(2,1)S(1)}, u32[]{:S(2)}, u32[]{:S(2)}) collective-permute-start(bf16[8,512,128]{2,1,0:T(8,128)(2,1)S(1)} %copy-done.2), channel_id=1, source_target_pairs={{0,2},{1,3},{6,4},{7,5},{8,10},{9,11},{14,12},{15,13},{16,18},{17,... | collective-permute-start | bytes 3145736 | tf_op jit(solution)/shard_map/ppermute | solution.py:610
  232.4 36.7 %collective-permute-start.22 = (bf16[6,768,128]{2,1,0:T(8,128)(2,1)}, bf16[6,768,128]{2,1,0:T(8,128)(2,1)}, u32[]{:S(2)}, u32[]{:S(2)}) collective-permute-start(bf16[6,768,128]{2,1,0:T(8,128)(2,1)} %get-tuple-element.188), channel_id=1, source_target_pairs={{2,0},{3,1},{4,6},{5,7},{10,8},{11,9},{12,14},{13,15},{18,16},{19,... | collective-permute-start | bytes 3538952 | tf_op jit(solution)/shard_map/ppermute | solution.py:610
  233.7 39.6 %collective-permute-start.21 = (bf16[8,512,128]{2,1,0:T(8,128)(2,1)S(1)}, bf16[8,512,128]{2,1,0:T(8,128)(2,1)S(1)}, u32[]{:S(2)}, u32[]{:S(2)}) collective-permute-start(bf16[8,512,128]{2,1,0:T(8,128)(2,1)S(1)} %copy-done.3), channel_id=1, source_target_pairs={{0,2},{1,3},{6,4},{7,5},{8,10},{9,11},{14,12},{15,13},{16,18},{17,... | collective-permute-start | bytes 3145736 | tf_op jit(solution)/shard_map/ppermute | solution.py:610
  255.5 43.0 %collective-permute-start.27 = (bf16[4096,128]{1,0:T(8,128)(2,1)}, bf16[4096,128]{1,0:T(8,128)(2,1)S(1)}, u32[]{:S(2)}, u32[]{:S(2)}) collective-permute-start(bf16[4096,128]{1,0:T(8,128)(2,1)} %forward_rows.15.refs_5_), channel_id=1, source_target_pairs={{2,4},{3,5},{4,2},{5,3},{10,12},{11,13},{12,10},{13,11},{18,20},{1... | collective-permute-start | bytes 3145736 | tf_op jit(solution)/shard_map/ppermute | solution.py:610
  260.3 43.7 %collective-permute-start.26 = (bf16[6,768,128]{2,1,0:T(8,128)(2,1)}, bf16[6,768,128]{2,1,0:T(8,128)(2,1)S(1)}, u32[]{:S(2)}, u32[]{:S(2)}) collective-permute-start(bf16[6,768,128]{2,1,0:T(8,128)(2,1)} %get-tuple-element.202), channel_id=1, source_target_pairs={{2,0},{3,1},{4,6},{5,7},{10,8},{11,9},{12,14},{13,15},{18,16},{19,... | collective-permute-start | bytes 3538952 | tf_op jit(solution)/shard_map/ppermute | solution.py:610
  274.3 35.7 %collective-permute-start.25 = (bf16[3072,128]{1,0:T(8,128)(2,1)}, bf16[3072,128]{1,0:T(8,128)(2,1)S(1)}, u32[]{:S(2)}, u32[]{:S(2)}) collective-permute-start(bf16[3072,128]{1,0:T(8,128)(2,1)} %forward_rows.16.refs_6_), channel_id=1, source_target_pairs={{2,4},{3,5},{4,2},{5,3},{10,12},{11,13},{12,10},{13,11},{18,20},{1... | collective-permute-start | bytes 2359304 | tf_op jit(solution)/shard_map/ppermute | solution.py:610
  275.0 34.2 %collective-permute-start.20 = (bf16[8,256,128]{2,1,0:T(8,128)(2,1)S(1)}, bf16[8,256,128]{2,1,0:T(8,128)(2,1)S(1)}, u32[]{:S(2)}, u32[]{:S(2)}) collective-permute-start(bf16[8,256,128]{2,1,0:T(8,128)(2,1)S(1)} %copy-done.13), channel_id=1, source_target_pairs={{0,2},{1,3},{6,4},{7,5},{8,10},{9,11},{14,12},{15,13},{16,18},{17,... | collective-permute-start | bytes 1572872 | tf_op jit(solution)/shard_map/ppermute | solution.py:610
  300.8 38.5 %collective-permute-start.30 = (bf16[6,768,128]{2,1,0:T(8,128)(2,1)}, bf16[6,768,128]{2,1,0:T(8,128)(2,1)S(1)}, u32[]{:S(2)}, u32[]{:S(2)}) collective-permute-start(bf16[6,768,128]{2,1,0:T(8,128)(2,1)} %get-tuple-element.216), channel_id=1, source_target_pairs={{2,0},{3,1},{4,6},{5,7},{10,8},{11,9},{12,14},{13,15},{18,16},{19,... | collective-permute-start | bytes 3538952 | tf_op jit(solution)/shard_map/ppermute | solution.py:610
  312.3 40.8 %collective-permute-start.32 = (bf16[6,512,128]{2,1,0:T(8,128)(2,1)}, bf16[6,512,128]{2,1,0:T(8,128)(2,1)S(1)}, u32[]{:S(2)}, u32[]{:S(2)}) collective-permute-start(bf16[6,512,128]{2,1,0:T(8,128)(2,1)} %get-tuple-element.230), channel_id=1, source_target_pairs={{2,0},{3,1},{4,6},{5,7},{10,8},{11,9},{12,14},{13,15},{18,16},{19,... | collective-permute-start | bytes 2359304 | tf_op jit(solution)/shard_map/ppermute | solution.py:610
  313.6 30.9 %collective-permute-start.29 = (bf16[1024,128]{1,0:T(8,128)(2,1)S(1)}, bf16[1024,128]{1,0:T(8,128)(2,1)S(1)}, u32[]{:S(2)}, u32[]{:S(2)}) collective-permute-start(bf16[1024,128]{1,0:T(8,128)(2,1)S(1)} %copy-done.24), channel_id=1, source_target_pairs={{2,4},{3,5},{4,2},{5,3},{10,12},{11,13},{12,10},{13,11},{18,20},{1... | collective-permute-start | bytes 786440 | tf_op jit(solution)/shard_map/ppermute | solution.py:610
  314.3 31.6 %collective-permute-start.33 = (bf16[128,128]{1,0:T(8,128)(2,1)S(1)}, bf16[128,128]{1,0:T(8,128)(2,1)S(1)}, u32[]{:S(2)}, u32[]{:S(2)}) collective-permute-start(bf16[128,128]{1,0:T(8,128)(2,1)S(1)} %copy-done.80), channel_id=1, source_target_pairs={{4,2},{5,3},{12,10},{13,11},{20,18},{21,19},{28,26},{29,27}} | collective-permute-start | bytes 98312 | tf_op jit(solution)/shard_map/ppermute | solution.py:610
  358.2 44.5 %collective-permute-start.40 = (bf16[3,5120,128]{2,1,0:T(8,128)(2,1)}, bf16[3,5120,128]{2,1,0:T(8,128)(2,1)}, u32[]{:S(2)}, u32[]{:S(2)}) collective-permute-start(bf16[3,5120,128]{2,1,0:T(8,128)(2,1)} %get-tuple-element.255), channel_id=1, source_target_pairs={{0,1},{1,0},{2,3},{3,2},{4,5},{5,4},{6,7},{7,6},{8,9},{9,8},{10,11... | collective-permute-start | bytes 11796488 | tf_op jit(solution)/shard_map/ppermute | solution.py:610
  372.4 29.0 %collective-permute-start.43 = (f32[2,10,128]{2,0,1:T(2,128)S(1)}, f32[2,10,128]{2,0,1:T(2,128)S(1)}, u32[]{:S(2)}, u32[]{:S(2)}) collective-permute-start(f32[2,10,128]{2,0,1:T(2,128)S(1)} %add.128), channel_id=1, source_target_pairs={{2,0},{3,1},{4,6},{5,7},{10,8},{11,9},{12,14},{13,15},{18,16},{19,... | collective-permute-start | bytes 30728 | tf_op jit(solution)/shard_map/ppermute | solution.py:610
  373.7 27.7 %collective-permute-start.37 = (bf16[3,512,128]{2,1,0:T(8,128)(2,1)S(1)}, bf16[3,512,128]{2,1,0:T(8,128)(2,1)S(1)}, u32[]{:S(2)}, u32[]{:S(2)}) collective-permute-start(bf16[3,512,128]{2,1,0:T(8,128)(2,1)S(1)} %copy-done.30), channel_id=1, source_target_pairs={{0,1},{1,0},{2,3},{3,2},{4,5},{5,4},{6,7},{7,6},{8,9},{9,8},{10,11... | collective-permute-start | bytes 1179656 | tf_op jit(solution)/shard_map/ppermute | solution.py:610
  374.0 37.4 %collective-permute-start.38 = (bf16[3,512,128]{2,1,0:T(8,128)(2,1)S(1)}, bf16[3,512,128]{2,1,0:T(8,128)(2,1)S(1)}, u32[]{:S(2)}, u32[]{:S(2)}) collective-permute-start(bf16[3,512,128]{2,1,0:T(8,128)(2,1)S(1)} %copy-done.31), channel_id=1, source_target_pairs={{2,0},{3,1},{4,6},{5,7},{10,8},{11,9},{12,14},{13,15},{18,16},{19,... | collective-permute-start | bytes 1179656 | tf_op jit(solution)/shard_map/ppermute | solution.py:610
  375.3 43.8 %collective-permute-start.39 = (bf16[3,512,128]{2,1,0:T(8,128)(2,1)S(1)}, bf16[3,512,128]{2,1,0:T(8,128)(2,1)S(1)}, u32[]{:S(2)}, u32[]{:S(2)}) collective-permute-start(bf16[3,512,128]{2,1,0:T(8,128)(2,1)S(1)} %copy-done.32), channel_id=1, source_target_pairs={{2,1},{3,0},{4,7},{5,6},{10,9},{11,8},{12,15},{13,14},{18,17},{19,... | collective-permute-start | bytes 1179656 | tf_op jit(solution)/shard_map/ppermute | solution.py:610
  401.4 22.5 %collective-permute-start.34 = (bf16[3,256,128]{2,1,0:T(8,128)(2,1)}, bf16[3,256,128]{2,1,0:T(8,128)(2,1)S(1)}, u32[]{:S(2)}, u32[]{:S(2)}) collective-permute-start(bf16[3,256,128]{2,1,0:T(8,128)(2,1)} %get-tuple-element.248), channel_id=1, source_target_pairs={{0,1},{1,0},{2,3},{3,2},{4,5},{5,4},{6,7},{7,6},{8,9},{9,8},{10,11... | collective-permute-start | bytes 589832 | tf_op jit(solution)/shard_map/ppermute | solution.py:610
  402.7 24.8 %collective-permute-start.36 = (bf16[3,256,128]{2,1,0:T(8,128)(2,1)}, bf16[3,256,128]{2,1,0:T(8,128)(2,1)S(1)}, u32[]{:S(2)}, u32[]{:S(2)}) collective-permute-start(bf16[3,256,128]{2,1,0:T(8,128)(2,1)} %get-tuple-element.250), channel_id=1, source_target_pairs={{2,1},{3,0},{4,7},{5,6},{10,9},{11,8},{12,15},{13,14},{18,17},{19,... | collective-permute-start | bytes 589832 | tf_op jit(solution)/shard_map/ppermute | solution.py:610
  (95 other events, 383.3 us)

commit v7 on v6

--- a/solution.py
+++ b/solution.py
@@ -13,8 +13,10 @@
 GROUP = 16
 SLOTS = 4
 WIDE = GROUP * SLOTS
-TOGETHER = 64
-CUTS = (3, 3, 3, 3, 3, 2, 2, 1)
+TOGETHER = 128
+CUTS = (3, 3, 3, 3, 3, 3, 2)
+LAG = 2
+DIRECT = 2
 
 EDGE = ((0, 2), (1, 3), (6, 4), (7, 5))
 MIDDLE = ((2, 4), (3, 5), (4, 2), (5, 3))
@@ -57,8 +59,14 @@
     return CUTS[chunk] * BLOCK
 
 
+def chunk_of(slot, high):
+    chunk = slot if high else slot - LAG
+    return chunk if 0 <= chunk < len(CUTS) else None
+
+
 def out_rows(slot):
-    return max(CUTS[max(slot - 1, 0) : slot + 1]) * BLOCK
+    chunks = [chunk_of(slot, high) for high in (False, True)]
+    return max(rows_of(chunk) for chunk in chunks if chunk is not None)
 
 
 def copy_cost(rows, tensors):
@@ -160,6 +168,14 @@
     def _():
         start = 0
         for rows, src in zip(sizes, sources):
+            if len(src.shape) == 2:
+                pltpu.emit_pipeline(
+                    copy_all,
+                    grid=(1,),
+                    in_specs=[pl.BlockSpec((rows, 128), lambda i: (0, 0))],
+                    out_specs=[pl.BlockSpec((rows, 128), lambda i: (0, 0))],
+                )(src, out.at[pl.ds(start, rows)])
+                continue
             tile = tile_of(rows)
             pltpu.emit_pipeline(
                 move,
@@ -171,13 +187,14 @@
 
 
 def forward(sources, after):
-    sizes = [x.shape[1] for x in sources]
+    sizes = [x.shape[-2] for x in sources]
+    total = sum(n if x.ndim == 2 else 4 * n for n, x in zip(sizes, sources))
     return call(
         functools.partial(forward_kernel, sizes),
         sources,
         [ANY] * len(sources),
         after,
-        out_shape=jax.ShapeDtypeStruct((4 * sum(sizes), 128), BF16),
+        out_shape=jax.ShapeDtypeStruct((total, 128), BF16),
         out_specs=ANY,
         cost_estimate=copy_cost(sum(sizes), 4),
         name="forward_rows",
@@ -196,8 +213,8 @@
 def by_chip(slot, run):
     chip, _ = place()
     for which in range(4):
-        chunk = slot if which >= 2 else slot - 1
-        if 0 <= chunk < len(CUTS):
+        chunk = chunk_of(slot, which >= 2)
+        if chunk is not None:
             pl.when(chip == which)(functools.partial(run, chunk, which in (1, 2)))
 
 
@@ -241,11 +258,11 @@
 
     @pl.when(chip < 2)
     def _():
-        run(first_of(slot))
+        run(first_of(slot - LAG + 1))
 
     @pl.when(chip >= 2)
     def _():
-        run(first_of(slot + 1))
+        run(first_of(min(slot + 1, len(CUTS))))
 
 
 def settle_rows(kernel, half, pieces, kept, count, rows, after=()):
@@ -461,7 +478,7 @@
         sum_k[...] = jnp.zeros_like(sum_k)
 
 
-def lower_kernel(chunk, skip, heads, own, edge, other, far, packed, gain_q, gain_k, *refs):
+def lower_kernel(chunk, skip, at, heads, own, edge, other, far, packed, gain_q, gain_k, *refs):
     outs, (sum_q, sum_k, acc_q, acc_k, mask) = refs[:-5], refs[-5:]
     outs = outs[len(outs) // 2 :]
     chip, core = place()
@@ -536,7 +553,7 @@
             *hub_refs(steps, skip, own, edge, other, far),
             gain_q,
             gain_k,
-            packed,
+            packed.at[pl.ds(at, steps * WIDE)],
             *grad_refs(outs),
         )
         sum_q[...] = sum_heads(acc_q, heads)
@@ -555,7 +572,7 @@
 
 
 def grad_shapes(slot):
-    sizes = (3, 3, 6) if slot < len(CUTS) - 1 else (3, 3, 3, 3)
+    sizes = (3, 3, 6) if slot < len(CUTS) + LAG - DIRECT else (3, 3, 3, 3)
     return [jax.ShapeDtypeStruct((n, out_rows(slot), 128), BF16) for n in sizes]
 
 
@@ -578,12 +595,12 @@
     )
 
 
-def lower(slot, heads, data, packed, skip, gains, outs, after):
-    chunk = slot - 1
+def lower(slot, heads, data, packed, at, skip, gains, outs, after):
+    chunk = slot - LAG
     cycle = gains[0].shape[0]
     shapes = grad_shapes(slot)
     return call(
-        functools.partial(lower_kernel, chunk, skip, heads),
+        functools.partial(lower_kernel, chunk, skip, at, heads),
         (*data, packed, *gains, *outs),
         [ANY] * (7 + len(outs)),
         after,
@@ -610,11 +627,24 @@
     return lax.ppermute(array, "seq", pairs)
 
 
-def sum_gains(part):
+def add_pieces(pieces, after):
+    def kernel(src, out):
+        total = src[:, 0]
+        for i in range(1, src.shape[1]):
+            total = total + src[:, i]
+        out[...] = total
+
+    shape = (pieces.shape[0], *pieces.shape[2:])
+    return call(
+        kernel, (pieces,), [VMEM], after, out_shape=jax.ShapeDtypeStruct(shape, F32), out_specs=VMEM, name="add_pieces"
+    )
+
+
+def sum_gains(part, after):
     count = lax.axis_size("dp")
     mine = part.shape[1] // count
     pieces = part.reshape(2, count, mine, part.shape[2])
-    total = jnp.sum(lax.all_to_all(pieces, "dp", split_axis=1, concat_axis=1, tiled=True), axis=1)
+    total = add_pieces(lax.all_to_all(pieces, "dp", split_axis=1, concat_axis=1, tiled=True), after)
     total = total + send(total, SWAP)
     total = total + send(total, MIDDLE)
     edge = send(total, BACK_S)
@@ -630,7 +660,8 @@
     cycle = math.lcm(BLOCK, heads)
     chunks = len(CUTS)
 
-    edges, grads, crossed, middle, traded = {}, {}, {}, {}, []
+    edges, grads, crossed, middle, packs, traded = {}, {}, {}, {}, {}, []
+    slots = chunks + LAG
     sums, kept, chain = [], {-1: None}, []
 
     def then(token):
@@ -642,7 +673,7 @@
         traded.append((send(rows, SWAP), low))
 
     def bring(chunk):
-        swapped, offset = traded[min(chunk, 1)]
+        swapped, offset = traded[min(chunk, 2)]
         rows = pack(chunk, offset, arrays, swapped, chain)
         then(rows)
         edges[chunk] = (rows, send(rows, EDGE))
@@ -651,10 +682,11 @@
         sources = [edges[chunk][1]] if chunk >= 0 else []
         if chunk + 1 < chunks:
             sources.append(edges[chunk + 1][0])
+        if chunk >= LAG:
+            sources.append(packs[chunk - LAG])
+            crossed[chunk - LAG] = (chunk, sum(4 * x.shape[1] for x in sources[:-1]))
         if chunk == 0:
             chain.append(middle[-1])
-        if chunk >= 2:
-            chain.append(crossed[chunk - 2])
         rows = forward(sources, chain)
         then(rows)
         middle[chunk] = send(rows, MIDDLE)
@@ -667,34 +699,41 @@
 
     def work(slot):
         if slot < chunks:
-            *parts, packed, sum_q, sum_k = upper(slot, skip_of(slot), heads, data_of(slot), gains, chain)
-            crossed[slot] = send(packed, DOWN)
+            *parts, packs[slot], sum_q, sum_k = upper(
+                slot, skip_of(slot), heads, data_of(slot), gains, chain
+            )
+            if slot >= chunks - LAG:
+                packs[slot] = send(packs[slot], DOWN)
             sums.append((sum_q, sum_k))
         else:
             parts = blank(slot, chain)
-        if slot > 0:
-            chunk = slot - 1
+        if slot >= LAG:
+            chunk = slot - LAG
+            packed, at = packs[chunk], 0
+            if chunk in crossed:
+                packed, at = middle[crossed[chunk][0]], crossed[chunk][1]
+            after = [sum_q] if slot < chunks else []
             *parts, sum_q, sum_k = lower(
-                slot, heads, data_of(chunk), crossed[chunk], skip_of(chunk), gains, parts, [sum_q] if slot < chunks else ()
+                slot, heads, data_of(chunk), packed, at, skip_of(chunk), gains, parts, after
             )
             sums.append((sum_q, sum_k))
         then(sum_q)
         own, other, *edge = parts
-        if slot < chunks - 1:
+        if slot < slots - DIRECT:
             grads[slot] = (own, other, send(edge[0], BACK_S))
         else:
             grads[slot] = (own, send(other, SWAP), send(edge[0], BACK_S), send(edge[1], BACK_X))
 
     def settle_slot(slot):
         rows = out_rows(slot)
-        if slot < chunks - 1:
+        if slot < slots - DIRECT:
             kernel = functools.partial(place_kernel, slot)
             *kept[slot], token = settle_rows(kernel, half, grads[slot], kept[slot - 1], 4, rows, chain)
-            if slot == chunks - 2:
+            if slot == slots - DIRECT - 1:
                 grads["late"] = send(kept[slot][3], SWAP)
         else:
             outs = kept[slot - 1]
-            if slot == chunks - 1:
+            if slot == slots - DIRECT:
                 kernel = functools.partial(place_late_kernel, slot - 1)
                 *outs, token = settle_rows(kernel, half, (grads["late"],), outs[:3], 3, half // 2, chain)
                 then(token)
@@ -704,14 +743,15 @@
 
     trade(0, rows_of(0))
     bring(0)
+    trade(rows_of(0), first_of(2))
     cross(-1)
-    trade(rows_of(0), half)
     bring(1)
     both = lax.all_gather(jnp.stack([query_gain, key_gain]), "dp", axis=1, tiled=True)
     gains = [jnp.tile(both[t], (cycle // heads, 1)) for t in range(2)]
     cross(0)
+    trade(first_of(2), half)
     bring(2)
-    for slot in range(chunks + 1):
+    for slot in range(slots):
         if slot + 1 < chunks:
             cross(slot + 1)
         if slot + 3 < chunks:
@@ -719,12 +759,12 @@
         work(slot)
         if slot >= 1:
             settle_slot(slot - 1)
-    for slot in range(chunks + 1 - 1, chunks + 1):
+    for slot in range(slots - 1, slots):
         settle_slot(slot)
 
     totals = jnp.stack([functools.reduce(jnp.add, [s[t] for s in sums]) for t in range(2)])
-    totals = sum_gains(totals)
-    return (*[x.reshape(shape) for x in kept[chunks]], totals[0], totals[1])
+    totals = sum_gains(totals, chain)
+    return (*[x.reshape(shape) for x in kept[slots - 1]], totals[0], totals[1])
 
 
 def wide_attention(query_norm, key_norm, value_in, grad_in):

time: 435 us -> 412 us (0.947)
  starting transfers between devices: 157 us -> 103 us
  waiting for transfers between devices: 151 us -> 188 us
  Pallas kernels: 76.9 us -> 70.5 us
    ppermute x44 -> x37, starting transfers between devices: 157 us -> 103 us  [send(): return lax.ppermute(array, 'seq', pairs)]
    ppermute x44 -> x37, waiting for transfers between devices: 151 us -> 188 us  [send(): return lax.ppermute(array, 'seq', pairs)]
    pallas_call x46 -> x45, Pallas kernels: 76.9 us -> 70.5 us  [call(): pl.pallas_call(trimmed, in_specs=list(in_specs) + [ANY] * extra, compiler...]
    unnamed x167 -> x110, local copies, waits for them, and re-layouts: 25.4 us -> 23.4 us
  transfers between devices with their start and end apart: 44 -> 37, of which waited for: 14 -> 18; matrix products, arithmetic and copies ran while one was open for 1% -> 1% of each run, Pallas kernels for 13% -> 13%
where the time goes in v7:
time: 412 us; the launch traced here: 409 us
  waiting for transfers between devices  188 us (46%)
  starting transfers between devices  103 us (25%)
  Pallas kernels  70.5 us (17%)
  local copies, waits for them, and re-layouts  26.6 us (6%)
  blocking collectives  16.5 us (4%)
    ppermute x37, waiting for transfers between devices, send(): return lax.ppermute(array, 'seq', pairs)  188 us
    ppermute x37, starting transfers between devices, send(): return lax.ppermute(array, 'seq', pairs)  103 us
    pallas_call x45, Pallas kernels, call(): pl.pallas_call(trimmed, in_specs=list(in_specs) + [ANY] * extra, compiler...  70.5 us
    unnamed x110, local copies, waits for them, and re-layouts  23.4 us
    all_to_all x1, blocking collectives, sum_gains(): lax.all_to_all(pieces, 'dp', split_axis=1, concat_axis=1, tiled=True)  8.31 us
  transfers between devices with their start and end apart: 37, of which 18 were waited for; matrix products, arithmetic and copies ran while one was open for 1% of the time, Pallas kernels for 13%

profile of v7, /device:TPU:0, one launch (start us, length us, event | category | flops | bytes accessed | tf_op | source)
XLA Modules:
  0.0 409.3 jit_solution(15123611620238522280)
XLA Ops:
  8.5 4.9 %collective-permute-start.1 = (bf16[8,768,128]{2,1,0:T(8,128)(2,1)}, bf16[8,768,128]{2,1,0:T(8,128)(2,1)S(1)}, u32[]{:S(2)}, u32[]{:S(2)}) collective-permute-start(bf16[8,768,128]{2,1,0:T(8,128)(2,1)} %pack_rows.7.refs_4_.refs_0_), channel_id=1, source_target_pairs={{0,2},{1,3},{6,4},{7,5},{8,10},{9,11},{14,12},{15,13},{16,18},{17,... | collective-permute-start | bytes 4718600 | tf_op jit(solution)/shard_map/ppermute | solution.py:627
  21.2 26.4 %collective-permute-done.1.refs_0_.refs_1_ = bf16[8,768,128]{2,1,0:T(8,128)(2,1)S(1)} collective-permute-done((bf16[8,768,128]{2,1,0:T(8,128)(2,1)}, bf16[8,768,128]{2,1,0:T(8,128)(2,1)S(1)}, u32[]{:S(2)}, u32[]{:S(2)}) %collective-permute-start.1) | collective-permute-done | bytes 1572896 | tf_op jit(solution)/shard_map/ppermute | solution.py:627
  48.8 4.6 %other_half.5.refs_5_ = bf16[4,3584,128]{2,1,0:T(8,128)(2,1)} custom-call(bf16[2,5120,128]{2,1,0:T(8,128)(2,1)} %bitcast.19, bf16[2,5120,128]{2,1,0:T(8,128)(2,1)} %bitcast.29, bf16[2,5120,128]{2,1,0:T(8,128)(2,1)} %bitcast.39, bf16[2,5120,128]{2,1,0:T(8,128)(2,1)} %bitcast.49, bf16[6144,128]{1,0:T(8,128)(2,1)} %forward_rows.9.refs_4_), custom_call_target="tpu_custom_call" | custom-call | bytes 7340032 | tf_op jit(solution)/shard_map/other_half/pallas_call | solution.py:46
  53.4 9.2 %collective-permute-start.6 = (bf16[8,768,128]{2,1,0:T(8,128)(2,1)S(1)}, bf16[8,768,128]{2,1,0:T(8,128)(2,1)}, u32[]{:S(2)}, u32[]{:S(2)}) collective-permute-start(bf16[8,768,128]{2,1,0:T(8,128)(2,1)S(1)} %copy-done.4), channel_id=1, source_target_pairs={{0,2},{1,3},{6,4},{7,5},{8,10},{9,11},{14,12},{15,13},{16,18},{17,... | collective-permute-start | bytes 4718600 | tf_op jit(solution)/shard_map/ppermute | solution.py:627
  67.7 4.7 %collective-permute-start.5 = (bf16[8,768,128]{2,1,0:T(8,128)(2,1)}, bf16[8,768,128]{2,1,0:T(8,128)(2,1)S(1)}, u32[]{:S(2)}, u32[]{:S(2)}) collective-permute-start(bf16[8,768,128]{2,1,0:T(8,128)(2,1)} %pack_rows.9.refs_1_.refs_2_.refs_0_), channel_id=1, source_target_pairs={{0,2},{1,3},{6,4},{7,5},{8,10},{9,11},{14,12},{15,13},{16,18},{17,... | collective-permute-start | bytes 4718600 | tf_op jit(solution)/shard_map/ppermute | solution.py:627
  72.4 23.6 %collective-permute-done.6.refs_0_.refs_1_ = bf16[8,768,128]{2,1,0:T(8,128)(2,1)} collective-permute-done((bf16[8,768,128]{2,1,0:T(8,128)(2,1)S(1)}, bf16[8,768,128]{2,1,0:T(8,128)(2,1)}, u32[]{:S(2)}, u32[]{:S(2)}) %collective-permute-start.6) | collective-permute-done | bytes 1572896 | tf_op jit(solution)/shard_map/ppermute | solution.py:627
  99.5 11.0 %collective-permute-start.9 = (bf16[8,768,128]{2,1,0:T(8,128)(2,1)}, bf16[8,768,128]{2,1,0:T(8,128)(2,1)S(1)}, u32[]{:S(2)}, u32[]{:S(2)}) collective-permute-start(bf16[8,768,128]{2,1,0:T(8,128)(2,1)} %pack_rows.10.refs_6_.refs_1_.refs_0_), channel_id=1, source_target_pairs={{0,2},{1,3},{6,4},{7,5},{8,10},{9,11},{14,12},{15,13},{16,18},{17,... | collective-permute-start | bytes 4718600 | tf_op jit(solution)/shard_map/ppermute | solution.py:627
  110.6 8.2 %all_gather.3 = f32[2,40,128]{2,0,1:T(2,128)S(1)} all-gather(f32[2,10,128]{2,0,1:T(2,128)S(1)} %pad_maximum_fusion.1), channel_id=1, replica_groups=mesh['dp'=4,'seq'=8] {'dp'}, dimensions={1}, use_global_device_ids=true | all-gather | bytes 51200 | tf_op jit(solution)/shard_map/all_gather | solution.py:749
  122.6 7.3 %collective-permute-done.5.refs_0_.refs_1_ = bf16[8,768,128]{2,1,0:T(8,128)(2,1)S(1)} collective-permute-done((bf16[8,768,128]{2,1,0:T(8,128)(2,1)}, bf16[8,768,128]{2,1,0:T(8,128)(2,1)S(1)}, u32[]{:S(2)}, u32[]{:S(2)}) %collective-permute-start.5) | collective-permute-done | bytes 1572896 | tf_op jit(solution)/shard_map/ppermute | solution.py:627
  134.3 12.5 %collective-permute-start.8 = (bf16[8,768,128]{2,1,0:T(8,128)(2,1)}, bf16[8,768,128]{2,1,0:T(8,128)(2,1)S(1)}, u32[]{:S(2)}, u32[]{:S(2)}) collective-permute-start(bf16[8,768,128]{2,1,0:T(8,128)(2,1)} %pack_rows.11.refs_6_.refs_1_.refs_0_), channel_id=1, source_target_pairs={{0,2},{1,3},{6,4},{7,5},{8,10},{9,11},{14,12},{15,13},{16,18},{17,... | collective-permute-start | bytes 4718600 | tf_op jit(solution)/shard_map/ppermute | solution.py:627
  150.6 13.0 %collective-permute-done.9.refs_0_.refs_1_ = bf16[8,768,128]{2,1,0:T(8,128)(2,1)S(1)} collective-permute-done((bf16[8,768,128]{2,1,0:T(8,128)(2,1)}, bf16[8,768,128]{2,1,0:T(8,128)(2,1)S(1)}, u32[]{:S(2)}, u32[]{:S(2)}) %collective-permute-start.9) | collective-permute-done | bytes 1572896 | tf_op jit(solution)/shard_map/ppermute | solution.py:627
  168.0 12.3 %collective-permute-start.15 = (bf16[8,768,128]{2,1,0:T(8,128)(2,1)}, bf16[8,768,128]{2,1,0:T(8,128)(2,1)S(1)}, u32[]{:S(2)}, u32[]{:S(2)}) collective-permute-start(bf16[8,768,128]{2,1,0:T(8,128)(2,1)} %pack_rows.12.refs_6_.refs_1_.refs_0_), channel_id=1, source_target_pairs={{0,2},{1,3},{6,4},{7,5},{8,10},{9,11},{14,12},{15,13},{16,18},{17,... | collective-permute-start | bytes 4718600 | tf_op jit(solution)/shard_map/ppermute | solution.py:627
  183.3 14.0 %collective-permute-done.8.refs_0_.refs_1_ = bf16[8,768,128]{2,1,0:T(8,128)(2,1)S(1)} collective-permute-done((bf16[8,768,128]{2,1,0:T(8,128)(2,1)}, bf16[8,768,128]{2,1,0:T(8,128)(2,1)S(1)}, u32[]{:S(2)}, u32[]{:S(2)}) %collective-permute-start.8) | collective-permute-done | bytes 1572896 | tf_op jit(solution)/shard_map/ppermute | solution.py:627
  206.3 23.5 %collective-permute-start.14 = (bf16[8,512,128]{2,1,0:T(8,128)(2,1)S(1)}, bf16[8,512,128]{2,1,0:T(8,128)(2,1)S(1)}, u32[]{:S(2)}, u32[]{:S(2)}) collective-permute-start(bf16[8,512,128]{2,1,0:T(8,128)(2,1)S(1)} %copy-done.6), channel_id=1, source_target_pairs={{0,2},{1,3},{6,4},{7,5},{8,10},{9,11},{14,12},{15,13},{16,18},{17,... | collective-permute-start | bytes 3145736 | tf_op jit(solution)/shard_map/ppermute | solution.py:627
  229.9 8.2 %collective-permute-done.17.refs_2_ = bf16[6,768,128]{2,1,0:T(8,128)(2,1)} collective-permute-done((bf16[6,768,128]{2,1,0:T(8,128)(2,1)}, bf16[6,768,128]{2,1,0:T(8,128)(2,1)}, u32[]{:S(2)}, u32[]{:S(2)}) %collective-permute-start.17) | collective-permute-done | bytes 1179680 | tf_op jit(solution)/shard_map/ppermute | solution.py:627
  238.0 4.2 %place_rows.12 = (bf16[2,5120,128]{2,1,0:T(8,128)(2,1)}, bf16[2,5120,128]{2,1,0:T(8,128)(2,1)}, bf16[2,5120,128]{2,1,0:T(8,128)(2,1)}, bf16[3,5120,128]{2,1,0:T(8,128)(2,1)}, f32[8,128]{1,0:T(8,128)}) custom-call(bf16[3,768,128]{2,1,0:T(8,128)(2,1)} %get-tuple-element.162.refs_0_, ...), custom_call_target="tpu_custom_call", output_to_operand_aliasing={{0}: (3, {}), {1}: (4, {}), {2}: (5, {}), {3}: (6, {})} | custom-call | bytes 2359296 | tf_op jit(solution)/shard_map/place_rows/pallas_call | solution.py:46
  247.9 13.6 %collective-permute-done.20.refs_2_ = bf16[6,768,128]{2,1,0:T(8,128)(2,1)S(1)} collective-permute-done((bf16[6,768,128]{2,1,0:T(8,128)(2,1)}, bf16[6,768,128]{2,1,0:T(8,128)(2,1)S(1)}, u32[]{:S(2)}, u32[]{:S(2)}) %collective-permute-start.20) | collective-permute-done | bytes 1179680 | tf_op jit(solution)/shard_map/ppermute | solution.py:627
  262.6 4.2 %place_rows.13 = (bf16[2,5120,128]{2,1,0:T(8,128)(2,1)}, bf16[2,5120,128]{2,1,0:T(8,128)(2,1)}, bf16[2,5120,128]{2,1,0:T(8,128)(2,1)}, bf16[3,5120,128]{2,1,0:T(8,128)(2,1)}, f32[8,128]{1,0:T(8,128)}) custom-call(bf16[3,768,128]{2,1,0:T(8,128)(2,1)} %get-tuple-element.176.refs_0_, ...), custom_call_target="tpu_custom_call", output_to_operand_aliasing={{0}: (3, {}), {1}: (4, {}), {2}: (5, {}), {3}: (6, {})} | custom-call | bytes 2359296 | tf_op jit(solution)/shard_map/place_rows/pallas_call | solution.py:46
  272.1 14.8 %collective-permute-done.22.refs_2_ = bf16[6,768,128]{2,1,0:T(8,128)(2,1)S(1)} collective-permute-done((bf16[6,768,128]{2,1,0:T(8,128)(2,1)}, bf16[6,768,128]{2,1,0:T(8,128)(2,1)S(1)}, u32[]{:S(2)}, u32[]{:S(2)}) %collective-permute-start.22) | collective-permute-done | bytes 1179680 | tf_op jit(solution)/shard_map/ppermute | solution.py:627
  288.0 4.1 %place_rows.14 = (bf16[2,5120,128]{2,1,0:T(8,128)(2,1)}, bf16[2,5120,128]{2,1,0:T(8,128)(2,1)}, bf16[2,5120,128]{2,1,0:T(8,128)(2,1)}, bf16[3,5120,128]{2,1,0:T(8,128)(2,1)}, f32[8,128]{1,0:T(8,128)}) custom-call(bf16[3,768,128]{2,1,0:T(8,128)(2,1)} %get-tuple-element.189.refs_0_, ...), custom_call_target="tpu_custom_call", output_to_operand_aliasing={{0}: (3, {}), {1}: (4, {}), {2}: (5, {}), {3}: (6, {})} | custom-call | bytes 2359296 | tf_op jit(solution)/shard_map/place_rows/pallas_call | solution.py:46
  296.1 24.8 %collective-permute-done.25.refs_2_ = bf16[6,768,128]{2,1,0:T(8,128)(2,1)S(1)} collective-permute-done((bf16[6,768,128]{2,1,0:T(8,128)(2,1)}, bf16[6,768,128]{2,1,0:T(8,128)(2,1)S(1)}, u32[]{:S(2)}, u32[]{:S(2)}) %collective-permute-start.25) | collective-permute-done | bytes 1179680 | tf_op jit(solution)/shard_map/ppermute | solution.py:627
  322.0 4.2 %place_rows.15 = (bf16[2,5120,128]{2,1,0:T(8,128)(2,1)}, bf16[2,5120,128]{2,1,0:T(8,128)(2,1)}, bf16[2,5120,128]{2,1,0:T(8,128)(2,1)}, bf16[3,5120,128]{2,1,0:T(8,128)(2,1)}, f32[8,128]{1,0:T(8,128)}) custom-call(bf16[3,768,128]{2,1,0:T(8,128)(2,1)} %get-tuple-element.210.refs_0_, ...), custom_call_target="tpu_custom_call", output_to_operand_aliasing={{0}: (3, {}), {1}: (4, {}), {2}: (5, {}), {3}: (6, {})} | custom-call | bytes 2359296 | tf_op jit(solution)/shard_map/place_rows/pallas_call | solution.py:46
  327.4 12.3 %collective-permute-done.24.refs_2_ = bf16[6,768,128]{2,1,0:T(8,128)(2,1)S(1)} collective-permute-done((bf16[6,768,128]{2,1,0:T(8,128)(2,1)}, bf16[6,768,128]{2,1,0:T(8,128)(2,1)S(1)}, u32[]{:S(2)}, u32[]{:S(2)}) %collective-permute-start.24) | collective-permute-done | bytes 1179680 | tf_op jit(solution)/shard_map/ppermute | solution.py:627
  340.8 4.3 %place_rows.16 = (bf16[2,5120,128]{2,1,0:T(8,128)(2,1)}, bf16[2,5120,128]{2,1,0:T(8,128)(2,1)}, bf16[2,5120,128]{2,1,0:T(8,128)(2,1)}, bf16[3,5120,128]{2,1,0:T(8,128)(2,1)}, f32[8,128]{1,0:T(8,128)}) custom-call(bf16[3,768,128]{2,1,0:T(8,128)(2,1)} %get-tuple-element.207.refs_0_, ...), custom_call_target="tpu_custom_call", output_to_operand_aliasing={{0}: (3, {}), {1}: (4, {}), {2}: (5, {}), {3}: (6, {})} | custom-call | bytes 2359296 | tf_op jit(solution)/shard_map/place_rows/pallas_call | solution.py:46
  357.2 8.3 %all_to_all.5 = f32[2,4,10,128]{3,0,2,1:T(2,128)S(1)} all-to-all(f32[2,4,10,128]{3,0,2,1:T(2,128)S(1)} %copy.67), channel_id=1, replica_groups=mesh['dp'=4,'seq'=8] {'dp'}, dimensions={1} | all-to-all | bytes 81920 | tf_op jit(solution)/shard_map/all_to_all | solution.py:647
  366.1 4.6 %place_rows.17 = (bf16[2,5120,128]{2,1,0:T(8,128)(2,1)}, bf16[2,5120,128]{2,1,0:T(8,128)(2,1)}, bf16[2,5120,128]{2,1,0:T(8,128)(2,1)}, f32[8,128]{1,0:T(8,128)}) custom-call(bf16[3,5120,128]{2,1,0:T(8,128)(2,1)} %collective-permute-done.33.refs_0_, ...), custom_call_target="tpu_custom_call", output_to_operand_aliasing={{0}: (1, {}), {1}: (2, {}), {2}: (3, {})} | custom-call | bytes 7864320 | tf_op jit(solution)/shard_map/place_rows/pallas_call | solution.py:46
  370.7 4.4 %collective-permute-done.32.refs_3_ = bf16[3,768,128]{2,1,0:T(8,128)(2,1)S(1)} collective-permute-done((bf16[3,768,128]{2,1,0:T(8,128)(2,1)S(1)}, bf16[3,768,128]{2,1,0:T(8,128)(2,1)S(1)}, u32[]{:S(2)}, u32[]{:S(2)}) %collective-permute-start.32) | collective-permute-done | bytes 589856 | tf_op jit(solution)/shard_map/ppermute | solution.py:627
  375.9 4.1 %place_rows.18 = (bf16[2,5120,128]{2,1,0:T(8,128)(2,1)}, bf16[2,5120,128]{2,1,0:T(8,128)(2,1)}, bf16[2,5120,128]{2,1,0:T(8,128)(2,1)}, f32[8,128]{1,0:T(8,128)}) custom-call(bf16[3,768,128]{2,1,0:T(8,128)(2,1)} %get-tuple-element.238.refs_0_, bf16[3,768,128]{2,1,0:T(8,128)(2,1)} %copy-done.23, ...), custom_call_target="tpu_custom_call", output_to_operand_aliasing={{0}: (4, {}), {1}: (5, {}), {2}: (6, {})} | custom-call | bytes 2359296 | tf_op jit(solution)/shard_map/place_rows/pallas_call | solution.py:46
  380.1 5.5 %collective-permute-done.28.refs_2_ = bf16[3,512,128]{2,1,0:T(8,128)(2,1)} collective-permute-done((bf16[3,512,128]{2,1,0:T(8,128)(2,1)}, bf16[3,512,128]{2,1,0:T(8,128)(2,1)}, u32[]{:S(2)}, u32[]{:S(2)}) %collective-permute-start.28) | collective-permute-done | bytes 393248 | tf_op jit(solution)/shard_map/ppermute | solution.py:627
  385.5 6.5 %collective-permute-done.29.refs_3_ = bf16[3,512,128]{2,1,0:T(8,128)(2,1)} collective-permute-done((bf16[3,512,128]{2,1,0:T(8,128)(2,1)}, bf16[3,512,128]{2,1,0:T(8,128)(2,1)}, u32[]{:S(2)}, u32[]{:S(2)}) %collective-permute-start.29) | collective-permute-done | bytes 393248 | tf_op jit(solution)/shard_map/ppermute | solution.py:627
  392.1 4.0 place_rows.19
  402.0 6.7 %collective-permute-done.36 = f32[2,10,128]{2,1,0:T(8,128)S(1)} collective-permute-done((f32[2,10,128]{2,1,0:T(8,128)S(1)}, f32[2,10,128]{2,1,0:T(8,128)S(1)}, u32[]{:S(2)}, u32[]{:S(2)}) %collective-permute-start.36) | collective-permute-done | bytes 10272 | tf_op jit(solution)/shard_map/ppermute | solution.py:627
  (216 shorter events, 93.7 us)
Async XLA Ops:
  8.5 39.1 %collective-permute-start.1 = (bf16[8,768,128]{2,1,0:T(8,128)(2,1)}, bf16[8,768,128]{2,1,0:T(8,128)(2,1)S(1)}, u32[]{:S(2)}, u32[]{:S(2)}) collective-permute-start(bf16[8,768,128]{2,1,0:T(8,128)(2,1)} %pack_rows.7.refs_4_.refs_0_), channel_id=1, source_target_pairs={{0,2},{1,3},{6,4},{7,5},{8,10},{9,11},{14,12},{15,13},{16,18},{17,... | collective-permute-start | bytes 4718600 | tf_op jit(solution)/shard_map/ppermute | solution.py:627
  15.4 5.8 %collective-permute-start.3 = (bf16[3072,128]{1,0:T(8,128)(2,1)}, bf16[3072,128]{1,0:T(8,128)(2,1)S(1)}, u32[]{:S(2)}, u32[]{:S(2)}) collective-permute-start(bf16[3072,128]{1,0:T(8,128)(2,1)} %forward_rows.8.refs_5_), channel_id=1, source_target_pairs={{2,4},{3,5},{4,2},{5,3},{10,12},{11,13},{12,10},{13,11},{18,20},{1... | collective-permute-start | bytes 2359304 | tf_op jit(solution)/shard_map/ppermute | solution.py:627
  53.4 10.0 %collective-permute-start.4 = (bf16[4,3584,128]{2,1,0:T(8,128)(2,1)}, bf16[4,3584,128]{2,1,0:T(8,128)(2,1)S(1)}, u32[]{:S(2)}, u32[]{:S(2)}) collective-permute-start(bf16[4,3584,128]{2,1,0:T(8,128)(2,1)} %other_half.5.refs_5_), channel_id=1, source_target_pairs={{0,1},{1,0},{2,3},{3,2},{4,5},{5,4},{6,7},{7,6},{8,9},{9,8},{10,11... | collective-permute-start | bytes 11010056 | tf_op jit(solution)/shard_map/ppermute | solution.py:627
  53.4 42.7 %collective-permute-start.6 = (bf16[8,768,128]{2,1,0:T(8,128)(2,1)S(1)}, bf16[8,768,128]{2,1,0:T(8,128)(2,1)}, u32[]{:S(2)}, u32[]{:S(2)}) collective-permute-start(bf16[8,768,128]{2,1,0:T(8,128)(2,1)S(1)} %copy-done.4), channel_id=1, source_target_pairs={{0,2},{1,3},{6,4},{7,5},{8,10},{9,11},{14,12},{15,13},{16,18},{17,... | collective-permute-start | bytes 4718600 | tf_op jit(solution)/shard_map/ppermute | solution.py:627
  62.6 56.2 %collective-permute-start.7 = (bf16[6144,128]{1,0:T(8,128)(2,1)}, bf16[6144,128]{1,0:T(8,128)(2,1)S(1)}, u32[]{:S(2)}, u32[]{:S(2)}) collective-permute-start(bf16[6144,128]{1,0:T(8,128)(2,1)} %forward_rows.9.refs_4_), channel_id=1, source_target_pairs={{2,4},{3,5},{4,2},{5,3},{10,12},{11,13},{12,10},{13,11},{18,20},{1... | collective-permute-start | bytes 4718600 | tf_op jit(solution)/shard_map/ppermute | solution.py:627
  67.7 62.2 %collective-permute-start.5 = (bf16[8,768,128]{2,1,0:T(8,128)(2,1)}, bf16[8,768,128]{2,1,0:T(8,128)(2,1)S(1)}, u32[]{:S(2)}, u32[]{:S(2)}) collective-permute-start(bf16[8,768,128]{2,1,0:T(8,128)(2,1)} %pack_rows.9.refs_1_.refs_2_.refs_0_), channel_id=1, source_target_pairs={{0,2},{1,3},{6,4},{7,5},{8,10},{9,11},{14,12},{15,13},{16,18},{17,... | collective-permute-start | bytes 4718600 | tf_op jit(solution)/shard_map/ppermute | solution.py:627
  96.1 50.8 %collective-permute-start.10 = (bf16[6144,128]{1,0:T(8,128)(2,1)}, bf16[6144,128]{1,0:T(8,128)(2,1)S(1)}, u32[]{:S(2)}, u32[]{:S(2)}) collective-permute-start(bf16[6144,128]{1,0:T(8,128)(2,1)} %forward_rows.10.refs_5_), channel_id=1, source_target_pairs={{2,4},{3,5},{4,2},{5,3},{10,12},{11,13},{12,10},{13,11},{18,20},{1... | collective-permute-start | bytes 4718600 | tf_op jit(solution)/shard_map/ppermute | solution.py:627
  99.5 64.1 %collective-permute-start.9 = (bf16[8,768,128]{2,1,0:T(8,128)(2,1)}, bf16[8,768,128]{2,1,0:T(8,128)(2,1)S(1)}, u32[]{:S(2)}, u32[]{:S(2)}) collective-permute-start(bf16[8,768,128]{2,1,0:T(8,128)(2,1)} %pack_rows.10.refs_6_.refs_1_.refs_0_), channel_id=1, source_target_pairs={{0,2},{1,3},{6,4},{7,5},{8,10},{9,11},{14,12},{15,13},{16,18},{17,... | collective-permute-start | bytes 4718600 | tf_op jit(solution)/shard_map/ppermute | solution.py:627
  121.3 28.6 %collective-permute-start.11 = (bf16[6,768,128]{2,1,0:T(8,128)(2,1)}, bf16[6,768,128]{2,1,0:T(8,128)(2,1)}, u32[]{:S(2)}, u32[]{:S(2)}) collective-permute-start(bf16[6,768,128]{2,1,0:T(8,128)(2,1)} %get-tuple-element.144), channel_id=1, source_target_pairs={{2,0},{3,1},{4,6},{5,7},{10,8},{11,9},{12,14},{13,15},{18,16},{19,... | collective-permute-start | bytes 3538952 | tf_op jit(solution)/shard_map/ppermute | solution.py:627
  131.1 49.1 %collective-permute-start.12 = (bf16[6336,128]{1,0:T(8,128)(2,1)}, bf16[6336,128]{1,0:T(8,128)(2,1)S(1)}, u32[]{:S(2)}, u32[]{:S(2)}) collective-permute-start(bf16[6336,128]{1,0:T(8,128)(2,1)} %forward_rows.11.refs_5_), channel_id=1, source_target_pairs={{2,4},{3,5},{4,2},{5,3},{10,12},{11,13},{12,10},{13,11},{18,20},{1... | collective-permute-start | bytes 4866056 | tf_op jit(solution)/shard_map/ppermute | solution.py:627
  134.3 63.0 %collective-permute-start.8 = (bf16[8,768,128]{2,1,0:T(8,128)(2,1)}, bf16[8,768,128]{2,1,0:T(8,128)(2,1)S(1)}, u32[]{:S(2)}, u32[]{:S(2)}) collective-permute-start(bf16[8,768,128]{2,1,0:T(8,128)(2,1)} %pack_rows.11.refs_6_.refs_1_.refs_0_), channel_id=1, source_target_pairs={{0,2},{1,3},{6,4},{7,5},{8,10},{9,11},{14,12},{15,13},{16,18},{17,... | collective-permute-start | bytes 4718600 | tf_op jit(solution)/shard_map/ppermute | solution.py:627
  148.7 34.0 %collective-permute-start.13 = (bf16[6,768,128]{2,1,0:T(8,128)(2,1)}, bf16[6,768,128]{2,1,0:T(8,128)(2,1)}, u32[]{:S(2)}, u32[]{:S(2)}) collective-permute-start(bf16[6,768,128]{2,1,0:T(8,128)(2,1)} %get-tuple-element.150), channel_id=1, source_target_pairs={{2,0},{3,1},{4,6},{5,7},{10,8},{11,9},{12,14},{13,15},{18,16},{19,... | collective-permute-start | bytes 3538952 | tf_op jit(solution)/shard_map/ppermute | solution.py:627
  164.7 37.9 %collective-permute-start.16 = (bf16[6336,128]{1,0:T(8,128)(2,1)}, bf16[6336,128]{1,0:T(8,128)(2,1)S(1)}, u32[]{:S(2)}, u32[]{:S(2)}) collective-permute-start(bf16[6336,128]{1,0:T(8,128)(2,1)} %forward_rows.12.refs_5_), channel_id=1, source_target_pairs={{2,4},{3,5},{4,2},{5,3},{10,12},{11,13},{12,10},{13,11},{18,20},{1... | collective-permute-start | bytes 4866056 | tf_op jit(solution)/shard_map/ppermute | solution.py:627
  168.0 74.3 %collective-permute-start.15 = (bf16[8,768,128]{2,1,0:T(8,128)(2,1)}, bf16[8,768,128]{2,1,0:T(8,128)(2,1)S(1)}, u32[]{:S(2)}, u32[]{:S(2)}) collective-permute-start(bf16[8,768,128]{2,1,0:T(8,128)(2,1)} %pack_rows.12.refs_6_.refs_1_.refs_0_), channel_id=1, source_target_pairs={{0,2},{1,3},{6,4},{7,5},{8,10},{9,11},{14,12},{15,13},{16,18},{17,... | collective-permute-start | bytes 4718600 | tf_op jit(solution)/shard_map/ppermute | solution.py:627
  198.5 45.7 %collective-permute-start.19 = (bf16[6336,128]{1,0:T(8,128)(2,1)}, bf16[6336,128]{1,0:T(8,128)(2,1)S(1)}, u32[]{:S(2)}, u32[]{:S(2)}) collective-permute-start(bf16[6336,128]{1,0:T(8,128)(2,1)} %forward_rows.13.refs_5_), channel_id=1, source_target_pairs={{2,4},{3,5},{4,2},{5,3},{10,12},{11,13},{12,10},{13,11},{18,20},{1... | collective-permute-start | bytes 4866056 | tf_op jit(solution)/shard_map/ppermute | solution.py:627
  199.2 38.8 %collective-permute-start.17 = (bf16[6,768,128]{2,1,0:T(8,128)(2,1)}, bf16[6,768,128]{2,1,0:T(8,128)(2,1)}, u32[]{:S(2)}, u32[]{:S(2)}) collective-permute-start(bf16[6,768,128]{2,1,0:T(8,128)(2,1)} %get-tuple-element.164), channel_id=1, source_target_pairs={{2,0},{3,1},{4,6},{5,7},{10,8},{11,9},{12,14},{13,15},{18,16},{19,... | collective-permute-start | bytes 3538952 | tf_op jit(solution)/shard_map/ppermute | solution.py:627
  205.0 56.5 %collective-permute-start.20 = (bf16[6,768,128]{2,1,0:T(8,128)(2,1)}, bf16[6,768,128]{2,1,0:T(8,128)(2,1)S(1)}, u32[]{:S(2)}, u32[]{:S(2)}) collective-permute-start(bf16[6,768,128]{2,1,0:T(8,128)(2,1)} %get-tuple-element.178), channel_id=1, source_target_pairs={{2,0},{3,1},{4,6},{5,7},{10,8},{11,9},{12,14},{13,15},{18,16},{19,... | collective-permute-start | bytes 3538952 | tf_op jit(solution)/shard_map/ppermute | solution.py:627
  206.3 60.4 %collective-permute-start.14 = (bf16[8,512,128]{2,1,0:T(8,128)(2,1)S(1)}, bf16[8,512,128]{2,1,0:T(8,128)(2,1)S(1)}, u32[]{:S(2)}, u32[]{:S(2)}) collective-permute-start(bf16[8,512,128]{2,1,0:T(8,128)(2,1)S(1)} %copy-done.6), channel_id=1, source_target_pairs={{0,2},{1,3},{6,4},{7,5},{8,10},{9,11},{14,12},{15,13},{16,18},{17,... | collective-permute-start | bytes 3145736 | tf_op jit(solution)/shard_map/ppermute | solution.py:627
  243.4 25.0 %collective-permute-start.18 = (bf16[5312,128]{1,0:T(8,128)(2,1)}, bf16[5312,128]{1,0:T(8,128)(2,1)S(1)}, u32[]{:S(2)}, u32[]{:S(2)}) collective-permute-start(bf16[5312,128]{1,0:T(8,128)(2,1)} %forward_rows.14.refs_6_), channel_id=1, source_target_pairs={{2,4},{3,5},{4,2},{5,3},{10,12},{11,13},{12,10},{13,11},{18,20},{1... | collective-permute-start | bytes 4079624 | tf_op jit(solution)/shard_map/ppermute | solution.py:627
  246.6 40.3 %collective-permute-start.22 = (bf16[6,768,128]{2,1,0:T(8,128)(2,1)}, bf16[6,768,128]{2,1,0:T(8,128)(2,1)S(1)}, u32[]{:S(2)}, u32[]{:S(2)}) collective-permute-start(bf16[6,768,128]{2,1,0:T(8,128)(2,1)} %get-tuple-element.191), channel_id=1, source_target_pairs={{2,0},{3,1},{4,6},{5,7},{10,8},{11,9},{12,14},{13,15},{18,16},{19,... | collective-permute-start | bytes 3538952 | tf_op jit(solution)/shard_map/ppermute | solution.py:627
  267.8 24.4 %collective-permute-start.21 = (bf16[2240,128]{1,0:T(8,128)(2,1)}, bf16[2240,128]{1,0:T(8,128)(2,1)S(1)}, u32[]{:S(2)}, u32[]{:S(2)}) collective-permute-start(bf16[2240,128]{1,0:T(8,128)(2,1)} %forward_rows.15.refs_6_), channel_id=1, source_target_pairs={{2,4},{3,5},{4,2},{5,3},{10,12},{11,13},{12,10},{13,11},{18,20},{1... | collective-permute-start | bytes 1720328 | tf_op jit(solution)/shard_map/ppermute | solution.py:627
  270.8 50.2 %collective-permute-start.25 = (bf16[6,768,128]{2,1,0:T(8,128)(2,1)}, bf16[6,768,128]{2,1,0:T(8,128)(2,1)S(1)}, u32[]{:S(2)}, u32[]{:S(2)}) collective-permute-start(bf16[6,768,128]{2,1,0:T(8,128)(2,1)} %get-tuple-element.212), channel_id=1, source_target_pairs={{2,0},{3,1},{4,6},{5,7},{10,8},{11,9},{12,14},{13,15},{18,16},{19,... | collective-permute-start | bytes 3538952 | tf_op jit(solution)/shard_map/ppermute | solution.py:627
  294.2 45.5 %collective-permute-start.24 = (bf16[6,768,128]{2,1,0:T(8,128)(2,1)}, bf16[6,768,128]{2,1,0:T(8,128)(2,1)S(1)}, u32[]{:S(2)}, u32[]{:S(2)}) collective-permute-start(bf16[6,768,128]{2,1,0:T(8,128)(2,1)} %get-tuple-element.209), channel_id=1, source_target_pairs={{2,0},{3,1},{4,6},{5,7},{10,8},{11,9},{12,14},{13,15},{18,16},{19,... | collective-permute-start | bytes 3538952 | tf_op jit(solution)/shard_map/ppermute | solution.py:627
  295.5 30.7 %collective-permute-start.26 = (bf16[192,128]{1,0:T(8,128)(2,1)S(1)}, bf16[192,128]{1,0:T(8,128)(2,1)S(1)}, u32[]{:S(2)}, u32[]{:S(2)}) collective-permute-start(bf16[192,128]{1,0:T(8,128)(2,1)S(1)} %copy-done.53), channel_id=1, source_target_pairs={{4,2},{5,3},{12,10},{13,11},{20,18},{21,19},{28,26},{29,27}} | collective-permute-start | bytes 147464 | tf_op jit(solution)/shard_map/ppermute | solution.py:627
  345.1 8.9 %collective-permute-start.33 = (bf16[3,5120,128]{2,1,0:T(8,128)(2,1)}, bf16[3,5120,128]{2,1,0:T(8,128)(2,1)}, u32[]{:S(2)}, u32[]{:S(2)}) collective-permute-start(bf16[3,5120,128]{2,1,0:T(8,128)(2,1)} %get-tuple-element.242), channel_id=1, source_target_pairs={{0,1},{1,0},{2,3},{3,2},{4,5},{5,4},{6,7},{7,6},{8,9},{9,8},{10,11... | collective-permute-start | bytes 11796488 | tf_op jit(solution)/shard_map/ppermute | solution.py:627
  345.1 7.6 %collective-permute-start.30 = (bf16[3,768,128]{2,1,0:T(8,128)(2,1)S(1)}, bf16[3,768,128]{2,1,0:T(8,128)(2,1)S(1)}, u32[]{:S(2)}, u32[]{:S(2)}) collective-permute-start(bf16[3,768,128]{2,1,0:T(8,128)(2,1)S(1)} %copy-done.26), channel_id=1, source_target_pairs={{0,1},{1,0},{2,3},{3,2},{4,5},{5,4},{6,7},{7,6},{8,9},{9,8},{10,11... | collective-permute-start | bytes 1769480 | tf_op jit(solution)/shard_map/ppermute | solution.py:627
  346.3 24.5 %collective-permute-start.31 = (bf16[3,768,128]{2,1,0:T(8,128)(2,1)S(1)}, bf16[3,768,128]{2,1,0:T(8,128)(2,1)S(1)}, u32[]{:S(2)}, u32[]{:S(2)}) collective-permute-start(bf16[3,768,128]{2,1,0:T(8,128)(2,1)S(1)} %copy-done.27), channel_id=1, source_target_pairs={{2,0},{3,1},{4,6},{5,7},{10,8},{11,9},{12,14},{13,15},{18,16},{19,... | collective-permute-start | bytes 1769480 | tf_op jit(solution)/shard_map/ppermute | solution.py:627
  347.6 27.5 %collective-permute-start.32 = (bf16[3,768,128]{2,1,0:T(8,128)(2,1)S(1)}, bf16[3,768,128]{2,1,0:T(8,128)(2,1)S(1)}, u32[]{:S(2)}, u32[]{:S(2)}) collective-permute-start(bf16[3,768,128]{2,1,0:T(8,128)(2,1)S(1)} %copy-done.28), channel_id=1, source_target_pairs={{2,1},{3,0},{4,7},{5,6},{10,9},{11,8},{12,15},{13,14},{18,17},{19,... | collective-permute-start | bytes 1769480 | tf_op jit(solution)/shard_map/ppermute | solution.py:627
  350.3 29.7 %collective-permute-start.27 = (bf16[3,512,128]{2,1,0:T(8,128)(2,1)}, bf16[3,512,128]{2,1,0:T(8,128)(2,1)S(1)}, u32[]{:S(2)}, u32[]{:S(2)}) collective-permute-start(bf16[3,512,128]{2,1,0:T(8,128)(2,1)} %get-tuple-element.235), channel_id=1, source_target_pairs={{0,1},{1,0},{2,3},{3,2},{4,5},{5,4},{6,7},{7,6},{8,9},{9,8},{10,11... | collective-permute-start | bytes 1179656 | tf_op jit(solution)/shard_map/ppermute | solution.py:627
  352.7 32.9 %collective-permute-start.28 = (bf16[3,512,128]{2,1,0:T(8,128)(2,1)}, bf16[3,512,128]{2,1,0:T(8,128)(2,1)}, u32[]{:S(2)}, u32[]{:S(2)}) collective-permute-start(bf16[3,512,128]{2,1,0:T(8,128)(2,1)} %get-tuple-element.236), channel_id=1, source_target_pairs={{2,0},{3,1},{4,6},{5,7},{10,8},{11,9},{12,14},{13,15},{18,16},{19,... | collective-permute-start | bytes 1179656 | tf_op jit(solution)/shard_map/ppermute | solution.py:627
  354.0 38.1 %collective-permute-start.29 = (bf16[3,512,128]{2,1,0:T(8,128)(2,1)}, bf16[3,512,128]{2,1,0:T(8,128)(2,1)}, u32[]{:S(2)}, u32[]{:S(2)}) collective-permute-start(bf16[3,512,128]{2,1,0:T(8,128)(2,1)} %get-tuple-element.237), channel_id=1, source_target_pairs={{2,1},{3,0},{4,7},{5,6},{10,9},{11,8},{12,15},{13,14},{18,17},{19,... | collective-permute-start | bytes 1179656 | tf_op jit(solution)/shard_map/ppermute | solution.py:627
  400.7 8.0 %collective-permute-start.36 = (f32[2,10,128]{2,1,0:T(8,128)S(1)}, f32[2,10,128]{2,1,0:T(8,128)S(1)}, u32[]{:S(2)}, u32[]{:S(2)}) collective-permute-start(f32[2,10,128]{2,1,0:T(8,128)S(1)} %add.112), channel_id=1, source_target_pairs={{2,0},{3,1},{4,6},{5,7},{10,8},{11,9},{12,14},{13,15},{18,16},{19,... | collective-permute-start | bytes 30728 | tf_op jit(solution)/shard_map/ppermute | solution.py:627
  (60 other events, 270.4 us)
